TPU v7x, 32 devices: a whole 2x2x4 slice. The times are simulated.
32 devices in a mesh: rows: 8 (over z, core), expert: 4 (over y, x).
Axes of the slice: x: 2, y: 2, z: 4, core: 2. Of those that a mesh axis runs over, the one named last changes fastest.
Arguments:
- rows_in: float32 [32768, 256], P(('rows', 'expert')), may hold values from -6 to 6
- pred_grad: float32 [32768, 2], P(('rows', 'expert')), may hold values from -6 to 6
- lengths: int32 [256], replicated, may hold values from 1 to 200, 32768 in all
- session_type: int32 [256], replicated, may hold values from 0 to 31
- expert_in: bfloat16 [2, 16, 256, 256], P(None, 'expert'), may hold values from -0.375 to 0.375
- expert_in_bias: float32 [2, 16, 256], P(None, 'expert'), may hold values from -2 to 2
- expert_out: bfloat16 [2, 16, 256, 256], P(None, 'expert'), may hold values from -0.375 to 0.375
- expert_out_bias: float32 [2, 16, 256], P(None, 'expert'), may hold values from -2 to 2
- selector_logits: float32 [2, 32, 2, 4, 4], replicated, may hold values from -8 to 8, as said below
- selector_mix: float32 [2, 32, 2, 4], replicated, may hold values from -4 to 4
- tower_in: bfloat16 [2, 256, 128], replicated, may hold values from -0.375 to 0.375
- tower_bias: float32 [2, 128], replicated, may hold values from -2 to 2
- tower_out: float32 [2, 128], replicated, may hold values from -0.5 to 0.5
Outputs:
- predictions: float32 [32768, 2], P(('rows', 'expert'))
- rows_grad: float32 [32768, 256], P(('rows', 'expert'))
- expert_in_grad: float32 [2, 16, 256, 256], P(None, 'expert')
- expert_in_bias_grad: float32 [2, 16, 256], P(None, 'expert')
- expert_out_grad: float32 [2, 16, 256, 256], P(None, 'expert')
- expert_out_bias_grad: float32 [2, 16, 256], P(None, 'expert')
- logits_grad: float32 [2, 32, 2, 4, 4], replicated
- mix_grad: float32 [2, 32, 2, 4], replicated
- tower_in_grad: float32 [2, 256, 128], replicated
- tower_bias_grad: float32 [2, 128], replicated
- tower_out_grad: float32 [2, 128], replicated
Inputs may be any that keep to these rules, and one draw needn't show every extreme that they name: The lengths sum to 32768. `selector_logits`: every logit has magnitude 6 to 8, except that in some selectors one bit, the same for all selectors of one layer and type, lies in [-3, 3]; all selectors of one layer and type reach experts of at most 4 pairs that differ in that bit, so a row has nonzero gate on at most 8 of the 16 experts of a layer and exactly zero gate on the others.
All inputs are finite; a program needn't handle non-finite values.
Results may differ from a plain program's by a relative error of at most 0.018.
Values may be sent and summed in bfloat16 or wider, within the bound.
No kernel may reach another device: no remote copies, remote signals or barrier semaphores. Data moves between devices by JAX's collectives and lax.ppermute only.
A program may use at most 192 MiB of HBM per device.

v0:
```python
import jax
import jax.numpy as jnp
from jax import lax
from jax.sharding import PartitionSpec as P

SHARPNESS = 10.0
EXACT = lax.Precision.HIGHEST


def for_sending(array):
    return jax.tree.map(lambda a: a.astype(jnp.bfloat16) if a.dtype == jnp.float32 else a, array)


def smooth_step(logit):
    cubic = -2.0 / SHARPNESS**3 * logit**3 + 1.5 / SHARPNESS * logit + 0.5
    return jnp.where(logit <= -SHARPNESS / 2, 0.0, jnp.where(logit >= SHARPNESS / 2, 1.0, cubic))


def gate_table(logits, mixing):
    width_bits = logits.shape[-1]
    numbers = jnp.arange(2**width_bits)
    powers = 2 ** jnp.arange(width_bits)
    bit_table = (numbers[:, None] // powers[None, :] % 2).astype(logits.dtype)
    stepped = smooth_step(logits)[..., None, :]
    factor = bit_table * stepped + (1.0 - bit_table) * (1.0 - stepped)
    reaches = jnp.prod(factor, axis=-1)
    shares = jax.nn.softmax(mixing, axis=-1)[..., None]
    return jnp.sum(shares * reaches, axis=-2)


def row_types(lengths, session_type, offset, height, type_count):
    session_end = jnp.cumsum(lengths)
    session_begin = session_end - lengths
    position = offset + jnp.arange(height, dtype=jnp.int32)
    member = (
        (session_begin[None, :] <= position[:, None]) & (position[:, None] < session_end[None, :])
    ).astype(jnp.float32)
    type_hot = (session_type[:, None] == jnp.arange(type_count, dtype=jnp.int32)[None, :]).astype(
        jnp.float32
    )
    return jnp.dot(member, type_hot, precision=EXACT)


def expert_result(before, weight_out, bias_out, form):
    hidden = jax.nn.gelu(before).astype(jnp.bfloat16)
    return (
        jnp.einsum(form, hidden, weight_out, preferred_element_type=jnp.float32) + bias_out
    ).astype(jnp.bfloat16)


def run_layer(stream, gate_rows, weights):
    weight_in, bias_in, weight_out, bias_out = weights
    groups = lax.axis_size("expert")
    owned = weight_in.shape[0]
    height, width = stream.shape
    stream_low = stream.astype(jnp.bfloat16)
    in_use = jnp.sum(gate_rows, axis=1) > 0.0
    sendable = jnp.where(in_use.T[:, :, None], stream_low[None], jnp.zeros((), jnp.bfloat16))
    sendable = sendable.reshape(groups, owned, height, width)
    incoming_rows = lax.all_to_all(sendable, "expert", split_axis=0, concat_axis=0, tiled=True)
    before = (
        jnp.einsum("serd,edh->serh", incoming_rows, weight_in, preferred_element_type=jnp.float32)
        + bias_in[None, :, None, :]
    )
    produced = expert_result(before, weight_out, bias_out[None, :, None, :], "serh,ehd->serd")
    returned = lax.all_to_all(produced, "expert", split_axis=0, concat_axis=0, tiled=True)
    returned, incoming_rows, before = (returned, incoming_rows, before)
    return (returned.reshape(groups * owned, height, width), (incoming_rows, before))


def back_layer(stream, gate_rows, weights, outputs, stored, grad_out):
    weight_in = weights[0]
    weight_out = weights[2]
    groups = lax.axis_size("expert")
    owned = weight_in.shape[0]
    height, width = stream.shape
    gate_reduced = gate_rows.astype(jnp.bfloat16)
    gate_grad = jnp.einsum(
        "erd,rtd->rte", outputs, grad_out, precision=EXACT, preferred_element_type=jnp.float32
    )
    result_grad = jnp.einsum(
        "rte,rtd->erd", gate_reduced, grad_out, precision=EXACT, preferred_element_type=jnp.float32
    ).astype(jnp.bfloat16)
    incoming_rows, before = stored
    arrived = lax.all_to_all(
        result_grad.reshape(groups, owned, height, width),
        "expert",
        split_axis=0,
        concat_axis=0,
        tiled=True,
    )
    hidden = jax.nn.gelu(before).astype(jnp.bfloat16)
    hidden_grad = jnp.einsum(
        "serd,ehd->serh", arrived, weight_out, preferred_element_type=jnp.float32
    )
    before_grad = jax.vjp(jax.nn.gelu, before)[1](hidden_grad)[0].astype(jnp.bfloat16)
    grads = (
        jnp.einsum(
            "serd,serh->edh", incoming_rows, before_grad, preferred_element_type=jnp.float32
        ),
        jnp.sum(before_grad, axis=(0, 2), dtype=jnp.float32),
        jnp.einsum("serh,serd->ehd", hidden, arrived, preferred_element_type=jnp.float32),
        jnp.sum(arrived, axis=(0, 2), dtype=jnp.float32),
    )
    row_term = jnp.einsum(
        "serh,edh->serd", before_grad, weight_in, preferred_element_type=jnp.float32
    ).astype(jnp.bfloat16)
    homeward = lax.all_to_all(row_term, "expert", split_axis=0, concat_axis=0, tiled=True)
    input_grad = jnp.sum(homeward, axis=(0, 1), dtype=jnp.float32)
    return (gate_grad, input_grad, grads)


def body(
    rows_in,
    pred_grad,
    lengths,
    session_type,
    expert_in,
    expert_in_bias,
    expert_out,
    expert_out_bias,
    selector_logits,
    selector_mix,
    tower_in,
    tower_bias,
    tower_out,
):
    height, width = rows_in.shape
    layers = expert_in.shape[0]
    type_count = selector_logits.shape[1]
    task_count = selector_logits.shape[2]
    offset = lax.axis_index(("rows", "expert")) * height
    type_rows = row_types(lengths, session_type, offset, height, type_count)
    gate_values = gate_table(selector_logits, selector_mix)
    experts = gate_values.shape[-1]
    gate_rows = [
        jnp.dot(
            type_rows,
            gate_values[layer_at].reshape(type_count, task_count * experts),
            precision=EXACT,
        ).reshape(height, task_count, experts)
        for layer_at in range(layers)
    ]
    weights = [
        (
            expert_in[layer_at],
            expert_in_bias[layer_at],
            expert_out[layer_at],
            expert_out_bias[layer_at],
        )
        for layer_at in range(layers)
    ]
    streams = [rows_in]
    stored = []
    blended = None
    for layer_at in range(layers):
        outputs, keeping = run_layer(streams[-1], gate_rows[layer_at], weights[layer_at])
        blended = jnp.einsum(
            "rte,erd->rtd",
            gate_rows[layer_at].astype(jnp.bfloat16),
            outputs,
            preferred_element_type=jnp.float32,
        )
        stored.append((outputs, keeping))
        if layer_at + 1 < layers:
            streams.append(streams[-1] + jnp.mean(blended, axis=1))
    closing = streams[-1][:, None, :] + blended
    closing_low = closing.astype(jnp.bfloat16)
    tower_before = (
        jnp.einsum("rtd,tdk->rtk", closing_low, tower_in, preferred_element_type=jnp.float32)
        + tower_bias[None]
    )
    tower_act, tower_pull = jax.vjp(jax.nn.gelu, tower_before)
    predictions = jnp.sum(tower_act * tower_out[None], axis=-1)
    tower_out_grad = jnp.sum(tower_act * pred_grad[:, :, None], axis=0)
    tower_before_grad = tower_pull(pred_grad[:, :, None] * tower_out[None])[0].astype(jnp.bfloat16)
    tower_bias_grad = jnp.sum(tower_before_grad, axis=0, dtype=jnp.float32)
    tower_in_grad = jnp.einsum(
        "rtd,rtk->tdk", closing_low, tower_before_grad, preferred_element_type=jnp.float32
    )
    closing_grad = jnp.einsum(
        "rtk,tdk->rtd", tower_before_grad, tower_in, preferred_element_type=jnp.float32
    )
    grad_out = closing_grad
    stream_grad = jnp.sum(closing_grad, axis=1)
    table_grads = [None] * layers
    expert_grads = [None] * layers
    for layer_at in reversed(range(layers)):
        outputs, keeping = run_layer(streams[layer_at], gate_rows[layer_at], weights[layer_at])
        gate_grad, input_grad, grads = back_layer(
            streams[layer_at], gate_rows[layer_at], weights[layer_at], outputs, keeping, grad_out
        )
        table_grads[layer_at] = jnp.dot(
            type_rows.T, gate_grad.reshape(height, task_count * experts), precision=EXACT
        )
        expert_grads[layer_at] = grads
        stream_grad = stream_grad + input_grad
        if layer_at > 0:
            grad_out = jnp.broadcast_to(
                (stream_grad / task_count)[:, None, :], (height, task_count, width)
            )
    stacked = tuple(
        (
            jnp.stack([expert_grads[layer_at][slot_at] for layer_at in range(layers)])
            for slot_at in range(4)
        )
    )
    in_grad, in_bias_grad, out_grad, out_bias_grad = jax.tree.map(
        lambda part: part.astype(jnp.float32), lax.psum(for_sending(stacked), "rows")
    )
    table_total, tower_in_sum, tower_bias_sum, tower_out_sum = lax.psum(
        (jnp.stack(table_grads), tower_in_grad, tower_bias_grad, tower_out_grad), ("rows", "expert")
    )
    table_total = table_total.reshape(layers, type_count, task_count, experts)
    table_pull = jax.vjp(gate_table, selector_logits, selector_mix)[1]
    logits_grad, mix_grad = table_pull(table_total)
    return (
        predictions,
        stream_grad,
        in_grad,
        in_bias_grad,
        out_grad,
        out_bias_grad,
        logits_grad,
        mix_grad,
        tower_in_sum,
        tower_bias_sum,
        tower_out_sum,
    )


def solution(mesh):
    in_specs = (
        P(("rows", "expert"), None),
        P(("rows", "expert"), None),
        P(),
        P(),
        P(None, "expert", None, None),
        P(None, "expert", None),
        P(None, "expert", None, None),
        P(None, "expert", None),
        P(),
        P(),
        P(),
        P(),
        P(),
    )
    out_specs = (
        P(("rows", "expert"), None),
        P(("rows", "expert"), None),
        P(None, "expert", None, None),
        P(None, "expert", None),
        P(None, "expert", None, None),
        P(None, "expert", None),
        P(),
        P(),
        P(),
        P(),
        P(),
    )
    return jax.shard_map(body, mesh=mesh, in_specs=in_specs, out_specs=out_specs, check_vma=False)
```

profile of v0, /device:TPU:0, one launch (start us, length us, event | category | flops | bytes accessed | tf_op | source)
XLA Modules:
  0.0 1131.1 jit_solution(8990391160075559890)
XLA Ops:
  27.8 93.8 %all-to-all-done = bf16[4,4,1024,256]{3,2,1,0:T(8,128)(2,1)} async-done(((bf16[4,4,1024,256]{3,2,1,0:T(8,128)(2,1)}), bf16[4,4,1024,256]{3,2,1,0:T(8,128)(2,1)}, u32[]{:S(2)}, u32[]{:S(2)}) %all-to-all-start) | async-done | bytes 8388640 | tf_op jit(solution)/shard_map/all_to_all | solution.py:60
  121.6 11.4 %fusion.22 = (bf16[4,4,1024,256]{3,2,0,1:T(8,128)(2,1)S(1)}, f32[4,4,1024,256]{3,2,1,0:T(8,128)}) fusion(f32[4,256]{1,0:T(4,128)S(1)} %get-tuple-element.66, bf16[2,4,256,256]{3,2,1,0:T(8,128)(2,1)S(1)} %copy-done.18, bf16[4,4,1024,256]{3,2,1,0:T(8,128)(2,1)} %all-to-all-done), kind=kOutput, calls=%fused_computation.32 | convolution fusion | flops 2189426688 | bytes 34082816 | tf_op jit(solution)/shard_map/serd,edh->serh/dot_general | solution.py:62
  155.8 91.3 %all-to-all-done.1 = bf16[4,4,1024,256]{3,2,1,0:T(8,128)(2,1)} async-done(((bf16[4,4,1024,256]{3,2,1,0:T(8,128)(2,1)}), bf16[4,4,1024,256]{3,2,1,0:T(8,128)(2,1)}, u32[]{:S(2)}, u32[]{:S(2)}) %all-to-all-start.1) | async-done | bytes 8388640 | tf_op jit(solution)/shard_map/all_to_all | solution.py:66
  247.1 9.7 fusion.75
  259.9 96.7 %all_to_all.44 = bf16[4,4,1024,256]{3,2,1,0:T(8,128)(2,1)} all-to-all(bf16[4,4,1024,256]{3,2,1,0:T(8,128)(2,1)S(1)} %broadcast_select_fusion), channel_id=1, replica_groups=mesh['rows'=8,'expert'=4] {'expert'}, dimensions={0} | all-to-all | bytes 16777216 | tf_op jit(solution)/shard_map/all_to_all | solution.py:60
  356.6 11.4 %fusion.21 = (bf16[4,4,1024,256]{3,2,0,1:T(8,128)(2,1)S(1)}, f32[4,4,1024,256]{3,2,1,0:T(8,128)}) fusion(f32[4,256]{1,0:T(4,128)S(1)} %get-tuple-element.65, bf16[2,4,256,256]{3,2,1,0:T(8,128)(2,1)S(1)} %copy-done.19, bf16[4,4,1024,256]{3,2,1,0:T(8,128)(2,1)} %all_to_all.44), kind=kOutput, calls=%fused_computation.30 | convolution fusion | flops 2189426688 | bytes 34082816 | tf_op jit(solution)/shard_map/serd,edh->serh/dot_general | solution.py:62
  390.4 89.9 %all-to-all-done.3 = bf16[4,4,1024,256]{3,2,1,0:T(8,128)(2,1)} async-done(((bf16[4,4,1024,256]{3,2,1,0:T(8,128)(2,1)}), bf16[4,4,1024,256]{3,2,1,0:T(8,128)(2,1)}, u32[]{:S(2)}, u32[]{:S(2)}) %all-to-all-start.3) | async-done | bytes 8388640 | tf_op jit(solution)/shard_map/all_to_all | solution.py:66
  491.5 11.0 convert_bitcast_fusion.3
  502.5 9.7 copy.163
  512.1 96.5 %all_to_all.45 = bf16[4,4,1024,256]{3,2,1,0:T(8,128)(2,1)S(1)} all-to-all(bf16[4,4,1024,256]{3,2,1,0:T(8,128)(2,1)} %bitcast.246), channel_id=1, replica_groups=mesh['rows'=8,'expert'=4] {'expert'}, dimensions={0} | all-to-all | bytes 16777216 | tf_op jit(solution)/shard_map/all_to_all | solution.py:85
  608.7 19.6 %fusion.160 = (bf16[4,256]{1,0:T(4,128)(2,1)S(1)}, bf16[4,4,1024,256]{3,2,0,1:T(8,128)(2,1)}) fusion(f32[4,4,1024,256]{3,2,1,0:T(8,128)} %get-tuple-element.80, f32[4,256]{1,0:T(4,128)S(1)} %get-tuple-element.65, bf16[2,4,256,256]{3,2,1,0:T(8,128)(2,1)S(1)} %copy-done.17, bf16[4,4,1024,256]{3,2,1,0:T(8,128)(2,1)S(1)} %all_to_all.45), kind=kOutput, calls=%fused_computation.222 | convolution fusion | flops 2239757312 | bytes 34084864 | tf_op jit(solution)/shard_map/serd,ehd->serh/dot_general | solution.py:93
  628.3 9.0 convert_bitcast_fusion.2
  644.6 95.3 %all_to_all.46 = bf16[4,4,1024,256]{3,2,1,0:T(8,128)(2,1)S(1)} all-to-all(bf16[4,4,1024,256]{3,2,1,0:T(8,128)(2,1)} %copy.131), channel_id=1, replica_groups=mesh['rows'=8,'expert'=4] {'expert'}, dimensions={0} | all-to-all | bytes 16777216 | tf_op jit(solution)/shard_map/all_to_all | solution.py:108
  742.3 9.3 convert_bitcast_fusion.1
  751.5 9.6 copy.164
  768.1 9.4 fusion.87
  777.6 78.5 %all-to-all-done.6 = bf16[4,4,1024,256]{3,2,1,0:T(8,128)(2,1)} async-done(((bf16[4,4,1024,256]{3,2,1,0:T(8,128)(2,1)}), bf16[4,4,1024,256]{3,2,1,0:T(8,128)(2,1)}, u32[]{:S(2)}, u32[]{:S(2)}) %all-to-all-start.6) | async-done | bytes 8388640 | tf_op jit(solution)/shard_map/all_to_all | solution.py:85
  856.1 18.5 %fusion.161 = (bf16[4,256]{1,0:T(4,128)(2,1)S(1)}, bf16[4,4,1024,256]{3,2,0,1:T(8,128)(2,1)}) fusion(f32[4,4,1024,256]{3,2,1,0:T(8,128)} %get-tuple-element.78, f32[4,256]{1,0:T(4,128)S(1)} %get-tuple-element.66, bf16[2,4,256,256]{3,2,1,0:T(8,128)(2,1)} %param.21, bf16[4,4,1024,256]{3,2,1,0:T(8,128)(2,1)} %all-to-all-done.6), kind=kOutput, calls=%fused_computation.223 | convolution fusion | flops 2239757312 | bytes 34084864 | tf_op jit(solution)/shard_map/serd,ehd->serh/dot_general | solution.py:93
  874.5 9.0 convert_bitcast_fusion
  925.5 18.4 %fusion.37 = f32[1024,2,16]{2,1,0:T(2,128)} fusion(bf16[16,1024,256]{2,1,0:T(8,128)(2,1)} %bitcast.35, f32[1024,2,256]{2,0,1:T(8,128)S(1)} %get-tuple-element.82), kind=kOutput, calls=%fused_computation.57 | convolution fusion | flops 100663296 | bytes 10616832 | tf_op jit(solution)/shard_map/erd,rtd->rte/dot_general | solution.py:78
  953.5 14.4 %fusion.41 = f32[1024,2,16]{2,1,0:T(2,128)S(1)} fusion(bf16[16,1024,256]{2,1,0:T(8,128)(2,1)} %bitcast.20, f32[1024,256]{1,0:T(8,128)S(1)} %get-tuple-element.49), kind=kOutput, calls=%fused_computation.61 | convolution fusion | flops 100663296 | bytes 9568256 | tf_op jit(solution)/shard_map/erd,rtd->rte/dot_general | solution.py:78
  968.7 54.3 %all-reduce.4 = (f32[2,32,2,16]{1,3,2,0:T(8,128)S(1)}, f32[2,128]{1,0:T(2,128)}, f32[2,128]{1,0:T(2,128)}) all-reduce(f32[2,32,2,16]{1,3,2,0:T(8,128)S(1)} %bitcast.250, f32[2,128]{1,0:T(2,128)S(1)} %copy-done.41, f32[2,128]{1,0:T(2,128)S(1)} %copy-done.42), channel_id=1, replica_groups=mesh['rows'=8,'expert'=4] {'rows','expert'}, use_global_device_ids=true, to_apply=%region_21.23 | all-reduce | flops 2560 | bytes 20480 | tf_op jit(solution)/shard_map/psum | solution.py:211
  1029.3 14.6 %all-reduce.5 = (bf16[2,4,256]{2,1,0:T(4,128)(2,1)S(1)}, bf16[2,4,256]{2,1,0:T(4,128)(2,1)S(1)}) all-reduce(bf16[2,4,256]{2,1,0:T(4,128)(2,1)S(1)} %pad_maximum_fusion.3, bf16[2,4,256]{2,1,0:T(4,128)(2,1)S(1)} %pad_maximum_fusion.4), channel_id=1, replica_groups=mesh['rows'=8,'expert'=4] {'rows'}, use_global_device_ids=true, to_apply=%region_16.18 | all-reduce | flops 4096 | bytes 16384 | tf_op jit(solution)/shard_map/psum | solution.py:209
  1056.4 66.0 %all-reduce.10.cloned.1.call-done = f32[2,256,128]{2,1,0:T(8,128)} async-done(((f32[2,256,128]{2,1,0:T(8,128)}), f32[2,256,128]{2,1,0:T(8,128)}) %all-reduce.10.cloned.1.call-update) | async-done | bytes 262160 | tf_op jit(solution)/shard_map/psum | solution.py:211
  (180 shorter events, 168.8 us)
Async XLA Ops:
  7.2 481.7 %copy-start = (bf16[2,256,128]{2,1,0:T(8,128)(2,1)S(1)}, bf16[2,256,128]{2,1,0:T(8,128)(2,1)}, u32[]{:S(2)}) copy-start(bf16[2,256,128]{2,1,0:T(8,128)(2,1)} %param.25) | copy-start | bytes 393220
  14.8 140.7 %copy-start.13 = (f32[1024,32]{0,1:T(8,128)}, f32[1024,32]{0,1:T(8,128)S(1)}, u32[]{:S(2)}) copy-start(f32[1024,32]{0,1:T(8,128)S(1)} %fusion.104) | copy-start | bytes 393220
  21.9 99.6 %copy-start.18 = (bf16[2,4,256,256]{3,2,1,0:T(8,128)(2,1)S(1)}, bf16[2,4,256,256]{3,2,1,0:T(8,128)(2,1)}, u32[]{:S(2)}) copy-start(bf16[2,4,256,256]{3,2,1,0:T(8,128)(2,1)} %param.19) | copy-start | bytes 3145732
  21.9 99.6 %all-to-all-start = ((bf16[4,4,1024,256]{3,2,1,0:T(8,128)(2,1)}), bf16[4,4,1024,256]{3,2,1,0:T(8,128)(2,1)}, u32[]{:S(2)}, u32[]{:S(2)}) async-start(bf16[4,4,1024,256]{3,2,1,0:T(8,128)(2,1)} %broadcast_select_fusion.1), calls=%async_computation | async-start | bytes 16777216 | tf_op jit(solution)/shard_map/all_to_all | solution.py:60
  149.1 98.0 %all-to-all-start.1 = ((bf16[4,4,1024,256]{3,2,1,0:T(8,128)(2,1)}), bf16[4,4,1024,256]{3,2,1,0:T(8,128)(2,1)}, u32[]{:S(2)}, u32[]{:S(2)}) async-start(bf16[4,4,1024,256]{3,2,1,0:T(8,128)(2,1)} %copy.119), calls=%async_computation.1 | async-start | bytes 16777216 | tf_op jit(solution)/shard_map/all_to_all | solution.py:66
  155.0 101.8 %copy-start.8 = (f32[1024,256]{1,0:T(8,128)S(1)}, f32[1024,256]{1,0:T(8,128)}, u32[]{:S(2)}) copy-start(f32[1024,256]{1,0:T(8,128)} %param.15) | copy-start | bytes 3145732
  155.5 91.7 %copy-start.11 = (bf16[1024,2,16]{2,1,0:T(2,128)(2,1)}, bf16[1024,2,16]{2,1,0:T(2,128)(2,1)S(1)}, u32[]{:S(2)}) copy-start(bf16[1024,2,16]{2,1,0:T(2,128)(2,1)S(1)} %copy.120) | copy-start | bytes 196612
  257.0 231.8 %copy-start.10 = (f32[1024,256]{1,0:T(8,128)}, f32[1024,256]{1,0:T(8,128)S(1)}, u32[]{:S(2)}) copy-start(f32[1024,256]{1,0:T(8,128)S(1)} %get-tuple-element.52) | copy-start | bytes 3145732
  259.9 96.7 %copy-start.19 = (bf16[2,4,256,256]{3,2,1,0:T(8,128)(2,1)S(1)}, bf16[2,4,256,256]{3,2,1,0:T(8,128)(2,1)}, u32[]{:S(2)}) copy-start(bf16[2,4,256,256]{3,2,1,0:T(8,128)(2,1)} %param.19) | copy-start | bytes 3145732
  384.1 96.2 %all-to-all-start.3 = ((bf16[4,4,1024,256]{3,2,1,0:T(8,128)(2,1)}), bf16[4,4,1024,256]{3,2,1,0:T(8,128)(2,1)}, u32[]{:S(2)}, u32[]{:S(2)}) async-start(bf16[4,4,1024,256]{3,2,1,0:T(8,128)(2,1)} %copy.123), calls=%async_computation.3 | async-start | bytes 16777216 | tf_op jit(solution)/shard_map/all_to_all | solution.py:66
  389.9 98.9 %copy-start.43 = (f32[1024,2]{0,1:T(2,128)S(1)}, f32[1024,2]{0,1:T(2,128)}, u32[]{:S(2)}) copy-start(f32[1024,2]{0,1:T(2,128)} %param.16) | copy-start | bytes 24580
  390.0 98.9 %copy-start.44 = (f32[2,128]{1,0:T(2,128)S(1)}, f32[2,128]{1,0:T(2,128)}, u32[]{:S(2)}) copy-start(f32[2,128]{1,0:T(2,128)} %param.27) | copy-start | bytes 3076
  390.0 98.9 %copy-start.45 = (f32[2,128]{1,0:T(2,128)S(1)}, f32[2,128]{1,0:T(2,128)}, u32[]{:S(2)}) copy-start(f32[2,128]{1,0:T(2,128)} %param.26) | copy-start | bytes 3076
  512.1 96.5 %copy-start.17 = (bf16[2,4,256,256]{3,2,1,0:T(8,128)(2,1)S(1)}, bf16[2,4,256,256]{3,2,1,0:T(8,128)(2,1)}, u32[]{:S(2)}) copy-start(bf16[2,4,256,256]{3,2,1,0:T(8,128)(2,1)} %param.21) | copy-start | bytes 3145732
  761.1 94.9 %all-to-all-start.6 = ((bf16[4,4,1024,256]{3,2,1,0:T(8,128)(2,1)}), bf16[4,4,1024,256]{3,2,1,0:T(8,128)(2,1)}, u32[]{:S(2)}, u32[]{:S(2)}) async-start(bf16[4,4,1024,256]{3,2,1,0:T(8,128)(2,1)} %bitcast.245), calls=%async_computation.6 | async-start | bytes 16777216 | tf_op jit(solution)/shard_map/all_to_all | solution.py:85
  890.8 159.8 %all-to-all-start.7 = ((bf16[4,4,1024,256]{3,2,1,0:T(8,128)(2,1)}), bf16[4,4,1024,256]{3,2,1,0:T(8,128)(2,1)}, u32[]{:S(2)}, u32[]{:S(2)}) async-start(bf16[4,4,1024,256]{3,2,1,0:T(8,128)(2,1)} %copy.135), calls=%async_computation.7 | async-start | bytes 16777216 | tf_op jit(solution)/shard_map/all_to_all | solution.py:108
  896.5 148.6 %all-reduce.12.cloned.1.call-start = ((), (), s32[]{:S(2)}) async-start(), calls=%async_computation.9 | async-start | bytes 4194304 | tf_op jit(solution)/shard_map/psum | solution.py:209
  925.0 197.4 %all-reduce.10.cloned.1.call-start = ((), (), s32[]{:S(2)}) async-start(), calls=%async_computation.8 | async-start | bytes 524288 | tf_op jit(solution)/shard_map/psum | solution.py:211
  953.5 69.6 %copy-start.28 = (f32[2,32,2,4]{1,3,2,0:T(4,128)S(1)}, f32[2,32,2,4]{1,3,2,0:T(4,128)}, u32[]{:S(2)}) copy-start(f32[2,32,2,4]{1,3,2,0:T(4,128)} %copy-done.27) | copy-start | bytes 6148
  953.5 69.6 %copy-start.7 = (f32[4,2,32,2,4,16]{2,5,4,3,1,0:T(8,128)S(1)}, f32[4,2,32,2,4,16]{2,5,4,3,1,0:T(8,128)}, u32[]{:S(2)}) copy-start(f32[4,2,32,2,4,16]{2,5,4,3,1,0:T(8,128)} %copy-done.6) | copy-start | bytes 393220
  953.5 69.7 %copy-start.32 = (f32[16,4]{0,1:T(4,128)S(1)}, f32[16,4]{0,1:T(4,128)}, u32[]{:S(2)}) copy-start(f32[16,4]{0,1:T(4,128)} %copy-done.31) | copy-start | bytes 772
  953.5 69.7 %copy-start.34 = (f32[16,4]{0,1:T(4,128)S(1)}, f32[16,4]{0,1:T(4,128)}, u32[]{:S(2)}) copy-start(f32[16,4]{0,1:T(4,128)} %copy-done.33) | copy-start | bytes 772
  953.5 70.0 %copy-start.26 = (f32[2,32,2,4,4]{1,4,3,2,0:T(4,128)S(1)}, f32[2,32,2,4,4]{1,4,3,2,0:T(4,128)}, u32[]{:S(2)}) copy-start(f32[2,32,2,4,4]{1,4,3,2,0:T(4,128)} %param.23) | copy-start | bytes 24580
  1045.1 79.0 %copy-start.1 = (bf16[2,256,128]{2,1,0:T(8,128)(2,1)S(1)}, bf16[2,256,128]{2,1,0:T(8,128)(2,1)}, u32[]{:S(2)}) copy-start(bf16[2,256,128]{2,1,0:T(8,128)(2,1)} %param.25) | copy-start | bytes 393220
  (29 other events, 335.0 us)
Sparse Core Ops, SparseCore 0:
  925.1 66.8 all-reduce.11
  998.1 124.2 all-reduce.9
where the time goes:
time: 1140 us; the launch traced here: 1130 us
  waiting for transfers between devices  420 us (37%)
  blocking collectives  357 us (31%)
  matrix products  205 us (18%)
  local copies, waits for them, and re-layouts  61.7 us (5%)
  other arithmetic  42.9 us (4%)
  starting transfers between devices  29.8 us (3%)
  between operations  15 us (1%)
    all_to_all x2, waiting for transfers between devices, run_layer(): lax.all_to_all(produced, 'expert', split_axis=0, concat_axis=0, tiled=True)  181 us
    all_to_all x1, blocking collectives, run_layer(): lax.all_to_all(sendable, 'expert', split_axis=0, concat_axis=0, tiled=True)  96.7 us
    all_to_all x1, blocking collectives, back_layer(): lax.all_to_all(result_grad.reshape(groups, owned, height, width), 'expert...  96.5 us
    all_to_all x1, blocking collectives, back_layer(): lax.all_to_all(row_term, 'expert', split_axis=0, concat_axis=0, tiled=True)  95.3 us
    all_to_all x1, waiting for transfers between devices, run_layer(): lax.all_to_all(sendable, 'expert', split_axis=0, concat_axis=0, tiled=True)  93.8 us
    all_to_all x1, waiting for transfers between devices, back_layer(): lax.all_to_all(result_grad.reshape(groups, owned, height, width), 'expert...  78.5 us
    psum x1, waiting for transfers between devices, body(): lax.psum((jnp.stack(table_grads), tower_in_grad, tower_bias_grad, tower_o...  66 us
    psum x1, blocking collectives, body(): lax.psum((jnp.stack(table_grads), tower_in_grad, tower_bias_grad, tower_o...  54.3 us
  transfers between devices with their start and end apart: 7, of which 5 were waited for; matrix products, arithmetic and copies ran while one was open for 9% of the time, Pallas kernels for 0%

commit v1 on v0

v1 whole, which is shorter than its diff:
```python
import functools
import math

import jax
import jax.numpy as jnp
import numpy as np
from jax import lax
from jax.experimental import pallas as pl
from jax.experimental.pallas import tpu as pltpu
from jax.sharding import PartitionSpec as P

SHARPNESS = 10.0
EXACT = lax.Precision.HIGHEST
bf16 = jnp.bfloat16
f32 = jnp.float32
INNER = math.sqrt(2.0 / math.pi)
CUBE = 0.044715 * INNER
TILE = 1024
TOWER_TILE = 256
LANES = 128
EXTRA = 16


def mm(a, b):
    return jnp.dot(a, b, preferred_element_type=f32)


def mm_exact(a, b):
    return jnp.dot(a, b, precision=EXACT, preferred_element_type=f32)


def mm_nt(a, b):
    return lax.dot_general(a, b, (((1,), (1,)), ((), ())), preferred_element_type=f32)


def mm_tn(a, b):
    return lax.dot_general(a, b, (((0,), (0,)), ((), ())), preferred_element_type=f32)


def gelu_both(v):
    square = v * v
    half = 0.5 + 0.5 * jnp.tanh(v * (INNER + CUBE * square))
    value = v * half
    slope = half + value * (1.0 - half) * (2.0 * INNER + 6.0 * CUBE * square)
    return value, slope


def gelu_low(v):
    square = v * v
    half = 0.5 + 0.5 * jnp.tanh(v * (INNER + CUBE * square))
    value = (v * half).astype(bf16)
    bend = (2.0 * INNER + 6.0 * CUBE * square).astype(bf16)
    half = half.astype(bf16)
    return value, half + value * (1.0 - half) * bend


FAR = pl.BlockSpec(memory_space=pl.ANY)
NEAR = pl.BlockSpec(memory_space=pltpu.VMEM)
SCALARS = pl.BlockSpec(memory_space=pltpu.SMEM)


def kernel_params():
    return pltpu.CompilerParams(vmem_limit_bytes=58 * 2**20)


def whole_spec(shape):
    zeros = (0,) * len(shape)
    return pl.BlockSpec(shape, lambda i: zeros)


def prepare_kernel(sizes, place_ref, length_ref, kind_ref, logit_ref, mix_ref, spread_logit_ref, spread_mix_ref, *outs):
    owned, halves, held, selectors, bits, tasks = sizes
    type_ref, across_ref, slope_ref, *value_refs = outs
    height, type_count = type_ref.shape
    experts = 2**bits
    sessions = length_ref.shape[1]
    chunk = min(256, sessions)
    position = (place_ref[0] + lax.broadcasted_iota(jnp.int32, (height, 1), 0)).astype(f32)
    earlier = lax.broadcasted_iota(jnp.int32, (chunk, chunk), 0) < lax.broadcasted_iota(jnp.int32, (chunk, chunk), 1)
    earlier = jnp.where(earlier, 1.0, 0.0).astype(bf16)
    kinds = lax.broadcasted_iota(jnp.int32, (type_count, chunk), 0)
    before = jnp.zeros((1, 1), f32)
    types = jnp.zeros((height, type_count), f32)
    across = jnp.zeros((type_count, height), f32)
    for at in range(0, sessions, chunk):
        lengths = length_ref[:, at : at + chunk].astype(f32)
        begin = before + mm(jnp.broadcast_to(lengths.astype(bf16), (EXTRA, chunk)), earlier)[0:1]
        before += jnp.sum(lengths, axis=1, keepdims=True)
        member = jnp.where((position >= begin) & (position < begin + lengths), 1.0, 0.0).astype(bf16)
        of_type = jnp.where(kinds == kind_ref[:, at : at + chunk], 1.0, 0.0).astype(bf16)
        types += mm_nt(member, of_type)
        across += mm_nt(of_type, member)
    type_ref[...] = types.astype(bf16)
    across_ref[...] = across.astype(bf16)

    rows = logit_ref.shape[0]
    place = lax.broadcasted_iota(jnp.int32, (rows, LANES), 1) % experts
    expert = (
        owned * ((place // owned) ^ place_ref[1])
        + held * ((place % halves) ^ place_ref[2])
        + (place // halves) % held
    )
    logits = mm_exact(logit_ref[...], spread_logit_ref[...])
    mixes = mm_exact(mix_ref[...], spread_mix_ref[...])
    mixes = [mixes[:, k * LANES : (k + 1) * LANES] for k in range(selectors)]
    top = functools.reduce(jnp.maximum, mixes)
    shares = [jnp.exp(mix - top) for mix in mixes]
    whole = functools.reduce(jnp.add, shares)
    shares = [share / whole for share in shares]
    value = jnp.zeros((rows, LANES), f32)
    reaches = []
    for k in range(selectors):
        factors, signed = [], []
        for bit in range(bits):
            at = (k * bits + bit) * LANES
            logit = logits[:, at : at + LANES]
            cubic = (-2.0 / SHARPNESS**3) * logit * logit * logit + (1.5 / SHARPNESS) * logit + 0.5
            step = jnp.where(logit <= -SHARPNESS / 2, 0.0, jnp.where(logit >= SHARPNESS / 2, 1.0, cubic))
            slope = (-6.0 / SHARPNESS**3) * logit * logit + 1.5 / SHARPNESS
            slope = jnp.where((logit > -SHARPNESS / 2) & (logit < SHARPNESS / 2), slope, 0.0)
            on = (expert >> bit) & 1 == 1
            factors.append(jnp.where(on, step, 1.0 - step))
            signed.append(jnp.where(on, slope, -slope))
        reaches.append(functools.reduce(jnp.multiply, factors))
        value += shares[k] * reaches[k]
        for bit in range(bits):
            others = [factors[b] for b in range(bits) if b != bit]
            slope_ref[k * bits + bit] = shares[k] * signed[bit] * functools.reduce(jnp.multiply, others)
    for k in range(selectors):
        slope_ref[selectors * bits + k] = shares[k] * (reaches[k] - value)

    value = value.astype(bf16).astype(f32)
    for layer_at, ref in enumerate(value_refs):
        table = value[layer_at * type_count : (layer_at + 1) * type_count]
        columns = [table[:, t * experts : (t + 1) * experts] for t in range(tasks)]
        if layer_at < len(value_refs) - 1:
            columns = [functools.reduce(jnp.add, columns) / tasks]
        for pair in range(ref.shape[0]):
            lanes = []
            for half in range(halves):
                at = pair * halves + half
                lanes += [jnp.broadcast_to(c[:, at : at + 1], (type_count, LANES)) for c in columns]
            ref[pair] = jnp.concatenate(lanes, axis=1).astype(bf16)


def prepare_call(place, lengths, session_type, logits, mixing, height, sizes):
    owned, halves, held, selectors, bits, tasks = sizes
    layers, type_count = logits.shape[:2]
    experts = 2**bits
    rows = layers * type_count
    lane = np.arange(LANES)
    source = np.arange(tasks * selectors * bits)
    task, number = source // (selectors * bits), source % (selectors * bits)
    mine = (lane[None, :] // experts == task[:, None])[:, None, :]
    spread_logit = mine & (number[:, None, None] == np.arange(selectors * bits)[None, :, None])
    source = np.arange(tasks * selectors)
    mine = (lane[None, :] // experts == (source // selectors)[:, None])[:, None, :]
    spread_mix = mine & ((source % selectors)[:, None, None] == np.arange(selectors)[None, :, None])
    spread_logit = spread_logit.reshape(spread_logit.shape[0], -1).astype(np.float32)
    spread_mix = spread_mix.reshape(spread_mix.shape[0], -1).astype(np.float32)
    outs = [
        jax.ShapeDtypeStruct((height, type_count), bf16),
        jax.ShapeDtypeStruct((type_count, height), bf16),
        jax.ShapeDtypeStruct((selectors * (bits + 1), rows, LANES), f32),
    ]
    for layer_at in range(layers):
        each = tasks if layer_at == layers - 1 else 1
        outs.append(jax.ShapeDtypeStruct((experts // halves, type_count, halves * each * LANES), bf16))
    return pl.pallas_call(
        functools.partial(prepare_kernel, sizes),
        out_shape=outs,
        in_specs=[SCALARS] + [NEAR] * 6,
        out_specs=[NEAR] * len(outs),
        compiler_params=kernel_params(),
        cost_estimate=pl.CostEstimate(flops=2 * height * lengths.size * 64, bytes_accessed=2**21, transcendentals=2**16),
    )(
        place,
        lengths.reshape(1, -1),
        session_type.reshape(1, -1),
        logits.reshape(rows, -1),
        mixing.reshape(rows, -1),
        spread_logit,
        spread_mix,
    )


def bias_rows(weights, width):
    rows = weights[2 * width : 2 * width + EXTRA].astype(f32)
    return rows[0:1] + rows[1:2], rows[2:3] + rows[3:4]


def twice(a):
    return jnp.concatenate([a, a], axis=1)


def tiles(height, most):
    tile = min(most, height)
    return [pl.ds(at, tile) for at in range(0, height, tile)]


def joined(parts, axis):
    return parts[0] if len(parts) == 1 else jnp.concatenate(parts, axis=axis)


def gates_of(types, value_ref, count):
    gates = mm(types, value_ref[...]).astype(bf16)
    return [gates[:, at * LANES : (at + 1) * LANES] for at in range(count)]


def forward_step(weights, value_ref, x_low, type_ref, total_ref, biases, keep):
    height, width = x_low.shape
    kinds = total_ref.shape[0]
    bias_in, bias_out = zip(*(bias_rows(w, width) for w in weights))
    second = joined([w[width : 2 * width] for w in weights], 0)
    for rows in tiles(height, TILE):
        gates = gates_of(type_ref[rows], value_ref, len(weights) * kinds)
        scaled = [[] for _ in range(kinds)]
        for i, w in enumerate(weights):
            hidden, slope = gelu_low(mm(x_low[rows], w[0:width]) + bias_in[i])
            keep(i, rows, hidden, slope)
            for t in range(kinds):
                scaled[t].append(twice(gates[i * kinds + t]) * hidden)
        for t in range(kinds):
            total_ref[t, rows] += mm(joined(scaled[t], 1), second)
    for i in range(len(weights)):
        for t in range(kinds):
            at = (i * kinds + t) * LANES
            biases[t] += twice(value_ref[:, at : at + LANES].astype(f32)) * bias_out[i]


def forward_end(type_ref, total_ref, biases):
    for t in range(total_ref.shape[0]):
        high = biases[t].astype(bf16)
        rest = (biases[t] - high.astype(f32)).astype(bf16)
        for rows in tiles(total_ref.shape[1], TILE):
            total_ref[t, rows] += mm(type_ref[rows], high) + mm(type_ref[rows], rest)


def backward_start(x_low, type_across, low, across, share):
    width = x_low.shape[1]
    across[0:width] = x_low[...].T
    ones = lax.broadcasted_iota(jnp.int32, (EXTRA, x_low.shape[0]), 0) == 0
    across[width:] = jnp.where(ones, 1.0, 0.0).astype(bf16)
    for t in range(low.shape[0]):
        share[t] = mm(type_across[...], low[t])


def backward_step(weights, value_ref, hiddens, slopes, outs, pair, experts, type_ref, type_across, low, stream_ref, across, share, table, scratch):
    before_grads, result_grads, products = scratch
    kinds, height, width = low.shape
    count = len(weights)
    first = joined([w[0:width] for w in weights], 1)
    for rows in tiles(height, TILE):
        gates = [twice(gate) for gate in gates_of(type_ref[rows], value_ref, count * kinds)]
        befores = []
        for i, w in enumerate(weights):
            hidden, slope = hiddens[i][rows], slopes[i][rows]
            second = w[width : 2 * width]
            result_grad = gates[i * kinds] * low[0, rows]
            for t in range(1, kinds):
                result_grad += gates[i * kinds + t] * low[t, rows]
            if kinds == 1:
                hidden_grad = mm_nt(result_grad, second).astype(bf16)
                backs = [hidden_grad]
            else:
                backs = [mm_nt(low[t, rows], second).astype(bf16) for t in range(kinds)]
                hidden_grad = gates[i * kinds] * backs[0]
                for t in range(1, kinds):
                    hidden_grad += gates[i * kinds + t] * backs[t]
            for t in range(kinds):
                product = hidden * backs[t]
                at = (i * kinds + t) * LANES
                products[rows, at : at + LANES] = functools.reduce(
                    jnp.add, [product[:, lane : lane + LANES] for lane in range(0, width, LANES)]
                )
            before = slope * hidden_grad
            before_grads[i, rows] = before
            result_grads[i, rows] = result_grad
            befores.append(before)
        stream_ref[rows] += mm_nt(joined(befores, 1), first)
    sums = mm(type_across[...], products[...])
    lanes = lax.broadcasted_iota(jnp.int32, (type_ref.shape[1], LANES), 1)
    for i, w in enumerate(weights):
        _, bias_out = bias_rows(w, width)
        first_grad = mm(across[...], before_grads[i])
        outs[i][0:width] = first_grad[0:width].astype(bf16)
        outs[i][width : 2 * width] = mm_tn(hiddens[i][...], result_grads[i]).astype(bf16)
        out_bias = jnp.zeros((1, width), f32)
        place = pair * count + i
        for t in range(kinds):
            at = (i * kinds + t) * LANES
            gate = value_ref[:, at : at + LANES].astype(f32)
            out_bias += jnp.sum(twice(gate) * share[t], axis=0, keepdims=True)
            found = jnp.sum(sums[:, at : at + LANES], axis=1, keepdims=True)
            bias_part = jnp.sum(share[t] * bias_out, axis=1, keepdims=True)
            if kinds == 1:
                some = gate > 0.0
                found = jnp.where(some, 0.5 * found / jnp.where(some, gate, 1.0), 0.0)
                table[...] = jnp.where(lanes % experts == place, found + 0.5 * bias_part, table[...])
            else:
                table[...] = jnp.where(lanes == t * experts + place, found + bias_part, table[...])
        tail = jnp.concatenate([first_grad[width : width + 1], out_bias, jnp.zeros((EXTRA - 2, width), f32)])
        outs[i][2 * width : 2 * width + EXTRA] = tail.astype(bf16)


def through_gates(table, gate_slope_ref, experts, tasks):
    quantities, type_count = gate_slope_ref.shape[:2]
    lanes = lax.broadcasted_iota(jnp.int32, (type_count, LANES), 1)
    small = jnp.zeros((type_count, LANES), f32)
    for q in range(quantities):
        product = gate_slope_ref[q] * table[...]
        for t in range(tasks):
            part = jnp.sum(jnp.where(lanes // experts == t, product, 0.0), axis=1, keepdims=True)
            small = jnp.where(lanes == t * quantities + q, part, small)
    half = type_count // 2
    return jnp.concatenate([small[:half], small[half:]], axis=1).astype(bf16)


def fetch_weights(places, buffer, sems, each):
    step = pl.program_id(0)
    for of in range(len(places) // each):

        @pl.when(step == max(of - 1, 0))
        def _(of=of):
            for i, (ref, at) in enumerate(places[of * each : (of + 1) * each]):
                pltpu.make_async_copy(ref.at[at], buffer.at[of % 2, i], sems.at[of % 2, i]).start()

    slot = lax.rem(step, 2)
    for i in range(each):
        ref, at = places[0]
        pltpu.make_async_copy(ref.at[at], buffer.at[slot, i], sems.at[slot, i]).wait()
    return [buffer.at[slot, i] for i in range(each)]


def forward_kernel(places, pieces, each, first, *refs):
    refs = list(refs)
    take = lambda count: [refs.pop(0) for _ in range(count)]
    x_ref, type_ref, value_ref = take(3)
    if not first:
        total_ref, _, _ = take(3)
    weight_refs = take(pieces)
    out_ref, hidden_ref, slope_ref, x_low, biases, buffer, sems = take(7)
    step = pl.program_id(0)
    weights = fetch_weights([(weight_refs[piece], at) for piece, at in places], buffer, sems, each)

    @pl.when(step == 0)
    def _():
        x_low[...] = x_ref[...].astype(bf16)
        biases[...] = jnp.zeros_like(biases)
        out_ref[0] = x_ref[...] if first else total_ref[0]

    def keep(i, rows, hidden, slope):
        hidden_ref[0, i, rows] = hidden
        slope_ref[0, i, rows] = slope

    forward_step(weights, value_ref.at[0], x_low, type_ref, out_ref, biases, keep)

    @pl.when(step == pl.num_programs(0) - 1)
    def _():
        forward_end(type_ref, out_ref, biases)


def forward_call(x, types, values, total, stash, pieces, places, base):
    height, width = x.shape
    pairs, type_count, lanes = values.shape
    each = lanes // LANES
    operands = [x, types, values]
    specs = [whole_spec(x.shape), whole_spec(types.shape)]
    specs.append(pl.BlockSpec((1, type_count, lanes), lambda i: (base + i, 0, 0)))
    aliases = {}
    if total is not None:
        operands += [total, *stash]
        specs += [whole_spec(total.shape), FAR, FAR]
        aliases = {4: 1, 5: 2}
    summed = jax.ShapeDtypeStruct((1, height, width), f32)
    kept = jax.ShapeDtypeStruct((pairs, each, height, width), bf16)
    kept_spec = pl.BlockSpec((1, each, height, width), lambda i: (base + i, 0, 0, 0))
    number = len(places)
    results = pl.pallas_call(
        functools.partial(forward_kernel, places, len(pieces), each, total is None),
        grid=(number // each,),
        out_shape=[summed, kept, kept],
        in_specs=specs + [FAR] * len(pieces),
        out_specs=[whole_spec(summed.shape), kept_spec, kept_spec],
        scratch_shapes=[
            pltpu.VMEM((height, width), bf16),
            pltpu.VMEM((1, type_count, width), f32),
            pltpu.VMEM((2, each, *pieces[0].shape[1:]), bf16),
            pltpu.SemaphoreType.DMA((2, each)),
        ],
        input_output_aliases=aliases,
        compiler_params=kernel_params(),
        cost_estimate=pl.CostEstimate(
            flops=4 * number * height * width * width,
            bytes_accessed=number * (4 * width * width + 4 * height * width) + 8 * height * width,
            transcendentals=number * height * width,
        ),
    )(*operands, *pieces)
    return results[0], results[1:]


def middle_kernel(places, pieces, groups, halves, held, *refs):
    refs = list(refs)
    take = lambda count: [refs.pop(0) for _ in range(count)]
    place_ref, x_ref, type_ref, across_types_ref, value_ref, gate_slope_ref, pred_grad_ref = take(7)
    tower_in_ref, tower_bias_ref, tower_out_ref = take(3)
    weight_refs = take(pieces)
    pred_ref, stream_ref, small_ref, tower_small_ref, *tower_refs = take(4 + halves)
    out_refs = [take(halves) for _ in range(held)]
    x_low, weights, hidden_all, slope_all, total, biases, low, across, share, table = take(10)
    before_grads, result_grads, products, ready, in_grad, bias_grad, out_grad, load_sem, store_sem = take(9)
    height, width = x_ref.shape
    pairs = value_ref.shape[0]
    experts = pairs * halves
    tasks = total.shape[0]

    def load(pair, i, ref, at):
        return pltpu.make_async_copy(ref.at[at], weights.at[pair, i], load_sem.at[pair, i])

    for j, (piece, at) in enumerate(places):
        load(j // halves, j % halves, weight_refs[piece], at).start()
    x_low[...] = x_ref[...].astype(bf16)
    biases[...] = jnp.zeros_like(biases)
    for t in range(tasks):
        total[t] = x_ref[...]

    def forward_pair(pair, carry):
        for i in range(halves):
            load(pair, i, weight_refs[0], 0).wait()

        def keep(i, rows, hidden, slope):
            hidden_all[pair, i, rows] = hidden
            slope_all[pair, i, rows] = slope

        forward_step(
            [weights.at[pair, i] for i in range(halves)], value_ref.at[pair], x_low, type_ref, total, biases, keep
        )
        return carry

    lax.fori_loop(0, pairs, forward_pair, 0)
    forward_end(type_ref, total, biases)

    in_grad[...] = jnp.zeros_like(in_grad)
    bias_grad[...] = jnp.zeros_like(bias_grad)
    out_grad[...] = jnp.zeros_like(out_grad)
    for rows in tiles(height, TOWER_TILE):
        summed = None
        predicted = []
        for t in range(tasks):
            closing_low = total[t, rows].astype(bf16)
            act, slope = gelu_both(mm(closing_low, tower_in_ref[t]) + tower_bias_ref[t : t + 1])
            vector = tower_out_ref[t : t + 1]
            predicted.append(jnp.sum(act * vector, axis=1, keepdims=True))
            cotangent = pred_grad_ref[rows, t : t + 1]
            out_grad[t : t + 1] += jnp.sum(act * cotangent, axis=0, keepdims=True)
            before_grad = (slope * (cotangent * vector)).astype(bf16)
            bias_grad[t : t + 1] += jnp.sum(before_grad.astype(f32), axis=0, keepdims=True)
            in_grad[t] += mm_tn(closing_low, before_grad)
            closing_grad = mm_nt(before_grad, tower_in_ref[t])
            low[t, rows] = closing_grad.astype(bf16)
            summed = closing_grad if summed is None else summed + closing_grad
        stream_ref[rows] = summed
        pred_ref[rows] = jnp.concatenate(predicted, axis=1)
    narrow = in_grad.shape[2]
    for t in range(tasks):
        wide = jnp.concatenate([in_grad[t, : width * narrow // width], in_grad[t, width * narrow // width :]], axis=1)
        if halves == 2:

            @pl.when(place_ref[2] == t)
            def _(wide=wide):
                tower_refs[0][...] = wide.astype(bf16)

            @pl.when(place_ref[2] != t)
            def _(wide=wide):
                tower_refs[1][...] = wide.astype(bf16)

        else:
            tower_refs[0][t * wide.shape[0] : (t + 1) * wide.shape[0]] = wide.astype(bf16)
    ends = [jnp.concatenate([ref[0:1], ref[1:2]], axis=1) for ref in (bias_grad, out_grad)]
    tower_small_ref[...] = jnp.concatenate([*ends, jnp.zeros((EXTRA - 2, width), f32)]).astype(bf16)

    backward_start(x_low, across_types_ref, low, across, share)
    table[...] = jnp.zeros_like(table)

    def store(unit, group, half):
        pair = group * held + unit
        return pltpu.make_async_copy(ready.at[pair, half], out_refs[unit][half].at[group], store_sem.at[pair, half])

    for unit in range(held):

        def backward_group(group, carry, unit=unit):
            pair = group * held + unit
            backward_step(
                [weights.at[pair, i] for i in range(halves)],
                value_ref.at[pair],
                [hidden_all.at[pair, i] for i in range(halves)],
                [slope_all.at[pair, i] for i in range(halves)],
                [ready.at[pair, i] for i in range(halves)],
                pair,
                experts,
                type_ref,
                across_types_ref,
                low,
                stream_ref,
                across,
                share,
                table,
                (before_grads, result_grads, products),
            )
            for half in range(halves):
                store(unit, group, half).start()
            return carry

        lax.fori_loop(0, groups, backward_group, 0)
    small_ref[...] = through_gates(table, gate_slope_ref, experts, tasks)
    for unit in range(held):

        def drain(group, carry, unit=unit):
            for half in range(halves):
                store(unit, group, half).wait()
            return carry

        lax.fori_loop(0, groups, drain, 0)


def middle_call(place, x, types, across_types, values, gate_slopes, tower, pieces, places, groups, halves, held):
    height, width = x.shape
    pairs, type_count, lanes = values.shape
    pred_grad, tower_in, tower_bias, tower_out = tower
    tasks = tower_in.shape[0]
    stride = 2 * width + EXTRA
    experts = pairs * halves
    payload = jax.ShapeDtypeStruct((groups, stride, width), bf16)
    outs = [jax.ShapeDtypeStruct(shape, f32) for shape in (pred_grad.shape, (height, width))]
    outs.append(jax.ShapeDtypeStruct((type_count // 2, 2 * LANES), bf16))
    outs.append(jax.ShapeDtypeStruct((EXTRA, width), bf16))
    outs += [jax.ShapeDtypeStruct((tower_in.size // width // halves, width), bf16)] * halves
    near = len(outs)
    outs += [payload] * (halves * held)
    layer_at = gate_slopes.shape[1] // type_count - 1
    slope_spec = pl.BlockSpec((gate_slopes.shape[0], type_count, LANES), lambda i: (0, layer_at, 0))
    kept = pltpu.VMEM((pairs, halves, height, width), bf16)
    operands = [x, types, across_types, values, gate_slopes, *tower]
    specs = [whole_spec(a.shape) for a in operands]
    specs[4] = slope_spec
    return pl.pallas_call(
        functools.partial(middle_kernel, places, len(pieces), groups, halves, held),
        grid=(1,),
        out_shape=outs,
        in_specs=[SCALARS] + specs + [FAR] * len(pieces),
        out_specs=[whole_spec(out.shape) for out in outs[:near]] + [FAR] * (halves * held),
        scratch_shapes=[
            pltpu.VMEM((height, width), bf16),
            pltpu.VMEM((pairs, halves, stride, width), bf16),
            kept,
            kept,
            pltpu.VMEM((tasks, height, width), f32),
            pltpu.VMEM((tasks, type_count, width), f32),
            pltpu.VMEM((tasks, height, width), bf16),
            pltpu.VMEM((width + EXTRA, height), bf16),
            pltpu.VMEM((tasks, type_count, width), f32),
            pltpu.VMEM((type_count, LANES), f32),
            pltpu.VMEM((halves, height, width), bf16),
            pltpu.VMEM((halves, height, width), bf16),
            pltpu.VMEM((height, lanes), bf16),
            pltpu.VMEM((pairs, halves, stride, width), bf16),
            pltpu.VMEM(tower_in.shape, f32),
            pltpu.VMEM(tower_bias.shape, f32),
            pltpu.VMEM(tower_out.shape, f32),
            pltpu.SemaphoreType.DMA((pairs, halves)),
            pltpu.SemaphoreType.DMA((pairs, halves)),
        ],
        compiler_params=kernel_params(),
        cost_estimate=pl.CostEstimate(
            flops=14 * experts * height * width * width,
            bytes_accessed=experts * 8 * width * width + 16 * height * width,
            transcendentals=experts * height * width,
        ),
    )(place, *operands, *pieces)


def backward_kernel(places, pieces, each, held, unit, tasks, *refs):
    refs = list(refs)
    take = lambda count: [refs.pop(0) for _ in range(count)]
    x_ref, type_ref, across_types_ref, grad_ref, stream_ref, gate_slope_ref, value_ref, hidden_ref, slope_ref = take(9)
    weight_refs = take(pieces)
    stream_out_ref, small_ref = take(2)
    out_refs = take(each)
    x_low, across, low, share, table, before_grads, result_grads, products, buffer, sems = take(10)
    step = pl.program_id(0)
    groups = pl.num_programs(0)
    weights = fetch_weights([(weight_refs[piece], at) for piece, at in places], buffer, sems, each)

    @pl.when(step == 0)
    def _():
        x_low[...] = x_ref[...].astype(bf16)
        low[0] = grad_ref[...].astype(bf16)
        stream_out_ref[...] = stream_ref[...]
        table[...] = jnp.zeros_like(table)
        backward_start(x_low, across_types_ref, low, across, share)

    experts = len(places) * held
    backward_step(
        weights,
        value_ref.at[0],
        [hidden_ref.at[0, i] for i in range(each)],
        [slope_ref.at[0, i] for i in range(each)],
        [ref.at[0] for ref in out_refs],
        step * held + unit,
        experts,
        type_ref,
        across_types_ref,
        low,
        stream_out_ref,
        across,
        share,
        table,
        (before_grads, result_grads, products),
    )

    @pl.when(step == groups - 1)
    def _():
        small_ref[...] = through_gates(table, gate_slope_ref, experts, tasks)


def backward_call(x, types, across_types, grad, stream, gate_slopes, layer_at, values, stash, pieces, places, held, unit, tasks):
    height, width = x.shape
    pairs, type_count, lanes = values.shape
    each = lanes // LANES
    groups = pairs // held
    stride = 2 * width + EXTRA
    operands = [x, types, across_types, grad, stream, gate_slopes, values, *stash]
    specs = [whole_spec(a.shape) for a in operands[:5]]
    specs.append(pl.BlockSpec((gate_slopes.shape[0], type_count, LANES), lambda i: (0, layer_at, 0)))
    specs.append(pl.BlockSpec((1, type_count, lanes), lambda i: (i * held + unit, 0, 0)))
    specs += [pl.BlockSpec((1, each, height, width), lambda i: (i * held + unit, 0, 0, 0))] * 2
    payload = jax.ShapeDtypeStruct((groups, stride, width), bf16)
    small = jax.ShapeDtypeStruct((type_count // 2, 2 * LANES), bf16)
    number = groups * each
    return pl.pallas_call(
        functools.partial(backward_kernel, places, len(pieces), each, held, unit, tasks),
        grid=(groups,),
        out_shape=[jax.ShapeDtypeStruct(stream.shape, f32), small] + [payload] * each,
        in_specs=specs + [FAR] * len(pieces),
        out_specs=[whole_spec(stream.shape), whole_spec(small.shape)]
        + [pl.BlockSpec((1, stride, width), lambda i: (i, 0, 0))] * each,
        scratch_shapes=[
            pltpu.VMEM((height, width), bf16),
            pltpu.VMEM((width + EXTRA, height), bf16),
            pltpu.VMEM((1, height, width), bf16),
            pltpu.VMEM((1, type_count, width), f32),
            pltpu.VMEM((type_count, LANES), f32),
            pltpu.VMEM((each, height, width), bf16),
            pltpu.VMEM((each, height, width), bf16),
            pltpu.VMEM((height, lanes), bf16),
            pltpu.VMEM((2, each, stride, width), bf16),
            pltpu.SemaphoreType.DMA((2, each)),
        ],
        compiler_params=kernel_params(),
        cost_estimate=pl.CostEstimate(
            flops=8 * number * height * width * width,
            bytes_accessed=number * (8 * width * width + 4 * height * width) + 16 * height * width,
            transcendentals=0,
        ),
    )(*operands, *pieces)


def finish_kernel(layer_at, unit, held, halves, rows, first, *refs):
    refs = list(refs)
    take = lambda count: [refs.pop(0) for _ in range(count)]
    place_ref = take(1)[0]
    sources = take(halves)
    if not first:
        _, _, in_bias_ref, out_bias_ref = take(4)
    in_ref, out_ref, in_bias_out_ref, out_bias_out_ref, ready, sems = refs
    copies = []
    for half, source in enumerate(sources):
        where = held * (place_ref[2] ^ half) + unit
        for which, ref in enumerate((in_ref, out_ref)):
            ready[half, which] = source[which * rows : (which + 1) * rows].astype(f32)
            copy = pltpu.make_async_copy(ready.at[half, which], ref.at[layer_at, where], sems.at[half, which])
            copy.start()
            copies.append(copy)
    in_bias_out_ref[...] = jnp.zeros_like(in_bias_out_ref) if first else in_bias_ref[...]
    out_bias_out_ref[...] = jnp.zeros_like(out_bias_out_ref) if first else out_bias_ref[...]
    for half, source in enumerate(sources):
        where = held * (place_ref[2] ^ half) + unit
        tail = source[2 * rows : 2 * rows + EXTRA].astype(f32)
        in_bias_out_ref[layer_at, pl.ds(where, 1)] = tail[0:1]
        out_bias_out_ref[layer_at, pl.ds(where, 1)] = tail[1:2]
    for copy in copies:
        copy.wait()


def finish_call(place, sources, held_arrays, layer_at, unit, held, shape):
    halves = len(sources)
    rows, width = shape[2:]
    outs = [jax.ShapeDtypeStruct(shape, f32)] * 2
    outs += [jax.ShapeDtypeStruct((*shape[:2], width), f32)] * 2
    first = held_arrays is None
    aliases = {} if first else {1 + halves: 0, 2 + halves: 1}
    return pl.pallas_call(
        functools.partial(finish_kernel, layer_at, unit, held, halves, rows, first),
        out_shape=outs,
        in_specs=[SCALARS] + [NEAR] * halves + ([] if first else [FAR, FAR, NEAR, NEAR]),
        out_specs=[FAR, FAR, NEAR, NEAR],
        scratch_shapes=[
            pltpu.VMEM((halves, 2, rows, width), f32),
            pltpu.SemaphoreType.DMA((halves, 2)),
        ],
        input_output_aliases=aliases,
        compiler_params=kernel_params(),
        cost_estimate=pl.CostEstimate(flops=0, bytes_accessed=halves * 12 * rows * width, transcendentals=0),
    )(place, *sources, *([] if first else held_arrays))


def flip(array, axis, bits):
    size = lax.axis_size(axis)
    return lax.ppermute(array, axis, [(i, i ^ bits) for i in range(size)])


def add_low(*arrays):
    level = [a.astype(f32) for a in arrays]
    while len(level) > 1:
        level = [level[i] + level[i + 1] for i in range(0, len(level), 2)]
    return level[0].astype(bf16)


def after(arrays, others):
    return lax.optimization_barrier((arrays, others))[0]


def near(mine, groups):
    if groups == 4 and mine.shape[0] == 2:
        return {1: [flip(mine, "expert", 1)], 2: [flip(mine, "expert", 2)]}
    return {ro: [flip(mine, "expert", ro)] for ro in range(1, groups)}


def relay(arrived, groups, held):
    if groups == 4 and held == 2:
        return {3: [flip(arrived[1][0][:1], "expert", 2), flip(arrived[2][0][1:], "expert", 1)]}
    return {}


def crossed(parts, halves):
    return [] if halves == 1 else [flip(part, "rows", 1) for part in parts]


def scatter_start(sums, groups):
    return [sums[0]] + [flip(sums[ro], "expert", ro) for ro in range(1, groups)]


def body(
    rows_in,
    pred_grad,
    lengths,
    session_type,
    expert_in,
    expert_in_bias,
    expert_out,
    expert_out_bias,
    selector_logits,
    selector_mix,
    tower_in,
    tower_bias,
    tower_out,
):
    height, width = rows_in.shape
    layers, owned = expert_in.shape[:2]
    type_count, tasks = selector_logits.shape[1:3]
    selectors, bits = selector_logits.shape[3:]
    groups = lax.axis_size("expert")
    halves = 2 if owned % 2 == 0 else 1
    held = owned // halves
    stride = 2 * width + EXTRA
    me, row_at = lax.axis_index("expert"), lax.axis_index("rows")
    core = row_at % 2 if halves == 2 else jnp.int32(0)
    place = jnp.stack([(row_at * groups + me) * height, me, core]).astype(jnp.int32)

    def rows_of(layer_at, first):
        cut = lambda a: lax.dynamic_slice_in_dim(a[layer_at], first, held)
        tail = []
        for bias in (cut(expert_in_bias), cut(expert_out_bias)):
            high = bias.astype(bf16)
            tail += [high, (bias - high.astype(f32)).astype(bf16)]
        tail = jnp.pad(jnp.stack(tail, axis=1), ((0, 0), (0, EXTRA - len(tail)), (0, 0)))
        return jnp.concatenate([cut(expert_in), cut(expert_out), tail], axis=1)

    own = [[rows_of(layer_at, held * (core ^ half)) for half in range(halves)] for layer_at in range(layers)]
    sizes = (owned, halves, held, selectors, bits, tasks)
    types, across_types, gate_slopes, *values = prepare_call(
        place, lengths, session_type, selector_logits, selector_mix, height, sizes
    )

    def parts_of(got, across):
        pieces, places = [], {}
        for ro in got:
            spots = []
            for parts in (got[ro], across[ro]):
                here = []
                for part in parts:
                    here += [(len(pieces), at) for at in range(part.shape[0])]
                    pieces.append(part)
                if here:
                    spots.append(here)
            places[ro] = [[spots[half][unit] for half in range(halves)] for unit in range(held)]
        return pieces, places

    def pair_order(places, units):
        return tuple(spot for ro in sorted(places) for unit in units for spot in places[ro][unit])

    streams, stashes, weights = [rows_in], [], []
    for layer_at in range(layers):
        last = layer_at == layers - 1
        got = near(own[layer_at][0], groups)
        if layer_at == 0:
            got = after(got, types)
        far = relay(got, groups, held)
        across = {ro: crossed(got[ro], halves) for ro in got}
        if not last:
            own[layer_at + 1] = after(own[layer_at + 1], across)
        got = {0: own[layer_at][:1], **got}
        across[0] = own[layer_at][1:]
        if not last:
            pieces, places = parts_of(got, across)
            total, stash = forward_call(
                streams[-1], types, values[layer_at], None, None, pieces, pair_order(places, range(held)), 0
            )
            far = after(far, total)
        elif streams[1:]:
            far = after(far, streams[-1])
        far_across = {ro: crossed(far[ro], halves) for ro in far}
        if not last:
            if far:
                pieces, places = parts_of(far, far_across)
                base = held * min(far)
                order = pair_order(places, range(held))
                total, stash = forward_call(
                    streams[-1], types, values[layer_at], total, stash, pieces, order, base
                )
            streams.append(total[0])
            stashes.append(stash)
        weights.append(parts_of({**got, **far}, {**across, **far_across}))

    pieces, places = weights[-1]
    predictions, stream, small, tower_small, *rest = middle_call(
        place,
        streams[-1],
        types,
        across_types,
        values[-1],
        gate_slopes,
        (pred_grad, tower_in, tower_bias, tower_out),
        pieces,
        pair_order(places, range(held)),
        groups,
        halves,
        held,
    )
    tower_rows, rest = rest[:halves], rest[halves:]
    payloads = [rest[unit * halves : (unit + 1) * halves] for unit in range(held)]

    tower_tail = tower_rows[0]
    if halves == 2:
        tower_tail = add_low(tower_rows[0], flip(tower_rows[1], "rows", 1))
    tails = [[] for _ in range(held - 1)] + [[small, tower_small, tower_tail]]

    shards = lax.axis_size("rows")
    if shards == 8 and halves == 2:
        hops = [[(0, 1), (3, 2)], [(1, 2), (2, 1)], [(1, 0), (2, 3)]]
        hops = [[(2 * a + c, 2 * b + c) for a, b in hop for c in range(2)] for hop in hops]
    else:
        hops = [[(i, i ^ (2 << at)) for i in range(shards)] for at in range(shards.bit_length() - 2)]
    outer = (row_at < 2) | (row_at >= shards - 2)
    line = shards == 8 and halves == 2

    class Moving:
        def __init__(self, layer_at, unit, sums):
            self.layer_at, self.unit, self.sums, self.got, self.hops = layer_at, unit, sums, None, -1

        def ask(self, token):
            if self.got is None:
                self.got = scatter_start(after(self.sums, token), groups)
            elif self.hops < len(hops):
                total = after(self.total, token)
                self.got = [total, lax.ppermute(total, "rows", hops[self.hops])]
            else:
                self.got = [self.total] + ([flip(after(self.total, token), "rows", 1)] if halves == 2 else [])

        def add(self):
            if self.hops == len(hops):
                return True
            if line and self.hops == len(hops) - 1:
                self.total = jnp.where(outer, self.got[1], self.got[0])
            else:
                self.total = add_low(*self.got)
            self.hops += 1
            return False

    def arrive(entries, others):
        got, others = lax.optimization_barrier(([entry.got for entry in entries], others))
        for entry, what in zip(entries, got):
            entry.got = what
        ended = [entry for entry in entries if entry.add()]
        return ([entry.total for entry in entries], others), ended

    def core_received(payloads):
        return lax.optimization_barrier([flip(payload[-1], "rows", 1) for payload in payloads])

    def core_sums(payload, received, tails):
        if halves == 1:
            tails = [add_low(a, flip(a, "rows", 1)) for a in tails]
        return [
            jnp.concatenate([add_low(payload[0][ro], received[ro]), *tails], axis=0) for ro in range(groups)
        ]

    moving = []
    for unit, received in enumerate(core_received(payloads)):
        sums = core_sums(payloads[unit], received, tails[unit])
        stream = after(stream, sums)
        moving.append(Moving(layers - 1, unit, sums))
    moving[0].ask(())

    for layer_at in reversed(range(layers - 1)):
        pieces, places = weights[layer_at]
        fresh = []
        grad = stream
        for unit in range(held):
            stream, small, *payload = backward_call(
                streams[layer_at],
                types,
                across_types,
                grad,
                stream,
                gate_slopes,
                layer_at,
                values[layer_at],
                stashes[layer_at],
                pieces,
                pair_order(places, [unit]),
                held,
                unit,
                tasks,
            )
            beside = moving if unit == held - 1 else moving[: unit + 1]
            token, _ = arrive(beside, stream)
            stream = after(stream, token)
            if unit < held - 1:
                for entry in moving[: unit + 2]:
                    entry.ask(token)
            fresh.append((payload, small))
        received = core_received(after([payload for payload, _ in fresh], token))
        small = sum(part.astype(f32) for _, part in fresh).astype(bf16)
        for unit, (payload, _) in enumerate(fresh):
            sums = core_sums(payload, received[unit], [] if unit else [small])
            token = (token, sums)
            moving = moving + [Moving(layer_at, unit, sums)]

    arrays = None
    gate_grads = [0.0] * layers

    def finish(entry):
        nonlocal arrays, tower_bias_sum, tower_out_sum, tower_rows
        layer_at, unit, sources = entry.layer_at, entry.unit, entry.got
        arrays = finish_call(place, sources, arrays, layer_at, unit, held, expert_in.shape)
        if sources[0].shape[0] > stride:
            both = functools.reduce(jnp.add, [a[stride:].astype(f32) for a in sources])
            gate_grads[layer_at] = gate_grads[layer_at] + both[: type_count // 2]
            if layer_at == layers - 1:
                at = type_count // 2
                tower_bias_sum = both[at].reshape(tower_bias.shape)
                tower_out_sum = both[at + 1].reshape(tower_out.shape)
                tower_rows = [a[stride + at + EXTRA :].astype(f32) for a in sources]

    tower_bias_sum = tower_out_sum = tower_rows = None
    others = ()
    started = layers * held - held + 1
    while moving:
        for entry in moving[:started]:
            entry.ask(token)
        token, ended = arrive(moving[:started], others)
        moving = [entry for entry in moving if entry not in ended]
        started += 1 - len(ended)
        for entry in ended:
            finish(entry)
        others = (arrays, gate_grads, tower_rows) if ended else ()
    if halves == 2:
        tower_rows = [jnp.where(core == 0, *tower_rows), jnp.where(core == 0, *tower_rows[::-1])]
    wide = jnp.concatenate(tower_rows).reshape(tasks, -1, width)
    narrow = tower_in.shape[2]
    tower_in_sum = jnp.concatenate([wide[:, :, at : at + narrow] for at in range(0, width, narrow)], axis=1)
    quantities = selectors * (bits + 1)
    small = jnp.stack(gate_grads)
    small = jnp.concatenate([small[..., :LANES], small[..., LANES:]], axis=1)[..., : tasks * quantities]
    small = small.reshape(layers, type_count, tasks, quantities)
    logits_grad = small[..., : selectors * bits].reshape(selector_logits.shape)
    return (
        predictions,
        stream,
        arrays[0],
        arrays[2],
        arrays[1],
        arrays[3],
        logits_grad,
        small[..., selectors * bits :],
        tower_in_sum,
        tower_bias_sum,
        tower_out_sum,
    )


def solution(mesh):
    in_specs = (
        P(("rows", "expert"), None),
        P(("rows", "expert"), None),
        P(),
        P(),
        P(None, "expert", None, None),
        P(None, "expert", None),
        P(None, "expert", None, None),
        P(None, "expert", None),
        P(),
        P(),
        P(),
        P(),
        P(),
    )
    out_specs = (
        P(("rows", "expert"), None),
        P(("rows", "expert"), None),
        P(None, "expert", None, None),
        P(None, "expert", None),
        P(None, "expert", None, None),
        P(None, "expert", None),
        P(),
        P(),
        P(),
        P(),
        P(),
    )
    return jax.shard_map(body, mesh=mesh, in_specs=in_specs, out_specs=out_specs, check_vma=False)
```

time: 1140 us -> 231 us (0.20)
  waiting for transfers between devices: 420 us -> 51.4 us
  blocking collectives: 357 us -> 0 us
  matrix products: 205 us -> 0 us
  Pallas kernels: 0 us -> 102 us
  local copies, waits for them, and re-layouts: 61.7 us -> 13.8 us
  other arithmetic: 42.9 us -> 8.24 us
  starting transfers between devices: 29.8 us -> 52.1 us
  between operations: 15 us -> 1.9 us
    all_to_all x5 -> x0, waiting for transfers between devices: 354 us -> none  [the longest x2 181 us: run_layer(): lax.all_to_all(produced, 'expert', split_axis=0, concat_axis=0, tiled=True)]
    all_to_all x3 -> x0, blocking collectives: 289 us -> none  [the longest x1 96.7 us: run_layer(): lax.all_to_all(sendable, 'expert', split_axis=0, concat_axis=0, tiled=True)]
    dot_general x26 -> x0, matrix products: 205 us -> none  [the longest x2 38.1 us: back_layer(): jnp.einsum('serd,ehd->serh', arrived, weight_out, preferred_element_type=...]
    pallas_call x0 -> x10, Pallas kernels: none -> 102 us  [the longest x1 40.3 us: middle_call(): pl.pallas_call(functools.partial(middle_kernel, places, len(pieces), grou...]
    psum x2 -> x0, blocking collectives: 68.8 us -> none  [the longest x1 54.3 us: body(): lax.psum((jnp.stack(table_grads), tower_in_grad, tower_bias_grad, tower_o...]
    psum x2 -> x0, waiting for transfers between devices: 66 us -> none  [the longest x1 66 us: body(): lax.psum((jnp.stack(table_grads), tower_in_grad, tower_bias_grad, tower_o...]
    ppermute x0 -> x49, starting transfers between devices: none -> 52.1 us  [the longest x37 27.8 us: flip(): return lax.ppermute(array, axis, [(i, i ^ bits) for i in range(size)])]
    ppermute x0 -> x49, waiting for transfers between devices: none -> 51.4 us  [the longest x37 36.3 us: flip(): return lax.ppermute(array, axis, [(i, i ^ bits) for i in range(size)])]
  transfers between devices with their start and end apart: 7 -> 49, of which waited for: 5 -> 14; matrix products, arithmetic and copies ran while one was open for 9% -> 4% of each run, Pallas kernels for 0% -> 26%
where the time goes in v1:
time: 231 us; the launch traced here: 230 us
  Pallas kernels  102 us (44%)
  starting transfers between devices  52.1 us (23%)
  waiting for transfers between devices  51.4 us (22%)
  local copies, waits for them, and re-layouts  13.8 us (6%)
  other arithmetic  8.24 us (4%)
    pallas_call x1, Pallas kernels, middle_call(): pl.pallas_call(functools.partial(middle_kernel, places, len(pieces), grou...  40.3 us
    ppermute x37, waiting for transfers between devices, flip(): return lax.ppermute(array, axis, [(i, i ^ bits) for i in range(size)])  36.3 us
    ppermute x37, starting transfers between devices, flip(): return lax.ppermute(array, axis, [(i, i ^ bits) for i in range(size)])  27.8 us
    pallas_call x2, Pallas kernels, backward_call(): pl.pallas_call(functools.partial(backward_kernel, places, len(pieces), ea...  25.5 us
    ppermute x12, starting transfers between devices, ask(): self.got = [total, lax.ppermute(total, 'rows', hops[self.hops])]  24.3 us
    pallas_call x2, Pallas kernels, forward_call(): pl.pallas_call(functools.partial(forward_kernel, places, len(pieces), eac...  22.5 us
    ppermute x12, waiting for transfers between devices, ask(): self.got = [total, lax.ppermute(total, 'rows', hops[self.hops])]  15.1 us
    pallas_call x4, Pallas kernels, finish_call(): pl.pallas_call(functools.partial(finish_kernel, layer_at, unit, held, hal...  10.7 us
  transfers between devices with their start and end apart: 49, of which 14 were waited for; matrix products, arithmetic and copies ran while one was open for 4% of the time, Pallas kernels for 26%

profile of v1, /device:TPU:0, one launch (start us, length us, event | category | flops | bytes accessed | tf_op | source)
XLA Modules:
  0.0 229.6 jit_solution(3711275399403747809)
XLA Ops:
  3.8 3.0 %collective-permute-start = (bf16[2,528,256]{2,1,0:T(8,128)(2,1)S(1)}, bf16[2,528,256]{2,1,0:T(8,128)(2,1)S(1)}, u32[]{:S(2)}, u32[]{:S(2)}) collective-permute-start(bf16[2,528,256]{2,1,0:T(8,128)(2,1)S(1)} %pad_maximum_fusion.16.refs_3_.refs_9_), channel_id=1, source_target_pairs={{0,1},{1,0},{2,3},{3,2},{4,5},{5,4},{6,7},{7,6},{8,9},{9,8},{10,11... | collective-permute-start | bytes 1622024 | tf_op jit(solution)/shard_map/ppermute | solution.py:719
  10.7 3.2 %shard_map.230 = (bf16[1024,32]{1,0:T(8,128)(2,1)}, bf16[32,1024]{1,0:T(8,128)(2,1)}, f32[20,64,128]{2,1,0:T(8,128)}, bf16[8,32,256]{2,1,0:T(8,128)(2,1)}, bf16[8,32,512]{2,1,0:T(8,128)(2,1)}) custom-call(s32[3]{0:T(128)} %pad_add_fusion.place_ref.refs_0_, s32[1,256]{1,0:T(1,128)} %bitcast.71, s32[1,256]{1,0:T(1,128)} %bitcast.72, f32[64,32]{1,0:T(8,128)} %copy.42.logit_ref, ...), custom_call_target="tpu_custom_call" | custom-call | flops 33554432 | bytes 2097152 | tf_op jit(solution)/shard_map/pallas_call | solution.py:169
  14.0 5.1 %collective-permute-done.refs_5_.refs_11_ = bf16[2,528,256]{2,1,0:T(8,128)(2,1)S(1)} collective-permute-done((bf16[2,528,256]{2,1,0:T(8,128)(2,1)S(1)}, bf16[2,528,256]{2,1,0:T(8,128)(2,1)S(1)}, u32[]{:S(2)}, u32[]{:S(2)}) %collective-permute-start) | collective-permute-done | bytes 540704 | tf_op jit(solution)/shard_map/ppermute | solution.py:719
  27.3 14.5 %shard_map.231 = (f32[1,1024,256]{2,1,0:T(8,128)}, bf16[8,2,1024,256]{3,2,1,0:T(8,128)(2,1)}, bf16[8,2,1024,256]{3,2,1,0:T(8,128)(2,1)}) custom-call(f32[1024,256]{1,0:T(8,128)} %refs_0_.7, bf16[1024,32]{1,0:T(8,128)(2,1)} %get-tuple-element.162.refs_1_.refs_2_, bf16[8,32,256]{2,1,0:T(8,128)(2,1)} %get-tuple-element.163.refs_2_.refs_6_, ...), custom_call_target="tpu_custom_call" | custom-call | flops 3221225472 | bytes 17825792 | tf_op jit(solution)/shard_map/pallas_call | solution.py:379
  46.7 8.0 %shard_map.232 = (f32[1,1024,256]{2,1,0:T(8,128)}, bf16[8,2,1024,256]{3,2,1,0:T(8,128)(2,1)}, bf16[8,2,1024,256]{3,2,1,0:T(8,128)(2,1)}) custom-call(f32[1024,256]{1,0:T(8,128)} %refs_0_.7, bf16[1024,32]{1,0:T(8,128)(2,1)} %get-tuple-element.162.refs_1_.refs_2_, ...), custom_call_target="tpu_custom_call", output_to_operand_aliasing={{1}: (4, {}), {2}: (5, {})} | custom-call | flops 1073741824 | bytes 7340032 | tf_op jit(solution)/shard_map/pallas_call | solution.py:379
  57.8 40.3 %shard_map.233 = (f32[1024,2]{1,0:T(8,128)}, f32[1024,256]{1,0:T(8,128)}, bf16[16,256]{1,0:T(8,128)(2,1)}, bf16[16,256]{1,0:T(8,128)(2,1)}, bf16[128,256]{1,0:T(...) custom-call(s32[3]{0:T(128)} %pad_add_fusion.place_ref.refs_0_, ...), custom_call_target="tpu_custom_call" | custom-call | flops 15032385536 | bytes 12582912 | tf_op jit(solution)/shard_map/pallas_call | solution.py:546
  98.8 3.9 %collective-permute-done.18 = bf16[128,256]{1,0:T(8,128)(2,1)S(1)} collective-permute-done((bf16[128,256]{1,0:T(8,128)(2,1)}, bf16[128,256]{1,0:T(8,128)(2,1)S(1)}, u32[]{:S(2)}, u32[]{:S(2)}) %collective-permute-start.18) | collective-permute-done | bytes 65568 | tf_op jit(solution)/shard_map/ppermute | solution.py:719
  109.6 13.0 %shard_map.234 = (f32[1024,256]{1,0:T(8,128)}, bf16[16,256]{1,0:T(8,128)(2,1)}, bf16[4,528,256]{2,1,0:T(8,128)(2,1)}, bf16[4,528,256]{2,1,0:T(8,128)(2,1)}) custom-call(f32[1024,256]{1,0:T(8,128)} %refs_0_.7, bf16[1024,32]{1,0:T(8,128)(2,1)} %get-tuple-element.162.refs_1_.refs_2_, bf16[32,1024]{1,0:T(8,128)(2,1)} %get-tuple-element.172.refs_3_.refs_2_, ...), custom_call_target="tpu_custom_call" | custom-call | flops 4294967296 | bytes 16777216 | tf_op jit(solution)/shard_map/pallas_call | solution.py:640
  126.3 3.6 %collective-permute-start.22 = (bf16[528,256]{1,0:T(8,128)(2,1)S(1)}, bf16[528,256]{1,0:T(8,128)(2,1)S(1)}, u32[]{:S(2)}, u32[]{:S(2)}) collective-permute-start(bf16[528,256]{1,0:T(8,128)(2,1)S(1)} %add_convert_fusion.19), channel_id=1, source_target_pairs={{0,8},{4,12},{24,16},{28,20},{1,9},{5,13},{25,17},{29,21},{2,10},{... | collective-permute-start | bytes 811016 | tf_op jit(solution)/shard_map/ppermute | solution.py:886
  129.9 12.5 %shard_map.235 = (f32[1024,256]{1,0:T(8,128)}, bf16[16,256]{1,0:T(8,128)(2,1)}, bf16[4,528,256]{2,1,0:T(8,128)(2,1)}, bf16[4,528,256]{2,1,0:T(8,128)(2,1)}) custom-call(f32[1024,256]{1,0:T(8,128)} %refs_0_.7, bf16[1024,32]{1,0:T(8,128)(2,1)} %get-tuple-element.162.refs_1_.refs_2_, bf16[32,1024]{1,0:T(8,128)(2,1)} %get-tuple-element.172.refs_3_.refs_2_, ...), custom_call_target="tpu_custom_call" | custom-call | flops 4294967296 | bytes 16777216 | tf_op jit(solution)/shard_map/pallas_call | solution.py:640
  144.3 3.7 %collective-permute-done.26 = bf16[4,528,256]{2,1,0:T(8,128)(2,1)S(1)} collective-permute-done((bf16[4,528,256]{2,1,0:T(8,128)(2,1)S(1)}, bf16[4,528,256]{2,1,0:T(8,128)(2,1)S(1)}, u32[]{:S(2)}, u32[]{:S(2)}) %collective-permute-start.26) | collective-permute-done | bytes 1081376 | tf_op jit(solution)/shard_map/ppermute | solution.py:719
  148.8 2.1 collective-permute-start.29
  155.2 5.4 %collective-permute-done.30 = bf16[544,256]{1,0:T(8,128)(2,1)S(1)} collective-permute-done((bf16[544,256]{1,0:T(8,128)(2,1)S(1)}, bf16[544,256]{1,0:T(8,128)(2,1)S(1)}, u32[]{:S(2)}, u32[]{:S(2)}) %collective-permute-start.30) | collective-permute-done | bytes 278560 | tf_op jit(solution)/shard_map/ppermute | solution.py:719
  160.6 4.6 %collective-permute-done.31 = bf16[544,256]{1,0:T(8,128)(2,1)S(1)} collective-permute-done((bf16[544,256]{1,0:T(8,128)(2,1)S(1)}, bf16[544,256]{1,0:T(8,128)(2,1)S(1)}, u32[]{:S(2)}, u32[]{:S(2)}) %collective-permute-start.31) | collective-permute-done | bytes 278560 | tf_op jit(solution)/shard_map/ppermute | solution.py:719
  168.4 4.2 %collective-permute-start.35 = (bf16[544,256]{1,0:T(8,128)(2,1)S(1)}, bf16[544,256]{1,0:T(8,128)(2,1)S(1)}, u32[]{:S(2)}, u32[]{:S(2)}) collective-permute-start(bf16[544,256]{1,0:T(8,128)(2,1)S(1)} %add_convert_fusion.5), channel_id=1, source_target_pairs={{0,8},{4,12},{24,16},{28,20},{1,9},{5,13},{25,17},{29,21},{2,10},{... | collective-permute-start | bytes 835592 | tf_op jit(solution)/shard_map/ppermute | solution.py:886
  177.0 8.3 %collective-permute-done.37 = bf16[528,256]{1,0:T(8,128)(2,1)S(1)} collective-permute-done((bf16[528,256]{1,0:T(8,128)(2,1)S(1)}, bf16[528,256]{1,0:T(8,128)(2,1)S(1)}, u32[]{:S(2)}, u32[]{:S(2)}) %collective-permute-start.37) | collective-permute-done | bytes 270368 | tf_op jit(solution)/shard_map/ppermute | solution.py:719
  187.7 6.3 %collective-permute-start.42 = (bf16[528,256]{1,0:T(8,128)(2,1)S(1)}, bf16[528,256]{1,0:T(8,128)(2,1)S(1)}, u32[]{:S(2)}, u32[]{:S(2)}) collective-permute-start(bf16[528,256]{1,0:T(8,128)(2,1)S(1)} %add_convert_fusion.8), channel_id=1, source_target_pairs={{0,8},{4,12},{24,16},{28,20},{1,9},{5,13},{25,17},{29,21},{2,10},{... | collective-permute-start | bytes 811016 | tf_op jit(solution)/shard_map/ppermute | solution.py:886
  194.0 3.9 %collective-permute-done.42 = bf16[528,256]{1,0:T(8,128)(2,1)S(1)} collective-permute-done((bf16[528,256]{1,0:T(8,128)(2,1)S(1)}, bf16[528,256]{1,0:T(8,128)(2,1)S(1)}, u32[]{:S(2)}, u32[]{:S(2)}) %collective-permute-start.42) | collective-permute-done | bytes 270368 | tf_op jit(solution)/shard_map/ppermute | solution.py:886
  201.4 2.7 %shard_map.236 = (f32[2,4,256,256]{3,2,1,0:T(8,128)}, f32[2,4,256,256]{3,2,1,0:T(8,128)}, f32[2,4,256]{2,1,0:T(4,128)}, f32[2,4,256]{2,1,0:T(4,128)}) custom-call(s32[3]{0:T(128)} %pad_add_fusion.place_ref.refs_0_, bf16[528,256]{1,0:T(8,128)(2,1)} %copy-done.15, bf16[528,256]{1,0:T(8,128)(2,1)} %copy-done.22), custom_call_target="tpu_custom_call" | custom-call | bytes 1572864 | tf_op jit(solution)/shard_map/pallas_call | solution.py:702
  204.1 5.6 %collective-permute-done.44 = bf16[544,256]{1,0:T(8,128)(2,1)S(1)} collective-permute-done((bf16[544,256]{1,0:T(8,128)(2,1)S(1)}, bf16[544,256]{1,0:T(8,128)(2,1)S(1)}, u32[]{:S(2)}, u32[]{:S(2)}) %collective-permute-start.44) | collective-permute-done | bytes 278560 | tf_op jit(solution)/shard_map/ppermute | solution.py:886
  213.1 2.7 %shard_map.237 = (f32[2,4,256,256]{3,2,1,0:T(8,128)}, f32[2,4,256,256]{3,2,1,0:T(8,128)}, f32[2,4,256]{2,1,0:T(4,128)}, f32[2,4,256]{2,1,0:T(4,128)}) custom-call(s32[3]{0:T(128)} %pad_add_fusion.place_ref.refs_0_, bf16[688,256]{1,0:T(8,128)(2,1)} %copy-done.9, bf16[688,256]{1,0:T(8,128)(2,1)} %copy-done.17, ...), custom_call_target="tpu_custom_call", output_to_operand_aliasing={{0}: (3, {}), {1}: (4, {})} | custom-call | bytes 1572864 | tf_op jit(solution)/shard_map/pallas_call | solution.py:702
  215.9 5.6 %collective-permute-done.47 = bf16[528,256]{1,0:T(8,128)(2,1)S(1)} collective-permute-done((bf16[528,256]{1,0:T(8,128)(2,1)S(1)}, bf16[528,256]{1,0:T(8,128)(2,1)S(1)}, u32[]{:S(2)}, u32[]{:S(2)}) %collective-permute-start.47) | collective-permute-done | bytes 270368 | tf_op jit(solution)/shard_map/ppermute | solution.py:886
  222.2 2.7 %shard_map.238 = (f32[2,4,256,256]{3,2,1,0:T(8,128)}, f32[2,4,256,256]{3,2,1,0:T(8,128)}, f32[2,4,256]{2,1,0:T(4,128)}, f32[2,4,256]{2,1,0:T(4,128)}) custom-call(s32[3]{0:T(128)} %pad_add_fusion.place_ref.refs_0_, bf16[544,256]{1,0:T(8,128)(2,1)} %copy-done.10, bf16[544,256]{1,0:T(8,128)(2,1)} %copy-done.20, ...), custom_call_target="tpu_custom_call", output_to_operand_aliasing={{0}: (3, {}), {1}: (4, {})} | custom-call | bytes 1572864 | tf_op jit(solution)/shard_map/pallas_call | solution.py:702
  226.8 2.7 %shard_map.239 = (f32[2,4,256,256]{3,2,1,0:T(8,128)}, f32[2,4,256,256]{3,2,1,0:T(8,128)}, f32[2,4,256]{2,1,0:T(4,128)}, f32[2,4,256]{2,1,0:T(4,128)}) custom-call(s32[3]{0:T(128)} %pad_add_fusion.place_ref.refs_0_, bf16[528,256]{1,0:T(8,128)(2,1)} %copy-done.14, bf16[528,256]{1,0:T(8,128)(2,1)} %copy-done.21, ...), custom_call_target="tpu_custom_call", output_to_operand_aliasing={{0}: (3, {}), {1}: (4, {})} | custom-call | bytes 1572864 | tf_op jit(solution)/shard_map/pallas_call | solution.py:702
  (246 shorter events, 60.3 us)
Async XLA Ops:
  3.8 15.3 %collective-permute-start = (bf16[2,528,256]{2,1,0:T(8,128)(2,1)S(1)}, bf16[2,528,256]{2,1,0:T(8,128)(2,1)S(1)}, u32[]{:S(2)}, u32[]{:S(2)}) collective-permute-start(bf16[2,528,256]{2,1,0:T(8,128)(2,1)S(1)} %pad_maximum_fusion.16.refs_3_.refs_9_), channel_id=1, source_target_pairs={{0,1},{1,0},{2,3},{3,2},{4,5},{5,4},{6,7},{7,6},{8,9},{9,8},{10,11... | collective-permute-start | bytes 1622024 | tf_op jit(solution)/shard_map/ppermute | solution.py:719
  6.8 13.7 %collective-permute-start.1 = (bf16[2,528,256]{2,1,0:T(8,128)(2,1)S(1)}, bf16[2,528,256]{2,1,0:T(8,128)(2,1)S(1)}, u32[]{:S(2)}, u32[]{:S(2)}) collective-permute-start(bf16[2,528,256]{2,1,0:T(8,128)(2,1)S(1)} %pad_maximum_fusion.16.refs_3_.refs_9_), channel_id=1, source_target_pairs={{0,2},{1,3},{2,0},{3,1},{4,6},{5,7},{6,4},{7,5},{8,10},{9,11},{10,... | collective-permute-start | bytes 1622024 | tf_op jit(solution)/shard_map/ppermute | solution.py:719
  23.0 18.7 %collective-permute-start.4 = (bf16[1,528,256]{2,1,0:T(8,128)(2,1)S(1)}, bf16[1,528,256]{2,1,0:T(8,128)(2,1)S(1)}, u32[]{:S(2)}, u32[]{:S(2)}) collective-permute-start(bf16[1,528,256]{2,1,0:T(8,128)(2,1)S(1)} %slice.192), channel_id=1, source_target_pairs={{0,2},{1,3},{2,0},{3,1},{4,6},{5,7},{6,4},{7,5},{8,10},{9,11},{10,... | collective-permute-start | bytes 811016 | tf_op jit(solution)/shard_map/ppermute | solution.py:719
  24.6 17.1 %collective-permute-start.5 = (bf16[1,528,256]{2,1,0:T(8,128)(2,1)S(1)}, bf16[1,528,256]{2,1,0:T(8,128)(2,1)S(1)}, u32[]{:S(2)}, u32[]{:S(2)}) collective-permute-start(bf16[1,528,256]{2,1,0:T(8,128)(2,1)S(1)} %slice.193), channel_id=1, source_target_pairs={{0,1},{1,0},{2,3},{3,2},{4,5},{5,4},{6,7},{7,6},{8,9},{9,8},{10,11... | collective-permute-start | bytes 811016 | tf_op jit(solution)/shard_map/ppermute | solution.py:719
  25.2 19.1 %collective-permute-start.8 = (bf16[2,528,256]{2,1,0:T(8,128)(2,1)S(1)}, bf16[2,528,256]{2,1,0:T(8,128)(2,1)S(1)}, u32[]{:S(2)}, u32[]{:S(2)}) collective-permute-start(bf16[2,528,256]{2,1,0:T(8,128)(2,1)S(1)} %pad_maximum_fusion.18.refs_10_), channel_id=1, source_target_pairs={{0,1},{1,0},{2,3},{3,2},{4,5},{5,4},{6,7},{7,6},{8,9},{9,8},{10,11... | collective-permute-start | bytes 1622024 | tf_op jit(solution)/shard_map/ppermute | solution.py:719
  26.7 18.2 %collective-permute-start.10 = (bf16[2,528,256]{2,1,0:T(8,128)(2,1)S(1)}, bf16[2,528,256]{2,1,0:T(8,128)(2,1)S(1)}, u32[]{:S(2)}, u32[]{:S(2)}) collective-permute-start(bf16[2,528,256]{2,1,0:T(8,128)(2,1)S(1)} %pad_maximum_fusion.18.refs_10_), channel_id=1, source_target_pairs={{0,2},{1,3},{2,0},{3,1},{4,6},{5,7},{6,4},{7,5},{8,10},{9,11},{10,... | collective-permute-start | bytes 1622024 | tf_op jit(solution)/shard_map/ppermute | solution.py:719
  45.4 11.3 %collective-permute-start.11 = (bf16[2,528,256]{2,1,0:T(8,128)(2,1)S(1)}, bf16[2,528,256]{2,1,0:T(8,128)(2,1)S(1)}, u32[]{:S(2)}, u32[]{:S(2)}) collective-permute-start(bf16[2,528,256]{2,1,0:T(8,128)(2,1)S(1)} %collective-permute-done.10.refs_14_), channel_id=1, source_target_pairs={{0,4},{4,0},{8,12},{12,8},{16,20},{20,16},{24,28},{28,24},{1,5},{5... | collective-permute-start | bytes 1622024 | tf_op jit(solution)/shard_map/ppermute | solution.py:719
  45.4 11.3 %collective-permute-start.9 = (bf16[2,528,256]{2,1,0:T(8,128)(2,1)S(1)}, bf16[2,528,256]{2,1,0:T(8,128)(2,1)S(1)}, u32[]{:S(2)}, u32[]{:S(2)}) collective-permute-start(bf16[2,528,256]{2,1,0:T(8,128)(2,1)S(1)} %collective-permute-done.8.refs_12_), channel_id=1, source_target_pairs={{0,4},{4,0},{8,12},{12,8},{16,20},{20,16},{24,28},{28,24},{1,5},{5... | collective-permute-start | bytes 1622024 | tf_op jit(solution)/shard_map/ppermute | solution.py:719
  105.2 17.3 %collective-permute-start.19 = (bf16[528,256]{1,0:T(8,128)(2,1)S(1)}, bf16[528,256]{1,0:T(8,128)(2,1)S(1)}, u32[]{:S(2)}, u32[]{:S(2)}) collective-permute-start(bf16[528,256]{1,0:T(8,128)(2,1)S(1)} %get-tuple-element.197), channel_id=1, source_target_pairs={{0,1},{1,0},{2,3},{3,2},{4,5},{5,4},{6,7},{7,6},{8,9},{9,8},{10,11... | collective-permute-start | bytes 811016 | tf_op jit(solution)/shard_map/ppermute | solution.py:719
  106.9 15.7 %collective-permute-start.20 = (bf16[528,256]{1,0:T(8,128)(2,1)S(1)}, bf16[528,256]{1,0:T(8,128)(2,1)S(1)}, u32[]{:S(2)}, u32[]{:S(2)}) collective-permute-start(bf16[528,256]{1,0:T(8,128)(2,1)S(1)} %get-tuple-element.198), channel_id=1, source_target_pairs={{0,2},{1,3},{2,0},{3,1},{4,6},{5,7},{6,4},{7,5},{8,10},{9,11},{10,... | collective-permute-start | bytes 811016 | tf_op jit(solution)/shard_map/ppermute | solution.py:719
  108.4 14.2 %collective-permute-start.21 = (bf16[528,256]{1,0:T(8,128)(2,1)S(1)}, bf16[528,256]{1,0:T(8,128)(2,1)S(1)}, u32[]{:S(2)}, u32[]{:S(2)}) collective-permute-start(bf16[528,256]{1,0:T(8,128)(2,1)S(1)} %get-tuple-element.199), channel_id=1, source_target_pairs={{0,3},{1,2},{2,1},{3,0},{4,7},{5,6},{6,5},{7,4},{8,11},{9,10},{10,... | collective-permute-start | bytes 811016 | tf_op jit(solution)/shard_map/ppermute | solution.py:719
  122.7 19.7 %collective-permute-start.23 = (bf16[688,256]{1,0:T(8,128)(2,1)S(1)}, bf16[688,256]{1,0:T(8,128)(2,1)S(1)}, u32[]{:S(2)}, u32[]{:S(2)}) collective-permute-start(bf16[688,256]{1,0:T(8,128)(2,1)S(1)} %get-tuple-element.209), channel_id=1, source_target_pairs={{0,1},{1,0},{2,3},{3,2},{4,5},{5,4},{6,7},{7,6},{8,9},{9,8},{10,11... | collective-permute-start | bytes 1056776 | tf_op jit(solution)/shard_map/ppermute | solution.py:719
  124.4 18.1 %collective-permute-start.24 = (bf16[688,256]{1,0:T(8,128)(2,1)S(1)}, bf16[688,256]{1,0:T(8,128)(2,1)S(1)}, u32[]{:S(2)}, u32[]{:S(2)}) collective-permute-start(bf16[688,256]{1,0:T(8,128)(2,1)S(1)} %get-tuple-element.210), channel_id=1, source_target_pairs={{0,2},{1,3},{2,0},{3,1},{4,6},{5,7},{6,4},{7,5},{8,10},{9,11},{10,... | collective-permute-start | bytes 1056776 | tf_op jit(solution)/shard_map/ppermute | solution.py:719
  125.9 16.6 %collective-permute-start.25 = (bf16[688,256]{1,0:T(8,128)(2,1)S(1)}, bf16[688,256]{1,0:T(8,128)(2,1)S(1)}, u32[]{:S(2)}, u32[]{:S(2)}) collective-permute-start(bf16[688,256]{1,0:T(8,128)(2,1)S(1)} %get-tuple-element.211), channel_id=1, source_target_pairs={{0,3},{1,2},{2,1},{3,0},{4,7},{5,6},{6,5},{7,4},{8,11},{9,10},{10,... | collective-permute-start | bytes 1056776 | tf_op jit(solution)/shard_map/ppermute | solution.py:719
  126.3 16.2 %collective-permute-start.22 = (bf16[528,256]{1,0:T(8,128)(2,1)S(1)}, bf16[528,256]{1,0:T(8,128)(2,1)S(1)}, u32[]{:S(2)}, u32[]{:S(2)}) collective-permute-start(bf16[528,256]{1,0:T(8,128)(2,1)S(1)} %add_convert_fusion.19), channel_id=1, source_target_pairs={{0,8},{4,12},{24,16},{28,20},{1,9},{5,13},{25,17},{29,21},{2,10},{... | collective-permute-start | bytes 811016 | tf_op jit(solution)/shard_map/ppermute | solution.py:886
  148.8 17.6 %collective-permute-start.29 = (bf16[688,256]{1,0:T(8,128)(2,1)S(1)}, bf16[688,256]{1,0:T(8,128)(2,1)S(1)}, u32[]{:S(2)}, u32[]{:S(2)}) collective-permute-start(bf16[688,256]{1,0:T(8,128)(2,1)S(1)} %add_convert_fusion.2), channel_id=1, source_target_pairs={{0,8},{4,12},{24,16},{28,20},{1,9},{5,13},{25,17},{29,21},{2,10},{... | collective-permute-start | bytes 1056776 | tf_op jit(solution)/shard_map/ppermute | solution.py:886
  152.3 12.9 %collective-permute-start.31 = (bf16[544,256]{1,0:T(8,128)(2,1)S(1)}, bf16[544,256]{1,0:T(8,128)(2,1)S(1)}, u32[]{:S(2)}, u32[]{:S(2)}) collective-permute-start(bf16[544,256]{1,0:T(8,128)(2,1)S(1)} %get-tuple-element.234), channel_id=1, source_target_pairs={{0,2},{1,3},{2,0},{3,1},{4,6},{5,7},{6,4},{7,5},{8,10},{9,11},{10,... | collective-permute-start | bytes 835592 | tf_op jit(solution)/shard_map/ppermute | solution.py:719
  153.2 13.1 %collective-permute-start.32 = (bf16[544,256]{1,0:T(8,128)(2,1)S(1)}, bf16[544,256]{1,0:T(8,128)(2,1)S(1)}, u32[]{:S(2)}, u32[]{:S(2)}) collective-permute-start(bf16[544,256]{1,0:T(8,128)(2,1)S(1)} %get-tuple-element.235), channel_id=1, source_target_pairs={{0,3},{1,2},{2,1},{3,0},{4,7},{5,6},{6,5},{7,4},{8,11},{9,10},{10,... | collective-permute-start | bytes 835592 | tf_op jit(solution)/shard_map/ppermute | solution.py:719
  167.7 17.5 %collective-permute-start.34 = (bf16[688,256]{1,0:T(8,128)(2,1)S(1)}, bf16[688,256]{1,0:T(8,128)(2,1)S(1)}, u32[]{:S(2)}, u32[]{:S(2)}) collective-permute-start(bf16[688,256]{1,0:T(8,128)(2,1)S(1)} %add_convert_fusion.1), channel_id=1, source_target_pairs={{8,16},{12,20},{16,8},{20,12},{9,17},{13,21},{17,9},{21,13},{10,18... | collective-permute-start | bytes 1056776 | tf_op jit(solution)/shard_map/ppermute | solution.py:886
  168.4 16.8 %collective-permute-start.35 = (bf16[544,256]{1,0:T(8,128)(2,1)S(1)}, bf16[544,256]{1,0:T(8,128)(2,1)S(1)}, u32[]{:S(2)}, u32[]{:S(2)}) collective-permute-start(bf16[544,256]{1,0:T(8,128)(2,1)S(1)} %add_convert_fusion.5), channel_id=1, source_target_pairs={{0,8},{4,12},{24,16},{28,20},{1,9},{5,13},{25,17},{29,21},{2,10},{... | collective-permute-start | bytes 835592 | tf_op jit(solution)/shard_map/ppermute | solution.py:886
  172.6 12.6 %collective-permute-start.37 = (bf16[528,256]{1,0:T(8,128)(2,1)S(1)}, bf16[528,256]{1,0:T(8,128)(2,1)S(1)}, u32[]{:S(2)}, u32[]{:S(2)}) collective-permute-start(bf16[528,256]{1,0:T(8,128)(2,1)S(1)} %get-tuple-element.249), channel_id=1, source_target_pairs={{0,2},{1,3},{2,0},{3,1},{4,6},{5,7},{6,4},{7,5},{8,10},{9,11},{10,... | collective-permute-start | bytes 811016 | tf_op jit(solution)/shard_map/ppermute | solution.py:719
  185.7 12.2 %collective-permute-start.40 = (bf16[688,256]{1,0:T(8,128)(2,1)S(1)}, bf16[688,256]{1,0:T(8,128)(2,1)S(1)}, u32[]{:S(2)}, u32[]{:S(2)}) collective-permute-start(bf16[688,256]{1,0:T(8,128)(2,1)S(1)} %add_convert_fusion), channel_id=1, source_target_pairs={{8,0},{12,4},{16,24},{20,28},{9,1},{13,5},{17,25},{21,29},{10,2},{... | collective-permute-start | bytes 1056776 | tf_op jit(solution)/shard_map/ppermute | solution.py:886
  198.6 11.1 %collective-permute-start.43 = (bf16[688,256]{1,0:T(8,128)(2,1)S(1)}, bf16[688,256]{1,0:T(8,128)(2,1)S(1)}, u32[]{:S(2)}, u32[]{:S(2)}) collective-permute-start(bf16[688,256]{1,0:T(8,128)(2,1)S(1)} %broadcast_select_fusion.refs_1_), channel_id=1, source_target_pairs={{0,4},{4,0},{8,12},{12,8},{16,20},{20,16},{24,28},{28,24},{1,5},{5... | collective-permute-start | bytes 1056776 | tf_op jit(solution)/shard_map/ppermute | solution.py:719
  198.6 11.1 %collective-permute-start.44 = (bf16[544,256]{1,0:T(8,128)(2,1)S(1)}, bf16[544,256]{1,0:T(8,128)(2,1)S(1)}, u32[]{:S(2)}, u32[]{:S(2)}) collective-permute-start(bf16[544,256]{1,0:T(8,128)(2,1)S(1)} %add_convert_fusion.3), channel_id=1, source_target_pairs={{8,0},{12,4},{16,24},{20,28},{9,1},{13,5},{17,25},{21,29},{10,2},{... | collective-permute-start | bytes 835592 | tf_op jit(solution)/shard_map/ppermute | solution.py:886
  (64 other events, 315.8 us)

commit v2 on v1

--- a/solution.py
+++ b/solution.py
@@ -46,12 +46,12 @@
 
 
 def gelu_low(v):
-    square = v * v
-    half = 0.5 + 0.5 * jnp.tanh(v * (INNER + CUBE * square))
-    value = (v * half).astype(bf16)
-    bend = (2.0 * INNER + 6.0 * CUBE * square).astype(bf16)
-    half = half.astype(bf16)
-    return value, half + value * (1.0 - half) * bend
+    bend = 2.0 * INNER + 8.0 * CUBE * (v * v)
+    twice_share = 1.0 + jnp.tanh(v * bend)
+    value = (v * twice_share).astype(bf16)
+    bend, twice_share = bend.astype(bf16), twice_share.astype(bf16)
+    rise = 3.0 * bend - 4.0 * INNER
+    return value, twice_share + value * (2.0 - twice_share) * rise
 
 
 FAR = pl.BlockSpec(memory_space=pl.ANY)
@@ -207,13 +207,16 @@
     return [gates[:, at * LANES : (at + 1) * LANES] for at in range(count)]
 
 
-def forward_step(weights, value_ref, x_low, type_ref, total_ref, biases, keep):
+def forward_step(weights, value_ref, x_low, type_ref, total_ref, biases, keep, keep_gate=None):
     height, width = x_low.shape
     kinds = total_ref.shape[0]
     bias_in, bias_out = zip(*(bias_rows(w, width) for w in weights))
     second = joined([w[width : 2 * width] for w in weights], 0)
     for rows in tiles(height, TILE):
         gates = gates_of(type_ref[rows], value_ref, len(weights) * kinds)
+        if keep_gate is not None:
+            for at, gate in enumerate(gates):
+                keep_gate(at, rows, gate)
         scaled = [[] for _ in range(kinds)]
         for i, w in enumerate(weights):
             hidden, slope = gelu_low(mm(x_low[rows], w[0:width]) + bias_in[i])
@@ -245,13 +248,17 @@
         share[t] = mm(type_across[...], low[t])
 
 
-def backward_step(weights, value_ref, hiddens, slopes, outs, pair, experts, type_ref, type_across, low, stream_ref, across, share, table, scratch):
+def backward_step(weights, value_ref, hiddens, slopes, outs, pair, experts, type_ref, type_across, low, stream_ref, across, share, table, scratch, kept_gates=None):
     before_grads, result_grads, products = scratch
     kinds, height, width = low.shape
     count = len(weights)
     first = joined([w[0:width] for w in weights], 1)
     for rows in tiles(height, TILE):
-        gates = [twice(gate) for gate in gates_of(type_ref[rows], value_ref, count * kinds)]
+        if kept_gates is None:
+            gates = gates_of(type_ref[rows], value_ref, count * kinds)
+        else:
+            gates = [kept_gates[at, rows] for at in range(count * kinds)]
+        gates = [twice(gate) for gate in gates]
         befores = []
         for i, w in enumerate(weights):
             hidden, slope = hiddens[i][rows], slopes[i][rows]
@@ -282,7 +289,7 @@
     lanes = lax.broadcasted_iota(jnp.int32, (type_ref.shape[1], LANES), 1)
     for i, w in enumerate(weights):
         _, bias_out = bias_rows(w, width)
-        first_grad = mm(across[...], before_grads[i])
+        first_grad = 0.5 * mm(across[...], before_grads[i])
         outs[i][0:width] = first_grad[0:width].astype(bf16)
         outs[i][width : 2 * width] = mm_tn(hiddens[i][...], result_grads[i]).astype(bf16)
         out_bias = jnp.zeros((1, width), f32)
@@ -314,6 +321,30 @@
             small = jnp.where(lanes == t * quantities + q, part, small)
     half = type_count // 2
     return jnp.concatenate([small[:half], small[half:]], axis=1).astype(bf16)
+
+
+def store_copies(ready, pair, held, out_refs, sems):
+    group, unit = pair // held, lax.rem(pair, held)
+    copies = [(None, pltpu.make_async_copy(ready.at[0], out_refs[0].at[group, unit], sems.at[0]))]
+    for at, ref in enumerate(out_refs[1:]):
+        copies.append((group == at, pltpu.make_async_copy(ready.at[1], ref.at[unit], sems.at[1])))
+    return copies
+
+
+def for_each(copies, act):
+    for condition, copy in copies:
+        if condition is None:
+            act(copy)
+        else:
+            pl.when(condition)(functools.partial(act, copy))
+
+
+def start(copy):
+    copy.start()
+
+
+def wait(copy):
+    copy.wait()
 
 
 def fetch_weights(places, buffer, sems, each):
@@ -405,9 +436,9 @@
     place_ref, x_ref, type_ref, across_types_ref, value_ref, gate_slope_ref, pred_grad_ref = take(7)
     tower_in_ref, tower_bias_ref, tower_out_ref = take(3)
     weight_refs = take(pieces)
-    pred_ref, stream_ref, small_ref, tower_small_ref, *tower_refs = take(4 + halves)
-    out_refs = [take(halves) for _ in range(held)]
-    x_low, weights, hidden_all, slope_all, total, biases, low, across, share, table = take(10)
+    pred_ref, stream_ref, small_ref, *tower_refs = take(3 + halves)
+    out_refs = take(1 + groups * (halves - 1))
+    x_low, weights, hidden_all, slope_all, gates_all, total, biases, low, across, share, table = take(11)
     before_grads, result_grads, products, ready, in_grad, bias_grad, out_grad, load_sem, store_sem = take(9)
     height, width = x_ref.shape
     pairs = value_ref.shape[0]
@@ -432,8 +463,18 @@
             hidden_all[pair, i, rows] = hidden
             slope_all[pair, i, rows] = slope
 
+        def keep_gate(at, rows, gate):
+            gates_all[pair, at, rows] = gate
+
         forward_step(
-            [weights.at[pair, i] for i in range(halves)], value_ref.at[pair], x_low, type_ref, total, biases, keep
+            [weights.at[pair, i] for i in range(halves)],
+            value_ref.at[pair],
+            x_low,
+            type_ref,
+            total,
+            biases,
+            keep,
+            keep_gate,
         )
         return carry
 
@@ -477,50 +518,44 @@
         else:
             tower_refs[0][t * wide.shape[0] : (t + 1) * wide.shape[0]] = wide.astype(bf16)
     ends = [jnp.concatenate([ref[0:1], ref[1:2]], axis=1) for ref in (bias_grad, out_grad)]
-    tower_small_ref[...] = jnp.concatenate([*ends, jnp.zeros((EXTRA - 2, width), f32)]).astype(bf16)
+    tower_small = jnp.concatenate([*ends, jnp.zeros((EXTRA - 2, width), f32)]).astype(bf16)
 
     backward_start(x_low, across_types_ref, low, across, share)
     table[...] = jnp.zeros_like(table)
 
-    def store(unit, group, half):
-        pair = group * held + unit
-        return pltpu.make_async_copy(ready.at[pair, half], out_refs[unit][half].at[group], store_sem.at[pair, half])
-
-    for unit in range(held):
-
-        def backward_group(group, carry, unit=unit):
-            pair = group * held + unit
-            backward_step(
-                [weights.at[pair, i] for i in range(halves)],
-                value_ref.at[pair],
-                [hidden_all.at[pair, i] for i in range(halves)],
-                [slope_all.at[pair, i] for i in range(halves)],
-                [ready.at[pair, i] for i in range(halves)],
-                pair,
-                experts,
-                type_ref,
-                across_types_ref,
-                low,
-                stream_ref,
-                across,
-                share,
-                table,
-                (before_grads, result_grads, products),
-            )
-            for half in range(halves):
-                store(unit, group, half).start()
-            return carry
-
-        lax.fori_loop(0, groups, backward_group, 0)
-    small_ref[...] = through_gates(table, gate_slope_ref, experts, tasks)
-    for unit in range(held):
-
-        def drain(group, carry, unit=unit):
-            for half in range(halves):
-                store(unit, group, half).wait()
-            return carry
-
-        lax.fori_loop(0, groups, drain, 0)
+    def stores(pair):
+        return store_copies(ready.at[pair], pair, held, out_refs, store_sem.at[pair])
+
+    def backward_pair(pair, carry):
+        backward_step(
+            [weights.at[pair, i] for i in range(halves)],
+            value_ref.at[pair],
+            [hidden_all.at[pair, i] for i in range(halves)],
+            [slope_all.at[pair, i] for i in range(halves)],
+            [ready.at[pair, i] for i in range(halves)],
+            pair,
+            experts,
+            type_ref,
+            across_types_ref,
+            low,
+            stream_ref,
+            across,
+            share,
+            table,
+            (before_grads, result_grads, products),
+            gates_all.at[pair],
+        )
+        for_each(stores(pair), start)
+        return carry
+
+    lax.fori_loop(0, pairs, backward_pair, 0)
+    small_ref[...] = jnp.concatenate([through_gates(table, gate_slope_ref, experts, tasks), tower_small])
+
+    def drain(pair, carry):
+        for_each(stores(pair), wait)
+        return carry
+
+    lax.fori_loop(0, pairs, drain, 0)
 
 
 def middle_call(place, x, types, across_types, values, gate_slopes, tower, pieces, places, groups, halves, held):
@@ -530,13 +565,12 @@
     tasks = tower_in.shape[0]
     stride = 2 * width + EXTRA
     experts = pairs * halves
-    payload = jax.ShapeDtypeStruct((groups, stride, width), bf16)
     outs = [jax.ShapeDtypeStruct(shape, f32) for shape in (pred_grad.shape, (height, width))]
-    outs.append(jax.ShapeDtypeStruct((type_count // 2, 2 * LANES), bf16))
-    outs.append(jax.ShapeDtypeStruct((EXTRA, width), bf16))
+    outs.append(jax.ShapeDtypeStruct((type_count // 2 + EXTRA, 2 * LANES), bf16))
     outs += [jax.ShapeDtypeStruct((tower_in.size // width // halves, width), bf16)] * halves
     near = len(outs)
-    outs += [payload] * (halves * held)
+    outs.append(jax.ShapeDtypeStruct((groups, held, stride, width), bf16))
+    outs += [jax.ShapeDtypeStruct((held, stride, width), bf16)] * (groups * (halves - 1))
     layer_at = gate_slopes.shape[1] // type_count - 1
     slope_spec = pl.BlockSpec((gate_slopes.shape[0], type_count, LANES), lambda i: (0, layer_at, 0))
     kept = pltpu.VMEM((pairs, halves, height, width), bf16)
@@ -548,12 +582,13 @@
         grid=(1,),
         out_shape=outs,
         in_specs=[SCALARS] + specs + [FAR] * len(pieces),
-        out_specs=[whole_spec(out.shape) for out in outs[:near]] + [FAR] * (halves * held),
+        out_specs=[whole_spec(out.shape) for out in outs[:near]] + [FAR] * (len(outs) - near),
         scratch_shapes=[
             pltpu.VMEM((height, width), bf16),
             pltpu.VMEM((pairs, halves, stride, width), bf16),
             kept,
             kept,
+            pltpu.VMEM((pairs, halves * tasks, height, LANES), bf16),
             pltpu.VMEM((tasks, height, width), f32),
             pltpu.VMEM((tasks, type_count, width), f32),
             pltpu.VMEM((tasks, height, width), bf16),
@@ -579,34 +614,42 @@
     )(place, *operands, *pieces)
 
 
-def backward_kernel(places, pieces, each, held, unit, tasks, *refs):
+def backward_kernel(places, pieces, each, held, tasks, *refs):
     refs = list(refs)
     take = lambda count: [refs.pop(0) for _ in range(count)]
-    x_ref, type_ref, across_types_ref, grad_ref, stream_ref, gate_slope_ref, value_ref, hidden_ref, slope_ref = take(9)
+    x_ref, type_ref, across_types_ref, stream_ref, gate_slope_ref, value_ref, hidden_ref, slope_ref = take(8)
     weight_refs = take(pieces)
     stream_out_ref, small_ref = take(2)
-    out_refs = take(each)
-    x_low, across, low, share, table, before_grads, result_grads, products, buffer, sems = take(10)
+    out_refs = take(1 + len(places) // each // held * (each - 1))
+    x_low, across, low, share, table, before_grads, result_grads, products, buffer, ready, sems, store_sem = take(12)
     step = pl.program_id(0)
-    groups = pl.num_programs(0)
+    slot = lax.rem(step, 2)
+    experts = len(places)
     weights = fetch_weights([(weight_refs[piece], at) for piece, at in places], buffer, sems, each)
 
     @pl.when(step == 0)
     def _():
         x_low[...] = x_ref[...].astype(bf16)
-        low[0] = grad_ref[...].astype(bf16)
+        low[0] = stream_ref[...].astype(bf16)
         stream_out_ref[...] = stream_ref[...]
         table[...] = jnp.zeros_like(table)
         backward_start(x_low, across_types_ref, low, across, share)
 
-    experts = len(places) * held
+    def stores(pair):
+        at = lax.rem(pair, 2)
+        return store_copies(ready.at[at], pair, held, out_refs, store_sem.at[at])
+
+    @pl.when(step >= 2)
+    def _():
+        for_each(stores(step - 2), wait)
+
     backward_step(
         weights,
         value_ref.at[0],
         [hidden_ref.at[0, i] for i in range(each)],
         [slope_ref.at[0, i] for i in range(each)],
-        [ref.at[0] for ref in out_refs],
-        step * held + unit,
+        [ready.at[slot, i] for i in range(each)],
+        step,
         experts,
         type_ref,
         across_types_ref,
@@ -618,32 +661,36 @@
         (before_grads, result_grads, products),
     )
 
-    @pl.when(step == groups - 1)
+    for_each(stores(step), start)
+
+    @pl.when(step == pl.num_programs(0) - 1)
     def _():
         small_ref[...] = through_gates(table, gate_slope_ref, experts, tasks)
-
-
-def backward_call(x, types, across_types, grad, stream, gate_slopes, layer_at, values, stash, pieces, places, held, unit, tasks):
+        for_each(stores(step - 1), wait)
+        for_each(stores(step), wait)
+
+
+def backward_call(x, types, across_types, stream, gate_slopes, layer_at, values, stash, pieces, places, held, tasks):
     height, width = x.shape
     pairs, type_count, lanes = values.shape
     each = lanes // LANES
     groups = pairs // held
     stride = 2 * width + EXTRA
-    operands = [x, types, across_types, grad, stream, gate_slopes, values, *stash]
-    specs = [whole_spec(a.shape) for a in operands[:5]]
+    operands = [x, types, across_types, stream, gate_slopes, values, *stash]
+    specs = [whole_spec(a.shape) for a in operands[:4]]
     specs.append(pl.BlockSpec((gate_slopes.shape[0], type_count, LANES), lambda i: (0, layer_at, 0)))
-    specs.append(pl.BlockSpec((1, type_count, lanes), lambda i: (i * held + unit, 0, 0)))
-    specs += [pl.BlockSpec((1, each, height, width), lambda i: (i * held + unit, 0, 0, 0))] * 2
-    payload = jax.ShapeDtypeStruct((groups, stride, width), bf16)
+    specs.append(pl.BlockSpec((1, type_count, lanes), lambda i: (i, 0, 0)))
+    specs += [pl.BlockSpec((1, each, height, width), lambda i: (i, 0, 0, 0))] * 2
+    mine = jax.ShapeDtypeStruct((groups, held, stride, width), bf16)
+    others = [jax.ShapeDtypeStruct((held, stride, width), bf16)] * (groups * (each - 1))
     small = jax.ShapeDtypeStruct((type_count // 2, 2 * LANES), bf16)
-    number = groups * each
+    number = pairs * each
     return pl.pallas_call(
-        functools.partial(backward_kernel, places, len(pieces), each, held, unit, tasks),
-        grid=(groups,),
-        out_shape=[jax.ShapeDtypeStruct(stream.shape, f32), small] + [payload] * each,
+        functools.partial(backward_kernel, places, len(pieces), each, held, tasks),
+        grid=(pairs,),
+        out_shape=[jax.ShapeDtypeStruct(stream.shape, f32), small, mine, *others],
         in_specs=specs + [FAR] * len(pieces),
-        out_specs=[whole_spec(stream.shape), whole_spec(small.shape)]
-        + [pl.BlockSpec((1, stride, width), lambda i: (i, 0, 0))] * each,
+        out_specs=[whole_spec(stream.shape), whole_spec(small.shape)] + [FAR] * (1 + len(others)),
         scratch_shapes=[
             pltpu.VMEM((height, width), bf16),
             pltpu.VMEM((width + EXTRA, height), bf16),
@@ -654,6 +701,8 @@
             pltpu.VMEM((each, height, width), bf16),
             pltpu.VMEM((height, lanes), bf16),
             pltpu.VMEM((2, each, stride, width), bf16),
+            pltpu.VMEM((2, each, stride, width), bf16),
+            pltpu.SemaphoreType.DMA((2, each)),
             pltpu.SemaphoreType.DMA((2, each)),
         ],
         compiler_params=kernel_params(),
@@ -665,52 +714,51 @@
     )(*operands, *pieces)
 
 
-def finish_kernel(layer_at, unit, held, halves, rows, first, *refs):
-    refs = list(refs)
-    take = lambda count: [refs.pop(0) for _ in range(count)]
-    place_ref = take(1)[0]
-    sources = take(halves)
-    if not first:
-        _, _, in_bias_ref, out_bias_ref = take(4)
-    in_ref, out_ref, in_bias_out_ref, out_bias_out_ref, ready, sems = refs
+def finish_kernel(names, held, rows, first, *refs):
+    place_ref, *refs = refs
+    sources, refs = refs[: len(names)], refs[len(names) :]
+    in_ref, out_ref, in_bias_out_ref, out_bias_out_ref, ready, sems = refs[-6:]
+    in_bias_out_ref[...] = jnp.zeros_like(in_bias_out_ref) if first else refs[2][...]
+    out_bias_out_ref[...] = jnp.zeros_like(out_bias_out_ref) if first else refs[3][...]
     copies = []
-    for half, source in enumerate(sources):
-        where = held * (place_ref[2] ^ half) + unit
-        for which, ref in enumerate((in_ref, out_ref)):
-            ready[half, which] = source[which * rows : (which + 1) * rows].astype(f32)
-            copy = pltpu.make_async_copy(ready.at[half, which], ref.at[layer_at, where], sems.at[half, which])
-            copy.start()
-            copies.append(copy)
-    in_bias_out_ref[...] = jnp.zeros_like(in_bias_out_ref) if first else in_bias_ref[...]
-    out_bias_out_ref[...] = jnp.zeros_like(out_bias_out_ref) if first else out_bias_ref[...]
-    for half, source in enumerate(sources):
-        where = held * (place_ref[2] ^ half) + unit
-        tail = source[2 * rows : 2 * rows + EXTRA].astype(f32)
-        in_bias_out_ref[layer_at, pl.ds(where, 1)] = tail[0:1]
-        out_bias_out_ref[layer_at, pl.ds(where, 1)] = tail[1:2]
+    for at, ((layer_at, half), source) in enumerate(zip(names, sources)):
+        for unit in range(held):
+            base = unit * (2 * rows + EXTRA)
+            where = held * (place_ref[2] ^ half) + unit
+            for which, ref in enumerate((in_ref, out_ref)):
+                begin = base + which * rows
+                ready[at, unit, which] = source[begin : begin + rows].astype(f32)
+                copy = pltpu.make_async_copy(
+                    ready.at[at, unit, which], ref.at[layer_at, where], sems.at[at, unit, which]
+                )
+                copy.start()
+                copies.append(copy)
+            tail = source[base + 2 * rows : base + 2 * rows + EXTRA].astype(f32)
+            in_bias_out_ref[layer_at, pl.ds(where, 1)] = tail[0:1]
+            out_bias_out_ref[layer_at, pl.ds(where, 1)] = tail[1:2]
     for copy in copies:
         copy.wait()
 
 
-def finish_call(place, sources, held_arrays, layer_at, unit, held, shape):
-    halves = len(sources)
+def finish_call(place, named, held_arrays, held, shape):
     rows, width = shape[2:]
+    names, sources = tuple(named), list(named.values())
     outs = [jax.ShapeDtypeStruct(shape, f32)] * 2
     outs += [jax.ShapeDtypeStruct((*shape[:2], width), f32)] * 2
     first = held_arrays is None
-    aliases = {} if first else {1 + halves: 0, 2 + halves: 1}
+    number = len(names)
     return pl.pallas_call(
-        functools.partial(finish_kernel, layer_at, unit, held, halves, rows, first),
+        functools.partial(finish_kernel, names, held, rows, first),
         out_shape=outs,
-        in_specs=[SCALARS] + [NEAR] * halves + ([] if first else [FAR, FAR, NEAR, NEAR]),
+        in_specs=[SCALARS] + [NEAR] * number + ([] if first else [FAR, FAR, NEAR, NEAR]),
         out_specs=[FAR, FAR, NEAR, NEAR],
         scratch_shapes=[
-            pltpu.VMEM((halves, 2, rows, width), f32),
-            pltpu.SemaphoreType.DMA((halves, 2)),
+            pltpu.VMEM((number, held, 2, rows, width), f32),
+            pltpu.SemaphoreType.DMA((number, held, 2)),
         ],
-        input_output_aliases=aliases,
+        input_output_aliases={} if first else {1 + number: 0, 2 + number: 1},
         compiler_params=kernel_params(),
-        cost_estimate=pl.CostEstimate(flops=0, bytes_accessed=halves * 12 * rows * width, transcendentals=0),
+        cost_estimate=pl.CostEstimate(flops=0, bytes_accessed=number * held * 12 * rows * width, transcendentals=0),
     )(place, *sources, *([] if first else held_arrays))
 
 
@@ -744,10 +792,6 @@
 
 def crossed(parts, halves):
     return [] if halves == 1 else [flip(part, "rows", 1) for part in parts]
-
-
-def scatter_start(sums, groups):
-    return [sums[0]] + [flip(sums[ro], "expert", ro) for ro in range(1, groups)]
 
 
 def body(
@@ -779,12 +823,13 @@
 
     def rows_of(layer_at, first):
         cut = lambda a: lax.dynamic_slice_in_dim(a[layer_at], first, held)
+        half = lambda a: a * jnp.asarray(0.5, a.dtype)
         tail = []
-        for bias in (cut(expert_in_bias), cut(expert_out_bias)):
+        for bias in (half(cut(expert_in_bias)), cut(expert_out_bias)):
             high = bias.astype(bf16)
             tail += [high, (bias - high.astype(f32)).astype(bf16)]
         tail = jnp.pad(jnp.stack(tail, axis=1), ((0, 0), (0, EXTRA - len(tail)), (0, 0)))
-        return jnp.concatenate([cut(expert_in), cut(expert_out), tail], axis=1)
+        return jnp.concatenate([half(cut(expert_in)), cut(expert_out), tail], axis=1)
 
     own = [[rows_of(layer_at, held * (core ^ half)) for half in range(halves)] for layer_at in range(layers)]
     sizes = (owned, halves, held, selectors, bits, tasks)
@@ -843,7 +888,7 @@
         weights.append(parts_of({**got, **far}, {**across, **far_across}))
 
     pieces, places = weights[-1]
-    predictions, stream, small, tower_small, *rest = middle_call(
+    predictions, stream, small, *rest = middle_call(
         place,
         streams[-1],
         types,
@@ -857,43 +902,55 @@
         halves,
         held,
     )
-    tower_rows, rest = rest[:halves], rest[halves:]
-    payloads = [rest[unit * halves : (unit + 1) * halves] for unit in range(held)]
-
-    tower_tail = tower_rows[0]
-    if halves == 2:
-        tower_tail = add_low(tower_rows[0], flip(tower_rows[1], "rows", 1))
-    tails = [[] for _ in range(held - 1)] + [[small, tower_small, tower_tail]]
+    tower_rows, payload = rest[:halves], rest[halves:]
 
     shards = lax.axis_size("rows")
-    if shards == 8 and halves == 2:
-        hops = [[(0, 1), (3, 2)], [(1, 2), (2, 1)], [(1, 0), (2, 3)]]
-        hops = [[(2 * a + c, 2 * b + c) for a, b in hop for c in range(2)] for hop in hops]
-    else:
-        hops = [[(i, i ^ (2 << at)) for i in range(shards)] for at in range(shards.bit_length() - 2)]
-    outer = (row_at < 2) | (row_at >= shards - 2)
-    line = shards == 8 and halves == 2
+    paired = shards > 2
+    hops = ["share"] + [4 << at for at in range(shards.bit_length() - 3)] + ["join"] if paired else []
+    upper = (row_at & 2) > 0
 
     class Moving:
-        def __init__(self, layer_at, unit, sums):
-            self.layer_at, self.unit, self.sums, self.got, self.hops = layer_at, unit, sums, None, -1
+        def __init__(self, layer_at, payload, small, end=None):
+            self.layer_at, self.mine, self.end = layer_at, payload[0], [] if end is None else [end]
+            self.others = payload[1:] or [payload[0][ro] for ro in range(groups)]
+            self.small = small
+            self.got = [flip(part, "rows", 1) for part in [self.small, *self.others[1:]]]
+            self.total, self.sums, self.hops = None, None, -2
 
         def ask(self, token):
-            if self.got is None:
-                self.got = scatter_start(after(self.sums, token), groups)
-            elif self.hops < len(hops):
-                total = after(self.total, token)
-                self.got = [total, lax.ppermute(total, "rows", hops[self.hops])]
+            if self.hops == -1:
+                sums, own = after((self.sums, self.others[0]), token)
+                self.got = [flip(own, "rows", 1)] + [flip(sums[ro], "expert", ro) for ro in range(1, groups)]
+                return
+            total = after(self.total, token)
+            if self.hops == len(hops):
+                self.got = [total] + ([flip(total, "rows", 1)] if halves == 2 else [])
+            elif hops[self.hops] == "share":
+                cut = total.shape[0] // 2
+                self.got = [
+                    jnp.where(upper, total[cut:], total[:cut]),
+                    flip(jnp.where(upper, total[:cut], total[cut:]), "rows", 2),
+                ]
             else:
-                self.got = [self.total] + ([flip(after(self.total, token), "rows", 1)] if halves == 2 else [])
+                self.got = [total, flip(total, "rows", 2 if hops[self.hops] == "join" else hops[self.hops])]
+
+        def core_sum(self, ro, received):
+            rows = add_low(self.mine[ro], received).reshape(held * stride, width)
+            return jnp.concatenate([rows, self.small, *self.end])
 
         def add(self):
             if self.hops == len(hops):
                 return True
-            if line and self.hops == len(hops) - 1:
-                self.total = jnp.where(outer, self.got[1], self.got[0])
+            if self.hops == -2:
+                self.small = add_low(self.small, self.got[0])
+                self.sums = {ro: self.core_sum(ro, self.got[ro]) for ro in range(1, groups)}
+            elif self.hops == -1:
+                self.total = add_low(self.core_sum(0, self.got[0]), *self.got[1:])
+            elif hops[self.hops] != "join":
+                self.total = add_low(*self.got)
             else:
-                self.total = add_low(*self.got)
+                here, there = self.got
+                self.total = jnp.concatenate([jnp.where(upper, there, here), jnp.where(upper, here, there)])
             self.hops += 1
             return False
 
@@ -902,88 +959,57 @@
         for entry, what in zip(entries, got):
             entry.got = what
         ended = [entry for entry in entries if entry.add()]
-        return ([entry.total for entry in entries], others), ended
-
-    def core_received(payloads):
-        return lax.optimization_barrier([flip(payload[-1], "rows", 1) for payload in payloads])
-
-    def core_sums(payload, received, tails):
-        if halves == 1:
-            tails = [add_low(a, flip(a, "rows", 1)) for a in tails]
-        return [
-            jnp.concatenate([add_low(payload[0][ro], received[ro]), *tails], axis=0) for ro in range(groups)
-        ]
-
-    moving = []
-    for unit, received in enumerate(core_received(payloads)):
-        sums = core_sums(payloads[unit], received, tails[unit])
-        stream = after(stream, sums)
-        moving.append(Moving(layers - 1, unit, sums))
-    moving[0].ask(())
-
+        return ([entry.sums if entry.total is None else entry.total for entry in entries], others), ended
+
+    tower_tail = tower_rows[0]
+    if halves == 2:
+        tower_tail = add_low(tower_rows[0], flip(tower_rows[1], "rows", 1))
+    moving = [Moving(layers - 1, payload, small, tower_tail)]
+    token, _ = arrive(moving, ())
+    stream = after(stream, token)
     for layer_at in reversed(range(layers - 1)):
+        for entry in moving:
+            entry.ask(token)
         pieces, places = weights[layer_at]
-        fresh = []
-        grad = stream
-        for unit in range(held):
-            stream, small, *payload = backward_call(
-                streams[layer_at],
-                types,
-                across_types,
-                grad,
-                stream,
-                gate_slopes,
-                layer_at,
-                values[layer_at],
-                stashes[layer_at],
-                pieces,
-                pair_order(places, [unit]),
-                held,
-                unit,
-                tasks,
-            )
-            beside = moving if unit == held - 1 else moving[: unit + 1]
-            token, _ = arrive(beside, stream)
-            stream = after(stream, token)
-            if unit < held - 1:
-                for entry in moving[: unit + 2]:
-                    entry.ask(token)
-            fresh.append((payload, small))
-        received = core_received(after([payload for payload, _ in fresh], token))
-        small = sum(part.astype(f32) for _, part in fresh).astype(bf16)
-        for unit, (payload, _) in enumerate(fresh):
-            sums = core_sums(payload, received[unit], [] if unit else [small])
-            token = (token, sums)
-            moving = moving + [Moving(layer_at, unit, sums)]
-
-    arrays = None
-    gate_grads = [0.0] * layers
-
-    def finish(entry):
-        nonlocal arrays, tower_bias_sum, tower_out_sum, tower_rows
-        layer_at, unit, sources = entry.layer_at, entry.unit, entry.got
-        arrays = finish_call(place, sources, arrays, layer_at, unit, held, expert_in.shape)
-        if sources[0].shape[0] > stride:
-            both = functools.reduce(jnp.add, [a[stride:].astype(f32) for a in sources])
-            gate_grads[layer_at] = gate_grads[layer_at] + both[: type_count // 2]
-            if layer_at == layers - 1:
-                at = type_count // 2
-                tower_bias_sum = both[at].reshape(tower_bias.shape)
-                tower_out_sum = both[at + 1].reshape(tower_out.shape)
-                tower_rows = [a[stride + at + EXTRA :].astype(f32) for a in sources]
-
-    tower_bias_sum = tower_out_sum = tower_rows = None
-    others = ()
-    started = layers * held - held + 1
+        stream, small, *payload = backward_call(
+            streams[layer_at],
+            types,
+            across_types,
+            stream,
+            gate_slopes,
+            layer_at,
+            values[layer_at],
+            stashes[layer_at],
+            pieces,
+            pair_order(places, range(held)),
+            held,
+            tasks,
+        )
+        token, _ = arrive(moving, stream)
+        moving.append(Moving(layer_at, payload, small))
+        token, _ = arrive(moving[-1:], token)
+
+    whole = {}
     while moving:
-        for entry in moving[:started]:
+        for entry in moving:
             entry.ask(token)
-        token, ended = arrive(moving[:started], others)
-        moving = [entry for entry in moving if entry not in ended]
-        started += 1 - len(ended)
-        for entry in ended:
-            finish(entry)
-        others = (arrays, gate_grads, tower_rows) if ended else ()
+        for entry in [entry for entry in moving if entry.hops == len(hops)]:
+            moving.remove(entry)
+            whole[entry.layer_at] = entry.got
+        if moving:
+            token, _ = arrive(moving, ())
+    first = {(layer_at, 0): got[0] for layer_at, got in whole.items()}
+    if halves == 2:
+        first.update({(layer_at, 1): got[1] for layer_at, got in whole.items() if layer_at > 0})
+    arrays = finish_call(place, first, None, held, expert_in.shape)
+    ends = {layer_at: got[0][held * stride :].astype(f32) for layer_at, got in whole.items()}
+    gate_grads = [ends[layer_at][: type_count // 2] for layer_at in range(layers)]
+    end = ends[layers - 1]
+    at = type_count // 2
+    tower_bias_sum = end[at].reshape(tower_bias.shape)
+    tower_out_sum = end[at + 1].reshape(tower_out.shape)
+    at = held * stride + at + EXTRA
+    tower_rows = [array[at:].astype(f32) for array in whole[layers - 1]]
     if halves == 2:
         tower_rows = [jnp.where(core == 0, *tower_rows), jnp.where(core == 0, *tower_rows[::-1])]
     wide = jnp.concatenate(tower_rows).reshape(tasks, -1, width)
@@ -994,6 +1020,10 @@
     small = jnp.concatenate([small[..., :LANES], small[..., LANES:]], axis=1)[..., : tasks * quantities]
     small = small.reshape(layers, type_count, tasks, quantities)
     logits_grad = small[..., : selectors * bits].reshape(selector_logits.shape)
+    smalls = (logits_grad, small[..., selectors * bits :], tower_in_sum, tower_bias_sum, tower_out_sum)
+    if halves == 2:
+        last, (arrays, smalls) = lax.optimization_barrier((whole[0][1], (arrays, smalls)))
+        arrays = finish_call(place, {(0, 1): last}, arrays, held, expert_in.shape)
     return (
         predictions,
         stream,
@@ -1001,11 +1031,7 @@
         arrays[2],
         arrays[1],
         arrays[3],
-        logits_grad,
-        small[..., selectors * bits :],
-        tower_in_sum,
-        tower_bias_sum,
-        tower_out_sum,
+        *smalls,
     )
 
 

time: 231 us -> 218 us (0.944)
  waiting for transfers between devices: 51.4 us -> 69.4 us
  starting transfers between devices: 52.1 us -> 35 us
  Pallas kernels: 102 us -> 88.6 us
    ppermute x37 -> x41, waiting for transfers between devices: 36.3 us -> 69.4 us  [flip(): return lax.ppermute(array, axis, [(i, i ^ bits) for i in range(size)])]
    ppermute x12 -> x0, starting transfers between devices: 24.3 us -> none  [ask(): self.got = [total, lax.ppermute(total, 'rows', hops[self.hops])]]
    ppermute x12 -> x0, waiting for transfers between devices: 15.1 us -> none  [ask(): self.got = [total, lax.ppermute(total, 'rows', hops[self.hops])]]
    ppermute x37 -> x41, starting transfers between devices: 27.8 us -> 35 us  [flip(): return lax.ppermute(array, axis, [(i, i ^ bits) for i in range(size)])]
    pallas_call x2 -> x1, Pallas kernels: 25.5 us -> 19.8 us  [backward_call(): pl.pallas_call(functools.partial(backward_kernel, places, len(pieces), ea...]
    pallas_call x4 -> x2, Pallas kernels: 10.7 us -> 6.5 us  [finish_call(): pl.pallas_call(functools.partial(finish_kernel, names, held, rows, first)...]
    pallas_call x1, Pallas kernels: 40.3 us -> 37.4 us  [middle_call(): pl.pallas_call(functools.partial(middle_kernel, places, len(pieces), grou...]
    unnamed x84 -> x66, local copies, waits for them, and re-layouts: 8.44 us -> 6.89 us
  transfers between devices with their start and end apart: 49 -> 41, of which waited for: 14 -> 16; matrix products, arithmetic and copies ran while one was open for 4% -> 5% of each run, Pallas kernels for 26% -> 22%
where the time goes in v2:
time: 218 us; the launch traced here: 217 us
  Pallas kernels  88.6 us (41%)
  waiting for transfers between devices  69.4 us (32%)
  starting transfers between devices  35 us (16%)
  local copies, waits for them, and re-layouts  12.1 us (6%)
  other arithmetic  9.97 us (5%)
    ppermute x41, waiting for transfers between devices, flip(): return lax.ppermute(array, axis, [(i, i ^ bits) for i in range(size)])  69.4 us
    pallas_call x1, Pallas kernels, middle_call(): pl.pallas_call(functools.partial(middle_kernel, places, len(pieces), grou...  37.4 us
    ppermute x41, starting transfers between devices, flip(): return lax.ppermute(array, axis, [(i, i ^ bits) for i in range(size)])  35 us
    pallas_call x2, Pallas kernels, forward_call(): pl.pallas_call(functools.partial(forward_kernel, places, len(pieces), eac...  21.7 us
    pallas_call x1, Pallas kernels, backward_call(): pl.pallas_call(functools.partial(backward_kernel, places, len(pieces), ea...  19.8 us
    unnamed x66, local copies, waits for them, and re-layouts  6.89 us
    pallas_call x2, Pallas kernels, finish_call(): pl.pallas_call(functools.partial(finish_kernel, names, held, rows, first)...  6.5 us
    convert_element_type x13, other arithmetic, add_low(): return level[0].astype(bf16)  6 us
  transfers between devices with their start and end apart: 41, of which 16 were waited for; matrix products, arithmetic and copies ran while one was open for 5% of the time, Pallas kernels for 22%

profile of v2, /device:TPU:0, one launch (start us, length us, event | category | flops | bytes accessed | tf_op | source)
XLA Modules:
  0.0 216.7 jit_solution(5692854236739013266)
XLA Ops:
  3.8 3.0 %collective-permute-start = (bf16[2,528,256]{2,1,0:T(8,128)(2,1)S(1)}, bf16[2,528,256]{2,1,0:T(8,128)(2,1)S(1)}, u32[]{:S(2)}, u32[]{:S(2)}) collective-permute-start(bf16[2,528,256]{2,1,0:T(8,128)(2,1)S(1)} %pad_maximum_fusion.14.refs_3_.refs_8_), channel_id=1, source_target_pairs={{0,1},{1,0},{2,3},{3,2},{4,5},{5,4},{6,7},{7,6},{8,9},{9,8},{10,11... | collective-permute-start | bytes 1622024 | tf_op jit(solution)/shard_map/ppermute | solution.py:767
  10.7 3.2 %shard_map.230 = (bf16[1024,32]{1,0:T(8,128)(2,1)}, bf16[32,1024]{1,0:T(8,128)(2,1)}, f32[20,64,128]{2,1,0:T(8,128)}, bf16[8,32,256]{2,1,0:T(8,128)(2,1)}, bf16[8,32,512]{2,1,0:T(8,128)(2,1)}) custom-call(s32[3]{0:T(128)} %pad_add_fusion.place_ref.refs_0_, s32[1,256]{1,0:T(1,128)} %bitcast.122, s32[1,256]{1,0:T(1,128)} %bitcast.123, ...), custom_call_target="tpu_custom_call" | custom-call | flops 33554432 | bytes 2097152 | tf_op jit(solution)/shard_map/pallas_call | solution.py:169
  14.0 5.1 %collective-permute-done.refs_5_.refs_10_ = bf16[2,528,256]{2,1,0:T(8,128)(2,1)S(1)} collective-permute-done((bf16[2,528,256]{2,1,0:T(8,128)(2,1)S(1)}, bf16[2,528,256]{2,1,0:T(8,128)(2,1)S(1)}, u32[]{:S(2)}, u32[]{:S(2)}) %collective-permute-start) | collective-permute-done | bytes 540704 | tf_op jit(solution)/shard_map/ppermute | solution.py:767
  27.2 13.8 %shard_map.231 = (f32[1,1024,256]{2,1,0:T(8,128)}, bf16[8,2,1024,256]{3,2,1,0:T(8,128)(2,1)}, bf16[8,2,1024,256]{3,2,1,0:T(8,128)(2,1)}) custom-call(f32[1024,256]{1,0:T(8,128)} %refs_0_.5, bf16[1024,32]{1,0:T(8,128)(2,1)} %get-tuple-element.112.refs_1_.refs_2_, bf16[8,32,256]{2,1,0:T(8,128)(2,1)} %get-tuple-element.113.refs_2_.refs_5_, ...), custom_call_target="tpu_custom_call" | custom-call | flops 3221225472 | bytes 17825792 | tf_op jit(solution)/shard_map/pallas_call | solution.py:410
  41.6 2.7 %collective-permute-done.8.refs_12_ = bf16[2,528,256]{2,1,0:T(8,128)(2,1)S(1)} collective-permute-done((bf16[2,528,256]{2,1,0:T(8,128)(2,1)S(1)}, bf16[2,528,256]{2,1,0:T(8,128)(2,1)S(1)}, u32[]{:S(2)}, u32[]{:S(2)}) %collective-permute-start.8) | collective-permute-done | bytes 540704 | tf_op jit(solution)/shard_map/ppermute | solution.py:767
  46.6 7.9 %shard_map.232 = (f32[1,1024,256]{2,1,0:T(8,128)}, bf16[8,2,1024,256]{3,2,1,0:T(8,128)(2,1)}, bf16[8,2,1024,256]{3,2,1,0:T(8,128)(2,1)}) custom-call(f32[1024,256]{1,0:T(8,128)} %refs_0_.5, bf16[1024,32]{1,0:T(8,128)(2,1)} %get-tuple-element.112.refs_1_.refs_2_, ...), custom_call_target="tpu_custom_call", output_to_operand_aliasing={{1}: (4, {}), {2}: (5, {})} | custom-call | flops 1073741824 | bytes 7340032 | tf_op jit(solution)/shard_map/pallas_call | solution.py:410
  57.7 37.4 %shard_map.233 = (f32[1024,2]{1,0:T(8,128)}, f32[1024,256]{1,0:T(8,128)}, bf16[32,256]{1,0:T(8,128)(2,1)}, bf16[128,256]{1,0:T(8,128)(2,1)}, bf16[128,256]{1,0:T...) custom-call(s32[3]{0:T(128)} %pad_add_fusion.place_ref.refs_0_, ...), custom_call_target="tpu_custom_call" | custom-call | flops 15032385536 | bytes 12582912 | tf_op jit(solution)/shard_map/pallas_call | solution.py:580
  96.3 2.6 %collective-permute-done.20 = bf16[128,256]{1,0:T(8,128)(2,1)S(1)} collective-permute-done((bf16[128,256]{1,0:T(8,128)(2,1)}, bf16[128,256]{1,0:T(8,128)(2,1)S(1)}, u32[]{:S(2)}, u32[]{:S(2)}) %collective-permute-start.20) | collective-permute-done | bytes 65568 | tf_op jit(solution)/shard_map/ppermute | solution.py:767
  100.6 1.7 fusion.5
  102.5 1.7 collective-permute-start.22
  106.0 19.8 %shard_map.234 = (f32[1024,256]{1,0:T(8,128)}, bf16[16,256]{1,0:T(8,128)(2,1)}, bf16[4,2,528,256]{3,2,1,0:T(8,128)(2,1)}, bf16[2,528,256]{2,1,0:T(8,128)(2,1)}, ...) custom-call(f32[1024,256]{1,0:T(8,128)} %refs_0_.5, ...), custom_call_target="tpu_custom_call" | custom-call | flops 8589934592 | bytes 29360128 | tf_op jit(solution)/shard_map/pallas_call | solution.py:688
  126.9 6.3 %collective-permute-done.23 = bf16[1216,256]{1,0:T(8,128)(2,1)S(1)} collective-permute-done((bf16[1216,256]{1,0:T(8,128)(2,1)S(1)}, bf16[1216,256]{1,0:T(8,128)(2,1)S(1)}, u32[]{:S(2)}, u32[]{:S(2)}) %collective-permute-start.23) | collective-permute-done | bytes 622624 | tf_op jit(solution)/shard_map/ppermute | solution.py:767
  141.8 8.2 %collective-permute-done.29 = bf16[608,256]{1,0:T(8,128)(2,1)S(1)} collective-permute-done((bf16[608,256]{1,0:T(8,128)(2,1)S(1)}, bf16[608,256]{1,0:T(8,128)(2,1)S(1)}, u32[]{:S(2)}, u32[]{:S(2)}) %collective-permute-start.29) | collective-permute-done | bytes 311328 | tf_op jit(solution)/shard_map/ppermute | solution.py:767
  150.0 1.9 collective-permute-done.31
  151.9 10.7 %collective-permute-done.32 = bf16[1072,256]{1,0:T(8,128)(2,1)S(1)} collective-permute-done((bf16[1072,256]{1,0:T(8,128)(2,1)S(1)}, bf16[1072,256]{1,0:T(8,128)(2,1)S(1)}, u32[]{:S(2)}, u32[]{:S(2)}) %collective-permute-start.32) | collective-permute-done | bytes 548896 | tf_op jit(solution)/shard_map/ppermute | solution.py:767
  164.8 2.7 %collective-permute-start.34 = (bf16[608,256]{1,0:T(8,128)(2,1)S(1)}, bf16[608,256]{1,0:T(8,128)(2,1)S(1)}, u32[]{:S(2)}, u32[]{:S(2)}) collective-permute-start(bf16[608,256]{1,0:T(8,128)(2,1)S(1)} %add_convert_fusion.3), channel_id=1, source_target_pairs={{0,16},{4,20},{8,24},{12,28},{16,0},{20,4},{24,8},{28,12},{1,17},{... | collective-permute-start | bytes 933896 | tf_op jit(solution)/shard_map/ppermute | solution.py:767
  167.5 1.6 collective-permute-start.35
  169.1 10.7 %collective-permute-done.35 = bf16[536,256]{1,0:T(8,128)(2,1)S(1)} collective-permute-done((bf16[536,256]{1,0:T(8,128)(2,1)S(1)}, bf16[536,256]{1,0:T(8,128)(2,1)S(1)}, u32[]{:S(2)}, u32[]{:S(2)}) %collective-permute-start.35) | collective-permute-done | bytes 274464 | tf_op jit(solution)/shard_map/ppermute | solution.py:767
  182.6 3.1 %collective-permute-start.37 = (bf16[536,256]{1,0:T(8,128)(2,1)S(1)}, bf16[536,256]{1,0:T(8,128)(2,1)S(1)}, u32[]{:S(2)}, u32[]{:S(2)}) collective-permute-start(bf16[536,256]{1,0:T(8,128)(2,1)S(1)} %add_convert_fusion.5), channel_id=1, source_target_pairs={{0,16},{4,20},{8,24},{12,28},{16,0},{20,4},{24,8},{28,12},{1,17},{... | collective-permute-start | bytes 823304 | tf_op jit(solution)/shard_map/ppermute | solution.py:767
  186.5 8.6 %collective-permute-done.37 = bf16[536,256]{1,0:T(8,128)(2,1)S(1)} collective-permute-done((bf16[536,256]{1,0:T(8,128)(2,1)S(1)}, bf16[536,256]{1,0:T(8,128)(2,1)S(1)}, u32[]{:S(2)}, u32[]{:S(2)}) %collective-permute-start.37) | collective-permute-done | bytes 274464 | tf_op jit(solution)/shard_map/ppermute | solution.py:767
  196.0 3.4 %collective-permute-start.38 = (bf16[536,256]{1,0:T(8,128)(2,1)S(1)}, bf16[536,256]{1,0:T(8,128)(2,1)S(1)}, u32[]{:S(2)}, u32[]{:S(2)}) collective-permute-start(bf16[536,256]{1,0:T(8,128)(2,1)S(1)} %add_convert_fusion.4), channel_id=1, source_target_pairs={{0,8},{4,12},{8,0},{12,4},{16,24},{20,28},{24,16},{28,20},{1,9},{5... | collective-permute-start | bytes 823304 | tf_op jit(solution)/shard_map/ppermute | solution.py:767
  200.0 6.7 %collective-permute-done.38 = bf16[536,256]{1,0:T(8,128)(2,1)S(1)} collective-permute-done((bf16[536,256]{1,0:T(8,128)(2,1)S(1)}, bf16[536,256]{1,0:T(8,128)(2,1)S(1)}, u32[]{:S(2)}, u32[]{:S(2)}) %collective-permute-start.38) | collective-permute-done | bytes 274464 | tf_op jit(solution)/shard_map/ppermute | solution.py:767
  207.9 3.8 %shard_map.235 = (f32[2,4,256,256]{3,2,1,0:T(8,128)}, f32[2,4,256,256]{3,2,1,0:T(8,128)}, f32[2,4,256]{2,1,0:T(4,128)}, f32[2,4,256]{2,1,0:T(4,128)}) custom-call(s32[3]{0:T(128)} %pad_add_fusion.place_ref.refs_0_, bf16[1216,256]{1,0:T(8,128)(2,1)} %copy-done, bf16[1072,256]{1,0:T(8,128)(2,1)} %copy-done.1, bf16[1216,256]{1,0:T(8,128)(2,1)} %copy-done.4), custom_call_target="tpu_custom_call" | custom-call | bytes 4718592 | tf_op jit(solution)/shard_map/pallas_call | solution.py:750
  213.8 2.7 %shard_map.236 = (f32[2,4,256,256]{3,2,1,0:T(8,128)}, f32[2,4,256,256]{3,2,1,0:T(8,128)}, f32[2,4,256]{2,1,0:T(4,128)}, f32[2,4,256]{2,1,0:T(4,128)}) custom-call(s32[3]{0:T(128)} %pad_add_fusion.place_ref.refs_0_, bf16[1072,256]{1,0:T(8,128)(2,1)} %copy-done.5, ...), custom_call_target="tpu_custom_call", output_to_operand_aliasing={{0}: (2, {}), {1}: (3, {})} | custom-call | bytes 1572864 | tf_op jit(solution)/shard_map/pallas_call | solution.py:750
  (202 shorter events, 45.7 us)
Async XLA Ops:
  3.8 15.3 %collective-permute-start = (bf16[2,528,256]{2,1,0:T(8,128)(2,1)S(1)}, bf16[2,528,256]{2,1,0:T(8,128)(2,1)S(1)}, u32[]{:S(2)}, u32[]{:S(2)}) collective-permute-start(bf16[2,528,256]{2,1,0:T(8,128)(2,1)S(1)} %pad_maximum_fusion.14.refs_3_.refs_8_), channel_id=1, source_target_pairs={{0,1},{1,0},{2,3},{3,2},{4,5},{5,4},{6,7},{7,6},{8,9},{9,8},{10,11... | collective-permute-start | bytes 1622024 | tf_op jit(solution)/shard_map/ppermute | solution.py:767
  6.8 13.7 %collective-permute-start.1 = (bf16[2,528,256]{2,1,0:T(8,128)(2,1)S(1)}, bf16[2,528,256]{2,1,0:T(8,128)(2,1)S(1)}, u32[]{:S(2)}, u32[]{:S(2)}) collective-permute-start(bf16[2,528,256]{2,1,0:T(8,128)(2,1)S(1)} %pad_maximum_fusion.14.refs_3_.refs_8_), channel_id=1, source_target_pairs={{0,2},{1,3},{2,0},{3,1},{4,6},{5,7},{6,4},{7,5},{8,10},{9,11},{10,... | collective-permute-start | bytes 1622024 | tf_op jit(solution)/shard_map/ppermute | solution.py:767
  23.0 18.0 %collective-permute-start.4 = (bf16[1,528,256]{2,1,0:T(8,128)(2,1)S(1)}, bf16[1,528,256]{2,1,0:T(8,128)(2,1)S(1)}, u32[]{:S(2)}, u32[]{:S(2)}) collective-permute-start(bf16[1,528,256]{2,1,0:T(8,128)(2,1)S(1)} %slice.130), channel_id=1, source_target_pairs={{0,2},{1,3},{2,0},{3,1},{4,6},{5,7},{6,4},{7,5},{8,10},{9,11},{10,... | collective-permute-start | bytes 811016 | tf_op jit(solution)/shard_map/ppermute | solution.py:767
  24.6 16.4 %collective-permute-start.5 = (bf16[1,528,256]{2,1,0:T(8,128)(2,1)S(1)}, bf16[1,528,256]{2,1,0:T(8,128)(2,1)S(1)}, u32[]{:S(2)}, u32[]{:S(2)}) collective-permute-start(bf16[1,528,256]{2,1,0:T(8,128)(2,1)S(1)} %slice.131), channel_id=1, source_target_pairs={{0,1},{1,0},{2,3},{3,2},{4,5},{5,4},{6,7},{7,6},{8,9},{9,8},{10,11... | collective-permute-start | bytes 811016 | tf_op jit(solution)/shard_map/ppermute | solution.py:767
  25.2 19.1 %collective-permute-start.8 = (bf16[2,528,256]{2,1,0:T(8,128)(2,1)S(1)}, bf16[2,528,256]{2,1,0:T(8,128)(2,1)S(1)}, u32[]{:S(2)}, u32[]{:S(2)}) collective-permute-start(bf16[2,528,256]{2,1,0:T(8,128)(2,1)S(1)} %pad_maximum_fusion.16.refs_10_), channel_id=1, source_target_pairs={{0,1},{1,0},{2,3},{3,2},{4,5},{5,4},{6,7},{7,6},{8,9},{9,8},{10,11... | collective-permute-start | bytes 1622024 | tf_op jit(solution)/shard_map/ppermute | solution.py:767
  26.7 18.2 %collective-permute-start.10 = (bf16[2,528,256]{2,1,0:T(8,128)(2,1)S(1)}, bf16[2,528,256]{2,1,0:T(8,128)(2,1)S(1)}, u32[]{:S(2)}, u32[]{:S(2)}) collective-permute-start(bf16[2,528,256]{2,1,0:T(8,128)(2,1)S(1)} %pad_maximum_fusion.16.refs_10_), channel_id=1, source_target_pairs={{0,2},{1,3},{2,0},{3,1},{4,6},{5,7},{6,4},{7,5},{8,10},{9,11},{10,... | collective-permute-start | bytes 1622024 | tf_op jit(solution)/shard_map/ppermute | solution.py:767
  44.3 10.2 %collective-permute-start.12 = (bf16[1,528,256]{2,1,0:T(8,128)(2,1)S(1)}, bf16[1,528,256]{2,1,0:T(8,128)(2,1)}, u32[]{:S(2)}, u32[]{:S(2)}) collective-permute-start(bf16[1,528,256]{2,1,0:T(8,128)(2,1)S(1)} %slice.164), channel_id=1, source_target_pairs={{0,2},{1,3},{2,0},{3,1},{4,6},{5,7},{6,4},{7,5},{8,10},{9,11},{10,... | collective-permute-start | bytes 811016 | tf_op jit(solution)/shard_map/ppermute | solution.py:767
  45.4 11.4 %collective-permute-start.11 = (bf16[2,528,256]{2,1,0:T(8,128)(2,1)S(1)}, bf16[2,528,256]{2,1,0:T(8,128)(2,1)S(1)}, u32[]{:S(2)}, u32[]{:S(2)}) collective-permute-start(bf16[2,528,256]{2,1,0:T(8,128)(2,1)S(1)} %collective-permute-done.10.refs_14_), channel_id=1, source_target_pairs={{0,4},{4,0},{8,12},{12,8},{16,20},{20,16},{24,28},{28,24},{1,5},{5... | collective-permute-start | bytes 1622024 | tf_op jit(solution)/shard_map/ppermute | solution.py:767
  45.4 11.4 %collective-permute-start.9 = (bf16[2,528,256]{2,1,0:T(8,128)(2,1)S(1)}, bf16[2,528,256]{2,1,0:T(8,128)(2,1)}, u32[]{:S(2)}, u32[]{:S(2)}) collective-permute-start(bf16[2,528,256]{2,1,0:T(8,128)(2,1)S(1)} %collective-permute-done.8.refs_12_), channel_id=1, source_target_pairs={{0,4},{4,0},{8,12},{12,8},{16,20},{20,16},{24,28},{28,24},{1,5},{5... | collective-permute-start | bytes 1622024 | tf_op jit(solution)/shard_map/ppermute | solution.py:767
  102.5 24.0 %collective-permute-start.22 = (bf16[1216,256]{1,0:T(8,128)(2,1)S(1)}, bf16[1216,256]{1,0:T(8,128)(2,1)S(1)}, u32[]{:S(2)}, u32[]{:S(2)}) collective-permute-start(bf16[1216,256]{1,0:T(8,128)(2,1)S(1)} %get-tuple-element.148), channel_id=1, source_target_pairs={{0,1},{1,0},{2,3},{3,2},{4,5},{5,4},{6,7},{7,6},{8,9},{9,8},{10,11... | collective-permute-start | bytes 1867784 | tf_op jit(solution)/shard_map/ppermute | solution.py:767
  104.1 29.1 %collective-permute-start.23 = (bf16[1216,256]{1,0:T(8,128)(2,1)S(1)}, bf16[1216,256]{1,0:T(8,128)(2,1)S(1)}, u32[]{:S(2)}, u32[]{:S(2)}) collective-permute-start(bf16[1216,256]{1,0:T(8,128)(2,1)S(1)} %get-tuple-element.149), channel_id=1, source_target_pairs={{0,2},{1,3},{2,0},{3,1},{4,6},{5,7},{6,4},{7,5},{8,10},{9,11},{10,... | collective-permute-start | bytes 1867784 | tf_op jit(solution)/shard_map/ppermute | solution.py:767
  105.6 27.6 %collective-permute-start.24 = (bf16[1216,256]{1,0:T(8,128)(2,1)S(1)}, bf16[1216,256]{1,0:T(8,128)(2,1)S(1)}, u32[]{:S(2)}, u32[]{:S(2)}) collective-permute-start(bf16[1216,256]{1,0:T(8,128)(2,1)S(1)} %get-tuple-element.150), channel_id=1, source_target_pairs={{0,3},{1,2},{2,1},{3,0},{4,7},{5,6},{6,5},{7,4},{8,11},{9,10},{10,... | collective-permute-start | bytes 1867784 | tf_op jit(solution)/shard_map/ppermute | solution.py:767
  106.0 20.4 %collective-permute-start.21 = (bf16[2,528,256]{2,1,0:T(8,128)(2,1)S(1)}, bf16[2,528,256]{2,1,0:T(8,128)(2,1)S(1)}, u32[]{:S(2)}, u32[]{:S(2)}) collective-permute-start(bf16[2,528,256]{2,1,0:T(8,128)(2,1)S(1)} %copy-done.23), channel_id=1, source_target_pairs={{0,4},{4,0},{8,12},{12,8},{16,20},{20,16},{24,28},{28,24},{1,5},{5... | collective-permute-start | bytes 1622024 | tf_op jit(solution)/shard_map/ppermute | solution.py:767
  136.6 15.3 %collective-permute-start.31 = (bf16[1072,256]{1,0:T(8,128)(2,1)S(1)}, bf16[1072,256]{1,0:T(8,128)(2,1)S(1)}, u32[]{:S(2)}, u32[]{:S(2)}) collective-permute-start(bf16[1072,256]{1,0:T(8,128)(2,1)S(1)} %get-tuple-element.170), channel_id=1, source_target_pairs={{0,1},{1,0},{2,3},{3,2},{4,5},{5,4},{6,7},{7,6},{8,9},{9,8},{10,11... | collective-permute-start | bytes 1646600 | tf_op jit(solution)/shard_map/ppermute | solution.py:767
  137.9 24.7 %collective-permute-start.32 = (bf16[1072,256]{1,0:T(8,128)(2,1)S(1)}, bf16[1072,256]{1,0:T(8,128)(2,1)S(1)}, u32[]{:S(2)}, u32[]{:S(2)}) collective-permute-start(bf16[1072,256]{1,0:T(8,128)(2,1)S(1)} %get-tuple-element.171), channel_id=1, source_target_pairs={{0,2},{1,3},{2,0},{3,1},{4,6},{5,7},{6,4},{7,5},{8,10},{9,11},{10,... | collective-permute-start | bytes 1646600 | tf_op jit(solution)/shard_map/ppermute | solution.py:767
  138.7 25.5 %collective-permute-start.33 = (bf16[1072,256]{1,0:T(8,128)(2,1)S(1)}, bf16[1072,256]{1,0:T(8,128)(2,1)S(1)}, u32[]{:S(2)}, u32[]{:S(2)}) collective-permute-start(bf16[1072,256]{1,0:T(8,128)(2,1)S(1)} %get-tuple-element.172), channel_id=1, source_target_pairs={{0,3},{1,2},{2,1},{3,0},{4,7},{5,6},{6,5},{7,4},{8,11},{9,10},{10,... | collective-permute-start | bytes 1646600 | tf_op jit(solution)/shard_map/ppermute | solution.py:767
  140.1 9.9 %collective-permute-start.30 = (bf16[2,528,256]{2,1,0:T(8,128)(2,1)S(1)}, bf16[2,528,256]{2,1,0:T(8,128)(2,1)S(1)}, u32[]{:S(2)}, u32[]{:S(2)}) collective-permute-start(bf16[2,528,256]{2,1,0:T(8,128)(2,1)S(1)} %copy-done.24), channel_id=1, source_target_pairs={{0,4},{4,0},{8,12},{12,8},{16,20},{20,16},{24,28},{28,24},{1,5},{5... | collective-permute-start | bytes 1622024 | tf_op jit(solution)/shard_map/ppermute | solution.py:767
  140.2 9.8 %collective-permute-start.29 = (bf16[608,256]{1,0:T(8,128)(2,1)S(1)}, bf16[608,256]{1,0:T(8,128)(2,1)S(1)}, u32[]{:S(2)}, u32[]{:S(2)}) collective-permute-start(bf16[608,256]{1,0:T(8,128)(2,1)S(1)} %get-tuple-element.249), channel_id=1, source_target_pairs={{0,8},{4,12},{8,0},{12,4},{16,24},{20,28},{24,16},{28,20},{1,9},{5... | collective-permute-start | bytes 933896 | tf_op jit(solution)/shard_map/ppermute | solution.py:767
  164.8 16.6 %collective-permute-start.34 = (bf16[608,256]{1,0:T(8,128)(2,1)S(1)}, bf16[608,256]{1,0:T(8,128)(2,1)S(1)}, u32[]{:S(2)}, u32[]{:S(2)}) collective-permute-start(bf16[608,256]{1,0:T(8,128)(2,1)S(1)} %add_convert_fusion.3), channel_id=1, source_target_pairs={{0,16},{4,20},{8,24},{12,28},{16,0},{20,4},{24,8},{28,12},{1,17},{... | collective-permute-start | bytes 933896 | tf_op jit(solution)/shard_map/ppermute | solution.py:767
  167.5 12.4 %collective-permute-start.35 = (bf16[536,256]{1,0:T(8,128)(2,1)S(1)}, bf16[536,256]{1,0:T(8,128)(2,1)S(1)}, u32[]{:S(2)}, u32[]{:S(2)}) collective-permute-start(bf16[536,256]{1,0:T(8,128)(2,1)S(1)} %get-tuple-element.253), channel_id=1, source_target_pairs={{0,8},{4,12},{8,0},{12,4},{16,24},{20,28},{24,16},{28,20},{1,9},{5... | collective-permute-start | bytes 823304 | tf_op jit(solution)/shard_map/ppermute | solution.py:767
  181.6 14.2 %collective-permute-start.36 = (bf16[608,256]{1,0:T(8,128)(2,1)S(1)}, bf16[608,256]{1,0:T(8,128)(2,1)S(1)}, u32[]{:S(2)}, u32[]{:S(2)}) collective-permute-start(bf16[608,256]{1,0:T(8,128)(2,1)S(1)} %add_convert_fusion.2), channel_id=1, source_target_pairs={{0,8},{4,12},{8,0},{12,4},{16,24},{20,28},{24,16},{28,20},{1,9},{5... | collective-permute-start | bytes 933896 | tf_op jit(solution)/shard_map/ppermute | solution.py:767
  182.6 12.5 %collective-permute-start.37 = (bf16[536,256]{1,0:T(8,128)(2,1)S(1)}, bf16[536,256]{1,0:T(8,128)(2,1)S(1)}, u32[]{:S(2)}, u32[]{:S(2)}) collective-permute-start(bf16[536,256]{1,0:T(8,128)(2,1)S(1)} %add_convert_fusion.5), channel_id=1, source_target_pairs={{0,16},{4,20},{8,24},{12,28},{16,0},{20,4},{24,8},{28,12},{1,17},{... | collective-permute-start | bytes 823304 | tf_op jit(solution)/shard_map/ppermute | solution.py:767
  195.9 11.1 %collective-permute-start.40 = (bf16[1216,256]{1,0:T(8,128)(2,1)S(1)}, bf16[1216,256]{1,0:T(8,128)(2,1)S(1)}, u32[]{:S(2)}, u32[]{:S(2)}) collective-permute-start(bf16[1216,256]{1,0:T(8,128)(2,1)S(1)} %pad_maximum_fusion.12.refs_1_), channel_id=1, source_target_pairs={{0,4},{4,0},{8,12},{12,8},{16,20},{20,16},{24,28},{28,24},{1,5},{5... | collective-permute-start | bytes 1867784 | tf_op jit(solution)/shard_map/ppermute | solution.py:767
  196.0 10.7 %collective-permute-start.38 = (bf16[536,256]{1,0:T(8,128)(2,1)S(1)}, bf16[536,256]{1,0:T(8,128)(2,1)S(1)}, u32[]{:S(2)}, u32[]{:S(2)}) collective-permute-start(bf16[536,256]{1,0:T(8,128)(2,1)S(1)} %add_convert_fusion.4), channel_id=1, source_target_pairs={{0,8},{4,12},{8,0},{12,4},{16,24},{20,28},{24,16},{28,20},{1,9},{5... | collective-permute-start | bytes 823304 | tf_op jit(solution)/shard_map/ppermute | solution.py:767
  (45 other events, 229.5 us)

commit v3 on v2

--- a/solution.py
+++ b/solution.py
@@ -16,7 +16,7 @@
 INNER = math.sqrt(2.0 / math.pi)
 CUBE = 0.044715 * INNER
 TILE = 1024
-TOWER_TILE = 256
+TOWER_TILE = 512
 LANES = 128
 EXTRA = 16
 
@@ -207,7 +207,7 @@
     return [gates[:, at * LANES : (at + 1) * LANES] for at in range(count)]
 
 
-def forward_step(weights, value_ref, x_low, type_ref, total_ref, biases, keep, keep_gate=None):
+def forward_step(weights, value_ref, x_low, type_ref, total_ref, biases, keep, keep_gate=None, keep_result=None):
     height, width = x_low.shape
     kinds = total_ref.shape[0]
     bias_in, bias_out = zip(*(bias_rows(w, width) for w in weights))
@@ -221,10 +221,16 @@
         for i, w in enumerate(weights):
             hidden, slope = gelu_low(mm(x_low[rows], w[0:width]) + bias_in[i])
             keep(i, rows, hidden, slope)
+            if keep_result is not None:
+                result = mm(hidden, w[width : 2 * width]).astype(bf16)
+                keep_result(i, rows, result)
             for t in range(kinds):
-                scaled[t].append(twice(gates[i * kinds + t]) * hidden)
+                scaled[t].append(twice(gates[i * kinds + t]) * (hidden if keep_result is None else result))
         for t in range(kinds):
-            total_ref[t, rows] += mm(joined(scaled[t], 1), second)
+            if keep_result is None:
+                total_ref[t, rows] += mm(joined(scaled[t], 1), second)
+            else:
+                total_ref[t, rows] += functools.reduce(jnp.add, scaled[t]).astype(f32)
     for i in range(len(weights)):
         for t in range(kinds):
             at = (i * kinds + t) * LANES
@@ -236,7 +242,7 @@
         high = biases[t].astype(bf16)
         rest = (biases[t] - high.astype(f32)).astype(bf16)
         for rows in tiles(total_ref.shape[1], TILE):
-            total_ref[t, rows] += mm(type_ref[rows], high) + mm(type_ref[rows], rest)
+            total_ref[t, rows] += mm(twice(type_ref[rows]), jnp.concatenate([high, rest], axis=0))
 
 
 def backward_start(x_low, type_across, low, across, share):
@@ -248,7 +254,7 @@
         share[t] = mm(type_across[...], low[t])
 
 
-def backward_step(weights, value_ref, hiddens, slopes, outs, pair, experts, type_ref, type_across, low, stream_ref, across, share, table, scratch, kept_gates=None):
+def backward_step(weights, value_ref, hiddens, slopes, outs, pair, experts, type_ref, type_across, low, stream_ref, across, share, table, scratch, kept_gates=None, results=None, dots=None):
     before_grads, result_grads, products = scratch
     kinds, height, width = low.shape
     count = len(weights)
@@ -266,26 +272,25 @@
             result_grad = gates[i * kinds] * low[0, rows]
             for t in range(1, kinds):
                 result_grad += gates[i * kinds + t] * low[t, rows]
-            if kinds == 1:
-                hidden_grad = mm_nt(result_grad, second).astype(bf16)
-                backs = [hidden_grad]
-            else:
-                backs = [mm_nt(low[t, rows], second).astype(bf16) for t in range(kinds)]
-                hidden_grad = gates[i * kinds] * backs[0]
-                for t in range(1, kinds):
-                    hidden_grad += gates[i * kinds + t] * backs[t]
+            hidden_grad = mm_nt(result_grad, second).astype(bf16)
             for t in range(kinds):
-                product = hidden * backs[t]
-                at = (i * kinds + t) * LANES
-                products[rows, at : at + LANES] = functools.reduce(
+                product = hidden * hidden_grad if results is None else results[i][rows] * low[t, rows]
+                product = functools.reduce(
                     jnp.add, [product[:, lane : lane + LANES] for lane in range(0, width, LANES)]
                 )
+                if dots is None:
+                    at = (i * kinds + t) * LANES
+                    products[rows, at : at + LANES] = product
+                else:
+                    found = jnp.sum(product.astype(f32), axis=1, keepdims=True)
+                    lanes = lax.broadcasted_iota(jnp.int32, (1, LANES), 1)
+                    dots[rows] = jnp.where(lanes == t * experts + pair * count + i, found, dots[rows])
             before = slope * hidden_grad
             before_grads[i, rows] = before
             result_grads[i, rows] = result_grad
             befores.append(before)
         stream_ref[rows] += mm_nt(joined(befores, 1), first)
-    sums = mm(type_across[...], products[...])
+    sums = None if dots is not None else mm(type_across[...], products[...])
     lanes = lax.broadcasted_iota(jnp.int32, (type_ref.shape[1], LANES), 1)
     for i, w in enumerate(weights):
         _, bias_out = bias_rows(w, width)
@@ -298,7 +303,7 @@
             at = (i * kinds + t) * LANES
             gate = value_ref[:, at : at + LANES].astype(f32)
             out_bias += jnp.sum(twice(gate) * share[t], axis=0, keepdims=True)
-            found = jnp.sum(sums[:, at : at + LANES], axis=1, keepdims=True)
+            found = 0.0 if sums is None else jnp.sum(sums[:, at : at + LANES], axis=1, keepdims=True)
             bias_part = jnp.sum(share[t] * bias_out, axis=1, keepdims=True)
             if kinds == 1:
                 some = gate > 0.0
@@ -325,10 +330,22 @@
 
 def store_copies(ready, pair, held, out_refs, sems):
     group, unit = pair // held, lax.rem(pair, held)
-    copies = [(None, pltpu.make_async_copy(ready.at[0], out_refs[0].at[group, unit], sems.at[0]))]
+    rows = pl.ds(pl.multiple_of(unit * ready.shape[1], EXTRA), ready.shape[1])
+    copies = [(None, pltpu.make_async_copy(ready.at[0], out_refs[0].at[group, rows], sems.at[0]))]
     for at, ref in enumerate(out_refs[1:]):
-        copies.append((group == at, pltpu.make_async_copy(ready.at[1], ref.at[unit], sems.at[1])))
+        copies.append((group == at, pltpu.make_async_copy(ready.at[1], ref.at[rows], sems.at[1])))
     return copies
+
+
+def end_copies(ends, out_refs, sems):
+    rows = out_refs[0].shape[1]
+    last = pl.ds(rows - ends.shape[1], ends.shape[1])
+    groups = out_refs[0].shape[0]
+    copies = [pltpu.make_async_copy(ends.at[0], out_refs[0].at[at, last], sems.at[0, at]) for at in range(groups)]
+    copies += [
+        pltpu.make_async_copy(ends.at[1], ref.at[last], sems.at[1, at]) for at, ref in enumerate(out_refs[1:])
+    ]
+    return [(None, copy) for copy in copies]
 
 
 def for_each(copies, act):
@@ -436,10 +453,10 @@
     place_ref, x_ref, type_ref, across_types_ref, value_ref, gate_slope_ref, pred_grad_ref = take(7)
     tower_in_ref, tower_bias_ref, tower_out_ref = take(3)
     weight_refs = take(pieces)
-    pred_ref, stream_ref, small_ref, *tower_refs = take(3 + halves)
+    pred_ref, stream_ref = take(2)
     out_refs = take(1 + groups * (halves - 1))
-    x_low, weights, hidden_all, slope_all, gates_all, total, biases, low, across, share, table = take(11)
-    before_grads, result_grads, products, ready, in_grad, bias_grad, out_grad, load_sem, store_sem = take(9)
+    x_low, weights, hidden_all, slope_all, result_all, gates_all, total, biases, low, across, share, table = take(12)
+    before_grads, result_grads, dots, cotangents, ready, ends, in_grad, bias_grad, out_grad, load_sem, store_sem, end_sem = take(12)
     height, width = x_ref.shape
     pairs = value_ref.shape[0]
     experts = pairs * halves
@@ -465,6 +482,9 @@
 
         def keep_gate(at, rows, gate):
             gates_all[pair, at, rows] = gate
+
+        def keep_result(i, rows, result):
+            result_all[pair, i, rows] = result
 
         forward_step(
             [weights.at[pair, i] for i in range(halves)],
@@ -475,12 +495,16 @@
             biases,
             keep,
             keep_gate,
+            keep_result,
         )
         return carry
 
     lax.fori_loop(0, pairs, forward_pair, 0)
     forward_end(type_ref, total, biases)
 
+    cotangents[...] = jnp.concatenate(
+        [pred_grad_ref[...], jnp.zeros((cotangents.shape[1] - tasks, height), f32)]
+    ).T
     in_grad[...] = jnp.zeros_like(in_grad)
     bias_grad[...] = jnp.zeros_like(bias_grad)
     out_grad[...] = jnp.zeros_like(out_grad)
@@ -492,7 +516,7 @@
             act, slope = gelu_both(mm(closing_low, tower_in_ref[t]) + tower_bias_ref[t : t + 1])
             vector = tower_out_ref[t : t + 1]
             predicted.append(jnp.sum(act * vector, axis=1, keepdims=True))
-            cotangent = pred_grad_ref[rows, t : t + 1]
+            cotangent = cotangents[rows, t : t + 1]
             out_grad[t : t + 1] += jnp.sum(act * cotangent, axis=0, keepdims=True)
             before_grad = (slope * (cotangent * vector)).astype(bf16)
             bias_grad[t : t + 1] += jnp.sum(before_grad.astype(f32), axis=0, keepdims=True)
@@ -501,27 +525,25 @@
             low[t, rows] = closing_grad.astype(bf16)
             summed = closing_grad if summed is None else summed + closing_grad
         stream_ref[rows] = summed
-        pred_ref[rows] = jnp.concatenate(predicted, axis=1)
+        blank = jnp.zeros((predicted[0].shape[0], cotangents.shape[1] - tasks), f32)
+        pred_ref[:, rows] = jnp.concatenate([*predicted, blank], axis=1).T[0:tasks]
     narrow = in_grad.shape[2]
+    tall = width * narrow // width
+    begin = type_ref.shape[1] // 2 + EXTRA
     for t in range(tasks):
-        wide = jnp.concatenate([in_grad[t, : width * narrow // width], in_grad[t, width * narrow // width :]], axis=1)
+        wide = jnp.concatenate([in_grad[t, :tall], in_grad[t, tall:]], axis=1).astype(bf16)
         if halves == 2:
-
-            @pl.when(place_ref[2] == t)
-            def _(wide=wide):
-                tower_refs[0][...] = wide.astype(bf16)
-
-            @pl.when(place_ref[2] != t)
-            def _(wide=wide):
-                tower_refs[1][...] = wide.astype(bf16)
-
+            ends[place_ref[2] ^ t, begin:] = wide
         else:
-            tower_refs[0][t * wide.shape[0] : (t + 1) * wide.shape[0]] = wide.astype(bf16)
-    ends = [jnp.concatenate([ref[0:1], ref[1:2]], axis=1) for ref in (bias_grad, out_grad)]
-    tower_small = jnp.concatenate([*ends, jnp.zeros((EXTRA - 2, width), f32)]).astype(bf16)
+            ends[0, begin + t * tall : begin + (t + 1) * tall] = wide
+    vectors = [jnp.concatenate([ref[0:1], ref[1:2]], axis=1) for ref in (bias_grad, out_grad)]
+    vectors = jnp.concatenate([*vectors, jnp.zeros((EXTRA - 2, width), f32)]).astype(bf16)
+    for half in range(halves):
+        ends[half, begin - EXTRA : begin] = vectors
 
     backward_start(x_low, across_types_ref, low, across, share)
     table[...] = jnp.zeros_like(table)
+    dots[...] = jnp.zeros_like(dots)
 
     def stores(pair):
         return store_copies(ready.at[pair], pair, held, out_refs, store_sem.at[pair])
@@ -542,20 +564,29 @@
             across,
             share,
             table,
-            (before_grads, result_grads, products),
+            (before_grads, result_grads, None),
             gates_all.at[pair],
+            [result_all.at[pair, i] for i in range(halves)],
+            dots,
         )
         for_each(stores(pair), start)
         return carry
 
     lax.fori_loop(0, pairs, backward_pair, 0)
-    small_ref[...] = jnp.concatenate([through_gates(table, gate_slope_ref, experts, tasks), tower_small])
+    high = dots[...].astype(bf16)
+    rest = (dots[...] - high.astype(f32)).astype(bf16)
+    table[...] += mm(across_types_ref[...], high) + mm(across_types_ref[...], rest)
+    small = through_gates(table, gate_slope_ref, experts, tasks)
+    for half in range(halves):
+        ends[half, 0 : small.shape[0]] = small
+    for_each(end_copies(ends, out_refs, end_sem), start)
 
     def drain(pair, carry):
         for_each(stores(pair), wait)
         return carry
 
     lax.fori_loop(0, pairs, drain, 0)
+    for_each(end_copies(ends, out_refs, end_sem), wait)
 
 
 def middle_call(place, x, types, across_types, values, gate_slopes, tower, pieces, places, groups, halves, held):
@@ -566,11 +597,11 @@
     stride = 2 * width + EXTRA
     experts = pairs * halves
     outs = [jax.ShapeDtypeStruct(shape, f32) for shape in (pred_grad.shape, (height, width))]
-    outs.append(jax.ShapeDtypeStruct((type_count // 2 + EXTRA, 2 * LANES), bf16))
-    outs += [jax.ShapeDtypeStruct((tower_in.size // width // halves, width), bf16)] * halves
     near = len(outs)
-    outs.append(jax.ShapeDtypeStruct((groups, held, stride, width), bf16))
-    outs += [jax.ShapeDtypeStruct((held, stride, width), bf16)] * (groups * (halves - 1))
+    end_rows = type_count // 2 + EXTRA + tower_in.size // width // halves
+    rows = held * stride + end_rows
+    outs.append(jax.ShapeDtypeStruct((groups, rows, width), bf16))
+    outs += [jax.ShapeDtypeStruct((rows, width), bf16)] * (groups * (halves - 1))
     layer_at = gate_slopes.shape[1] // type_count - 1
     slope_spec = pl.BlockSpec((gate_slopes.shape[0], type_count, LANES), lambda i: (0, layer_at, 0))
     kept = pltpu.VMEM((pairs, halves, height, width), bf16)
@@ -588,6 +619,7 @@
             pltpu.VMEM((pairs, halves, stride, width), bf16),
             kept,
             kept,
+            kept,
             pltpu.VMEM((pairs, halves * tasks, height, LANES), bf16),
             pltpu.VMEM((tasks, height, width), f32),
             pltpu.VMEM((tasks, type_count, width), f32),
@@ -597,13 +629,16 @@
             pltpu.VMEM((type_count, LANES), f32),
             pltpu.VMEM((halves, height, width), bf16),
             pltpu.VMEM((halves, height, width), bf16),
-            pltpu.VMEM((height, lanes), bf16),
+            pltpu.VMEM((height, LANES), f32),
+            pltpu.VMEM((height, LANES), f32),
             pltpu.VMEM((pairs, halves, stride, width), bf16),
+            pltpu.VMEM((halves, end_rows, width), bf16),
             pltpu.VMEM(tower_in.shape, f32),
             pltpu.VMEM(tower_bias.shape, f32),
             pltpu.VMEM(tower_out.shape, f32),
             pltpu.SemaphoreType.DMA((pairs, halves)),
             pltpu.SemaphoreType.DMA((pairs, halves)),
+            pltpu.SemaphoreType.DMA((halves, groups)),
         ],
         compiler_params=kernel_params(),
         cost_estimate=pl.CostEstimate(
@@ -619,9 +654,10 @@
     take = lambda count: [refs.pop(0) for _ in range(count)]
     x_ref, type_ref, across_types_ref, stream_ref, gate_slope_ref, value_ref, hidden_ref, slope_ref = take(8)
     weight_refs = take(pieces)
-    stream_out_ref, small_ref = take(2)
+    stream_out_ref = take(1)[0]
     out_refs = take(1 + len(places) // each // held * (each - 1))
-    x_low, across, low, share, table, before_grads, result_grads, products, buffer, ready, sems, store_sem = take(12)
+    x_low, across, low, share, table, before_grads, result_grads, products, buffer, ready, ends = take(11)
+    sems, store_sem, end_sem = take(3)
     step = pl.program_id(0)
     slot = lax.rem(step, 2)
     experts = len(places)
@@ -665,9 +701,13 @@
 
     @pl.when(step == pl.num_programs(0) - 1)
     def _():
-        small_ref[...] = through_gates(table, gate_slope_ref, experts, tasks)
+        small = through_gates(table, gate_slope_ref, experts, tasks)
+        for half in range(each):
+            ends[half] = small
+        for_each(end_copies(ends, out_refs, end_sem), start)
         for_each(stores(step - 1), wait)
         for_each(stores(step), wait)
+        for_each(end_copies(ends, out_refs, end_sem), wait)
 
 
 def backward_call(x, types, across_types, stream, gate_slopes, layer_at, values, stash, pieces, places, held, tasks):
@@ -681,16 +721,16 @@
     specs.append(pl.BlockSpec((gate_slopes.shape[0], type_count, LANES), lambda i: (0, layer_at, 0)))
     specs.append(pl.BlockSpec((1, type_count, lanes), lambda i: (i, 0, 0)))
     specs += [pl.BlockSpec((1, each, height, width), lambda i: (i, 0, 0, 0))] * 2
-    mine = jax.ShapeDtypeStruct((groups, held, stride, width), bf16)
-    others = [jax.ShapeDtypeStruct((held, stride, width), bf16)] * (groups * (each - 1))
-    small = jax.ShapeDtypeStruct((type_count // 2, 2 * LANES), bf16)
+    rows = held * stride + type_count // 2
+    mine = jax.ShapeDtypeStruct((groups, rows, width), bf16)
+    others = [jax.ShapeDtypeStruct((rows, width), bf16)] * (groups * (each - 1))
     number = pairs * each
     return pl.pallas_call(
         functools.partial(backward_kernel, places, len(pieces), each, held, tasks),
         grid=(pairs,),
-        out_shape=[jax.ShapeDtypeStruct(stream.shape, f32), small, mine, *others],
+        out_shape=[jax.ShapeDtypeStruct(stream.shape, f32), mine, *others],
         in_specs=specs + [FAR] * len(pieces),
-        out_specs=[whole_spec(stream.shape), whole_spec(small.shape)] + [FAR] * (1 + len(others)),
+        out_specs=[whole_spec(stream.shape)] + [FAR] * (1 + len(others)),
         scratch_shapes=[
             pltpu.VMEM((height, width), bf16),
             pltpu.VMEM((width + EXTRA, height), bf16),
@@ -702,8 +742,10 @@
             pltpu.VMEM((height, lanes), bf16),
             pltpu.VMEM((2, each, stride, width), bf16),
             pltpu.VMEM((2, each, stride, width), bf16),
+            pltpu.VMEM((each, type_count // 2, width), bf16),
             pltpu.SemaphoreType.DMA((2, each)),
             pltpu.SemaphoreType.DMA((2, each)),
+            pltpu.SemaphoreType.DMA((each, groups)),
         ],
         compiler_params=kernel_params(),
         cost_estimate=pl.CostEstimate(
@@ -859,11 +901,11 @@
         last = layer_at == layers - 1
         got = near(own[layer_at][0], groups)
         if layer_at == 0:
-            got = after(got, types)
+            got = after(got, (types, own[0][1:], own[1:]))
         far = relay(got, groups, held)
         across = {ro: crossed(got[ro], halves) for ro in got}
         if not last:
-            own[layer_at + 1] = after(own[layer_at + 1], across)
+            own[layer_at + 1][0] = after(own[layer_at + 1][0], got)
         got = {0: own[layer_at][:1], **got}
         across[0] = own[layer_at][1:]
         if not last:
@@ -888,21 +930,20 @@
         weights.append(parts_of({**got, **far}, {**across, **far_across}))
 
     pieces, places = weights[-1]
-    predictions, stream, small, *rest = middle_call(
+    predictions, stream, *payload = middle_call(
         place,
         streams[-1],
         types,
         across_types,
         values[-1],
         gate_slopes,
-        (pred_grad, tower_in, tower_bias, tower_out),
+        (pred_grad.T, tower_in, tower_bias, tower_out),
         pieces,
         pair_order(places, range(held)),
         groups,
         halves,
         held,
     )
-    tower_rows, payload = rest[:halves], rest[halves:]
 
     shards = lax.axis_size("rows")
     paired = shards > 2
@@ -910,11 +951,10 @@
     upper = (row_at & 2) > 0
 
     class Moving:
-        def __init__(self, layer_at, payload, small, end=None):
-            self.layer_at, self.mine, self.end = layer_at, payload[0], [] if end is None else [end]
+        def __init__(self, layer_at, payload):
+            self.layer_at, self.mine = layer_at, payload[0]
             self.others = payload[1:] or [payload[0][ro] for ro in range(groups)]
-            self.small = small
-            self.got = [flip(part, "rows", 1) for part in [self.small, *self.others[1:]]]
+            self.got = [flip(part, "rows", 1) for part in self.others[1:]]
             self.total, self.sums, self.hops = None, None, -2
 
         def ask(self, token):
@@ -934,18 +974,13 @@
             else:
                 self.got = [total, flip(total, "rows", 2 if hops[self.hops] == "join" else hops[self.hops])]
 
-        def core_sum(self, ro, received):
-            rows = add_low(self.mine[ro], received).reshape(held * stride, width)
-            return jnp.concatenate([rows, self.small, *self.end])
-
         def add(self):
             if self.hops == len(hops):
                 return True
             if self.hops == -2:
-                self.small = add_low(self.small, self.got[0])
-                self.sums = {ro: self.core_sum(ro, self.got[ro]) for ro in range(1, groups)}
+                self.sums = {ro: add_low(self.mine[ro], self.got[ro - 1]) for ro in range(1, groups)}
             elif self.hops == -1:
-                self.total = add_low(self.core_sum(0, self.got[0]), *self.got[1:])
+                self.total = add_low(add_low(self.mine[0], self.got[0]), *self.got[1:])
             elif hops[self.hops] != "join":
                 self.total = add_low(*self.got)
             else:
@@ -961,17 +996,14 @@
         ended = [entry for entry in entries if entry.add()]
         return ([entry.sums if entry.total is None else entry.total for entry in entries], others), ended
 
-    tower_tail = tower_rows[0]
-    if halves == 2:
-        tower_tail = add_low(tower_rows[0], flip(tower_rows[1], "rows", 1))
-    moving = [Moving(layers - 1, payload, small, tower_tail)]
+    moving = [Moving(layers - 1, payload)]
     token, _ = arrive(moving, ())
     stream = after(stream, token)
     for layer_at in reversed(range(layers - 1)):
         for entry in moving:
             entry.ask(token)
         pieces, places = weights[layer_at]
-        stream, small, *payload = backward_call(
+        stream, *payload = backward_call(
             streams[layer_at],
             types,
             across_types,
@@ -986,46 +1018,64 @@
             tasks,
         )
         token, _ = arrive(moving, stream)
-        moving.append(Moving(layer_at, payload, small))
+        moving.append(Moving(layer_at, payload))
         token, _ = arrive(moving[-1:], token)
 
     whole = {}
+    arrays, tower_sums = None, ()
+
+    def ask(*entries):
+        nonlocal arrays, tower_sums
+        for entry in entries:
+            entry.ask(token)
+        for entry in entries:
+            if entry.hops < len(hops):
+                continue
+            moving.remove(entry)
+            layer_at, got = entry.layer_at, entry.got
+            whole[layer_at] = got
+            if layer_at == layers - 1:
+                end = got[0][held * stride + type_count // 2 :].astype(f32)
+                tower_rows = [array[held * stride + type_count // 2 + EXTRA :].astype(f32) for array in got]
+                if halves == 2:
+                    tower_rows = [jnp.where(core == 0, *tower_rows), jnp.where(core == 0, *tower_rows[::-1])]
+                wide = jnp.concatenate(tower_rows).reshape(tasks, -1, width)
+                narrow = tower_in.shape[2]
+                parts = [wide[:, :, at : at + narrow] for at in range(0, width, narrow)]
+                tower_sums = (
+                    jnp.concatenate(parts, axis=1),
+                    end[0].reshape(tower_bias.shape),
+                    end[1].reshape(tower_out.shape),
+                )
+            if moving:
+                sources = {(layer_at, half): array for half, array in enumerate(got)}
+                arrays = finish_call(place, sources, arrays, held, expert_in.shape)
+
+    if layers == 2 and len(hops) == 3:
+        later, earlier = moving
+        ask(earlier, later)
+        token, _ = arrive([later], ())
+        ask(later)
+        token, _ = arrive([earlier, later], ())
+        ask(earlier)
+        token, _ = arrive([earlier], ())
+        ask(earlier, later)
+        token, _ = arrive([earlier, later], ())
     while moving:
-        for entry in moving:
-            entry.ask(token)
-        for entry in [entry for entry in moving if entry.hops == len(hops)]:
-            moving.remove(entry)
-            whole[entry.layer_at] = entry.got
+        ask(*moving)
         if moving:
-            token, _ = arrive(moving, ())
-    first = {(layer_at, 0): got[0] for layer_at, got in whole.items()}
-    if halves == 2:
-        first.update({(layer_at, 1): got[1] for layer_at, got in whole.items() if layer_at > 0})
-    arrays = finish_call(place, first, None, held, expert_in.shape)
-    ends = {layer_at: got[0][held * stride :].astype(f32) for layer_at, got in whole.items()}
-    gate_grads = [ends[layer_at][: type_count // 2] for layer_at in range(layers)]
-    end = ends[layers - 1]
-    at = type_count // 2
-    tower_bias_sum = end[at].reshape(tower_bias.shape)
-    tower_out_sum = end[at + 1].reshape(tower_out.shape)
-    at = held * stride + at + EXTRA
-    tower_rows = [array[at:].astype(f32) for array in whole[layers - 1]]
-    if halves == 2:
-        tower_rows = [jnp.where(core == 0, *tower_rows), jnp.where(core == 0, *tower_rows[::-1])]
-    wide = jnp.concatenate(tower_rows).reshape(tasks, -1, width)
-    narrow = tower_in.shape[2]
-    tower_in_sum = jnp.concatenate([wide[:, :, at : at + narrow] for at in range(0, width, narrow)], axis=1)
+            token, _ = arrive(moving, (arrays, tower_sums))
+    gate_grads = [whole[layer_at][0][held * stride :][: type_count // 2].astype(f32) for layer_at in range(layers)]
     quantities = selectors * (bits + 1)
     small = jnp.stack(gate_grads)
     small = jnp.concatenate([small[..., :LANES], small[..., LANES:]], axis=1)[..., : tasks * quantities]
     small = small.reshape(layers, type_count, tasks, quantities)
     logits_grad = small[..., : selectors * bits].reshape(selector_logits.shape)
-    smalls = (logits_grad, small[..., selectors * bits :], tower_in_sum, tower_bias_sum, tower_out_sum)
-    if halves == 2:
-        last, (arrays, smalls) = lax.optimization_barrier((whole[0][1], (arrays, smalls)))
-        arrays = finish_call(place, {(0, 1): last}, arrays, held, expert_in.shape)
+    smalls = (logits_grad, small[..., selectors * bits :], *tower_sums)
+    got, (arrays, smalls) = lax.optimization_barrier((whole[0], (arrays, smalls)))
+    arrays = finish_call(place, {(0, half): array for half, array in enumerate(got)}, arrays, held, expert_in.shape)
     return (
-        predictions,
+        predictions.T,
         stream,
         arrays[0],
         arrays[2],

time: 218 us -> 197 us (0.904)
  waiting for transfers between devices: 69.4 us -> 58.8 us
  Pallas kernels: 88.6 us -> 82.9 us
    ppermute x41 -> x38, waiting for transfers between devices: 69.4 us -> 58.8 us  [flip(): return lax.ppermute(array, axis, [(i, i ^ bits) for i in range(size)])]
    pallas_call x1, Pallas kernels: 37.4 us -> 31.9 us  [middle_call(): pl.pallas_call(functools.partial(middle_kernel, places, len(pieces), grou...]
    unnamed x66 -> x62, local copies, waits for them, and re-layouts: 6.89 us -> 4.84 us
    convert_element_type x13 -> x8, other arithmetic: 6 us -> 4.68 us  [add_low(): return level[0].astype(bf16)]
    ppermute x41 -> x38, starting transfers between devices: 35 us -> 34.3 us  [flip(): return lax.ppermute(array, axis, [(i, i ^ bits) for i in range(size)])]
  transfers between devices with their start and end apart: 41 -> 38, of which waited for: 16 -> 17; matrix products, arithmetic and copies ran while one was open for 5% -> 4% of each run, Pallas kernels for 22% -> 24%
where the time goes in v3:
time: 197 us; the launch traced here: 196 us
  Pallas kernels  82.9 us (42%)
  waiting for transfers between devices  58.8 us (30%)
  starting transfers between devices  34.3 us (17%)
  local copies, waits for them, and re-layouts  10 us (5%)
  other arithmetic  8.5 us (4%)
    ppermute x38, waiting for transfers between devices, flip(): return lax.ppermute(array, axis, [(i, i ^ bits) for i in range(size)])  58.8 us
    ppermute x38, starting transfers between devices, flip(): return lax.ppermute(array, axis, [(i, i ^ bits) for i in range(size)])  34.3 us
    pallas_call x1, Pallas kernels, middle_call(): pl.pallas_call(functools.partial(middle_kernel, places, len(pieces), grou...  31.9 us
    pallas_call x2, Pallas kernels, forward_call(): pl.pallas_call(functools.partial(forward_kernel, places, len(pieces), eac...  21.4 us
    pallas_call x1, Pallas kernels, backward_call(): pl.pallas_call(functools.partial(backward_kernel, places, len(pieces), ea...  19.9 us
    pallas_call x2, Pallas kernels, finish_call(): pl.pallas_call(functools.partial(finish_kernel, names, held, rows, first)...  6.49 us
    unnamed x62, local copies, waits for them, and re-layouts  4.84 us
    convert_element_type x8, other arithmetic, add_low(): return level[0].astype(bf16)  4.68 us
  transfers between devices with their start and end apart: 38, of which 17 were waited for; matrix products, arithmetic and copies ran while one was open for 4% of the time, Pallas kernels for 24%

profile of v3, /device:TPU:0, one launch (start us, length us, event | category | flops | bytes accessed | tf_op | source)
XLA Modules:
  0.0 196.1 jit_solution(310864288909038083)
XLA Ops:
  3.8 3.0 %collective-permute-start = (bf16[2,528,256]{2,1,0:T(8,128)(2,1)S(1)}, bf16[2,528,256]{2,1,0:T(8,128)(2,1)S(1)}, u32[]{:S(2)}, u32[]{:S(2)}) collective-permute-start(bf16[2,528,256]{2,1,0:T(8,128)(2,1)S(1)} %pad_maximum_fusion.2.refs_3_.refs_8_), channel_id=1, source_target_pairs={{0,1},{1,0},{2,3},{3,2},{4,5},{5,4},{6,7},{7,6},{8,9},{9,8},{10,11... | collective-permute-start | bytes 1622024 | tf_op jit(solution)/shard_map/ppermute | solution.py:809
  10.8 3.2 %shard_map.230 = (bf16[1024,32]{1,0:T(8,128)(2,1)}, bf16[32,1024]{1,0:T(8,128)(2,1)}, f32[20,64,128]{2,1,0:T(8,128)}, bf16[8,32,256]{2,1,0:T(8,128)(2,1)}, bf16[8,32,512]{2,1,0:T(8,128)(2,1)}) custom-call(s32[3]{0:T(128)} %pad_add_fusion.place_ref.refs_0_, s32[1,256]{1,0:T(1,128)} %bitcast.105, s32[1,256]{1,0:T(1,128)} %bitcast.106, ...), custom_call_target="tpu_custom_call" | custom-call | flops 33554432 | bytes 2097152 | tf_op jit(solution)/shard_map/pallas_call | solution.py:169
  15.9 3.2 %collective-permute-done.refs_5_.refs_10_ = bf16[2,528,256]{2,1,0:T(8,128)(2,1)S(1)} collective-permute-done((bf16[2,528,256]{2,1,0:T(8,128)(2,1)S(1)}, bf16[2,528,256]{2,1,0:T(8,128)(2,1)S(1)}, u32[]{:S(2)}, u32[]{:S(2)}) %collective-permute-start) | collective-permute-done | bytes 540704 | tf_op jit(solution)/shard_map/ppermute | solution.py:809
  26.0 13.5 %shard_map.231 = (f32[1,1024,256]{2,1,0:T(8,128)}, bf16[8,2,1024,256]{3,2,1,0:T(8,128)(2,1)}, bf16[8,2,1024,256]{3,2,1,0:T(8,128)(2,1)}) custom-call(f32[1024,256]{1,0:T(8,128)} %refs_0_.5, bf16[1024,32]{1,0:T(8,128)(2,1)} %get-tuple-element.105.refs_1_.refs_2_, bf16[8,32,256]{2,1,0:T(8,128)(2,1)} %get-tuple-element.106.refs_2_.refs_5_, ...), custom_call_target="tpu_custom_call" | custom-call | flops 3221225472 | bytes 17825792 | tf_op jit(solution)/shard_map/pallas_call | solution.py:427
  39.6 1.7 collective-permute-done.4.refs_6_.refs_14_
  41.9 1.7 collective-permute-start.12
  46.4 7.8 %shard_map.232 = (f32[1,1024,256]{2,1,0:T(8,128)}, bf16[8,2,1024,256]{3,2,1,0:T(8,128)(2,1)}, bf16[8,2,1024,256]{3,2,1,0:T(8,128)(2,1)}) custom-call(f32[1024,256]{1,0:T(8,128)} %refs_0_.5, bf16[1024,32]{1,0:T(8,128)(2,1)} %get-tuple-element.105.refs_1_.refs_2_, ...), custom_call_target="tpu_custom_call", output_to_operand_aliasing={{1}: (4, {}), {2}: (5, {})} | custom-call | flops 1073741824 | bytes 7340032 | tf_op jit(solution)/shard_map/pallas_call | solution.py:427
  57.4 31.9 %shard_map.233 = (f32[2,1024]{1,0:T(2,128)}, f32[1024,256]{1,0:T(8,128)}, bf16[4,1216,256]{2,1,0:T(8,128)(2,1)}, bf16[1216,256]{1,0:T(8,128)(2,1)}, bf16[1216,25...) custom-call(s32[3]{0:T(128)} %pad_add_fusion.place_ref.refs_0_, f32[1024,256]{1,0:T(8,128)} %bitcast.109, ...), custom_call_target="tpu_custom_call" | custom-call | flops 15032385536 | bytes 12582912 | tf_op jit(solution)/shard_map/pallas_call | solution.py:611
  93.4 1.9 fusion.1
  96.5 2.6 %collective-permute-start.25 = (bf16[1216,256]{1,0:T(8,128)(2,1)S(1)}, bf16[1216,256]{1,0:T(8,128)(2,1)S(1)}, u32[]{:S(2)}, u32[]{:S(2)}) collective-permute-start(bf16[1216,256]{1,0:T(8,128)(2,1)S(1)} %get-tuple-element.142), channel_id=1, source_target_pairs={{0,3},{1,2},{2,1},{3,0},{4,7},{5,6},{6,5},{7,4},{8,11},{9,10},{10,... | collective-permute-start | bytes 1867784 | tf_op jit(solution)/shard_map/ppermute | solution.py:809
  99.0 19.9 %shard_map.234 = (f32[1024,256]{1,0:T(8,128)}, bf16[4,1072,256]{2,1,0:T(8,128)(2,1)}, bf16[1072,256]{1,0:T(8,128)(2,1)}, bf16[1072,256]{1,0:T(8,128)(2,1)}, bf16...) custom-call(f32[1024,256]{1,0:T(8,128)} %refs_0_.5, bf16[1024,32]{1,0:T(8,128)(2,1)} %get-tuple-element.105.refs_1_.refs_2_, ...), custom_call_target="tpu_custom_call" | custom-call | flops 8589934592 | bytes 29360128 | tf_op jit(solution)/shard_map/pallas_call | solution.py:728
  119.6 5.8 %collective-permute-done.24 = bf16[1216,256]{1,0:T(8,128)(2,1)S(1)} collective-permute-done((bf16[1216,256]{1,0:T(8,128)(2,1)S(1)}, bf16[1216,256]{1,0:T(8,128)(2,1)S(1)}, u32[]{:S(2)}, u32[]{:S(2)}) %collective-permute-start.24) | collective-permute-done | bytes 622624 | tf_op jit(solution)/shard_map/ppermute | solution.py:809
  132.9 3.5 %collective-permute-done.30 = bf16[608,256]{1,0:T(8,128)(2,1)S(1)} collective-permute-done((bf16[608,256]{1,0:T(8,128)(2,1)S(1)}, bf16[608,256]{1,0:T(8,128)(2,1)S(1)}, u32[]{:S(2)}, u32[]{:S(2)}) %collective-permute-start.30) | collective-permute-done | bytes 311328 | tf_op jit(solution)/shard_map/ppermute | solution.py:809
  136.5 2.7 %collective-permute-start.31 = (bf16[608,256]{1,0:T(8,128)(2,1)S(1)}, bf16[608,256]{1,0:T(8,128)(2,1)S(1)}, u32[]{:S(2)}, u32[]{:S(2)}) collective-permute-start(bf16[608,256]{1,0:T(8,128)(2,1)S(1)} %add_convert_fusion.3), channel_id=1, source_target_pairs={{0,16},{4,20},{8,24},{12,28},{16,0},{20,4},{24,8},{28,12},{1,17},{... | collective-permute-start | bytes 933896 | tf_op jit(solution)/shard_map/ppermute | solution.py:809
  139.1 5.5 %collective-permute-done.27 = bf16[1072,256]{1,0:T(8,128)(2,1)S(1)} collective-permute-done((bf16[1072,256]{1,0:T(8,128)(2,1)S(1)}, bf16[1072,256]{1,0:T(8,128)(2,1)S(1)}, u32[]{:S(2)}, u32[]{:S(2)}) %collective-permute-start.27) | collective-permute-done | bytes 548896 | tf_op jit(solution)/shard_map/ppermute | solution.py:809
  144.7 12.6 %collective-permute-done.28 = bf16[1072,256]{1,0:T(8,128)(2,1)S(1)} collective-permute-done((bf16[1072,256]{1,0:T(8,128)(2,1)S(1)}, bf16[1072,256]{1,0:T(8,128)(2,1)S(1)}, u32[]{:S(2)}, u32[]{:S(2)}) %collective-permute-start.28) | collective-permute-done | bytes 548896 | tf_op jit(solution)/shard_map/ppermute | solution.py:809
  158.8 6.7 %collective-permute-done.32 = bf16[536,256]{1,0:T(8,128)(2,1)S(1)} collective-permute-done((bf16[536,256]{1,0:T(8,128)(2,1)S(1)}, bf16[536,256]{1,0:T(8,128)(2,1)S(1)}, u32[]{:S(2)}, u32[]{:S(2)}) %collective-permute-start.32) | collective-permute-done | bytes 274464 | tf_op jit(solution)/shard_map/ppermute | solution.py:809
  166.6 2.6 %collective-permute-start.33 = (bf16[536,256]{1,0:T(8,128)(2,1)S(1)}, bf16[536,256]{1,0:T(8,128)(2,1)S(1)}, u32[]{:S(2)}, u32[]{:S(2)}) collective-permute-start(bf16[536,256]{1,0:T(8,128)(2,1)S(1)} %add_convert_fusion.5), channel_id=1, source_target_pairs={{0,16},{4,20},{8,24},{12,28},{16,0},{20,4},{24,8},{28,12},{1,17},{... | collective-permute-start | bytes 823304 | tf_op jit(solution)/shard_map/ppermute | solution.py:809
  169.2 8.4 %collective-permute-done.33 = bf16[536,256]{1,0:T(8,128)(2,1)S(1)} collective-permute-done((bf16[536,256]{1,0:T(8,128)(2,1)S(1)}, bf16[536,256]{1,0:T(8,128)(2,1)S(1)}, u32[]{:S(2)}, u32[]{:S(2)}) %collective-permute-start.33) | collective-permute-done | bytes 274464 | tf_op jit(solution)/shard_map/ppermute | solution.py:809
  179.4 2.7 %collective-permute-start.35 = (bf16[536,256]{1,0:T(8,128)(2,1)S(1)}, bf16[536,256]{1,0:T(8,128)(2,1)S(1)}, u32[]{:S(2)}, u32[]{:S(2)}) collective-permute-start(bf16[536,256]{1,0:T(8,128)(2,1)S(1)} %add_convert_fusion.4), channel_id=1, source_target_pairs={{0,8},{4,12},{8,0},{12,4},{16,24},{20,28},{24,16},{28,20},{1,9},{5... | collective-permute-start | bytes 823304 | tf_op jit(solution)/shard_map/ppermute | solution.py:809
  183.5 3.3 %shard_map.235 = (f32[2,4,256,256]{3,2,1,0:T(8,128)}, f32[2,4,256,256]{3,2,1,0:T(8,128)}, f32[2,4,256]{2,1,0:T(4,128)}, f32[2,4,256]{2,1,0:T(4,128)}) custom-call(s32[3]{0:T(128)} %pad_add_fusion.place_ref.refs_0_, bf16[1216,256]{1,0:T(8,128)(2,1)} %copy-done, bf16[1216,256]{1,0:T(8,128)(2,1)} %copy-done.4), custom_call_target="tpu_custom_call" | custom-call | bytes 3145728 | tf_op jit(solution)/shard_map/pallas_call | solution.py:792
  187.5 1.7 collective-permute-done.35
  189.6 1.8 collective-permute-done.37.refs_2_
  192.7 3.2 %shard_map.236 = (f32[2,4,256,256]{3,2,1,0:T(8,128)}, f32[2,4,256,256]{3,2,1,0:T(8,128)}, f32[2,4,256]{2,1,0:T(4,128)}, f32[2,4,256]{2,1,0:T(4,128)}) custom-call(s32[3]{0:T(128)} %pad_add_fusion.place_ref.refs_0_, bf16[1072,256]{1,0:T(8,128)(2,1)} %copy-done.1, bf16[1072,256]{1,0:T(8,128)(2,1)} %copy-done.5, ...), custom_call_target="tpu_custom_call", output_to_operand_aliasing={{0}: (3, {}), {1}: (4, {})} | custom-call | bytes 3145728 | tf_op jit(solution)/shard_map/pallas_call | solution.py:792
  (186 shorter events, 43.6 us)
Async XLA Ops:
  3.8 15.3 %collective-permute-start = (bf16[2,528,256]{2,1,0:T(8,128)(2,1)S(1)}, bf16[2,528,256]{2,1,0:T(8,128)(2,1)S(1)}, u32[]{:S(2)}, u32[]{:S(2)}) collective-permute-start(bf16[2,528,256]{2,1,0:T(8,128)(2,1)S(1)} %pad_maximum_fusion.2.refs_3_.refs_8_), channel_id=1, source_target_pairs={{0,1},{1,0},{2,3},{3,2},{4,5},{5,4},{6,7},{7,6},{8,9},{9,8},{10,11... | collective-permute-start | bytes 1622024 | tf_op jit(solution)/shard_map/ppermute | solution.py:809
  6.8 13.7 %collective-permute-start.1 = (bf16[2,528,256]{2,1,0:T(8,128)(2,1)S(1)}, bf16[2,528,256]{2,1,0:T(8,128)(2,1)S(1)}, u32[]{:S(2)}, u32[]{:S(2)}) collective-permute-start(bf16[2,528,256]{2,1,0:T(8,128)(2,1)S(1)} %pad_maximum_fusion.2.refs_3_.refs_8_), channel_id=1, source_target_pairs={{0,2},{1,3},{2,0},{3,1},{4,6},{5,7},{6,4},{7,5},{8,10},{9,11},{10,... | collective-permute-start | bytes 1622024 | tf_op jit(solution)/shard_map/ppermute | solution.py:809
  21.1 20.8 %collective-permute-start.8 = (bf16[2,528,256]{2,1,0:T(8,128)(2,1)S(1)}, bf16[2,528,256]{2,1,0:T(8,128)(2,1)S(1)}, u32[]{:S(2)}, u32[]{:S(2)}) collective-permute-start(bf16[2,528,256]{2,1,0:T(8,128)(2,1)S(1)} %pad_maximum_fusion.4.refs_10_), channel_id=1, source_target_pairs={{0,1},{1,0},{2,3},{3,2},{4,5},{5,4},{6,7},{7,6},{8,9},{9,8},{10,11... | collective-permute-start | bytes 1622024 | tf_op jit(solution)/shard_map/ppermute | solution.py:809
  21.5 22.1 %collective-permute-start.10 = (bf16[2,528,256]{2,1,0:T(8,128)(2,1)S(1)}, bf16[2,528,256]{2,1,0:T(8,128)(2,1)S(1)}, u32[]{:S(2)}, u32[]{:S(2)}) collective-permute-start(bf16[2,528,256]{2,1,0:T(8,128)(2,1)S(1)} %pad_maximum_fusion.4.refs_10_), channel_id=1, source_target_pairs={{0,2},{1,3},{2,0},{3,1},{4,6},{5,7},{6,4},{7,5},{8,10},{9,11},{10,... | collective-permute-start | bytes 1622024 | tf_op jit(solution)/shard_map/ppermute | solution.py:809
  23.2 18.1 %collective-permute-start.4 = (bf16[1,528,256]{2,1,0:T(8,128)(2,1)S(1)}, bf16[1,528,256]{2,1,0:T(8,128)(2,1)S(1)}, u32[]{:S(2)}, u32[]{:S(2)}) collective-permute-start(bf16[1,528,256]{2,1,0:T(8,128)(2,1)S(1)} %slice.136), channel_id=1, source_target_pairs={{0,2},{1,3},{2,0},{3,1},{4,6},{5,7},{6,4},{7,5},{8,10},{9,11},{10,... | collective-permute-start | bytes 811016 | tf_op jit(solution)/shard_map/ppermute | solution.py:809
  23.6 17.7 %collective-permute-start.5 = (bf16[1,528,256]{2,1,0:T(8,128)(2,1)S(1)}, bf16[1,528,256]{2,1,0:T(8,128)(2,1)S(1)}, u32[]{:S(2)}, u32[]{:S(2)}) collective-permute-start(bf16[1,528,256]{2,1,0:T(8,128)(2,1)S(1)} %slice.137), channel_id=1, source_target_pairs={{0,1},{1,0},{2,3},{3,2},{4,5},{5,4},{6,7},{7,6},{8,9},{9,8},{10,11... | collective-permute-start | bytes 811016 | tf_op jit(solution)/shard_map/ppermute | solution.py:809
  41.9 12.4 %collective-permute-start.12 = (bf16[1,528,256]{2,1,0:T(8,128)(2,1)S(1)}, bf16[1,528,256]{2,1,0:T(8,128)(2,1)S(1)}, u32[]{:S(2)}, u32[]{:S(2)}) collective-permute-start(bf16[1,528,256]{2,1,0:T(8,128)(2,1)S(1)} %slice.166), channel_id=1, source_target_pairs={{0,2},{1,3},{2,0},{3,1},{4,6},{5,7},{6,4},{7,5},{8,10},{9,11},{10,... | collective-permute-start | bytes 811016 | tf_op jit(solution)/shard_map/ppermute | solution.py:809
  43.6 10.7 %collective-permute-start.13 = (bf16[1,528,256]{2,1,0:T(8,128)(2,1)S(1)}, bf16[1,528,256]{2,1,0:T(8,128)(2,1)S(1)}, u32[]{:S(2)}, u32[]{:S(2)}) collective-permute-start(bf16[1,528,256]{2,1,0:T(8,128)(2,1)S(1)} %slice.167), channel_id=1, source_target_pairs={{0,1},{1,0},{2,3},{3,2},{4,5},{5,4},{6,7},{7,6},{8,9},{9,8},{10,11... | collective-permute-start | bytes 811016 | tf_op jit(solution)/shard_map/ppermute | solution.py:809
  45.2 11.1 %collective-permute-start.11 = (bf16[2,528,256]{2,1,0:T(8,128)(2,1)S(1)}, bf16[2,528,256]{2,1,0:T(8,128)(2,1)S(1)}, u32[]{:S(2)}, u32[]{:S(2)}) collective-permute-start(bf16[2,528,256]{2,1,0:T(8,128)(2,1)S(1)} %collective-permute-done.10.refs_14_), channel_id=1, source_target_pairs={{0,4},{4,0},{8,12},{12,8},{16,20},{20,16},{24,28},{28,24},{1,5},{5... | collective-permute-start | bytes 1622024 | tf_op jit(solution)/shard_map/ppermute | solution.py:809
  45.2 11.1 %collective-permute-start.9 = (bf16[2,528,256]{2,1,0:T(8,128)(2,1)S(1)}, bf16[2,528,256]{2,1,0:T(8,128)(2,1)S(1)}, u32[]{:S(2)}, u32[]{:S(2)}) collective-permute-start(bf16[2,528,256]{2,1,0:T(8,128)(2,1)S(1)} %collective-permute-done.8.refs_12_), channel_id=1, source_target_pairs={{0,4},{4,0},{8,12},{12,8},{16,20},{20,16},{24,28},{28,24},{1,5},{5... | collective-permute-start | bytes 1622024 | tf_op jit(solution)/shard_map/ppermute | solution.py:809
  95.3 23.7 %collective-permute-start.22 = (bf16[1216,256]{1,0:T(8,128)(2,1)}, bf16[1216,256]{1,0:T(8,128)(2,1)S(1)}, u32[]{:S(2)}, u32[]{:S(2)}) collective-permute-start(bf16[1216,256]{1,0:T(8,128)(2,1)} %get-tuple-element.139), channel_id=1, source_target_pairs={{0,4},{4,0},{8,12},{12,8},{16,20},{20,16},{24,28},{28,24},{1,5},{5... | collective-permute-start | bytes 1867784 | tf_op jit(solution)/shard_map/ppermute | solution.py:809
  95.5 24.0 %collective-permute-start.23 = (bf16[1216,256]{1,0:T(8,128)(2,1)S(1)}, bf16[1216,256]{1,0:T(8,128)(2,1)S(1)}, u32[]{:S(2)}, u32[]{:S(2)}) collective-permute-start(bf16[1216,256]{1,0:T(8,128)(2,1)S(1)} %get-tuple-element.140), channel_id=1, source_target_pairs={{0,1},{1,0},{2,3},{3,2},{4,5},{5,4},{6,7},{7,6},{8,9},{9,8},{10,11... | collective-permute-start | bytes 1867784 | tf_op jit(solution)/shard_map/ppermute | solution.py:809
  96.1 29.4 %collective-permute-start.24 = (bf16[1216,256]{1,0:T(8,128)(2,1)S(1)}, bf16[1216,256]{1,0:T(8,128)(2,1)S(1)}, u32[]{:S(2)}, u32[]{:S(2)}) collective-permute-start(bf16[1216,256]{1,0:T(8,128)(2,1)S(1)} %get-tuple-element.141), channel_id=1, source_target_pairs={{0,2},{1,3},{2,0},{3,1},{4,6},{5,7},{6,4},{7,5},{8,10},{9,11},{10,... | collective-permute-start | bytes 1867784 | tf_op jit(solution)/shard_map/ppermute | solution.py:809
  96.5 29.0 %collective-permute-start.25 = (bf16[1216,256]{1,0:T(8,128)(2,1)S(1)}, bf16[1216,256]{1,0:T(8,128)(2,1)S(1)}, u32[]{:S(2)}, u32[]{:S(2)}) collective-permute-start(bf16[1216,256]{1,0:T(8,128)(2,1)S(1)} %get-tuple-element.142), channel_id=1, source_target_pairs={{0,3},{1,2},{2,1},{3,0},{4,7},{5,6},{6,5},{7,4},{8,11},{9,10},{10,... | collective-permute-start | bytes 1867784 | tf_op jit(solution)/shard_map/ppermute | solution.py:809
  118.9 8.1 %collective-permute-start.19 = (bf16[1072,256]{1,0:T(8,128)(2,1)}, bf16[1072,256]{1,0:T(8,128)(2,1)S(1)}, u32[]{:S(2)}, u32[]{:S(2)}) collective-permute-start(bf16[1072,256]{1,0:T(8,128)(2,1)} %get-tuple-element.135), channel_id=1, source_target_pairs={{0,4},{4,0},{8,12},{12,8},{16,20},{20,16},{24,28},{28,24},{1,5},{5... | collective-permute-start | bytes 1646600 | tf_op jit(solution)/shard_map/ppermute | solution.py:809
  127.8 8.6 %collective-permute-start.30 = (bf16[608,256]{1,0:T(8,128)(2,1)S(1)}, bf16[608,256]{1,0:T(8,128)(2,1)S(1)}, u32[]{:S(2)}, u32[]{:S(2)}) collective-permute-start(bf16[608,256]{1,0:T(8,128)(2,1)S(1)} %get-tuple-element.224), channel_id=1, source_target_pairs={{0,8},{4,12},{8,0},{12,4},{16,24},{20,28},{24,16},{28,20},{1,9},{5... | collective-permute-start | bytes 933896 | tf_op jit(solution)/shard_map/ppermute | solution.py:809
  129.4 9.7 %collective-permute-start.26 = (bf16[1072,256]{1,0:T(8,128)(2,1)S(1)}, bf16[1072,256]{1,0:T(8,128)(2,1)S(1)}, u32[]{:S(2)}, u32[]{:S(2)}) collective-permute-start(bf16[1072,256]{1,0:T(8,128)(2,1)S(1)} %copy-done.18), channel_id=1, source_target_pairs={{0,4},{4,0},{8,12},{12,8},{16,20},{20,16},{24,28},{28,24},{1,5},{5... | collective-permute-start | bytes 1646600 | tf_op jit(solution)/shard_map/ppermute | solution.py:809
  129.4 15.2 %collective-permute-start.27 = (bf16[1072,256]{1,0:T(8,128)(2,1)S(1)}, bf16[1072,256]{1,0:T(8,128)(2,1)S(1)}, u32[]{:S(2)}, u32[]{:S(2)}) collective-permute-start(bf16[1072,256]{1,0:T(8,128)(2,1)S(1)} %get-tuple-element.155), channel_id=1, source_target_pairs={{0,1},{1,0},{2,3},{3,2},{4,5},{5,4},{6,7},{7,6},{8,9},{9,8},{10,11... | collective-permute-start | bytes 1646600 | tf_op jit(solution)/shard_map/ppermute | solution.py:809
  130.9 26.3 %collective-permute-start.28 = (bf16[1072,256]{1,0:T(8,128)(2,1)S(1)}, bf16[1072,256]{1,0:T(8,128)(2,1)S(1)}, u32[]{:S(2)}, u32[]{:S(2)}) collective-permute-start(bf16[1072,256]{1,0:T(8,128)(2,1)S(1)} %get-tuple-element.156), channel_id=1, source_target_pairs={{0,2},{1,3},{2,0},{3,1},{4,6},{5,7},{6,4},{7,5},{8,10},{9,11},{10,... | collective-permute-start | bytes 1646600 | tf_op jit(solution)/shard_map/ppermute | solution.py:809
  131.4 25.8 %collective-permute-start.29 = (bf16[1072,256]{1,0:T(8,128)(2,1)S(1)}, bf16[1072,256]{1,0:T(8,128)(2,1)S(1)}, u32[]{:S(2)}, u32[]{:S(2)}) collective-permute-start(bf16[1072,256]{1,0:T(8,128)(2,1)S(1)} %get-tuple-element.157), channel_id=1, source_target_pairs={{0,3},{1,2},{2,1},{3,0},{4,7},{5,6},{6,5},{7,4},{8,11},{9,10},{10,... | collective-permute-start | bytes 1646600 | tf_op jit(solution)/shard_map/ppermute | solution.py:809
  136.5 20.8 %collective-permute-start.31 = (bf16[608,256]{1,0:T(8,128)(2,1)S(1)}, bf16[608,256]{1,0:T(8,128)(2,1)S(1)}, u32[]{:S(2)}, u32[]{:S(2)}) collective-permute-start(bf16[608,256]{1,0:T(8,128)(2,1)S(1)} %add_convert_fusion.3), channel_id=1, source_target_pairs={{0,16},{4,20},{8,24},{12,28},{16,0},{20,4},{24,8},{28,12},{1,17},{... | collective-permute-start | bytes 933896 | tf_op jit(solution)/shard_map/ppermute | solution.py:809
  165.6 13.5 %collective-permute-start.34 = (bf16[608,256]{1,0:T(8,128)(2,1)S(1)}, bf16[608,256]{1,0:T(8,128)(2,1)S(1)}, u32[]{:S(2)}, u32[]{:S(2)}) collective-permute-start(bf16[608,256]{1,0:T(8,128)(2,1)S(1)} %add_convert_fusion.2), channel_id=1, source_target_pairs={{0,8},{4,12},{8,0},{12,4},{16,24},{20,28},{24,16},{28,20},{1,9},{5... | collective-permute-start | bytes 933896 | tf_op jit(solution)/shard_map/ppermute | solution.py:809
  166.6 11.0 %collective-permute-start.33 = (bf16[536,256]{1,0:T(8,128)(2,1)S(1)}, bf16[536,256]{1,0:T(8,128)(2,1)S(1)}, u32[]{:S(2)}, u32[]{:S(2)}) collective-permute-start(bf16[536,256]{1,0:T(8,128)(2,1)S(1)} %add_convert_fusion.5), channel_id=1, source_target_pairs={{0,16},{4,20},{8,24},{12,28},{16,0},{20,4},{24,8},{28,12},{1,17},{... | collective-permute-start | bytes 823304 | tf_op jit(solution)/shard_map/ppermute | solution.py:809
  179.4 9.8 %collective-permute-start.35 = (bf16[536,256]{1,0:T(8,128)(2,1)S(1)}, bf16[536,256]{1,0:T(8,128)(2,1)S(1)}, u32[]{:S(2)}, u32[]{:S(2)}) collective-permute-start(bf16[536,256]{1,0:T(8,128)(2,1)S(1)} %add_convert_fusion.4), channel_id=1, source_target_pairs={{0,8},{4,12},{8,0},{12,4},{16,24},{20,28},{24,16},{28,20},{1,9},{5... | collective-permute-start | bytes 823304 | tf_op jit(solution)/shard_map/ppermute | solution.py:809
  (41 other events, 155.6 us)

commit v4 on v3

--- a/solution.py
+++ b/solution.py
@@ -45,13 +45,15 @@
     return value, slope
 
 
-def gelu_low(v):
+def gelu_parts(v):
     bend = 2.0 * INNER + 8.0 * CUBE * (v * v)
     twice_share = 1.0 + jnp.tanh(v * bend)
-    value = (v * twice_share).astype(bf16)
-    bend, twice_share = bend.astype(bf16), twice_share.astype(bf16)
+    return v * twice_share, bend, twice_share
+
+
+def gelu_slope(value, bend, twice_share):
     rise = 3.0 * bend - 4.0 * INNER
-    return value, twice_share + value * (2.0 - twice_share) * rise
+    return twice_share + value * (2.0 - twice_share) * rise
 
 
 FAR = pl.BlockSpec(memory_space=pl.ANY)
@@ -219,8 +221,10 @@
                 keep_gate(at, rows, gate)
         scaled = [[] for _ in range(kinds)]
         for i, w in enumerate(weights):
-            hidden, slope = gelu_low(mm(x_low[rows], w[0:width]) + bias_in[i])
-            keep(i, rows, hidden, slope)
+            before = mm(x_low[rows], w[0:width]) + bias_in[i]
+            hidden, bend, twice_share = gelu_parts(before)
+            hidden = hidden.astype(bf16)
+            keep(i, rows, hidden, gelu_slope(hidden, bend.astype(bf16), twice_share.astype(bf16)))
             if keep_result is not None:
                 result = mm(hidden, w[width : 2 * width]).astype(bf16)
                 keep_result(i, rows, result)
@@ -864,7 +868,7 @@
     place = jnp.stack([(row_at * groups + me) * height, me, core]).astype(jnp.int32)
 
     def rows_of(layer_at, first):
-        cut = lambda a: lax.dynamic_slice_in_dim(a[layer_at], first, held)
+        cut = lambda a: lax.dynamic_slice(a, (layer_at, first) + (0,) * (a.ndim - 2), (1, held) + a.shape[2:])[0]
         half = lambda a: a * jnp.asarray(0.5, a.dtype)
         tail = []
         for bias in (half(cut(expert_in_bias)), cut(expert_out_bias)):
@@ -873,11 +877,17 @@
         tail = jnp.pad(jnp.stack(tail, axis=1), ((0, 0), (0, EXTRA - len(tail)), (0, 0)))
         return jnp.concatenate([half(cut(expert_in)), cut(expert_out), tail], axis=1)
 
-    own = [[rows_of(layer_at, held * (core ^ half)) for half in range(halves)] for layer_at in range(layers)]
+    first = rows_of(0, held * core)
+    asked = near(first, groups)
     sizes = (owned, halves, held, selectors, bits, tasks)
     types, across_types, gate_slopes, *values = prepare_call(
         place, lengths, session_type, selector_logits, selector_mix, height, sizes
     )
+
+    later = after((expert_in, expert_in_bias, expert_out, expert_out_bias), types)
+    expert_in, expert_in_bias, expert_out, expert_out_bias = later
+    own = [[rows_of(layer_at, held * (core ^ half)) for half in range(halves)] for layer_at in range(layers)]
+    own[0][0] = first
 
     def parts_of(got, across):
         pieces, places = [], {}
@@ -899,13 +909,11 @@
     streams, stashes, weights = [rows_in], [], []
     for layer_at in range(layers):
         last = layer_at == layers - 1
-        got = near(own[layer_at][0], groups)
-        if layer_at == 0:
-            got = after(got, (types, own[0][1:], own[1:]))
+        got = near(own[layer_at][0], groups) if layer_at else after(asked, (types, own[0][1:], own[1:]))
         far = relay(got, groups, held)
         across = {ro: crossed(got[ro], halves) for ro in got}
         if not last:
-            own[layer_at + 1][0] = after(own[layer_at + 1][0], got)
+            pass
         got = {0: own[layer_at][:1], **got}
         across[0] = own[layer_at][1:]
         if not last:

time: 197 us -> 195 us (0.990)
  local copies, waits for them, and re-layouts: 10 us -> 7.83 us
    slice x4 -> x0, local copies, waits for them, and re-layouts: 2.84 us -> none  [rows_of(): cut = lambda a: lax.dynamic_slice_in_dim(a[layer_at], first, held)]
    unnamed x62 -> x63, local copies, waits for them, and re-layouts: 4.84 us -> 4.51 us
  transfers between devices with their start and end apart: 38 -> 38, of which waited for: 17 -> 17; matrix products, arithmetic and copies ran while one was open for 4% -> 4% of each run, Pallas kernels for 24% -> 25%
where the time goes in v4:
time: 195 us
  Pallas kernels  82.9 us (43%)
  waiting for transfers between devices  57.6 us (30%)
  starting transfers between devices  34.4 us (18%)
  other arithmetic  10.4 us (5%)
  local copies, waits for them, and re-layouts  7.83 us (4%)
    ppermute x38, waiting for transfers between devices, flip(): return lax.ppermute(array, axis, [(i, i ^ bits) for i in range(size)])  57.6 us
    ppermute x38, starting transfers between devices, flip(): return lax.ppermute(array, axis, [(i, i ^ bits) for i in range(size)])  34.4 us
    pallas_call x1, Pallas kernels, middle_call(): pl.pallas_call(functools.partial(middle_kernel, places, len(pieces), grou...  31.9 us
    pallas_call x2, Pallas kernels, forward_call(): pl.pallas_call(functools.partial(forward_kernel, places, len(pieces), eac...  21.4 us
    pallas_call x1, Pallas kernels, backward_call(): pl.pallas_call(functools.partial(backward_kernel, places, len(pieces), ea...  19.9 us
    pallas_call x2, Pallas kernels, finish_call(): pl.pallas_call(functools.partial(finish_kernel, names, held, rows, first)...  6.48 us
    convert_element_type x8, other arithmetic, add_low(): return level[0].astype(bf16)  4.68 us
    unnamed x63, local copies, waits for them, and re-layouts  4.51 us
  transfers between devices with their start and end apart: 38, of which 17 were waited for; matrix products, arithmetic and copies ran while one was open for 4% of the time, Pallas kernels for 25%

profile of v4, /device:TPU:0, one launch (start us, length us, event | category | flops | bytes accessed | tf_op | source)
XLA Modules:
  0.0 194.6 jit_solution(14317698195381602151)
XLA Ops:
  2.7 3.0 %collective-permute-start = (bf16[2,528,256]{2,1,0:T(8,128)(2,1)S(1)}, bf16[2,528,256]{2,1,0:T(8,128)(2,1)S(1)}, u32[]{:S(2)}, u32[]{:S(2)}) collective-permute-start(bf16[2,528,256]{2,1,0:T(8,128)(2,1)S(1)} %pad_maximum_fusion.2.refs_3_.refs_8_), channel_id=1, source_target_pairs={{0,1},{1,0},{2,3},{3,2},{4,5},{5,4},{6,7},{7,6},{8,9},{9,8},{10,11... | collective-permute-start | bytes 1622024 | tf_op jit(solution)/shard_map/ppermute | solution.py:813
  9.5 3.2 %shard_map.230 = (bf16[1024,32]{1,0:T(8,128)(2,1)}, bf16[32,1024]{1,0:T(8,128)(2,1)}, f32[20,64,128]{2,1,0:T(8,128)}, bf16[8,32,256]{2,1,0:T(8,128)(2,1)}, bf16[8,32,512]{2,1,0:T(8,128)(2,1)}) custom-call(s32[3]{0:T(128)} %pad_add_fusion.place_ref.refs_0_, s32[1,256]{1,0:T(1,128)} %bitcast.93, s32[1,256]{1,0:T(1,128)} %bitcast.94, f32[64,32]{1,0:T(8,128)} %copy.40.logit_ref, ...), custom_call_target="tpu_custom_call" | custom-call | flops 33554432 | bytes 2097152 | tf_op jit(solution)/shard_map/pallas_call | solution.py:171
  14.9 3.1 %collective-permute-done.refs_5_.refs_10_ = bf16[2,528,256]{2,1,0:T(8,128)(2,1)S(1)} collective-permute-done((bf16[2,528,256]{2,1,0:T(8,128)(2,1)S(1)}, bf16[2,528,256]{2,1,0:T(8,128)(2,1)S(1)}, u32[]{:S(2)}, u32[]{:S(2)}) %collective-permute-start) | collective-permute-done | bytes 540704 | tf_op jit(solution)/shard_map/ppermute | solution.py:813
  20.4 1.7 collective-permute-start.10
  26.0 13.5 %shard_map.231 = (f32[1,1024,256]{2,1,0:T(8,128)}, bf16[8,2,1024,256]{3,2,1,0:T(8,128)(2,1)}, bf16[8,2,1024,256]{3,2,1,0:T(8,128)(2,1)}) custom-call(f32[1024,256]{1,0:T(8,128)} %refs_0_.5, bf16[1024,32]{1,0:T(8,128)(2,1)} %get-tuple-element.108.refs_1_.refs_2_, bf16[8,32,256]{2,1,0:T(8,128)(2,1)} %get-tuple-element.109.refs_2_.refs_5_, ...), custom_call_target="tpu_custom_call" | custom-call | flops 3221225472 | bytes 17825792 | tf_op jit(solution)/shard_map/pallas_call | solution.py:431
  40.7 1.8 collective-permute-start.12
  45.3 7.8 %shard_map.232 = (f32[1,1024,256]{2,1,0:T(8,128)}, bf16[8,2,1024,256]{3,2,1,0:T(8,128)(2,1)}, bf16[8,2,1024,256]{3,2,1,0:T(8,128)(2,1)}) custom-call(f32[1024,256]{1,0:T(8,128)} %refs_0_.5, bf16[1024,32]{1,0:T(8,128)(2,1)} %get-tuple-element.108.refs_1_.refs_2_, ...), custom_call_target="tpu_custom_call", output_to_operand_aliasing={{1}: (4, {}), {2}: (5, {})} | custom-call | flops 1073741824 | bytes 7340032 | tf_op jit(solution)/shard_map/pallas_call | solution.py:431
  55.9 31.9 %shard_map.233 = (f32[2,1024]{1,0:T(2,128)}, f32[1024,256]{1,0:T(8,128)}, bf16[4,1216,256]{2,1,0:T(8,128)(2,1)}, bf16[1216,256]{1,0:T(8,128)(2,1)}, bf16[1216,25...) custom-call(s32[3]{0:T(128)} %pad_add_fusion.place_ref.refs_0_, f32[1024,256]{1,0:T(8,128)} %bitcast.97, ...), custom_call_target="tpu_custom_call" | custom-call | flops 15032385536 | bytes 12582912 | tf_op jit(solution)/shard_map/pallas_call | solution.py:615
  92.0 1.9 fusion.1
  95.0 2.6 %collective-permute-start.25 = (bf16[1216,256]{1,0:T(8,128)(2,1)S(1)}, bf16[1216,256]{1,0:T(8,128)(2,1)S(1)}, u32[]{:S(2)}, u32[]{:S(2)}) collective-permute-start(bf16[1216,256]{1,0:T(8,128)(2,1)S(1)} %get-tuple-element.148), channel_id=1, source_target_pairs={{0,3},{1,2},{2,1},{3,0},{4,7},{5,6},{6,5},{7,4},{8,11},{9,10},{10,... | collective-permute-start | bytes 1867784 | tf_op jit(solution)/shard_map/ppermute | solution.py:813
  97.6 19.9 %shard_map.234 = (f32[1024,256]{1,0:T(8,128)}, bf16[4,1072,256]{2,1,0:T(8,128)(2,1)}, bf16[1072,256]{1,0:T(8,128)(2,1)}, bf16[1072,256]{1,0:T(8,128)(2,1)}, bf16...) custom-call(f32[1024,256]{1,0:T(8,128)} %refs_0_.5, bf16[1024,32]{1,0:T(8,128)(2,1)} %get-tuple-element.108.refs_1_.refs_2_, ...), custom_call_target="tpu_custom_call" | custom-call | flops 8589934592 | bytes 29360128 | tf_op jit(solution)/shard_map/pallas_call | solution.py:732
  118.1 5.8 %collective-permute-done.24 = bf16[1216,256]{1,0:T(8,128)(2,1)S(1)} collective-permute-done((bf16[1216,256]{1,0:T(8,128)(2,1)S(1)}, bf16[1216,256]{1,0:T(8,128)(2,1)S(1)}, u32[]{:S(2)}, u32[]{:S(2)}) %collective-permute-start.24) | collective-permute-done | bytes 622624 | tf_op jit(solution)/shard_map/ppermute | solution.py:813
  131.5 3.4 %collective-permute-done.30 = bf16[608,256]{1,0:T(8,128)(2,1)S(1)} collective-permute-done((bf16[608,256]{1,0:T(8,128)(2,1)S(1)}, bf16[608,256]{1,0:T(8,128)(2,1)S(1)}, u32[]{:S(2)}, u32[]{:S(2)}) %collective-permute-start.30) | collective-permute-done | bytes 311328 | tf_op jit(solution)/shard_map/ppermute | solution.py:813
  135.0 2.7 %collective-permute-start.31 = (bf16[608,256]{1,0:T(8,128)(2,1)S(1)}, bf16[608,256]{1,0:T(8,128)(2,1)S(1)}, u32[]{:S(2)}, u32[]{:S(2)}) collective-permute-start(bf16[608,256]{1,0:T(8,128)(2,1)S(1)} %add_convert_fusion.3), channel_id=1, source_target_pairs={{0,16},{4,20},{8,24},{12,28},{16,0},{20,4},{24,8},{28,12},{1,17},{... | collective-permute-start | bytes 933896 | tf_op jit(solution)/shard_map/ppermute | solution.py:813
  137.7 5.5 %collective-permute-done.27 = bf16[1072,256]{1,0:T(8,128)(2,1)S(1)} collective-permute-done((bf16[1072,256]{1,0:T(8,128)(2,1)S(1)}, bf16[1072,256]{1,0:T(8,128)(2,1)S(1)}, u32[]{:S(2)}, u32[]{:S(2)}) %collective-permute-start.27) | collective-permute-done | bytes 548896 | tf_op jit(solution)/shard_map/ppermute | solution.py:813
  143.2 12.6 %collective-permute-done.28 = bf16[1072,256]{1,0:T(8,128)(2,1)S(1)} collective-permute-done((bf16[1072,256]{1,0:T(8,128)(2,1)S(1)}, bf16[1072,256]{1,0:T(8,128)(2,1)S(1)}, u32[]{:S(2)}, u32[]{:S(2)}) %collective-permute-start.28) | collective-permute-done | bytes 548896 | tf_op jit(solution)/shard_map/ppermute | solution.py:813
  157.3 6.7 %collective-permute-done.32 = bf16[536,256]{1,0:T(8,128)(2,1)S(1)} collective-permute-done((bf16[536,256]{1,0:T(8,128)(2,1)S(1)}, bf16[536,256]{1,0:T(8,128)(2,1)S(1)}, u32[]{:S(2)}, u32[]{:S(2)}) %collective-permute-start.32) | collective-permute-done | bytes 274464 | tf_op jit(solution)/shard_map/ppermute | solution.py:813
  165.2 2.6 %collective-permute-start.33 = (bf16[536,256]{1,0:T(8,128)(2,1)S(1)}, bf16[536,256]{1,0:T(8,128)(2,1)S(1)}, u32[]{:S(2)}, u32[]{:S(2)}) collective-permute-start(bf16[536,256]{1,0:T(8,128)(2,1)S(1)} %add_convert_fusion.5), channel_id=1, source_target_pairs={{0,16},{4,20},{8,24},{12,28},{16,0},{20,4},{24,8},{28,12},{1,17},{... | collective-permute-start | bytes 823304 | tf_op jit(solution)/shard_map/ppermute | solution.py:813
  167.8 8.4 %collective-permute-done.33 = bf16[536,256]{1,0:T(8,128)(2,1)S(1)} collective-permute-done((bf16[536,256]{1,0:T(8,128)(2,1)S(1)}, bf16[536,256]{1,0:T(8,128)(2,1)S(1)}, u32[]{:S(2)}, u32[]{:S(2)}) %collective-permute-start.33) | collective-permute-done | bytes 274464 | tf_op jit(solution)/shard_map/ppermute | solution.py:813
  178.0 2.7 %collective-permute-start.35 = (bf16[536,256]{1,0:T(8,128)(2,1)S(1)}, bf16[536,256]{1,0:T(8,128)(2,1)S(1)}, u32[]{:S(2)}, u32[]{:S(2)}) collective-permute-start(bf16[536,256]{1,0:T(8,128)(2,1)S(1)} %add_convert_fusion.4), channel_id=1, source_target_pairs={{0,8},{4,12},{8,0},{12,4},{16,24},{20,28},{24,16},{28,20},{1,9},{5... | collective-permute-start | bytes 823304 | tf_op jit(solution)/shard_map/ppermute | solution.py:813
  182.1 3.3 %shard_map.235 = (f32[2,4,256,256]{3,2,1,0:T(8,128)}, f32[2,4,256,256]{3,2,1,0:T(8,128)}, f32[2,4,256]{2,1,0:T(4,128)}, f32[2,4,256]{2,1,0:T(4,128)}) custom-call(s32[3]{0:T(128)} %pad_add_fusion.place_ref.refs_0_, bf16[1216,256]{1,0:T(8,128)(2,1)} %copy-done, bf16[1216,256]{1,0:T(8,128)(2,1)} %copy-done.5), custom_call_target="tpu_custom_call" | custom-call | bytes 3145728 | tf_op jit(solution)/shard_map/pallas_call | solution.py:796
  186.1 1.7 collective-permute-done.35
  188.2 1.8 collective-permute-done.37.refs_2_
  191.2 3.2 %shard_map.236 = (f32[2,4,256,256]{3,2,1,0:T(8,128)}, f32[2,4,256,256]{3,2,1,0:T(8,128)}, f32[2,4,256]{2,1,0:T(4,128)}, f32[2,4,256]{2,1,0:T(4,128)}) custom-call(s32[3]{0:T(128)} %pad_add_fusion.place_ref.refs_0_, bf16[1072,256]{1,0:T(8,128)(2,1)} %copy-done.1, bf16[1072,256]{1,0:T(8,128)(2,1)} %copy-done.6, ...), custom_call_target="tpu_custom_call", output_to_operand_aliasing={{0}: (3, {}), {1}: (4, {})} | custom-call | bytes 3145728 | tf_op jit(solution)/shard_map/pallas_call | solution.py:796
  (182 shorter events, 42.2 us)
Async XLA Ops:
  2.7 15.3 %collective-permute-start = (bf16[2,528,256]{2,1,0:T(8,128)(2,1)S(1)}, bf16[2,528,256]{2,1,0:T(8,128)(2,1)S(1)}, u32[]{:S(2)}, u32[]{:S(2)}) collective-permute-start(bf16[2,528,256]{2,1,0:T(8,128)(2,1)S(1)} %pad_maximum_fusion.2.refs_3_.refs_8_), channel_id=1, source_target_pairs={{0,1},{1,0},{2,3},{3,2},{4,5},{5,4},{6,7},{7,6},{8,9},{9,8},{10,11... | collective-permute-start | bytes 1622024 | tf_op jit(solution)/shard_map/ppermute | solution.py:813
  5.7 13.8 %collective-permute-start.1 = (bf16[2,528,256]{2,1,0:T(8,128)(2,1)S(1)}, bf16[2,528,256]{2,1,0:T(8,128)(2,1)}, u32[]{:S(2)}, u32[]{:S(2)}) collective-permute-start(bf16[2,528,256]{2,1,0:T(8,128)(2,1)S(1)} %pad_maximum_fusion.2.refs_3_.refs_8_), channel_id=1, source_target_pairs={{0,2},{1,3},{2,0},{3,1},{4,6},{5,7},{6,4},{7,5},{8,10},{9,11},{10,... | collective-permute-start | bytes 1622024 | tf_op jit(solution)/shard_map/ppermute | solution.py:813
  20.1 20.6 %collective-permute-start.8 = (bf16[2,528,256]{2,1,0:T(8,128)(2,1)S(1)}, bf16[2,528,256]{2,1,0:T(8,128)(2,1)S(1)}, u32[]{:S(2)}, u32[]{:S(2)}) collective-permute-start(bf16[2,528,256]{2,1,0:T(8,128)(2,1)S(1)} %pad_maximum_fusion.4.refs_10_), channel_id=1, source_target_pairs={{0,1},{1,0},{2,3},{3,2},{4,5},{5,4},{6,7},{7,6},{8,9},{9,8},{10,11... | collective-permute-start | bytes 1622024 | tf_op jit(solution)/shard_map/ppermute | solution.py:813
  20.4 22.1 %collective-permute-start.10 = (bf16[2,528,256]{2,1,0:T(8,128)(2,1)S(1)}, bf16[2,528,256]{2,1,0:T(8,128)(2,1)S(1)}, u32[]{:S(2)}, u32[]{:S(2)}) collective-permute-start(bf16[2,528,256]{2,1,0:T(8,128)(2,1)S(1)} %pad_maximum_fusion.4.refs_10_), channel_id=1, source_target_pairs={{0,2},{1,3},{2,0},{3,1},{4,6},{5,7},{6,4},{7,5},{8,10},{9,11},{10,... | collective-permute-start | bytes 1622024 | tf_op jit(solution)/shard_map/ppermute | solution.py:813
  23.1 17.0 %collective-permute-start.4 = (bf16[1,528,256]{2,1,0:T(8,128)(2,1)S(1)}, bf16[1,528,256]{2,1,0:T(8,128)(2,1)S(1)}, u32[]{:S(2)}, u32[]{:S(2)}) collective-permute-start(bf16[1,528,256]{2,1,0:T(8,128)(2,1)S(1)} %slice.96), channel_id=1, source_target_pairs={{0,2},{1,3},{2,0},{3,1},{4,6},{5,7},{6,4},{7,5},{8,10},{9,11},{10,... | collective-permute-start | bytes 811016 | tf_op jit(solution)/shard_map/ppermute | solution.py:813
  23.5 16.6 %collective-permute-start.5 = (bf16[1,528,256]{2,1,0:T(8,128)(2,1)S(1)}, bf16[1,528,256]{2,1,0:T(8,128)(2,1)S(1)}, u32[]{:S(2)}, u32[]{:S(2)}) collective-permute-start(bf16[1,528,256]{2,1,0:T(8,128)(2,1)S(1)} %slice.97), channel_id=1, source_target_pairs={{0,1},{1,0},{2,3},{3,2},{4,5},{5,4},{6,7},{7,6},{8,9},{9,8},{10,11... | collective-permute-start | bytes 811016 | tf_op jit(solution)/shard_map/ppermute | solution.py:813
  40.7 12.4 %collective-permute-start.12 = (bf16[1,528,256]{2,1,0:T(8,128)(2,1)S(1)}, bf16[1,528,256]{2,1,0:T(8,128)(2,1)S(1)}, u32[]{:S(2)}, u32[]{:S(2)}) collective-permute-start(bf16[1,528,256]{2,1,0:T(8,128)(2,1)S(1)} %slice.126), channel_id=1, source_target_pairs={{0,2},{1,3},{2,0},{3,1},{4,6},{5,7},{6,4},{7,5},{8,10},{9,11},{10,... | collective-permute-start | bytes 811016 | tf_op jit(solution)/shard_map/ppermute | solution.py:813
  42.5 10.7 %collective-permute-start.13 = (bf16[1,528,256]{2,1,0:T(8,128)(2,1)S(1)}, bf16[1,528,256]{2,1,0:T(8,128)(2,1)S(1)}, u32[]{:S(2)}, u32[]{:S(2)}) collective-permute-start(bf16[1,528,256]{2,1,0:T(8,128)(2,1)S(1)} %slice.127), channel_id=1, source_target_pairs={{0,1},{1,0},{2,3},{3,2},{4,5},{5,4},{6,7},{7,6},{8,9},{9,8},{10,11... | collective-permute-start | bytes 811016 | tf_op jit(solution)/shard_map/ppermute | solution.py:813
  44.1 9.7 %collective-permute-start.11 = (bf16[2,528,256]{2,1,0:T(8,128)(2,1)S(1)}, bf16[2,528,256]{2,1,0:T(8,128)(2,1)S(1)}, u32[]{:S(2)}, u32[]{:S(2)}) collective-permute-start(bf16[2,528,256]{2,1,0:T(8,128)(2,1)S(1)} %collective-permute-done.10.refs_14_), channel_id=1, source_target_pairs={{0,4},{4,0},{8,12},{12,8},{16,20},{20,16},{24,28},{28,24},{1,5},{5... | collective-permute-start | bytes 1622024 | tf_op jit(solution)/shard_map/ppermute | solution.py:813
  44.1 9.7 %collective-permute-start.9 = (bf16[2,528,256]{2,1,0:T(8,128)(2,1)S(1)}, bf16[2,528,256]{2,1,0:T(8,128)(2,1)S(1)}, u32[]{:S(2)}, u32[]{:S(2)}) collective-permute-start(bf16[2,528,256]{2,1,0:T(8,128)(2,1)S(1)} %collective-permute-done.8.refs_12_), channel_id=1, source_target_pairs={{0,4},{4,0},{8,12},{12,8},{16,20},{20,16},{24,28},{28,24},{1,5},{5... | collective-permute-start | bytes 1622024 | tf_op jit(solution)/shard_map/ppermute | solution.py:813
  93.9 23.7 %collective-permute-start.22 = (bf16[1216,256]{1,0:T(8,128)(2,1)}, bf16[1216,256]{1,0:T(8,128)(2,1)S(1)}, u32[]{:S(2)}, u32[]{:S(2)}) collective-permute-start(bf16[1216,256]{1,0:T(8,128)(2,1)} %get-tuple-element.145), channel_id=1, source_target_pairs={{0,4},{4,0},{8,12},{12,8},{16,20},{20,16},{24,28},{28,24},{1,5},{5... | collective-permute-start | bytes 1867784 | tf_op jit(solution)/shard_map/ppermute | solution.py:813
  94.1 24.0 %collective-permute-start.23 = (bf16[1216,256]{1,0:T(8,128)(2,1)S(1)}, bf16[1216,256]{1,0:T(8,128)(2,1)S(1)}, u32[]{:S(2)}, u32[]{:S(2)}) collective-permute-start(bf16[1216,256]{1,0:T(8,128)(2,1)S(1)} %get-tuple-element.146), channel_id=1, source_target_pairs={{0,1},{1,0},{2,3},{3,2},{4,5},{5,4},{6,7},{7,6},{8,9},{9,8},{10,11... | collective-permute-start | bytes 1867784 | tf_op jit(solution)/shard_map/ppermute | solution.py:813
  94.6 29.4 %collective-permute-start.24 = (bf16[1216,256]{1,0:T(8,128)(2,1)S(1)}, bf16[1216,256]{1,0:T(8,128)(2,1)S(1)}, u32[]{:S(2)}, u32[]{:S(2)}) collective-permute-start(bf16[1216,256]{1,0:T(8,128)(2,1)S(1)} %get-tuple-element.147), channel_id=1, source_target_pairs={{0,2},{1,3},{2,0},{3,1},{4,6},{5,7},{6,4},{7,5},{8,10},{9,11},{10,... | collective-permute-start | bytes 1867784 | tf_op jit(solution)/shard_map/ppermute | solution.py:813
  95.0 29.0 %collective-permute-start.25 = (bf16[1216,256]{1,0:T(8,128)(2,1)S(1)}, bf16[1216,256]{1,0:T(8,128)(2,1)S(1)}, u32[]{:S(2)}, u32[]{:S(2)}) collective-permute-start(bf16[1216,256]{1,0:T(8,128)(2,1)S(1)} %get-tuple-element.148), channel_id=1, source_target_pairs={{0,3},{1,2},{2,1},{3,0},{4,7},{5,6},{6,5},{7,4},{8,11},{9,10},{10,... | collective-permute-start | bytes 1867784 | tf_op jit(solution)/shard_map/ppermute | solution.py:813
  117.5 8.1 %collective-permute-start.19 = (bf16[1072,256]{1,0:T(8,128)(2,1)}, bf16[1072,256]{1,0:T(8,128)(2,1)S(1)}, u32[]{:S(2)}, u32[]{:S(2)}) collective-permute-start(bf16[1072,256]{1,0:T(8,128)(2,1)} %get-tuple-element.141), channel_id=1, source_target_pairs={{0,4},{4,0},{8,12},{12,8},{16,20},{20,16},{24,28},{28,24},{1,5},{5... | collective-permute-start | bytes 1646600 | tf_op jit(solution)/shard_map/ppermute | solution.py:813
  126.3 8.6 %collective-permute-start.30 = (bf16[608,256]{1,0:T(8,128)(2,1)S(1)}, bf16[608,256]{1,0:T(8,128)(2,1)S(1)}, u32[]{:S(2)}, u32[]{:S(2)}) collective-permute-start(bf16[608,256]{1,0:T(8,128)(2,1)S(1)} %get-tuple-element.232), channel_id=1, source_target_pairs={{0,8},{4,12},{8,0},{12,4},{16,24},{20,28},{24,16},{28,20},{1,9},{5... | collective-permute-start | bytes 933896 | tf_op jit(solution)/shard_map/ppermute | solution.py:813
  128.0 9.7 %collective-permute-start.26 = (bf16[1072,256]{1,0:T(8,128)(2,1)S(1)}, bf16[1072,256]{1,0:T(8,128)(2,1)S(1)}, u32[]{:S(2)}, u32[]{:S(2)}) collective-permute-start(bf16[1072,256]{1,0:T(8,128)(2,1)S(1)} %copy-done.20), channel_id=1, source_target_pairs={{0,4},{4,0},{8,12},{12,8},{16,20},{20,16},{24,28},{28,24},{1,5},{5... | collective-permute-start | bytes 1646600 | tf_op jit(solution)/shard_map/ppermute | solution.py:813
  128.0 15.2 %collective-permute-start.27 = (bf16[1072,256]{1,0:T(8,128)(2,1)S(1)}, bf16[1072,256]{1,0:T(8,128)(2,1)S(1)}, u32[]{:S(2)}, u32[]{:S(2)}) collective-permute-start(bf16[1072,256]{1,0:T(8,128)(2,1)S(1)} %get-tuple-element.161), channel_id=1, source_target_pairs={{0,1},{1,0},{2,3},{3,2},{4,5},{5,4},{6,7},{7,6},{8,9},{9,8},{10,11... | collective-permute-start | bytes 1646600 | tf_op jit(solution)/shard_map/ppermute | solution.py:813
  129.5 26.3 %collective-permute-start.28 = (bf16[1072,256]{1,0:T(8,128)(2,1)S(1)}, bf16[1072,256]{1,0:T(8,128)(2,1)S(1)}, u32[]{:S(2)}, u32[]{:S(2)}) collective-permute-start(bf16[1072,256]{1,0:T(8,128)(2,1)S(1)} %get-tuple-element.162), channel_id=1, source_target_pairs={{0,2},{1,3},{2,0},{3,1},{4,6},{5,7},{6,4},{7,5},{8,10},{9,11},{10,... | collective-permute-start | bytes 1646600 | tf_op jit(solution)/shard_map/ppermute | solution.py:813
  130.0 25.8 %collective-permute-start.29 = (bf16[1072,256]{1,0:T(8,128)(2,1)S(1)}, bf16[1072,256]{1,0:T(8,128)(2,1)S(1)}, u32[]{:S(2)}, u32[]{:S(2)}) collective-permute-start(bf16[1072,256]{1,0:T(8,128)(2,1)S(1)} %get-tuple-element.163), channel_id=1, source_target_pairs={{0,3},{1,2},{2,1},{3,0},{4,7},{5,6},{6,5},{7,4},{8,11},{9,10},{10,... | collective-permute-start | bytes 1646600 | tf_op jit(solution)/shard_map/ppermute | solution.py:813
  135.0 20.8 %collective-permute-start.31 = (bf16[608,256]{1,0:T(8,128)(2,1)S(1)}, bf16[608,256]{1,0:T(8,128)(2,1)S(1)}, u32[]{:S(2)}, u32[]{:S(2)}) collective-permute-start(bf16[608,256]{1,0:T(8,128)(2,1)S(1)} %add_convert_fusion.3), channel_id=1, source_target_pairs={{0,16},{4,20},{8,24},{12,28},{16,0},{20,4},{24,8},{28,12},{1,17},{... | collective-permute-start | bytes 933896 | tf_op jit(solution)/shard_map/ppermute | solution.py:813
  164.2 13.5 %collective-permute-start.34 = (bf16[608,256]{1,0:T(8,128)(2,1)S(1)}, bf16[608,256]{1,0:T(8,128)(2,1)S(1)}, u32[]{:S(2)}, u32[]{:S(2)}) collective-permute-start(bf16[608,256]{1,0:T(8,128)(2,1)S(1)} %add_convert_fusion.2), channel_id=1, source_target_pairs={{0,8},{4,12},{8,0},{12,4},{16,24},{20,28},{24,16},{28,20},{1,9},{5... | collective-permute-start | bytes 933896 | tf_op jit(solution)/shard_map/ppermute | solution.py:813
  165.2 11.0 %collective-permute-start.33 = (bf16[536,256]{1,0:T(8,128)(2,1)S(1)}, bf16[536,256]{1,0:T(8,128)(2,1)S(1)}, u32[]{:S(2)}, u32[]{:S(2)}) collective-permute-start(bf16[536,256]{1,0:T(8,128)(2,1)S(1)} %add_convert_fusion.5), channel_id=1, source_target_pairs={{0,16},{4,20},{8,24},{12,28},{16,0},{20,4},{24,8},{28,12},{1,17},{... | collective-permute-start | bytes 823304 | tf_op jit(solution)/shard_map/ppermute | solution.py:813
  178.0 9.8 %collective-permute-start.35 = (bf16[536,256]{1,0:T(8,128)(2,1)S(1)}, bf16[536,256]{1,0:T(8,128)(2,1)S(1)}, u32[]{:S(2)}, u32[]{:S(2)}) collective-permute-start(bf16[536,256]{1,0:T(8,128)(2,1)S(1)} %add_convert_fusion.4), channel_id=1, source_target_pairs={{0,8},{4,12},{8,0},{12,4},{16,24},{20,28},{24,16},{28,20},{1,9},{5... | collective-permute-start | bytes 823304 | tf_op jit(solution)/shard_map/ppermute | solution.py:813
  (43 other events, 213.5 us)

commit v5 on v4

--- a/solution.py
+++ b/solution.py
@@ -61,8 +61,8 @@
 SCALARS = pl.BlockSpec(memory_space=pltpu.SMEM)
 
 
-def kernel_params():
-    return pltpu.CompilerParams(vmem_limit_bytes=58 * 2**20)
+def kernel_params(mebibytes):
+    return pltpu.CompilerParams(vmem_limit_bytes=mebibytes * 2**20)
 
 
 def whole_spec(shape):
@@ -173,7 +173,7 @@
         out_shape=outs,
         in_specs=[SCALARS] + [NEAR] * 6,
         out_specs=[NEAR] * len(outs),
-        compiler_params=kernel_params(),
+        compiler_params=kernel_params(58),
         cost_estimate=pl.CostEstimate(flops=2 * height * lengths.size * 64, bytes_accessed=2**21, transcendentals=2**16),
     )(
         place,
@@ -258,8 +258,8 @@
         share[t] = mm(type_across[...], low[t])
 
 
-def backward_step(weights, value_ref, hiddens, slopes, outs, pair, experts, type_ref, type_across, low, stream_ref, across, share, table, scratch, kept_gates=None, results=None, dots=None):
-    before_grads, result_grads, products = scratch
+def backward_step(weights, value_ref, hiddens, slopes, outs, pair, experts, type_ref, type_across, low, stream_ref, across, share, table, scratch, kept_gates=None, results=None, dots=None, gate_lanes=None):
+    before_grads, result_grads = scratch
     kinds, height, width = low.shape
     count = len(weights)
     first = joined([w[0:width] for w in weights], 1)
@@ -282,19 +282,16 @@
                 product = functools.reduce(
                     jnp.add, [product[:, lane : lane + LANES] for lane in range(0, width, LANES)]
                 )
-                if dots is None:
-                    at = (i * kinds + t) * LANES
-                    products[rows, at : at + LANES] = product
-                else:
-                    found = jnp.sum(product.astype(f32), axis=1, keepdims=True)
-                    lanes = lax.broadcasted_iota(jnp.int32, (1, LANES), 1)
-                    dots[rows] = jnp.where(lanes == t * experts + pair * count + i, found, dots[rows])
+                found = jnp.sum(product.astype(f32), axis=1, keepdims=True)
+                lanes = lax.broadcasted_iota(jnp.int32, (1, LANES), 1)
+                place = pair * count + i
+                chosen = lanes % experts == place if kinds == 1 else lanes == t * experts + place
+                dots[rows] = jnp.where(chosen, found, dots[rows])
             before = slope * hidden_grad
             before_grads[i, rows] = before
             result_grads[i, rows] = result_grad
             befores.append(before)
         stream_ref[rows] += mm_nt(joined(befores, 1), first)
-    sums = None if dots is not None else mm(type_across[...], products[...])
     lanes = lax.broadcasted_iota(jnp.int32, (type_ref.shape[1], LANES), 1)
     for i, w in enumerate(weights):
         _, bias_out = bias_rows(w, width)
@@ -307,16 +304,20 @@
             at = (i * kinds + t) * LANES
             gate = value_ref[:, at : at + LANES].astype(f32)
             out_bias += jnp.sum(twice(gate) * share[t], axis=0, keepdims=True)
-            found = 0.0 if sums is None else jnp.sum(sums[:, at : at + LANES], axis=1, keepdims=True)
             bias_part = jnp.sum(share[t] * bias_out, axis=1, keepdims=True)
             if kinds == 1:
-                some = gate > 0.0
-                found = jnp.where(some, 0.5 * found / jnp.where(some, gate, 1.0), 0.0)
-                table[...] = jnp.where(lanes % experts == place, found + 0.5 * bias_part, table[...])
+                table[...] = jnp.where(lanes % experts == place, 0.5 * bias_part, table[...])
+                gate_lanes[...] = jnp.where(lanes % experts == place, gate, gate_lanes[...])
             else:
-                table[...] = jnp.where(lanes == t * experts + place, found + bias_part, table[...])
+                table[...] = jnp.where(lanes == t * experts + place, bias_part, table[...])
         tail = jnp.concatenate([first_grad[width : width + 1], out_bias, jnp.zeros((EXTRA - 2, width), f32)])
         outs[i][2 * width : 2 * width + EXTRA] = tail.astype(bf16)
+
+
+def by_type(type_across, dots):
+    high = dots[...].astype(bf16)
+    rest = (dots[...] - high.astype(f32)).astype(bf16)
+    return mm(type_across[...], high) + mm(type_across[...], rest)
 
 
 def through_gates(table, gate_slope_ref, experts, tasks):
@@ -441,7 +442,7 @@
             pltpu.SemaphoreType.DMA((2, each)),
         ],
         input_output_aliases=aliases,
-        compiler_params=kernel_params(),
+        compiler_params=kernel_params(58),
         cost_estimate=pl.CostEstimate(
             flops=4 * number * height * width * width,
             bytes_accessed=number * (4 * width * width + 4 * height * width) + 8 * height * width,
@@ -458,9 +459,10 @@
     tower_in_ref, tower_bias_ref, tower_out_ref = take(3)
     weight_refs = take(pieces)
     pred_ref, stream_ref = take(2)
-    out_refs = take(1 + groups * (halves - 1))
+    out_refs = take(1 + (groups - 1) * (halves - 1))
+    left_refs = take(7)
     x_low, weights, hidden_all, slope_all, result_all, gates_all, total, biases, low, across, share, table = take(12)
-    before_grads, result_grads, dots, cotangents, ready, ends, in_grad, bias_grad, out_grad, load_sem, store_sem, end_sem = take(12)
+    before_grads, result_grads, dots, cotangents, ready, ends, in_grad, bias_grad, out_grad, load_sem, store_sem, end_sem, left_sem = take(13)
     height, width = x_ref.shape
     pairs = value_ref.shape[0]
     experts = pairs * halves
@@ -505,6 +507,13 @@
 
     lax.fori_loop(0, pairs, forward_pair, 0)
     forward_end(type_ref, total, biases)
+
+    def left(at, source):
+        return pltpu.make_async_copy(source, left_refs[at], left_sem.at[at])
+
+    own = [kept.at[0:held] for kept in (hidden_all, slope_all, result_all)]
+    for at, source in enumerate(own):
+        left(at, source).start()
 
     cotangents[...] = jnp.concatenate(
         [pred_grad_ref[...], jnp.zeros((cotangents.shape[1] - tasks, height), f32)]
@@ -545,12 +554,15 @@
     for half in range(halves):
         ends[half, begin - EXTRA : begin] = vectors
 
+    left(3, low).start()
     backward_start(x_low, across_types_ref, low, across, share)
+    left(4, across).start()
+    left(5, share).start()
     table[...] = jnp.zeros_like(table)
     dots[...] = jnp.zeros_like(dots)
 
     def stores(pair):
-        return store_copies(ready.at[pair], pair, held, out_refs, store_sem.at[pair])
+        return store_copies(ready.at[pair], pair - held, held, out_refs, store_sem.at[pair])
 
     def backward_pair(pair, carry):
         backward_step(
@@ -568,7 +580,7 @@
             across,
             share,
             table,
-            (before_grads, result_grads, None),
+            (before_grads, result_grads),
             gates_all.at[pair],
             [result_all.at[pair, i] for i in range(halves)],
             dots,
@@ -576,21 +588,22 @@
         for_each(stores(pair), start)
         return carry
 
-    lax.fori_loop(0, pairs, backward_pair, 0)
-    high = dots[...].astype(bf16)
-    rest = (dots[...] - high.astype(f32)).astype(bf16)
-    table[...] += mm(across_types_ref[...], high) + mm(across_types_ref[...], rest)
+    lax.fori_loop(held, pairs, backward_pair, 0)
+    table[...] += by_type(across_types_ref, dots)
     small = through_gates(table, gate_slope_ref, experts, tasks)
     for half in range(halves):
         ends[half, 0 : small.shape[0]] = small
+    left(6, ends).start()
     for_each(end_copies(ends, out_refs, end_sem), start)
 
     def drain(pair, carry):
         for_each(stores(pair), wait)
         return carry
 
-    lax.fori_loop(0, pairs, drain, 0)
+    lax.fori_loop(held, pairs, drain, 0)
     for_each(end_copies(ends, out_refs, end_sem), wait)
+    for at, source in enumerate([*own, low, across, share, ends]):
+        left(at, source).wait()
 
 
 def middle_call(place, x, types, across_types, values, gate_slopes, tower, pieces, places, groups, halves, held):
@@ -604,8 +617,13 @@
     near = len(outs)
     end_rows = type_count // 2 + EXTRA + tower_in.size // width // halves
     rows = held * stride + end_rows
-    outs.append(jax.ShapeDtypeStruct((groups, rows, width), bf16))
-    outs += [jax.ShapeDtypeStruct((rows, width), bf16)] * (groups * (halves - 1))
+    outs.append(jax.ShapeDtypeStruct((groups - 1, rows, width), bf16))
+    outs += [jax.ShapeDtypeStruct((rows, width), bf16)] * ((groups - 1) * (halves - 1))
+    outs += [jax.ShapeDtypeStruct((held, halves, height, width), bf16)] * 3
+    outs.append(jax.ShapeDtypeStruct((tasks, height, width), bf16))
+    outs.append(jax.ShapeDtypeStruct((width + EXTRA, height), bf16))
+    outs.append(jax.ShapeDtypeStruct((tasks, type_count, width), f32))
+    outs.append(jax.ShapeDtypeStruct((halves, end_rows, width), bf16))
     layer_at = gate_slopes.shape[1] // type_count - 1
     slope_spec = pl.BlockSpec((gate_slopes.shape[0], type_count, LANES), lambda i: (0, layer_at, 0))
     kept = pltpu.VMEM((pairs, halves, height, width), bf16)
@@ -643,8 +661,9 @@
             pltpu.SemaphoreType.DMA((pairs, halves)),
             pltpu.SemaphoreType.DMA((pairs, halves)),
             pltpu.SemaphoreType.DMA((halves, groups)),
+            pltpu.SemaphoreType.DMA((7,)),
         ],
-        compiler_params=kernel_params(),
+        compiler_params=kernel_params(58),
         cost_estimate=pl.CostEstimate(
             flops=14 * experts * height * width * width,
             bytes_accessed=experts * 8 * width * width + 16 * height * width,
@@ -657,22 +676,93 @@
     refs = list(refs)
     take = lambda count: [refs.pop(0) for _ in range(count)]
     x_ref, type_ref, across_types_ref, stream_ref, gate_slope_ref, value_ref, hidden_ref, slope_ref = take(8)
+    last_value_ref, last_low_ref, last_across_ref, last_share_ref, last_end_ref = take(5)
+    last_refs, last_weight_refs = take(3), take(each)
     weight_refs = take(pieces)
     stream_out_ref = take(1)[0]
-    out_refs = take(1 + len(places) // each // held * (each - 1))
-    x_low, across, low, share, table, before_grads, result_grads, products, buffer, ready, ends = take(11)
-    sems, store_sem, end_sem = take(3)
+    groups = len(places) // each // held
+    out_refs = take(1 + groups * (each - 1))
+    last_out_refs = take(each)
+    x_low, across, low, share, table, before_grads, result_grads, gate_lanes, buffer, ready, ends = take(11)
+    x_wide, gate_slopes, last_table, dots, kept, last_weights, last_ready = take(7)
+    sems, store_sem, end_sem, last_sem, last_store_sem, late_sem = take(6)
     step = pl.program_id(0)
     slot = lax.rem(step, 2)
     experts = len(places)
+    types = type_ref.shape[1]
+    stride = buffer.shape[2]
+    scratch = (before_grads, result_grads)
     weights = fetch_weights([(weight_refs[piece], at) for piece, at in places], buffer, sems, each)
+
+    late = [
+        (None, pltpu.make_async_copy(source, target, late_sem.at[at]))
+        for at, (source, target) in enumerate(((x_ref, x_wide), (gate_slope_ref, gate_slopes)))
+    ]
+
+    def last_loads(unit):
+        copies = [
+            pltpu.make_async_copy(last_refs[which].at[unit], kept.at[which, unit], last_sem.at[unit, which])
+            for which in range(3)
+        ]
+        for half in range(each):
+            source, sem = last_weight_refs[half].at[unit], last_sem.at[unit, 3 + half]
+            copies.append(pltpu.make_async_copy(source, last_weights.at[unit, half], sem))
+        return [(None, copy) for copy in copies]
+
+    def last_stores():
+        copies = []
+        for half, ref in enumerate(last_out_refs):
+            for unit in range(held):
+                rows = pl.ds(unit * stride, stride)
+                copies.append(
+                    pltpu.make_async_copy(last_ready.at[unit, half], ref.at[rows], last_store_sem.at[half, unit])
+                )
+            rows = pl.ds(held * stride, last_end_ref.shape[1])
+            copies.append(pltpu.make_async_copy(last_end_ref.at[half], ref.at[rows], last_store_sem.at[half, held]))
+        return [(None, copy) for copy in copies]
 
     @pl.when(step == 0)
     def _():
-        x_low[...] = x_ref[...].astype(bf16)
-        low[0] = stream_ref[...].astype(bf16)
+        for unit in range(held):
+            for_each(last_loads(unit), start)
+        for_each(late, start)
         stream_out_ref[...] = stream_ref[...]
+        last_table[...] = jnp.zeros_like(last_table)
+        dots[...] = jnp.zeros_like(dots)
+
+        def last_pair(unit, carry):
+            for_each(last_loads(unit), wait)
+            backward_step(
+                [last_weights.at[unit, i] for i in range(each)],
+                last_value_ref.at[unit],
+                [kept.at[0, unit, i] for i in range(each)],
+                [kept.at[1, unit, i] for i in range(each)],
+                [last_ready.at[unit, i] for i in range(each)],
+                unit,
+                experts,
+                type_ref,
+                across_types_ref,
+                last_low_ref,
+                stream_out_ref,
+                last_across_ref,
+                last_share_ref,
+                last_table,
+                scratch,
+                None,
+                [kept.at[2, unit, i] for i in range(each)],
+                dots,
+            )
+            return carry
+
+        lax.fori_loop(0, held, last_pair, 0)
+        for_each(last_stores(), start)
+        last_table[...] += by_type(across_types_ref, dots)
+        dots[...] = jnp.zeros_like(dots)
+        for_each(late[:1], wait)
+        x_low[...] = x_wide[...].astype(bf16)
+        low[0] = stream_out_ref[...].astype(bf16)
         table[...] = jnp.zeros_like(table)
+        gate_lanes[...] = jnp.zeros_like(gate_lanes)
         backward_start(x_low, across_types_ref, low, across, share)
 
     def stores(pair):
@@ -698,36 +788,52 @@
         across,
         share,
         table,
-        (before_grads, result_grads, products),
+        scratch,
+        None,
+        None,
+        dots,
+        gate_lanes,
     )
 
     for_each(stores(step), start)
 
     @pl.when(step == pl.num_programs(0) - 1)
     def _():
-        small = through_gates(table, gate_slope_ref, experts, tasks)
+        for_each(late[1:], wait)
+        gate = gate_lanes[...]
+        found = 0.5 * by_type(across_types_ref, dots) / jnp.where(gate > 0.0, gate, 1.0)
+        table[...] += jnp.where(gate > 0.0, found, 0.0)
+        both = ((table, 0), (last_table, types))
+        small = [through_gates(part, gate_slopes.at[:, pl.ds(at, types)], experts, tasks) for part, at in both]
         for half in range(each):
-            ends[half] = small
+            ends[half] = jnp.concatenate(small)
         for_each(end_copies(ends, out_refs, end_sem), start)
         for_each(stores(step - 1), wait)
         for_each(stores(step), wait)
         for_each(end_copies(ends, out_refs, end_sem), wait)
-
-
-def backward_call(x, types, across_types, stream, gate_slopes, layer_at, values, stash, pieces, places, held, tasks):
+        for_each(last_stores(), wait)
+
+
+def backward_call(x, types, across_types, stream, gate_slopes, values, stash, pieces, places, held, tasks, last):
     height, width = x.shape
     pairs, type_count, lanes = values.shape
     each = lanes // LANES
     groups = pairs // held
     stride = 2 * width + EXTRA
+    last_values, last_weights, *last_kept, last_low, last_across, last_share, last_ends = last
     operands = [x, types, across_types, stream, gate_slopes, values, *stash]
-    specs = [whole_spec(a.shape) for a in operands[:4]]
-    specs.append(pl.BlockSpec((gate_slopes.shape[0], type_count, LANES), lambda i: (0, layer_at, 0)))
+    specs = [FAR, *[whole_spec(a.shape) for a in operands[1:4]], FAR]
     specs.append(pl.BlockSpec((1, type_count, lanes), lambda i: (i, 0, 0)))
     specs += [pl.BlockSpec((1, each, height, width), lambda i: (i, 0, 0, 0))] * 2
-    rows = held * stride + type_count // 2
+    near = [last_low, last_across, last_share, last_ends]
+    operands += [last_values, *near, *last_kept, *last_weights]
+    specs.append(pl.BlockSpec((held, *last_values.shape[1:]), lambda i: (0, 0, 0)))
+    specs += [whole_spec(a.shape) for a in near]
+    specs += [FAR] * (len(last_kept) + each)
+    rows = held * stride + type_count
     mine = jax.ShapeDtypeStruct((groups, rows, width), bf16)
     others = [jax.ShapeDtypeStruct((rows, width), bf16)] * (groups * (each - 1))
+    others += [jax.ShapeDtypeStruct((held * stride + last_ends.shape[1], width), bf16)] * each
     number = pairs * each
     return pl.pallas_call(
         functools.partial(backward_kernel, places, len(pieces), each, held, tasks),
@@ -743,17 +849,27 @@
             pltpu.VMEM((type_count, LANES), f32),
             pltpu.VMEM((each, height, width), bf16),
             pltpu.VMEM((each, height, width), bf16),
-            pltpu.VMEM((height, lanes), bf16),
+            pltpu.VMEM((type_count, LANES), f32),
             pltpu.VMEM((2, each, stride, width), bf16),
             pltpu.VMEM((2, each, stride, width), bf16),
-            pltpu.VMEM((each, type_count // 2, width), bf16),
+            pltpu.VMEM((each, type_count, width), bf16),
+            pltpu.VMEM((height, width), f32),
+            pltpu.VMEM(gate_slopes.shape, f32),
+            pltpu.VMEM((type_count, LANES), f32),
+            pltpu.VMEM((height, LANES), f32),
+            pltpu.VMEM((3, held, each, height, width), bf16),
+            pltpu.VMEM((held, each, stride, width), bf16),
+            pltpu.VMEM((held, each, stride, width), bf16),
             pltpu.SemaphoreType.DMA((2, each)),
             pltpu.SemaphoreType.DMA((2, each)),
             pltpu.SemaphoreType.DMA((each, groups)),
+            pltpu.SemaphoreType.DMA((held, 3 + each)),
+            pltpu.SemaphoreType.DMA((each, held + 1)),
+            pltpu.SemaphoreType.DMA((2,)),
         ],
-        compiler_params=kernel_params(),
+        compiler_params=kernel_params(58),
         cost_estimate=pl.CostEstimate(
-            flops=8 * number * height * width * width,
+            flops=10 * number * height * width * width,
             bytes_accessed=number * (8 * width * width + 4 * height * width) + 16 * height * width,
             transcendentals=0,
         ),
@@ -803,7 +919,7 @@
             pltpu.SemaphoreType.DMA((number, held, 2)),
         ],
         input_output_aliases={} if first else {1 + number: 0, 2 + number: 1},
-        compiler_params=kernel_params(),
+        compiler_params=kernel_params(12),
         cost_estimate=pl.CostEstimate(flops=0, bytes_accessed=number * held * 12 * rows * width, transcendentals=0),
     )(place, *sources, *([] if first else held_arrays))
 
@@ -912,8 +1028,6 @@
         got = near(own[layer_at][0], groups) if layer_at else after(asked, (types, own[0][1:], own[1:]))
         far = relay(got, groups, held)
         across = {ro: crossed(got[ro], halves) for ro in got}
-        if not last:
-            pass
         got = {0: own[layer_at][:1], **got}
         across[0] = own[layer_at][1:]
         if not last:
@@ -959,16 +1073,17 @@
     upper = (row_at & 2) > 0
 
     class Moving:
-        def __init__(self, layer_at, payload):
-            self.layer_at, self.mine = layer_at, payload[0]
-            self.others = payload[1:] or [payload[0][ro] for ro in range(groups)]
-            self.got = [flip(part, "rows", 1) for part in self.others[1:]]
-            self.total, self.sums, self.hops = None, None, -2
+        def __init__(self, layer_at, mine, others):
+            self.layer_at, self.mine, self.own = layer_at, mine, None
+            self.got = [flip(part, "rows", 1) for part in others]
+            self.sums, self.parts, self.total, self.hops = None, None, None, -2
 
         def ask(self, token):
             if self.hops == -1:
-                sums, own = after((self.sums, self.others[0]), token)
-                self.got = [flip(own, "rows", 1)] + [flip(sums[ro], "expert", ro) for ro in range(1, groups)]
+                sums, own = after((self.sums, self.own), token)
+                ros = range(1, groups) if self.parts is None else ()
+                self.got = [flip(sums[ro - 1], "expert", ro) for ro in ros]
+                self.got += [] if own is None else [flip(own[1], "rows", 1)]
                 return
             total = after(self.total, token)
             if self.hops == len(hops):
@@ -983,51 +1098,68 @@
                 self.got = [total, flip(total, "rows", 2 if hops[self.hops] == "join" else hops[self.hops])]
 
         def add(self):
-            if self.hops == len(hops):
-                return True
             if self.hops == -2:
-                self.sums = {ro: add_low(self.mine[ro], self.got[ro - 1]) for ro in range(1, groups)}
+                self.sums = [add_low(*pair) for pair in zip(self.mine, self.got)]
             elif self.hops == -1:
-                self.total = add_low(add_low(self.mine[0], self.got[0]), *self.got[1:])
+                got = self.got
+                if self.parts is None:
+                    self.parts = []
+                    while len(got) >= 1 << len(self.parts) and (1 << len(self.parts)) < groups:
+                        size = 1 << len(self.parts)
+                        level, got = got[:size], got[size:]
+                        while len(level) > 1:
+                            level = [add_low(*level[i : i + 2]) for i in range(0, len(level), 2)]
+                        self.parts += level
+                if self.own is None:
+                    return
+                self.total = functools.reduce(add_low, self.parts, add_low(self.own[0], got[0]))
             elif hops[self.hops] != "join":
                 self.total = add_low(*self.got)
             else:
                 here, there = self.got
                 self.total = jnp.concatenate([jnp.where(upper, there, here), jnp.where(upper, here, there)])
             self.hops += 1
-            return False
 
     def arrive(entries, others):
         got, others = lax.optimization_barrier(([entry.got for entry in entries], others))
         for entry, what in zip(entries, got):
             entry.got = what
-        ended = [entry for entry in entries if entry.add()]
-        return ([entry.sums if entry.total is None else entry.total for entry in entries], others), ended
-
-    moving = [Moving(layers - 1, payload)]
-    token, _ = arrive(moving, ())
+            entry.add()
+        there = [[x for x in (entry.total, entry.parts, entry.sums) if x is not None][0] for entry in entries]
+        return there, others
+
+    assert layers == 2
+    mine, left = payload[0], payload[-7:]
+    mine = [mine[ro] for ro in range(groups - 1)]
+    later = Moving(1, mine, payload[1:-7] or mine)
+    token = arrive([later], ())
     stream = after(stream, token)
-    for layer_at in reversed(range(layers - 1)):
-        for entry in moving:
-            entry.ask(token)
-        pieces, places = weights[layer_at]
-        stream, *payload = backward_call(
-            streams[layer_at],
-            types,
-            across_types,
-            stream,
-            gate_slopes,
-            layer_at,
-            values[layer_at],
-            stashes[layer_at],
-            pieces,
-            pair_order(places, range(held)),
-            held,
-            tasks,
-        )
-        token, _ = arrive(moving, stream)
-        moving.append(Moving(layer_at, payload))
-        token, _ = arrive(moving[-1:], token)
+    later.ask(token)
+    pieces, places = weights[0]
+    stream, mine, *others = backward_call(
+        streams[0],
+        types,
+        across_types,
+        stream,
+        gate_slopes,
+        values[0],
+        stashes[0],
+        pieces,
+        pair_order(places, range(held)),
+        held,
+        tasks,
+        (values[1], own[1], *left),
+    )
+    token = arrive([later], stream)
+    others, last_own = others[:-halves], others[-halves:]
+    mine = [mine[ro] for ro in range(groups)]
+    others = others or mine
+    earlier = Moving(0, mine[1:], others[1:])
+    earlier.own = (mine[0], others[0])
+    later.own = (last_own[0], last_own[-1])
+    later.ask(())
+    token = arrive([earlier, later], token)
+    moving = [later, earlier]
 
     whole = {}
     arrays, tower_sums = None, ()
@@ -1059,21 +1191,22 @@
                 sources = {(layer_at, half): array for half, array in enumerate(got)}
                 arrays = finish_call(place, sources, arrays, held, expert_in.shape)
 
-    if layers == 2 and len(hops) == 3:
-        later, earlier = moving
+    if len(hops) == 3:
         ask(earlier, later)
-        token, _ = arrive([later], ())
+        token = arrive([later], ())
         ask(later)
-        token, _ = arrive([earlier, later], ())
+        token = arrive([earlier, later], ())
         ask(earlier)
-        token, _ = arrive([earlier], ())
+        token = arrive([earlier], ())
         ask(earlier, later)
-        token, _ = arrive([earlier, later], ())
+        token = arrive([earlier, later], ())
     while moving:
         ask(*moving)
         if moving:
-            token, _ = arrive(moving, (arrays, tower_sums))
-    gate_grads = [whole[layer_at][0][held * stride :][: type_count // 2].astype(f32) for layer_at in range(layers)]
+            token = arrive(moving, (arrays, tower_sums))
+    ends = [whole[layer_at][0][held * stride : held * stride + type_count].astype(f32) for layer_at in range(layers)]
+    cut = type_count // 2
+    gate_grads = [ends[0][:cut], ends[1][:cut] + ends[0][cut:]]
     quantities = selectors * (bits + 1)
     small = jnp.stack(gate_grads)
     small = jnp.concatenate([small[..., :LANES], small[..., LANES:]], axis=1)[..., : tasks * quantities]

time: 195 us -> 194 us (level)
    pallas_call x1, Pallas kernels: 19.9 us -> 25.1 us  [backward_call(): pl.pallas_call(functools.partial(backward_kernel, places, len(pieces), ea...]
    pallas_call x1, Pallas kernels: 31.9 us -> 29.4 us  [middle_call(): pl.pallas_call(functools.partial(middle_kernel, places, len(pieces), grou...]
    pallas_call x2, Pallas kernels: 6.48 us -> 4.47 us  [finish_call(): pl.pallas_call(functools.partial(finish_kernel, names, held, rows, first)...]
    convert_element_type x8 -> x9, other arithmetic: 4.68 us -> 5.84 us  [add_low(): return level[0].astype(bf16)]
    unnamed x63 -> x57, local copies, waits for them, and re-layouts: 4.51 us -> 3.54 us
  transfers between devices with their start and end apart: 38 -> 38, of which waited for: 17 -> 19; matrix products, arithmetic and copies ran while one was open for 4% -> 4% of each run, Pallas kernels for 25% -> 27%
where the time goes in v5:
time: 194 us; the launch traced here: 193 us
  Pallas kernels  83.5 us (43%)
  waiting for transfers between devices  56.1 us (29%)
  starting transfers between devices  32.8 us (17%)
  other arithmetic  11.4 us (6%)
  local copies, waits for them, and re-layouts  7.81 us (4%)
    ppermute x38, waiting for transfers between devices, flip(): return lax.ppermute(array, axis, [(i, i ^ bits) for i in range(size)])  56.1 us
    ppermute x38, starting transfers between devices, flip(): return lax.ppermute(array, axis, [(i, i ^ bits) for i in range(size)])  32.8 us
    pallas_call x1, Pallas kernels, middle_call(): pl.pallas_call(functools.partial(middle_kernel, places, len(pieces), grou...  29.4 us
    pallas_call x1, Pallas kernels, backward_call(): pl.pallas_call(functools.partial(backward_kernel, places, len(pieces), ea...  25.1 us
    pallas_call x2, Pallas kernels, forward_call(): pl.pallas_call(functools.partial(forward_kernel, places, len(pieces), eac...  21.3 us
    convert_element_type x9, other arithmetic, add_low(): return level[0].astype(bf16)  5.84 us
    pallas_call x2, Pallas kernels, finish_call(): pl.pallas_call(functools.partial(finish_kernel, names, held, rows, first)...  4.47 us
  transfers between devices with their start and end apart: 38, of which 19 were waited for; matrix products, arithmetic and copies ran while one was open for 4% of the time, Pallas kernels for 27%

profile of v5, /device:TPU:0, one launch (start us, length us, event | category | flops | bytes accessed | tf_op | source)
XLA Modules:
  0.0 193.2 jit_solution(11290445765089287514)
XLA Ops:
  2.7 3.0 %collective-permute-start = (bf16[2,528,256]{2,1,0:T(8,128)(2,1)S(1)}, bf16[2,528,256]{2,1,0:T(8,128)(2,1)}, u32[]{:S(2)}, u32[]{:S(2)}) collective-permute-start(bf16[2,528,256]{2,1,0:T(8,128)(2,1)S(1)} %pad_maximum_fusion.2.refs_3_.refs_18_), channel_id=1, source_target_pairs={{0,1},{1,0},{2,3},{3,2},{4,5},{5,4},{6,7},{7,6},{8,9},{9,8},{10,11... | collective-permute-start | bytes 1622024 | tf_op jit(solution)/shard_map/ppermute | solution.py:929
  9.5 3.2 %shard_map.230 = (bf16[1024,32]{1,0:T(8,128)(2,1)}, bf16[32,1024]{1,0:T(8,128)(2,1)}, f32[20,64,128]{2,1,0:T(8,128)}, bf16[8,32,256]{2,1,0:T(8,128)(2,1)}, bf16[8,32,512]{2,1,0:T(8,128)(2,1)}) custom-call(s32[3]{0:T(128)} %pad_add_fusion.place_ref.refs_0_, s32[1,256]{1,0:T(1,128)} %bitcast.91, s32[1,256]{1,0:T(1,128)} %bitcast.92, f32[64,32]{1,0:T(8,128)} %copy.40.logit_ref, ...), custom_call_target="tpu_custom_call" | custom-call | flops 33554432 | bytes 2097152 | tf_op jit(solution)/shard_map/pallas_call | solution.py:171
  14.9 3.3 %collective-permute-done.refs_5_.refs_20_ = bf16[2,528,256]{2,1,0:T(8,128)(2,1)} collective-permute-done((bf16[2,528,256]{2,1,0:T(8,128)(2,1)S(1)}, bf16[2,528,256]{2,1,0:T(8,128)(2,1)}, u32[]{:S(2)}, u32[]{:S(2)}) %collective-permute-start) | collective-permute-done | bytes 540704 | tf_op jit(solution)/shard_map/ppermute | solution.py:929
  27.0 13.5 %shard_map.231 = (f32[1,1024,256]{2,1,0:T(8,128)}, bf16[8,2,1024,256]{3,2,1,0:T(8,128)(2,1)}, bf16[8,2,1024,256]{3,2,1,0:T(8,128)(2,1)}) custom-call(f32[1024,256]{1,0:T(8,128)} %refs_0_.5, bf16[1024,32]{1,0:T(8,128)(2,1)} %get-tuple-element.117.refs_1_.refs_2_, bf16[8,32,256]{2,1,0:T(8,128)(2,1)} %get-tuple-element.118.refs_2_.refs_5_, ...), custom_call_target="tpu_custom_call" | custom-call | flops 3221225472 | bytes 17825792 | tf_op jit(solution)/shard_map/pallas_call | solution.py:432
  45.3 7.8 %shard_map.232 = (f32[1,1024,256]{2,1,0:T(8,128)}, bf16[8,2,1024,256]{3,2,1,0:T(8,128)(2,1)}, bf16[8,2,1024,256]{3,2,1,0:T(8,128)(2,1)}) custom-call(f32[1024,256]{1,0:T(8,128)} %refs_0_.5, bf16[1024,32]{1,0:T(8,128)(2,1)} %get-tuple-element.117.refs_1_.refs_2_, ...), custom_call_target="tpu_custom_call", output_to_operand_aliasing={{1}: (4, {}), {2}: (5, {})} | custom-call | flops 1073741824 | bytes 7340032 | tf_op jit(solution)/shard_map/pallas_call | solution.py:432
  55.9 29.4 %shard_map.233 = (f32[2,1024]{1,0:T(2,128)}, f32[1024,256]{1,0:T(8,128)}, bf16[3,1216,256]{2,1,0:T(8,128)(2,1)}, bf16[1216,256]{1,0:T(8,128)(2,1)}, bf16[1216,25...) custom-call(s32[3]{0:T(128)} %pad_add_fusion.place_ref.refs_0_, ...), custom_call_target="tpu_custom_call" | custom-call | flops 15032385536 | bytes 12582912 | tf_op jit(solution)/shard_map/pallas_call | solution.py:633
  89.4 2.8 %fusion = (bf16[1216,256]{1,0:T(8,128)(2,1)}, bf16[1216,256]{1,0:T(8,128)(2,1)S(1)}, bf16[1216,256]{1,0:T(8,128)(2,1)S(1)}) fusion(bf16[1216,256]{1,0:T(8,128)(2,1)S(1)} %collective-permute-done.18, bf16[3,1216,256]{2,1,0:T(8,128)(2,1)} %get-tuple-element.138, bf16[1216,256]{1,0:T(8,128)(2,1)S(1)} %collective-permute-done.17, ...), kind=kLoop, calls=%fused_computation.1 | loop fusion | flops 3735552 | bytes 5603328 | tf_op jit(solution)/shard_map/convert_element_type | solution.py:936
  93.4 2.2 %collective-permute-start.25 = (bf16[1216,256]{1,0:T(8,128)(2,1)}, bf16[1216,256]{1,0:T(8,128)(2,1)S(1)}, u32[]{:S(2)}, u32[]{:S(2)}) collective-permute-start(bf16[1216,256]{1,0:T(8,128)(2,1)} %get-tuple-element.165), channel_id=1, source_target_pairs={{0,3},{1,2},{2,1},{3,0},{4,7},{5,6},{6,5},{7,4},{8,11},{9,10},{10,... | collective-permute-start | bytes 1867784 | tf_op jit(solution)/shard_map/ppermute | solution.py:929
  95.6 25.1 %shard_map.234 = (f32[1024,256]{1,0:T(8,128)}, bf16[4,1088,256]{2,1,0:T(8,128)(2,1)}, bf16[1088,256]{1,0:T(8,128)(2,1)}, bf16[1088,256]{1,0:T(8,128)(2,1)}, bf16...) custom-call(f32[1024,256]{1,0:T(8,128)} %refs_0_.5, ...), custom_call_target="tpu_custom_call" | custom-call | flops 10737418240 | bytes 29360128 | tf_op jit(solution)/shard_map/pallas_call | solution.py:838
  122.2 1.8 collective-permute-done.19
  126.0 1.9 fusion.3
  130.8 2.2 %collective-permute-start.28 = (bf16[1088,256]{1,0:T(8,128)(2,1)S(1)}, bf16[1088,256]{1,0:T(8,128)(2,1)S(1)}, u32[]{:S(2)}, u32[]{:S(2)}) collective-permute-start(bf16[1088,256]{1,0:T(8,128)(2,1)S(1)} %get-tuple-element.180), channel_id=1, source_target_pairs={{0,3},{1,2},{2,1},{3,0},{4,7},{5,6},{6,5},{7,4},{8,11},{9,10},{10,... | collective-permute-start | bytes 1671176 | tf_op jit(solution)/shard_map/ppermute | solution.py:929
  133.0 4.3 %collective-permute-done.30 = bf16[608,256]{1,0:T(8,128)(2,1)S(1)} collective-permute-done((bf16[608,256]{1,0:T(8,128)(2,1)S(1)}, bf16[608,256]{1,0:T(8,128)(2,1)S(1)}, u32[]{:S(2)}, u32[]{:S(2)}) %collective-permute-start.30) | collective-permute-done | bytes 311328 | tf_op jit(solution)/shard_map/ppermute | solution.py:929
  137.5 2.6 %collective-permute-start.31 = (bf16[608,256]{1,0:T(8,128)(2,1)S(1)}, bf16[608,256]{1,0:T(8,128)(2,1)S(1)}, u32[]{:S(2)}, u32[]{:S(2)}) collective-permute-start(bf16[608,256]{1,0:T(8,128)(2,1)S(1)} %add_convert_fusion.9), channel_id=1, source_target_pairs={{0,16},{4,20},{8,24},{12,28},{16,0},{20,4},{24,8},{28,12},{1,17},{... | collective-permute-start | bytes 933896 | tf_op jit(solution)/shard_map/ppermute | solution.py:929
  140.1 5.0 %collective-permute-done.26 = bf16[1088,256]{1,0:T(8,128)(2,1)S(1)} collective-permute-done((bf16[1088,256]{1,0:T(8,128)(2,1)S(1)}, bf16[1088,256]{1,0:T(8,128)(2,1)S(1)}, u32[]{:S(2)}, u32[]{:S(2)}) %collective-permute-start.26) | collective-permute-done | bytes 557088 | tf_op jit(solution)/shard_map/ppermute | solution.py:929
  145.1 11.3 %collective-permute-done.27 = bf16[1088,256]{1,0:T(8,128)(2,1)S(1)} collective-permute-done((bf16[1088,256]{1,0:T(8,128)(2,1)S(1)}, bf16[1088,256]{1,0:T(8,128)(2,1)S(1)}, u32[]{:S(2)}, u32[]{:S(2)}) %collective-permute-start.27) | collective-permute-done | bytes 557088 | tf_op jit(solution)/shard_map/ppermute | solution.py:929
  157.4 6.6 %collective-permute-done.32 = bf16[544,256]{1,0:T(8,128)(2,1)S(1)} collective-permute-done((bf16[544,256]{1,0:T(8,128)(2,1)S(1)}, bf16[544,256]{1,0:T(8,128)(2,1)S(1)}, u32[]{:S(2)}, u32[]{:S(2)}) %collective-permute-start.32) | collective-permute-done | bytes 278560 | tf_op jit(solution)/shard_map/ppermute | solution.py:929
  164.6 2.6 %collective-permute-start.33 = (bf16[544,256]{1,0:T(8,128)(2,1)S(1)}, bf16[544,256]{1,0:T(8,128)(2,1)S(1)}, u32[]{:S(2)}, u32[]{:S(2)}) collective-permute-start(bf16[544,256]{1,0:T(8,128)(2,1)S(1)} %add_convert_fusion.11), channel_id=1, source_target_pairs={{0,16},{4,20},{8,24},{12,28},{16,0},{20,4},{24,8},{28,12},{1,17},{... | collective-permute-start | bytes 835592 | tf_op jit(solution)/shard_map/ppermute | solution.py:929
  167.2 7.8 %collective-permute-done.33 = bf16[544,256]{1,0:T(8,128)(2,1)S(1)} collective-permute-done((bf16[544,256]{1,0:T(8,128)(2,1)S(1)}, bf16[544,256]{1,0:T(8,128)(2,1)S(1)}, u32[]{:S(2)}, u32[]{:S(2)}) %collective-permute-start.33) | collective-permute-done | bytes 278560 | tf_op jit(solution)/shard_map/ppermute | solution.py:929
  175.0 2.0 %collective-permute-done.34 = bf16[608,256]{1,0:T(8,128)(2,1)S(1)} collective-permute-done((bf16[608,256]{1,0:T(8,128)(2,1)S(1)}, bf16[608,256]{1,0:T(8,128)(2,1)S(1)}, u32[]{:S(2)}, u32[]{:S(2)}) %collective-permute-start.34) | collective-permute-done | bytes 311328 | tf_op jit(solution)/shard_map/ppermute | solution.py:929
  177.2 2.7 %collective-permute-start.35 = (bf16[544,256]{1,0:T(8,128)(2,1)S(1)}, bf16[544,256]{1,0:T(8,128)(2,1)S(1)}, u32[]{:S(2)}, u32[]{:S(2)}) collective-permute-start(bf16[544,256]{1,0:T(8,128)(2,1)S(1)} %add_convert_fusion.10), channel_id=1, source_target_pairs={{0,8},{4,12},{8,0},{12,4},{16,24},{20,28},{24,16},{28,20},{1,9},{5... | collective-permute-start | bytes 835592 | tf_op jit(solution)/shard_map/ppermute | solution.py:929
  180.5 1.9 %shard_map.235 = (f32[2,4,256,256]{3,2,1,0:T(8,128)}, f32[2,4,256,256]{3,2,1,0:T(8,128)}, f32[2,4,256]{2,1,0:T(4,128)S(1)}, f32[2,4,256]{2,1,0:T(4,128)S(1)}) custom-call(s32[3]{0:T(128)S(1)} %copy-done, bf16[1216,256]{1,0:T(8,128)(2,1)S(1)} %pad_maximum_fusion.refs_1_, bf16[1216,256]{1,0:T(8,128)(2,1)S(1)} %collective-permute-done.36.refs_2_), custom_call_target="tpu_custom_call" | custom-call | bytes 3145728 | tf_op jit(solution)/shard_map/pallas_call | solution.py:912
  183.2 3.9 %collective-permute-done.35 = bf16[544,256]{1,0:T(8,128)(2,1)S(1)} collective-permute-done((bf16[544,256]{1,0:T(8,128)(2,1)S(1)}, bf16[544,256]{1,0:T(8,128)(2,1)S(1)}, u32[]{:S(2)}, u32[]{:S(2)}) %collective-permute-start.35) | collective-permute-done | bytes 278560 | tf_op jit(solution)/shard_map/ppermute | solution.py:929
  190.5 2.5 %shard_map.236 = (f32[2,4,256,256]{3,2,1,0:T(8,128)}, f32[2,4,256,256]{3,2,1,0:T(8,128)}, f32[2,4,256]{2,1,0:T(4,128)}, f32[2,4,256]{2,1,0:T(4,128)}) custom-call(s32[3]{0:T(128)S(1)} %copy-done, bf16[1088,256]{1,0:T(8,128)(2,1)S(1)} %pad_maximum_fusion.1.refs_1_, ...), custom_call_target="tpu_custom_call", output_to_operand_aliasing={{0}: (3, {}), {1}: (4, {})} | custom-call | bytes 3145728 | tf_op jit(solution)/shard_map/pallas_call | solution.py:912
  (176 shorter events, 42.3 us)
Async XLA Ops:
  2.7 15.4 %collective-permute-start = (bf16[2,528,256]{2,1,0:T(8,128)(2,1)S(1)}, bf16[2,528,256]{2,1,0:T(8,128)(2,1)}, u32[]{:S(2)}, u32[]{:S(2)}) collective-permute-start(bf16[2,528,256]{2,1,0:T(8,128)(2,1)S(1)} %pad_maximum_fusion.2.refs_3_.refs_18_), channel_id=1, source_target_pairs={{0,1},{1,0},{2,3},{3,2},{4,5},{5,4},{6,7},{7,6},{8,9},{9,8},{10,11... | collective-permute-start | bytes 1622024 | tf_op jit(solution)/shard_map/ppermute | solution.py:929
  5.7 13.8 %collective-permute-start.1 = (bf16[2,528,256]{2,1,0:T(8,128)(2,1)S(1)}, bf16[2,528,256]{2,1,0:T(8,128)(2,1)}, u32[]{:S(2)}, u32[]{:S(2)}) collective-permute-start(bf16[2,528,256]{2,1,0:T(8,128)(2,1)S(1)} %pad_maximum_fusion.2.refs_3_.refs_18_), channel_id=1, source_target_pairs={{0,2},{1,3},{2,0},{3,1},{4,6},{5,7},{6,4},{7,5},{8,10},{9,11},{10,... | collective-permute-start | bytes 1622024 | tf_op jit(solution)/shard_map/ppermute | solution.py:929
  19.6 6.6 %collective-permute-start.3 = (bf16[2,528,256]{2,1,0:T(8,128)(2,1)}, bf16[2,528,256]{2,1,0:T(8,128)(2,1)S(1)}, u32[]{:S(2)}, u32[]{:S(2)}) collective-permute-start(bf16[2,528,256]{2,1,0:T(8,128)(2,1)} %collective-permute-done.1.refs_7_.refs_22_), channel_id=1, source_target_pairs={{0,4},{4,0},{8,12},{12,8},{16,20},{20,16},{24,28},{28,24},{1,5},{5... | collective-permute-start | bytes 1622024 | tf_op jit(solution)/shard_map/ppermute | solution.py:929
  20.1 21.0 %collective-permute-start.8 = (bf16[2,528,256]{2,1,0:T(8,128)(2,1)S(1)}, bf16[2,528,256]{2,1,0:T(8,128)(2,1)S(1)}, u32[]{:S(2)}, u32[]{:S(2)}) collective-permute-start(bf16[2,528,256]{2,1,0:T(8,128)(2,1)S(1)} %pad_maximum_fusion.4.refs_10_.refs_16_), channel_id=1, source_target_pairs={{0,1},{1,0},{2,3},{3,2},{4,5},{5,4},{6,7},{7,6},{8,9},{9,8},{10,11... | collective-permute-start | bytes 1622024 | tf_op jit(solution)/shard_map/ppermute | solution.py:929
  20.5 22.3 %collective-permute-start.10 = (bf16[2,528,256]{2,1,0:T(8,128)(2,1)S(1)}, bf16[2,528,256]{2,1,0:T(8,128)(2,1)S(1)}, u32[]{:S(2)}, u32[]{:S(2)}) collective-permute-start(bf16[2,528,256]{2,1,0:T(8,128)(2,1)S(1)} %pad_maximum_fusion.4.refs_10_.refs_16_), channel_id=1, source_target_pairs={{0,2},{1,3},{2,0},{3,1},{4,6},{5,7},{6,4},{7,5},{8,10},{9,11},{10,... | collective-permute-start | bytes 1622024 | tf_op jit(solution)/shard_map/ppermute | solution.py:929
  24.1 16.4 %collective-permute-start.4 = (bf16[1,528,256]{2,1,0:T(8,128)(2,1)S(1)}, bf16[1,528,256]{2,1,0:T(8,128)(2,1)S(1)}, u32[]{:S(2)}, u32[]{:S(2)}) collective-permute-start(bf16[1,528,256]{2,1,0:T(8,128)(2,1)S(1)} %slice.102), channel_id=1, source_target_pairs={{0,2},{1,3},{2,0},{3,1},{4,6},{5,7},{6,4},{7,5},{8,10},{9,11},{10,... | collective-permute-start | bytes 811016 | tf_op jit(solution)/shard_map/ppermute | solution.py:929
  24.5 16.0 %collective-permute-start.5 = (bf16[1,528,256]{2,1,0:T(8,128)(2,1)S(1)}, bf16[1,528,256]{2,1,0:T(8,128)(2,1)S(1)}, u32[]{:S(2)}, u32[]{:S(2)}) collective-permute-start(bf16[1,528,256]{2,1,0:T(8,128)(2,1)S(1)} %slice.103), channel_id=1, source_target_pairs={{0,1},{1,0},{2,3},{3,2},{4,5},{5,4},{6,7},{7,6},{8,9},{9,8},{10,11... | collective-permute-start | bytes 811016 | tf_op jit(solution)/shard_map/ppermute | solution.py:929
  41.2 12.0 %collective-permute-start.12 = (bf16[1,528,256]{2,1,0:T(8,128)(2,1)S(1)}, bf16[1,528,256]{2,1,0:T(8,128)(2,1)S(1)}, u32[]{:S(2)}, u32[]{:S(2)}) collective-permute-start(bf16[1,528,256]{2,1,0:T(8,128)(2,1)S(1)} %slice.134), channel_id=1, source_target_pairs={{0,2},{1,3},{2,0},{3,1},{4,6},{5,7},{6,4},{7,5},{8,10},{9,11},{10,... | collective-permute-start | bytes 811016 | tf_op jit(solution)/shard_map/ppermute | solution.py:929
  42.8 10.4 %collective-permute-start.13 = (bf16[1,528,256]{2,1,0:T(8,128)(2,1)S(1)}, bf16[1,528,256]{2,1,0:T(8,128)(2,1)S(1)}, u32[]{:S(2)}, u32[]{:S(2)}) collective-permute-start(bf16[1,528,256]{2,1,0:T(8,128)(2,1)S(1)} %slice.135), channel_id=1, source_target_pairs={{0,1},{1,0},{2,3},{3,2},{4,5},{5,4},{6,7},{7,6},{8,9},{9,8},{10,11... | collective-permute-start | bytes 811016 | tf_op jit(solution)/shard_map/ppermute | solution.py:929
  44.1 9.6 %collective-permute-start.9 = (bf16[2,528,256]{2,1,0:T(8,128)(2,1)S(1)}, bf16[2,528,256]{2,1,0:T(8,128)(2,1)S(1)}, u32[]{:S(2)}, u32[]{:S(2)}) collective-permute-start(bf16[2,528,256]{2,1,0:T(8,128)(2,1)S(1)} %collective-permute-done.8.refs_12_), channel_id=1, source_target_pairs={{0,4},{4,0},{8,12},{12,8},{16,20},{20,16},{24,28},{28,24},{1,5},{5... | collective-permute-start | bytes 1622024 | tf_op jit(solution)/shard_map/ppermute | solution.py:929
  44.1 9.6 %collective-permute-start.11 = (bf16[2,528,256]{2,1,0:T(8,128)(2,1)S(1)}, bf16[2,528,256]{2,1,0:T(8,128)(2,1)S(1)}, u32[]{:S(2)}, u32[]{:S(2)}) collective-permute-start(bf16[2,528,256]{2,1,0:T(8,128)(2,1)S(1)} %collective-permute-done.10.refs_14_), channel_id=1, source_target_pairs={{0,4},{4,0},{8,12},{12,8},{16,20},{20,16},{24,28},{28,24},{1,5},{5... | collective-permute-start | bytes 1622024 | tf_op jit(solution)/shard_map/ppermute | solution.py:929
  92.1 29.2 %collective-permute-start.23 = (bf16[1216,256]{1,0:T(8,128)(2,1)S(1)}, bf16[1216,256]{1,0:T(8,128)(2,1)S(1)}, u32[]{:S(2)}, u32[]{:S(2)}) collective-permute-start(bf16[1216,256]{1,0:T(8,128)(2,1)S(1)} %get-tuple-element.163), channel_id=1, source_target_pairs={{0,1},{1,0},{2,3},{3,2},{4,5},{5,4},{6,7},{7,6},{8,9},{9,8},{10,11... | collective-permute-start | bytes 1867784 | tf_op jit(solution)/shard_map/ppermute | solution.py:929
  92.9 29.2 %collective-permute-start.24 = (bf16[1216,256]{1,0:T(8,128)(2,1)S(1)}, bf16[1216,256]{1,0:T(8,128)(2,1)S(1)}, u32[]{:S(2)}, u32[]{:S(2)}) collective-permute-start(bf16[1216,256]{1,0:T(8,128)(2,1)S(1)} %get-tuple-element.164), channel_id=1, source_target_pairs={{0,2},{1,3},{2,0},{3,1},{4,6},{5,7},{6,4},{7,5},{8,10},{9,11},{10,... | collective-permute-start | bytes 1867784 | tf_op jit(solution)/shard_map/ppermute | solution.py:929
  93.4 28.7 %collective-permute-start.25 = (bf16[1216,256]{1,0:T(8,128)(2,1)}, bf16[1216,256]{1,0:T(8,128)(2,1)S(1)}, u32[]{:S(2)}, u32[]{:S(2)}) collective-permute-start(bf16[1216,256]{1,0:T(8,128)(2,1)} %get-tuple-element.165), channel_id=1, source_target_pairs={{0,3},{1,2},{2,1},{3,0},{4,7},{5,6},{6,5},{7,4},{8,11},{9,10},{10,... | collective-permute-start | bytes 1867784 | tf_op jit(solution)/shard_map/ppermute | solution.py:929
  127.9 9.5 %collective-permute-start.30 = (bf16[608,256]{1,0:T(8,128)(2,1)S(1)}, bf16[608,256]{1,0:T(8,128)(2,1)S(1)}, u32[]{:S(2)}, u32[]{:S(2)}) collective-permute-start(bf16[608,256]{1,0:T(8,128)(2,1)S(1)} %get-tuple-element.250), channel_id=1, source_target_pairs={{0,8},{4,12},{8,0},{12,4},{16,24},{20,28},{24,16},{28,20},{1,9},{5... | collective-permute-start | bytes 933896 | tf_op jit(solution)/shard_map/ppermute | solution.py:929
  129.5 15.5 %collective-permute-start.26 = (bf16[1088,256]{1,0:T(8,128)(2,1)S(1)}, bf16[1088,256]{1,0:T(8,128)(2,1)S(1)}, u32[]{:S(2)}, u32[]{:S(2)}) collective-permute-start(bf16[1088,256]{1,0:T(8,128)(2,1)S(1)} %get-tuple-element.178), channel_id=1, source_target_pairs={{0,1},{1,0},{2,3},{3,2},{4,5},{5,4},{6,7},{7,6},{8,9},{9,8},{10,11... | collective-permute-start | bytes 1671176 | tf_op jit(solution)/shard_map/ppermute | solution.py:929
  130.3 26.0 %collective-permute-start.27 = (bf16[1088,256]{1,0:T(8,128)(2,1)S(1)}, bf16[1088,256]{1,0:T(8,128)(2,1)S(1)}, u32[]{:S(2)}, u32[]{:S(2)}) collective-permute-start(bf16[1088,256]{1,0:T(8,128)(2,1)S(1)} %get-tuple-element.179), channel_id=1, source_target_pairs={{0,2},{1,3},{2,0},{3,1},{4,6},{5,7},{6,4},{7,5},{8,10},{9,11},{10,... | collective-permute-start | bytes 1671176 | tf_op jit(solution)/shard_map/ppermute | solution.py:929
  130.8 25.6 %collective-permute-start.28 = (bf16[1088,256]{1,0:T(8,128)(2,1)S(1)}, bf16[1088,256]{1,0:T(8,128)(2,1)S(1)}, u32[]{:S(2)}, u32[]{:S(2)}) collective-permute-start(bf16[1088,256]{1,0:T(8,128)(2,1)S(1)} %get-tuple-element.180), channel_id=1, source_target_pairs={{0,3},{1,2},{2,1},{3,0},{4,7},{5,6},{6,5},{7,4},{8,11},{9,10},{10,... | collective-permute-start | bytes 1671176 | tf_op jit(solution)/shard_map/ppermute | solution.py:929
  133.0 23.3 %collective-permute-start.29 = (bf16[1088,256]{1,0:T(8,128)(2,1)S(1)}, bf16[1088,256]{1,0:T(8,128)(2,1)S(1)}, u32[]{:S(2)}, u32[]{:S(2)}) collective-permute-start(bf16[1088,256]{1,0:T(8,128)(2,1)S(1)} %copy-done.17), channel_id=1, source_target_pairs={{0,4},{4,0},{8,12},{12,8},{16,20},{20,16},{24,28},{28,24},{1,5},{5... | collective-permute-start | bytes 1671176 | tf_op jit(solution)/shard_map/ppermute | solution.py:929
  137.5 18.9 %collective-permute-start.31 = (bf16[608,256]{1,0:T(8,128)(2,1)S(1)}, bf16[608,256]{1,0:T(8,128)(2,1)S(1)}, u32[]{:S(2)}, u32[]{:S(2)}) collective-permute-start(bf16[608,256]{1,0:T(8,128)(2,1)S(1)} %add_convert_fusion.9), channel_id=1, source_target_pairs={{0,16},{4,20},{8,24},{12,28},{16,0},{20,4},{24,8},{28,12},{1,17},{... | collective-permute-start | bytes 933896 | tf_op jit(solution)/shard_map/ppermute | solution.py:929
  156.9 7.1 %collective-permute-start.32 = (bf16[544,256]{1,0:T(8,128)(2,1)S(1)}, bf16[544,256]{1,0:T(8,128)(2,1)S(1)}, u32[]{:S(2)}, u32[]{:S(2)}) collective-permute-start(bf16[544,256]{1,0:T(8,128)(2,1)S(1)} %get-tuple-element.254), channel_id=1, source_target_pairs={{0,8},{4,12},{8,0},{12,4},{16,24},{20,28},{24,16},{28,20},{1,9},{5... | collective-permute-start | bytes 835592 | tf_op jit(solution)/shard_map/ppermute | solution.py:929
  164.1 12.9 %collective-permute-start.34 = (bf16[608,256]{1,0:T(8,128)(2,1)S(1)}, bf16[608,256]{1,0:T(8,128)(2,1)S(1)}, u32[]{:S(2)}, u32[]{:S(2)}) collective-permute-start(bf16[608,256]{1,0:T(8,128)(2,1)S(1)} %add_convert_fusion.8), channel_id=1, source_target_pairs={{0,8},{4,12},{8,0},{12,4},{16,24},{20,28},{24,16},{28,20},{1,9},{5... | collective-permute-start | bytes 933896 | tf_op jit(solution)/shard_map/ppermute | solution.py:929
  164.6 10.4 %collective-permute-start.33 = (bf16[544,256]{1,0:T(8,128)(2,1)S(1)}, bf16[544,256]{1,0:T(8,128)(2,1)S(1)}, u32[]{:S(2)}, u32[]{:S(2)}) collective-permute-start(bf16[544,256]{1,0:T(8,128)(2,1)S(1)} %add_convert_fusion.11), channel_id=1, source_target_pairs={{0,16},{4,20},{8,24},{12,28},{16,0},{20,4},{24,8},{28,12},{1,17},{... | collective-permute-start | bytes 835592 | tf_op jit(solution)/shard_map/ppermute | solution.py:929
  177.2 9.9 %collective-permute-start.35 = (bf16[544,256]{1,0:T(8,128)(2,1)S(1)}, bf16[544,256]{1,0:T(8,128)(2,1)S(1)}, u32[]{:S(2)}, u32[]{:S(2)}) collective-permute-start(bf16[544,256]{1,0:T(8,128)(2,1)S(1)} %add_convert_fusion.10), channel_id=1, source_target_pairs={{0,8},{4,12},{8,0},{12,4},{16,24},{20,28},{24,16},{28,20},{1,9},{5... | collective-permute-start | bytes 835592 | tf_op jit(solution)/shard_map/ppermute | solution.py:929
  (40 other events, 197.3 us)

commit v6 on v5

--- a/solution.py
+++ b/solution.py
@@ -433,7 +433,7 @@
         functools.partial(forward_kernel, places, len(pieces), each, total is None),
         grid=(number // each,),
         out_shape=[summed, kept, kept],
-        in_specs=specs + [FAR] * len(pieces),
+        in_specs=specs + [whole_spec(piece.shape) for piece in pieces],
         out_specs=[whole_spec(summed.shape), kept_spec, kept_spec],
         scratch_shapes=[
             pltpu.VMEM((height, width), bf16),

time: 194 us -> 193 us (level)
  no operation moved by 1% of the time
where the time goes in v6:
time: 193 us; the launch traced here: 192 us
  Pallas kernels  83.2 us (43%)
  waiting for transfers between devices  56.2 us (29%)
  starting transfers between devices  32.1 us (17%)
  other arithmetic  11.4 us (6%)
  local copies, waits for them, and re-layouts  7.81 us (4%)
    ppermute x38, waiting for transfers between devices, flip(): return lax.ppermute(array, axis, [(i, i ^ bits) for i in range(size)])  56.2 us
    ppermute x38, starting transfers between devices, flip(): return lax.ppermute(array, axis, [(i, i ^ bits) for i in range(size)])  32.1 us
    pallas_call x1, Pallas kernels, middle_call(): pl.pallas_call(functools.partial(middle_kernel, places, len(pieces), grou...  29.4 us
    pallas_call x1, Pallas kernels, backward_call(): pl.pallas_call(functools.partial(backward_kernel, places, len(pieces), ea...  25.1 us
    pallas_call x2, Pallas kernels, forward_call(): pl.pallas_call(functools.partial(forward_kernel, places, len(pieces), eac...  21.1 us
    convert_element_type x9, other arithmetic, add_low(): return level[0].astype(bf16)  5.84 us
    pallas_call x2, Pallas kernels, finish_call(): pl.pallas_call(functools.partial(finish_kernel, names, held, rows, first)...  4.47 us
  transfers between devices with their start and end apart: 38, of which 19 were waited for; matrix products, arithmetic and copies ran while one was open for 4% of the time, Pallas kernels for 27%

profile of v6, /device:TPU:0, one launch (start us, length us, event | category | flops | bytes accessed | tf_op | source)
XLA Modules:
  0.0 192.3 jit_solution(14688044512614397199)
XLA Ops:
  2.7 3.0 %collective-permute-start = (bf16[2,528,256]{2,1,0:T(8,128)(2,1)S(1)}, bf16[2,528,256]{2,1,0:T(8,128)(2,1)}, u32[]{:S(2)}, u32[]{:S(2)}) collective-permute-start(bf16[2,528,256]{2,1,0:T(8,128)(2,1)S(1)} %pad_maximum_fusion.2.refs_3_.refs_18_), channel_id=1, source_target_pairs={{0,1},{1,0},{2,3},{3,2},{4,5},{5,4},{6,7},{7,6},{8,9},{9,8},{10,11... | collective-permute-start | bytes 1622024 | tf_op jit(solution)/shard_map/ppermute | solution.py:929
  9.5 3.2 %shard_map.230 = (bf16[1024,32]{1,0:T(8,128)(2,1)}, bf16[32,1024]{1,0:T(8,128)(2,1)}, f32[20,64,128]{2,1,0:T(8,128)}, bf16[8,32,256]{2,1,0:T(8,128)(2,1)}, bf16[8,32,512]{2,1,0:T(8,128)(2,1)}) custom-call(s32[3]{0:T(128)} %pad_add_fusion.place_ref.refs_0_, s32[1,256]{1,0:T(1,128)} %bitcast.91, s32[1,256]{1,0:T(1,128)} %bitcast.92, f32[64,32]{1,0:T(8,128)} %copy.40.logit_ref, ...), custom_call_target="tpu_custom_call" | custom-call | flops 33554432 | bytes 2097152 | tf_op jit(solution)/shard_map/pallas_call | solution.py:171
  14.9 3.3 %collective-permute-done.refs_5_.refs_20_ = bf16[2,528,256]{2,1,0:T(8,128)(2,1)} collective-permute-done((bf16[2,528,256]{2,1,0:T(8,128)(2,1)S(1)}, bf16[2,528,256]{2,1,0:T(8,128)(2,1)}, u32[]{:S(2)}, u32[]{:S(2)}) %collective-permute-start) | collective-permute-done | bytes 540704 | tf_op jit(solution)/shard_map/ppermute | solution.py:929
  20.5 1.7 collective-permute-start.10
  27.0 13.9 %shard_map.231 = (f32[1,1024,256]{2,1,0:T(8,128)}, bf16[8,2,1024,256]{3,2,1,0:T(8,128)(2,1)}, bf16[8,2,1024,256]{3,2,1,0:T(8,128)(2,1)}) custom-call(f32[1024,256]{1,0:T(8,128)} %refs_0_.5, bf16[1024,32]{1,0:T(8,128)(2,1)} %get-tuple-element.117.refs_1_.refs_2_, bf16[8,32,256]{2,1,0:T(8,128)(2,1)} %get-tuple-element.118.refs_2_.refs_5_, ...), custom_call_target="tpu_custom_call" | custom-call | flops 3221225472 | bytes 17825792 | tf_op jit(solution)/shard_map/pallas_call | solution.py:432
  45.3 7.1 %shard_map.232 = (f32[1,1024,256]{2,1,0:T(8,128)}, bf16[8,2,1024,256]{3,2,1,0:T(8,128)(2,1)}, bf16[8,2,1024,256]{3,2,1,0:T(8,128)(2,1)}) custom-call(f32[1024,256]{1,0:T(8,128)} %refs_0_.5, bf16[1024,32]{1,0:T(8,128)(2,1)} %get-tuple-element.117.refs_1_.refs_2_, ...), custom_call_target="tpu_custom_call", output_to_operand_aliasing={{1}: (4, {}), {2}: (5, {})} | custom-call | flops 1073741824 | bytes 7340032 | tf_op jit(solution)/shard_map/pallas_call | solution.py:432
  55.2 29.4 %shard_map.233 = (f32[2,1024]{1,0:T(2,128)}, f32[1024,256]{1,0:T(8,128)}, bf16[3,1216,256]{2,1,0:T(8,128)(2,1)}, bf16[1216,256]{1,0:T(8,128)(2,1)}, bf16[1216,25...) custom-call(s32[3]{0:T(128)} %pad_add_fusion.place_ref.refs_0_, ...), custom_call_target="tpu_custom_call" | custom-call | flops 15032385536 | bytes 12582912 | tf_op jit(solution)/shard_map/pallas_call | solution.py:633
  88.7 2.8 %fusion = (bf16[1216,256]{1,0:T(8,128)(2,1)}, bf16[1216,256]{1,0:T(8,128)(2,1)S(1)}, bf16[1216,256]{1,0:T(8,128)(2,1)S(1)}) fusion(bf16[1216,256]{1,0:T(8,128)(2,1)S(1)} %collective-permute-done.18, bf16[3,1216,256]{2,1,0:T(8,128)(2,1)} %get-tuple-element.138, bf16[1216,256]{1,0:T(8,128)(2,1)S(1)} %collective-permute-done.17, ...), kind=kLoop, calls=%fused_computation.1 | loop fusion | flops 3735552 | bytes 5603328 | tf_op jit(solution)/shard_map/convert_element_type | solution.py:936
  93.2 1.8 collective-permute-start.25
  95.0 25.1 %shard_map.234 = (f32[1024,256]{1,0:T(8,128)}, bf16[4,1088,256]{2,1,0:T(8,128)(2,1)}, bf16[1088,256]{1,0:T(8,128)(2,1)}, bf16[1088,256]{1,0:T(8,128)(2,1)}, bf16...) custom-call(f32[1024,256]{1,0:T(8,128)} %refs_0_.5, ...), custom_call_target="tpu_custom_call" | custom-call | flops 10737418240 | bytes 29360128 | tf_op jit(solution)/shard_map/pallas_call | solution.py:838
  125.3 1.9 fusion.3
  130.6 1.8 collective-permute-start.28
  132.4 4.3 %collective-permute-done.30 = bf16[608,256]{1,0:T(8,128)(2,1)S(1)} collective-permute-done((bf16[608,256]{1,0:T(8,128)(2,1)S(1)}, bf16[608,256]{1,0:T(8,128)(2,1)S(1)}, u32[]{:S(2)}, u32[]{:S(2)}) %collective-permute-start.30) | collective-permute-done | bytes 311328 | tf_op jit(solution)/shard_map/ppermute | solution.py:929
  136.8 2.6 %collective-permute-start.31 = (bf16[608,256]{1,0:T(8,128)(2,1)S(1)}, bf16[608,256]{1,0:T(8,128)(2,1)S(1)}, u32[]{:S(2)}, u32[]{:S(2)}) collective-permute-start(bf16[608,256]{1,0:T(8,128)(2,1)S(1)} %add_convert_fusion.9), channel_id=1, source_target_pairs={{0,16},{4,20},{8,24},{12,28},{16,0},{20,4},{24,8},{28,12},{1,17},{... | collective-permute-start | bytes 933896 | tf_op jit(solution)/shard_map/ppermute | solution.py:929
  139.5 5.0 %collective-permute-done.26 = bf16[1088,256]{1,0:T(8,128)(2,1)S(1)} collective-permute-done((bf16[1088,256]{1,0:T(8,128)(2,1)S(1)}, bf16[1088,256]{1,0:T(8,128)(2,1)S(1)}, u32[]{:S(2)}, u32[]{:S(2)}) %collective-permute-start.26) | collective-permute-done | bytes 557088 | tf_op jit(solution)/shard_map/ppermute | solution.py:929
  144.4 11.7 %collective-permute-done.27 = bf16[1088,256]{1,0:T(8,128)(2,1)S(1)} collective-permute-done((bf16[1088,256]{1,0:T(8,128)(2,1)S(1)}, bf16[1088,256]{1,0:T(8,128)(2,1)S(1)}, u32[]{:S(2)}, u32[]{:S(2)}) %collective-permute-start.27) | collective-permute-done | bytes 557088 | tf_op jit(solution)/shard_map/ppermute | solution.py:929
  157.2 6.5 %collective-permute-done.32 = bf16[544,256]{1,0:T(8,128)(2,1)S(1)} collective-permute-done((bf16[544,256]{1,0:T(8,128)(2,1)S(1)}, bf16[544,256]{1,0:T(8,128)(2,1)S(1)}, u32[]{:S(2)}, u32[]{:S(2)}) %collective-permute-start.32) | collective-permute-done | bytes 278560 | tf_op jit(solution)/shard_map/ppermute | solution.py:929
  164.0 2.6 %collective-permute-start.33 = (bf16[544,256]{1,0:T(8,128)(2,1)S(1)}, bf16[544,256]{1,0:T(8,128)(2,1)S(1)}, u32[]{:S(2)}, u32[]{:S(2)}) collective-permute-start(bf16[544,256]{1,0:T(8,128)(2,1)S(1)} %add_convert_fusion.11), channel_id=1, source_target_pairs={{0,16},{4,20},{8,24},{12,28},{16,0},{20,4},{24,8},{28,12},{1,17},{... | collective-permute-start | bytes 835592 | tf_op jit(solution)/shard_map/ppermute | solution.py:929
  166.6 7.9 %collective-permute-done.33 = bf16[544,256]{1,0:T(8,128)(2,1)S(1)} collective-permute-done((bf16[544,256]{1,0:T(8,128)(2,1)S(1)}, bf16[544,256]{1,0:T(8,128)(2,1)S(1)}, u32[]{:S(2)}, u32[]{:S(2)}) %collective-permute-start.33) | collective-permute-done | bytes 278560 | tf_op jit(solution)/shard_map/ppermute | solution.py:929
  176.3 2.7 %collective-permute-start.35 = (bf16[544,256]{1,0:T(8,128)(2,1)S(1)}, bf16[544,256]{1,0:T(8,128)(2,1)S(1)}, u32[]{:S(2)}, u32[]{:S(2)}) collective-permute-start(bf16[544,256]{1,0:T(8,128)(2,1)S(1)} %add_convert_fusion.10), channel_id=1, source_target_pairs={{0,8},{4,12},{8,0},{12,4},{16,24},{20,28},{24,16},{28,20},{1,9},{5... | collective-permute-start | bytes 835592 | tf_op jit(solution)/shard_map/ppermute | solution.py:929
  179.6 1.9 %shard_map.235 = (f32[2,4,256,256]{3,2,1,0:T(8,128)}, f32[2,4,256,256]{3,2,1,0:T(8,128)}, f32[2,4,256]{2,1,0:T(4,128)S(1)}, f32[2,4,256]{2,1,0:T(4,128)S(1)}) custom-call(s32[3]{0:T(128)S(1)} %copy-done, bf16[1216,256]{1,0:T(8,128)(2,1)S(1)} %pad_maximum_fusion.refs_1_, bf16[1216,256]{1,0:T(8,128)(2,1)S(1)} %collective-permute-done.36.refs_2_), custom_call_target="tpu_custom_call" | custom-call | bytes 3145728 | tf_op jit(solution)/shard_map/pallas_call | solution.py:912
  182.3 3.9 %collective-permute-done.35 = bf16[544,256]{1,0:T(8,128)(2,1)S(1)} collective-permute-done((bf16[544,256]{1,0:T(8,128)(2,1)S(1)}, bf16[544,256]{1,0:T(8,128)(2,1)S(1)}, u32[]{:S(2)}, u32[]{:S(2)}) %collective-permute-start.35) | collective-permute-done | bytes 278560 | tf_op jit(solution)/shard_map/ppermute | solution.py:929
  186.5 1.8 collective-permute-done.37.refs_2_
  189.5 2.5 %shard_map.236 = (f32[2,4,256,256]{3,2,1,0:T(8,128)}, f32[2,4,256,256]{3,2,1,0:T(8,128)}, f32[2,4,256]{2,1,0:T(4,128)}, f32[2,4,256]{2,1,0:T(4,128)}) custom-call(s32[3]{0:T(128)S(1)} %copy-done, bf16[1088,256]{1,0:T(8,128)(2,1)S(1)} %pad_maximum_fusion.1.refs_1_, ...), custom_call_target="tpu_custom_call", output_to_operand_aliasing={{0}: (3, {}), {1}: (4, {})} | custom-call | bytes 3145728 | tf_op jit(solution)/shard_map/pallas_call | solution.py:912
  (176 shorter events, 42.2 us)
Async XLA Ops:
  2.7 15.4 %collective-permute-start = (bf16[2,528,256]{2,1,0:T(8,128)(2,1)S(1)}, bf16[2,528,256]{2,1,0:T(8,128)(2,1)}, u32[]{:S(2)}, u32[]{:S(2)}) collective-permute-start(bf16[2,528,256]{2,1,0:T(8,128)(2,1)S(1)} %pad_maximum_fusion.2.refs_3_.refs_18_), channel_id=1, source_target_pairs={{0,1},{1,0},{2,3},{3,2},{4,5},{5,4},{6,7},{7,6},{8,9},{9,8},{10,11... | collective-permute-start | bytes 1622024 | tf_op jit(solution)/shard_map/ppermute | solution.py:929
  5.7 13.8 %collective-permute-start.1 = (bf16[2,528,256]{2,1,0:T(8,128)(2,1)S(1)}, bf16[2,528,256]{2,1,0:T(8,128)(2,1)}, u32[]{:S(2)}, u32[]{:S(2)}) collective-permute-start(bf16[2,528,256]{2,1,0:T(8,128)(2,1)S(1)} %pad_maximum_fusion.2.refs_3_.refs_18_), channel_id=1, source_target_pairs={{0,2},{1,3},{2,0},{3,1},{4,6},{5,7},{6,4},{7,5},{8,10},{9,11},{10,... | collective-permute-start | bytes 1622024 | tf_op jit(solution)/shard_map/ppermute | solution.py:929
  19.6 6.6 %collective-permute-start.3 = (bf16[2,528,256]{2,1,0:T(8,128)(2,1)}, bf16[2,528,256]{2,1,0:T(8,128)(2,1)S(1)}, u32[]{:S(2)}, u32[]{:S(2)}) collective-permute-start(bf16[2,528,256]{2,1,0:T(8,128)(2,1)} %collective-permute-done.1.refs_7_.refs_22_), channel_id=1, source_target_pairs={{0,4},{4,0},{8,12},{12,8},{16,20},{20,16},{24,28},{28,24},{1,5},{5... | collective-permute-start | bytes 1622024 | tf_op jit(solution)/shard_map/ppermute | solution.py:929
  20.1 21.5 %collective-permute-start.8 = (bf16[2,528,256]{2,1,0:T(8,128)(2,1)S(1)}, bf16[2,528,256]{2,1,0:T(8,128)(2,1)S(1)}, u32[]{:S(2)}, u32[]{:S(2)}) collective-permute-start(bf16[2,528,256]{2,1,0:T(8,128)(2,1)S(1)} %pad_maximum_fusion.4.refs_10_.refs_16_), channel_id=1, source_target_pairs={{0,1},{1,0},{2,3},{3,2},{4,5},{5,4},{6,7},{7,6},{8,9},{9,8},{10,11... | collective-permute-start | bytes 1622024 | tf_op jit(solution)/shard_map/ppermute | solution.py:929
  20.5 22.7 %collective-permute-start.10 = (bf16[2,528,256]{2,1,0:T(8,128)(2,1)S(1)}, bf16[2,528,256]{2,1,0:T(8,128)(2,1)S(1)}, u32[]{:S(2)}, u32[]{:S(2)}) collective-permute-start(bf16[2,528,256]{2,1,0:T(8,128)(2,1)S(1)} %pad_maximum_fusion.4.refs_10_.refs_16_), channel_id=1, source_target_pairs={{0,2},{1,3},{2,0},{3,1},{4,6},{5,7},{6,4},{7,5},{8,10},{9,11},{10,... | collective-permute-start | bytes 1622024 | tf_op jit(solution)/shard_map/ppermute | solution.py:929
  24.1 16.8 %collective-permute-start.4 = (bf16[1,528,256]{2,1,0:T(8,128)(2,1)S(1)}, bf16[1,528,256]{2,1,0:T(8,128)(2,1)S(1)}, u32[]{:S(2)}, u32[]{:S(2)}) collective-permute-start(bf16[1,528,256]{2,1,0:T(8,128)(2,1)S(1)} %slice.102), channel_id=1, source_target_pairs={{0,2},{1,3},{2,0},{3,1},{4,6},{5,7},{6,4},{7,5},{8,10},{9,11},{10,... | collective-permute-start | bytes 811016 | tf_op jit(solution)/shard_map/ppermute | solution.py:929
  24.5 16.4 %collective-permute-start.5 = (bf16[1,528,256]{2,1,0:T(8,128)(2,1)S(1)}, bf16[1,528,256]{2,1,0:T(8,128)(2,1)S(1)}, u32[]{:S(2)}, u32[]{:S(2)}) collective-permute-start(bf16[1,528,256]{2,1,0:T(8,128)(2,1)S(1)} %slice.103), channel_id=1, source_target_pairs={{0,1},{1,0},{2,3},{3,2},{4,5},{5,4},{6,7},{7,6},{8,9},{9,8},{10,11... | collective-permute-start | bytes 811016 | tf_op jit(solution)/shard_map/ppermute | solution.py:929
  41.6 10.9 %collective-permute-start.12 = (bf16[1,528,256]{2,1,0:T(8,128)(2,1)S(1)}, bf16[1,528,256]{2,1,0:T(8,128)(2,1)S(1)}, u32[]{:S(2)}, u32[]{:S(2)}) collective-permute-start(bf16[1,528,256]{2,1,0:T(8,128)(2,1)S(1)} %slice.134), channel_id=1, source_target_pairs={{0,2},{1,3},{2,0},{3,1},{4,6},{5,7},{6,4},{7,5},{8,10},{9,11},{10,... | collective-permute-start | bytes 811016 | tf_op jit(solution)/shard_map/ppermute | solution.py:929
  43.2 9.3 %collective-permute-start.13 = (bf16[1,528,256]{2,1,0:T(8,128)(2,1)S(1)}, bf16[1,528,256]{2,1,0:T(8,128)(2,1)S(1)}, u32[]{:S(2)}, u32[]{:S(2)}) collective-permute-start(bf16[1,528,256]{2,1,0:T(8,128)(2,1)S(1)} %slice.135), channel_id=1, source_target_pairs={{0,1},{1,0},{2,3},{3,2},{4,5},{5,4},{6,7},{7,6},{8,9},{9,8},{10,11... | collective-permute-start | bytes 811016 | tf_op jit(solution)/shard_map/ppermute | solution.py:929
  44.1 9.0 %collective-permute-start.9 = (bf16[2,528,256]{2,1,0:T(8,128)(2,1)S(1)}, bf16[2,528,256]{2,1,0:T(8,128)(2,1)S(1)}, u32[]{:S(2)}, u32[]{:S(2)}) collective-permute-start(bf16[2,528,256]{2,1,0:T(8,128)(2,1)S(1)} %collective-permute-done.8.refs_12_), channel_id=1, source_target_pairs={{0,4},{4,0},{8,12},{12,8},{16,20},{20,16},{24,28},{28,24},{1,5},{5... | collective-permute-start | bytes 1622024 | tf_op jit(solution)/shard_map/ppermute | solution.py:929
  44.1 9.0 %collective-permute-start.11 = (bf16[2,528,256]{2,1,0:T(8,128)(2,1)S(1)}, bf16[2,528,256]{2,1,0:T(8,128)(2,1)S(1)}, u32[]{:S(2)}, u32[]{:S(2)}) collective-permute-start(bf16[2,528,256]{2,1,0:T(8,128)(2,1)S(1)} %collective-permute-done.10.refs_14_), channel_id=1, source_target_pairs={{0,4},{4,0},{8,12},{12,8},{16,20},{20,16},{24,28},{28,24},{1,5},{5... | collective-permute-start | bytes 1622024 | tf_op jit(solution)/shard_map/ppermute | solution.py:929
  91.5 29.2 %collective-permute-start.23 = (bf16[1216,256]{1,0:T(8,128)(2,1)S(1)}, bf16[1216,256]{1,0:T(8,128)(2,1)S(1)}, u32[]{:S(2)}, u32[]{:S(2)}) collective-permute-start(bf16[1216,256]{1,0:T(8,128)(2,1)S(1)} %get-tuple-element.163), channel_id=1, source_target_pairs={{0,1},{1,0},{2,3},{3,2},{4,5},{5,4},{6,7},{7,6},{8,9},{9,8},{10,11... | collective-permute-start | bytes 1867784 | tf_op jit(solution)/shard_map/ppermute | solution.py:929
  92.7 29.2 %collective-permute-start.24 = (bf16[1216,256]{1,0:T(8,128)(2,1)S(1)}, bf16[1216,256]{1,0:T(8,128)(2,1)S(1)}, u32[]{:S(2)}, u32[]{:S(2)}) collective-permute-start(bf16[1216,256]{1,0:T(8,128)(2,1)S(1)} %get-tuple-element.164), channel_id=1, source_target_pairs={{0,2},{1,3},{2,0},{3,1},{4,6},{5,7},{6,4},{7,5},{8,10},{9,11},{10,... | collective-permute-start | bytes 1867784 | tf_op jit(solution)/shard_map/ppermute | solution.py:929
  93.2 28.7 %collective-permute-start.25 = (bf16[1216,256]{1,0:T(8,128)(2,1)}, bf16[1216,256]{1,0:T(8,128)(2,1)S(1)}, u32[]{:S(2)}, u32[]{:S(2)}) collective-permute-start(bf16[1216,256]{1,0:T(8,128)(2,1)} %get-tuple-element.165), channel_id=1, source_target_pairs={{0,3},{1,2},{2,1},{3,0},{4,7},{5,6},{6,5},{7,4},{8,11},{9,10},{10,... | collective-permute-start | bytes 1867784 | tf_op jit(solution)/shard_map/ppermute | solution.py:929
  127.3 9.5 %collective-permute-start.30 = (bf16[608,256]{1,0:T(8,128)(2,1)S(1)}, bf16[608,256]{1,0:T(8,128)(2,1)S(1)}, u32[]{:S(2)}, u32[]{:S(2)}) collective-permute-start(bf16[608,256]{1,0:T(8,128)(2,1)S(1)} %get-tuple-element.250), channel_id=1, source_target_pairs={{0,8},{4,12},{8,0},{12,4},{16,24},{20,28},{24,16},{28,20},{1,9},{5... | collective-permute-start | bytes 933896 | tf_op jit(solution)/shard_map/ppermute | solution.py:929
  128.9 15.5 %collective-permute-start.26 = (bf16[1088,256]{1,0:T(8,128)(2,1)S(1)}, bf16[1088,256]{1,0:T(8,128)(2,1)S(1)}, u32[]{:S(2)}, u32[]{:S(2)}) collective-permute-start(bf16[1088,256]{1,0:T(8,128)(2,1)S(1)} %get-tuple-element.178), channel_id=1, source_target_pairs={{0,1},{1,0},{2,3},{3,2},{4,5},{5,4},{6,7},{7,6},{8,9},{9,8},{10,11... | collective-permute-start | bytes 1671176 | tf_op jit(solution)/shard_map/ppermute | solution.py:929
  130.1 26.0 %collective-permute-start.27 = (bf16[1088,256]{1,0:T(8,128)(2,1)S(1)}, bf16[1088,256]{1,0:T(8,128)(2,1)S(1)}, u32[]{:S(2)}, u32[]{:S(2)}) collective-permute-start(bf16[1088,256]{1,0:T(8,128)(2,1)S(1)} %get-tuple-element.179), channel_id=1, source_target_pairs={{0,2},{1,3},{2,0},{3,1},{4,6},{5,7},{6,4},{7,5},{8,10},{9,11},{10,... | collective-permute-start | bytes 1671176 | tf_op jit(solution)/shard_map/ppermute | solution.py:929
  130.6 25.6 %collective-permute-start.28 = (bf16[1088,256]{1,0:T(8,128)(2,1)S(1)}, bf16[1088,256]{1,0:T(8,128)(2,1)S(1)}, u32[]{:S(2)}, u32[]{:S(2)}) collective-permute-start(bf16[1088,256]{1,0:T(8,128)(2,1)S(1)} %get-tuple-element.180), channel_id=1, source_target_pairs={{0,3},{1,2},{2,1},{3,0},{4,7},{5,6},{6,5},{7,4},{8,11},{9,10},{10,... | collective-permute-start | bytes 1671176 | tf_op jit(solution)/shard_map/ppermute | solution.py:929
  132.4 23.8 %collective-permute-start.29 = (bf16[1088,256]{1,0:T(8,128)(2,1)S(1)}, bf16[1088,256]{1,0:T(8,128)(2,1)S(1)}, u32[]{:S(2)}, u32[]{:S(2)}) collective-permute-start(bf16[1088,256]{1,0:T(8,128)(2,1)S(1)} %copy-done.17), channel_id=1, source_target_pairs={{0,4},{4,0},{8,12},{12,8},{16,20},{20,16},{24,28},{28,24},{1,5},{5... | collective-permute-start | bytes 1671176 | tf_op jit(solution)/shard_map/ppermute | solution.py:929
  136.8 19.3 %collective-permute-start.31 = (bf16[608,256]{1,0:T(8,128)(2,1)S(1)}, bf16[608,256]{1,0:T(8,128)(2,1)S(1)}, u32[]{:S(2)}, u32[]{:S(2)}) collective-permute-start(bf16[608,256]{1,0:T(8,128)(2,1)S(1)} %add_convert_fusion.9), channel_id=1, source_target_pairs={{0,16},{4,20},{8,24},{12,28},{16,0},{20,4},{24,8},{28,12},{1,17},{... | collective-permute-start | bytes 933896 | tf_op jit(solution)/shard_map/ppermute | solution.py:929
  156.7 7.0 %collective-permute-start.32 = (bf16[544,256]{1,0:T(8,128)(2,1)S(1)}, bf16[544,256]{1,0:T(8,128)(2,1)S(1)}, u32[]{:S(2)}, u32[]{:S(2)}) collective-permute-start(bf16[544,256]{1,0:T(8,128)(2,1)S(1)} %get-tuple-element.254), channel_id=1, source_target_pairs={{0,8},{4,12},{8,0},{12,4},{16,24},{20,28},{24,16},{28,20},{1,9},{5... | collective-permute-start | bytes 835592 | tf_op jit(solution)/shard_map/ppermute | solution.py:929
  163.8 12.2 %collective-permute-start.34 = (bf16[608,256]{1,0:T(8,128)(2,1)S(1)}, bf16[608,256]{1,0:T(8,128)(2,1)S(1)}, u32[]{:S(2)}, u32[]{:S(2)}) collective-permute-start(bf16[608,256]{1,0:T(8,128)(2,1)S(1)} %add_convert_fusion.8), channel_id=1, source_target_pairs={{0,8},{4,12},{8,0},{12,4},{16,24},{20,28},{24,16},{28,20},{1,9},{5... | collective-permute-start | bytes 933896 | tf_op jit(solution)/shard_map/ppermute | solution.py:929
  164.0 10.5 %collective-permute-start.33 = (bf16[544,256]{1,0:T(8,128)(2,1)S(1)}, bf16[544,256]{1,0:T(8,128)(2,1)S(1)}, u32[]{:S(2)}, u32[]{:S(2)}) collective-permute-start(bf16[544,256]{1,0:T(8,128)(2,1)S(1)} %add_convert_fusion.11), channel_id=1, source_target_pairs={{0,16},{4,20},{8,24},{12,28},{16,0},{20,4},{24,8},{28,12},{1,17},{... | collective-permute-start | bytes 835592 | tf_op jit(solution)/shard_map/ppermute | solution.py:929
  176.3 9.9 %collective-permute-start.35 = (bf16[544,256]{1,0:T(8,128)(2,1)S(1)}, bf16[544,256]{1,0:T(8,128)(2,1)S(1)}, u32[]{:S(2)}, u32[]{:S(2)}) collective-permute-start(bf16[544,256]{1,0:T(8,128)(2,1)S(1)} %add_convert_fusion.10), channel_id=1, source_target_pairs={{0,8},{4,12},{8,0},{12,4},{16,24},{20,28},{24,16},{28,20},{1,9},{5... | collective-permute-start | bytes 835592 | tf_op jit(solution)/shard_map/ppermute | solution.py:929
  (40 other events, 193.1 us)

commit v7 on v6

--- a/solution.py
+++ b/solution.py
@@ -634,7 +634,7 @@
         functools.partial(middle_kernel, places, len(pieces), groups, halves, held),
         grid=(1,),
         out_shape=outs,
-        in_specs=[SCALARS] + specs + [FAR] * len(pieces),
+        in_specs=[SCALARS] + specs + [whole_spec(a.shape) for a in pieces[:halves]] + [FAR] * (len(pieces) - halves),
         out_specs=[whole_spec(out.shape) for out in outs[:near]] + [FAR] * (len(outs) - near),
         scratch_shapes=[
             pltpu.VMEM((height, width), bf16),

time: 193 us -> 193 us (level)
  no operation moved by 1% of the time
where the time goes in v7:
time: 193 us; the launch traced here: 192 us
  Pallas kernels  82.9 us (43%)
  waiting for transfers between devices  56 us (29%)
  starting transfers between devices  32.2 us (17%)
  other arithmetic  11.4 us (6%)
  local copies, waits for them, and re-layouts  7.81 us (4%)
    ppermute x38, waiting for transfers between devices, flip(): return lax.ppermute(array, axis, [(i, i ^ bits) for i in range(size)])  56 us
    ppermute x38, starting transfers between devices, flip(): return lax.ppermute(array, axis, [(i, i ^ bits) for i in range(size)])  32.2 us
    pallas_call x1, Pallas kernels, middle_call(): pl.pallas_call(functools.partial(middle_kernel, places, len(pieces), grou...  29 us
    pallas_call x1, Pallas kernels, backward_call(): pl.pallas_call(functools.partial(backward_kernel, places, len(pieces), ea...  25.1 us
    pallas_call x2, Pallas kernels, forward_call(): pl.pallas_call(functools.partial(forward_kernel, places, len(pieces), eac...  21.1 us
    convert_element_type x9, other arithmetic, add_low(): return level[0].astype(bf16)  5.84 us
    pallas_call x2, Pallas kernels, finish_call(): pl.pallas_call(functools.partial(finish_kernel, names, held, rows, first)...  4.47 us
  transfers between devices with their start and end apart: 38, of which 19 were waited for; matrix products, arithmetic and copies ran while one was open for 4% of the time, Pallas kernels for 27%

profile of v7, /device:TPU:0, one launch (start us, length us, event | category | flops | bytes accessed | tf_op | source)
XLA Modules:
  0.0 191.9 jit_solution(14415016170069411724)
XLA Ops:
  2.7 3.0 %collective-permute-start = (bf16[2,528,256]{2,1,0:T(8,128)(2,1)S(1)}, bf16[2,528,256]{2,1,0:T(8,128)(2,1)}, u32[]{:S(2)}, u32[]{:S(2)}) collective-permute-start(bf16[2,528,256]{2,1,0:T(8,128)(2,1)S(1)} %pad_maximum_fusion.2.refs_3_.refs_18_), channel_id=1, source_target_pairs={{0,1},{1,0},{2,3},{3,2},{4,5},{5,4},{6,7},{7,6},{8,9},{9,8},{10,11... | collective-permute-start | bytes 1622024 | tf_op jit(solution)/shard_map/ppermute | solution.py:929
  9.5 3.2 %shard_map.230 = (bf16[1024,32]{1,0:T(8,128)(2,1)}, bf16[32,1024]{1,0:T(8,128)(2,1)}, f32[20,64,128]{2,1,0:T(8,128)}, bf16[8,32,256]{2,1,0:T(8,128)(2,1)}, bf16[8,32,512]{2,1,0:T(8,128)(2,1)}) custom-call(s32[3]{0:T(128)} %pad_add_fusion.place_ref.refs_0_, s32[1,256]{1,0:T(1,128)} %bitcast.91, s32[1,256]{1,0:T(1,128)} %bitcast.92, f32[64,32]{1,0:T(8,128)} %copy.40.logit_ref, ...), custom_call_target="tpu_custom_call" | custom-call | flops 33554432 | bytes 2097152 | tf_op jit(solution)/shard_map/pallas_call | solution.py:171
  14.9 3.3 %collective-permute-done.refs_5_.refs_20_ = bf16[2,528,256]{2,1,0:T(8,128)(2,1)} collective-permute-done((bf16[2,528,256]{2,1,0:T(8,128)(2,1)S(1)}, bf16[2,528,256]{2,1,0:T(8,128)(2,1)}, u32[]{:S(2)}, u32[]{:S(2)}) %collective-permute-start) | collective-permute-done | bytes 540704 | tf_op jit(solution)/shard_map/ppermute | solution.py:929
  20.5 1.7 collective-permute-start.10
  27.0 13.9 %shard_map.231 = (f32[1,1024,256]{2,1,0:T(8,128)}, bf16[8,2,1024,256]{3,2,1,0:T(8,128)(2,1)}, bf16[8,2,1024,256]{3,2,1,0:T(8,128)(2,1)}) custom-call(f32[1024,256]{1,0:T(8,128)} %refs_0_.5, bf16[1024,32]{1,0:T(8,128)(2,1)} %get-tuple-element.117.refs_1_.refs_2_, bf16[8,32,256]{2,1,0:T(8,128)(2,1)} %get-tuple-element.118.refs_2_.refs_5_, ...), custom_call_target="tpu_custom_call" | custom-call | flops 3221225472 | bytes 17825792 | tf_op jit(solution)/shard_map/pallas_call | solution.py:432
  45.3 7.1 %shard_map.232 = (f32[1,1024,256]{2,1,0:T(8,128)}, bf16[8,2,1024,256]{3,2,1,0:T(8,128)(2,1)}, bf16[8,2,1024,256]{3,2,1,0:T(8,128)(2,1)}) custom-call(f32[1024,256]{1,0:T(8,128)} %refs_0_.5, bf16[1024,32]{1,0:T(8,128)(2,1)} %get-tuple-element.117.refs_1_.refs_2_, ...), custom_call_target="tpu_custom_call", output_to_operand_aliasing={{1}: (4, {}), {2}: (5, {})} | custom-call | flops 1073741824 | bytes 7340032 | tf_op jit(solution)/shard_map/pallas_call | solution.py:432
  55.2 29.0 %shard_map.233 = (f32[2,1024]{1,0:T(2,128)}, f32[1024,256]{1,0:T(8,128)}, bf16[3,1216,256]{2,1,0:T(8,128)(2,1)}, bf16[1216,256]{1,0:T(8,128)(2,1)}, bf16[1216,25...) custom-call(s32[3]{0:T(128)} %pad_add_fusion.place_ref.refs_0_, ...), custom_call_target="tpu_custom_call" | custom-call | flops 15032385536 | bytes 12582912 | tf_op jit(solution)/shard_map/pallas_call | solution.py:633
  88.4 2.8 %fusion = (bf16[1216,256]{1,0:T(8,128)(2,1)}, bf16[1216,256]{1,0:T(8,128)(2,1)S(1)}, bf16[1216,256]{1,0:T(8,128)(2,1)S(1)}) fusion(bf16[1216,256]{1,0:T(8,128)(2,1)S(1)} %collective-permute-done.18, bf16[3,1216,256]{2,1,0:T(8,128)(2,1)} %get-tuple-element.138, bf16[1216,256]{1,0:T(8,128)(2,1)S(1)} %collective-permute-done.17, ...), kind=kLoop, calls=%fused_computation.1 | loop fusion | flops 3735552 | bytes 5603328 | tf_op jit(solution)/shard_map/convert_element_type | solution.py:936
  92.8 1.8 collective-permute-start.25
  94.6 25.1 %shard_map.234 = (f32[1024,256]{1,0:T(8,128)}, bf16[4,1088,256]{2,1,0:T(8,128)(2,1)}, bf16[1088,256]{1,0:T(8,128)(2,1)}, bf16[1088,256]{1,0:T(8,128)(2,1)}, bf16...) custom-call(f32[1024,256]{1,0:T(8,128)} %refs_0_.5, ...), custom_call_target="tpu_custom_call" | custom-call | flops 10737418240 | bytes 29360128 | tf_op jit(solution)/shard_map/pallas_call | solution.py:838
  125.0 1.9 fusion.3
  130.2 1.8 collective-permute-start.28
  132.0 4.4 %collective-permute-done.30 = bf16[608,256]{1,0:T(8,128)(2,1)S(1)} collective-permute-done((bf16[608,256]{1,0:T(8,128)(2,1)S(1)}, bf16[608,256]{1,0:T(8,128)(2,1)S(1)}, u32[]{:S(2)}, u32[]{:S(2)}) %collective-permute-start.30) | collective-permute-done | bytes 311328 | tf_op jit(solution)/shard_map/ppermute | solution.py:929
  136.5 2.6 %collective-permute-start.31 = (bf16[608,256]{1,0:T(8,128)(2,1)S(1)}, bf16[608,256]{1,0:T(8,128)(2,1)S(1)}, u32[]{:S(2)}, u32[]{:S(2)}) collective-permute-start(bf16[608,256]{1,0:T(8,128)(2,1)S(1)} %add_convert_fusion.9), channel_id=1, source_target_pairs={{0,16},{4,20},{8,24},{12,28},{16,0},{20,4},{24,8},{28,12},{1,17},{... | collective-permute-start | bytes 933896 | tf_op jit(solution)/shard_map/ppermute | solution.py:929
  139.1 4.9 %collective-permute-done.26 = bf16[1088,256]{1,0:T(8,128)(2,1)S(1)} collective-permute-done((bf16[1088,256]{1,0:T(8,128)(2,1)S(1)}, bf16[1088,256]{1,0:T(8,128)(2,1)S(1)}, u32[]{:S(2)}, u32[]{:S(2)}) %collective-permute-start.26) | collective-permute-done | bytes 557088 | tf_op jit(solution)/shard_map/ppermute | solution.py:929
  144.0 11.7 %collective-permute-done.27 = bf16[1088,256]{1,0:T(8,128)(2,1)S(1)} collective-permute-done((bf16[1088,256]{1,0:T(8,128)(2,1)S(1)}, bf16[1088,256]{1,0:T(8,128)(2,1)S(1)}, u32[]{:S(2)}, u32[]{:S(2)}) %collective-permute-start.27) | collective-permute-done | bytes 557088 | tf_op jit(solution)/shard_map/ppermute | solution.py:929
  156.8 6.2 %collective-permute-done.32 = bf16[544,256]{1,0:T(8,128)(2,1)S(1)} collective-permute-done((bf16[544,256]{1,0:T(8,128)(2,1)S(1)}, bf16[544,256]{1,0:T(8,128)(2,1)S(1)}, u32[]{:S(2)}, u32[]{:S(2)}) %collective-permute-start.32) | collective-permute-done | bytes 278560 | tf_op jit(solution)/shard_map/ppermute | solution.py:929
  163.7 2.6 %collective-permute-start.33 = (bf16[544,256]{1,0:T(8,128)(2,1)S(1)}, bf16[544,256]{1,0:T(8,128)(2,1)S(1)}, u32[]{:S(2)}, u32[]{:S(2)}) collective-permute-start(bf16[544,256]{1,0:T(8,128)(2,1)S(1)} %add_convert_fusion.11), channel_id=1, source_target_pairs={{0,16},{4,20},{8,24},{12,28},{16,0},{20,4},{24,8},{28,12},{1,17},{... | collective-permute-start | bytes 835592 | tf_op jit(solution)/shard_map/ppermute | solution.py:929
  166.3 7.9 %collective-permute-done.33 = bf16[544,256]{1,0:T(8,128)(2,1)S(1)} collective-permute-done((bf16[544,256]{1,0:T(8,128)(2,1)S(1)}, bf16[544,256]{1,0:T(8,128)(2,1)S(1)}, u32[]{:S(2)}, u32[]{:S(2)}) %collective-permute-start.33) | collective-permute-done | bytes 278560 | tf_op jit(solution)/shard_map/ppermute | solution.py:929
  176.0 2.6 %collective-permute-start.35 = (bf16[544,256]{1,0:T(8,128)(2,1)S(1)}, bf16[544,256]{1,0:T(8,128)(2,1)S(1)}, u32[]{:S(2)}, u32[]{:S(2)}) collective-permute-start(bf16[544,256]{1,0:T(8,128)(2,1)S(1)} %add_convert_fusion.10), channel_id=1, source_target_pairs={{0,8},{4,12},{8,0},{12,4},{16,24},{20,28},{24,16},{28,20},{1,9},{5... | collective-permute-start | bytes 835592 | tf_op jit(solution)/shard_map/ppermute | solution.py:929
  179.2 1.9 %shard_map.235 = (f32[2,4,256,256]{3,2,1,0:T(8,128)}, f32[2,4,256,256]{3,2,1,0:T(8,128)}, f32[2,4,256]{2,1,0:T(4,128)S(1)}, f32[2,4,256]{2,1,0:T(4,128)S(1)}) custom-call(s32[3]{0:T(128)S(1)} %copy-done, bf16[1216,256]{1,0:T(8,128)(2,1)S(1)} %pad_maximum_fusion.refs_1_, bf16[1216,256]{1,0:T(8,128)(2,1)S(1)} %collective-permute-done.36.refs_2_), custom_call_target="tpu_custom_call" | custom-call | bytes 3145728 | tf_op jit(solution)/shard_map/pallas_call | solution.py:912
  181.9 3.9 %collective-permute-done.35 = bf16[544,256]{1,0:T(8,128)(2,1)S(1)} collective-permute-done((bf16[544,256]{1,0:T(8,128)(2,1)S(1)}, bf16[544,256]{1,0:T(8,128)(2,1)S(1)}, u32[]{:S(2)}, u32[]{:S(2)}) %collective-permute-start.35) | collective-permute-done | bytes 278560 | tf_op jit(solution)/shard_map/ppermute | solution.py:929
  186.2 1.8 collective-permute-done.37.refs_2_
  189.2 2.5 %shard_map.236 = (f32[2,4,256,256]{3,2,1,0:T(8,128)}, f32[2,4,256,256]{3,2,1,0:T(8,128)}, f32[2,4,256]{2,1,0:T(4,128)}, f32[2,4,256]{2,1,0:T(4,128)}) custom-call(s32[3]{0:T(128)S(1)} %copy-done, bf16[1088,256]{1,0:T(8,128)(2,1)S(1)} %pad_maximum_fusion.1.refs_1_, ...), custom_call_target="tpu_custom_call", output_to_operand_aliasing={{0}: (3, {}), {1}: (4, {})} | custom-call | bytes 3145728 | tf_op jit(solution)/shard_map/pallas_call | solution.py:912
  (176 shorter events, 42.5 us)
Async XLA Ops:
  2.7 15.4 %collective-permute-start = (bf16[2,528,256]{2,1,0:T(8,128)(2,1)S(1)}, bf16[2,528,256]{2,1,0:T(8,128)(2,1)}, u32[]{:S(2)}, u32[]{:S(2)}) collective-permute-start(bf16[2,528,256]{2,1,0:T(8,128)(2,1)S(1)} %pad_maximum_fusion.2.refs_3_.refs_18_), channel_id=1, source_target_pairs={{0,1},{1,0},{2,3},{3,2},{4,5},{5,4},{6,7},{7,6},{8,9},{9,8},{10,11... | collective-permute-start | bytes 1622024 | tf_op jit(solution)/shard_map/ppermute | solution.py:929
  5.7 13.8 %collective-permute-start.1 = (bf16[2,528,256]{2,1,0:T(8,128)(2,1)S(1)}, bf16[2,528,256]{2,1,0:T(8,128)(2,1)}, u32[]{:S(2)}, u32[]{:S(2)}) collective-permute-start(bf16[2,528,256]{2,1,0:T(8,128)(2,1)S(1)} %pad_maximum_fusion.2.refs_3_.refs_18_), channel_id=1, source_target_pairs={{0,2},{1,3},{2,0},{3,1},{4,6},{5,7},{6,4},{7,5},{8,10},{9,11},{10,... | collective-permute-start | bytes 1622024 | tf_op jit(solution)/shard_map/ppermute | solution.py:929
  19.6 6.6 %collective-permute-start.3 = (bf16[2,528,256]{2,1,0:T(8,128)(2,1)}, bf16[2,528,256]{2,1,0:T(8,128)(2,1)S(1)}, u32[]{:S(2)}, u32[]{:S(2)}) collective-permute-start(bf16[2,528,256]{2,1,0:T(8,128)(2,1)} %collective-permute-done.1.refs_7_.refs_22_), channel_id=1, source_target_pairs={{0,4},{4,0},{8,12},{12,8},{16,20},{20,16},{24,28},{28,24},{1,5},{5... | collective-permute-start | bytes 1622024 | tf_op jit(solution)/shard_map/ppermute | solution.py:929
  20.1 21.5 %collective-permute-start.8 = (bf16[2,528,256]{2,1,0:T(8,128)(2,1)S(1)}, bf16[2,528,256]{2,1,0:T(8,128)(2,1)S(1)}, u32[]{:S(2)}, u32[]{:S(2)}) collective-permute-start(bf16[2,528,256]{2,1,0:T(8,128)(2,1)S(1)} %pad_maximum_fusion.4.refs_10_.refs_16_), channel_id=1, source_target_pairs={{0,1},{1,0},{2,3},{3,2},{4,5},{5,4},{6,7},{7,6},{8,9},{9,8},{10,11... | collective-permute-start | bytes 1622024 | tf_op jit(solution)/shard_map/ppermute | solution.py:929
  20.5 22.7 %collective-permute-start.10 = (bf16[2,528,256]{2,1,0:T(8,128)(2,1)S(1)}, bf16[2,528,256]{2,1,0:T(8,128)(2,1)S(1)}, u32[]{:S(2)}, u32[]{:S(2)}) collective-permute-start(bf16[2,528,256]{2,1,0:T(8,128)(2,1)S(1)} %pad_maximum_fusion.4.refs_10_.refs_16_), channel_id=1, source_target_pairs={{0,2},{1,3},{2,0},{3,1},{4,6},{5,7},{6,4},{7,5},{8,10},{9,11},{10,... | collective-permute-start | bytes 1622024 | tf_op jit(solution)/shard_map/ppermute | solution.py:929
  24.1 16.8 %collective-permute-start.4 = (bf16[1,528,256]{2,1,0:T(8,128)(2,1)S(1)}, bf16[1,528,256]{2,1,0:T(8,128)(2,1)S(1)}, u32[]{:S(2)}, u32[]{:S(2)}) collective-permute-start(bf16[1,528,256]{2,1,0:T(8,128)(2,1)S(1)} %slice.102), channel_id=1, source_target_pairs={{0,2},{1,3},{2,0},{3,1},{4,6},{5,7},{6,4},{7,5},{8,10},{9,11},{10,... | collective-permute-start | bytes 811016 | tf_op jit(solution)/shard_map/ppermute | solution.py:929
  24.5 16.4 %collective-permute-start.5 = (bf16[1,528,256]{2,1,0:T(8,128)(2,1)S(1)}, bf16[1,528,256]{2,1,0:T(8,128)(2,1)S(1)}, u32[]{:S(2)}, u32[]{:S(2)}) collective-permute-start(bf16[1,528,256]{2,1,0:T(8,128)(2,1)S(1)} %slice.103), channel_id=1, source_target_pairs={{0,1},{1,0},{2,3},{3,2},{4,5},{5,4},{6,7},{7,6},{8,9},{9,8},{10,11... | collective-permute-start | bytes 811016 | tf_op jit(solution)/shard_map/ppermute | solution.py:929
  41.6 10.9 %collective-permute-start.12 = (bf16[1,528,256]{2,1,0:T(8,128)(2,1)S(1)}, bf16[1,528,256]{2,1,0:T(8,128)(2,1)S(1)}, u32[]{:S(2)}, u32[]{:S(2)}) collective-permute-start(bf16[1,528,256]{2,1,0:T(8,128)(2,1)S(1)} %slice.134), channel_id=1, source_target_pairs={{0,2},{1,3},{2,0},{3,1},{4,6},{5,7},{6,4},{7,5},{8,10},{9,11},{10,... | collective-permute-start | bytes 811016 | tf_op jit(solution)/shard_map/ppermute | solution.py:929
  43.2 9.3 %collective-permute-start.13 = (bf16[1,528,256]{2,1,0:T(8,128)(2,1)S(1)}, bf16[1,528,256]{2,1,0:T(8,128)(2,1)S(1)}, u32[]{:S(2)}, u32[]{:S(2)}) collective-permute-start(bf16[1,528,256]{2,1,0:T(8,128)(2,1)S(1)} %slice.135), channel_id=1, source_target_pairs={{0,1},{1,0},{2,3},{3,2},{4,5},{5,4},{6,7},{7,6},{8,9},{9,8},{10,11... | collective-permute-start | bytes 811016 | tf_op jit(solution)/shard_map/ppermute | solution.py:929
  44.1 9.0 %collective-permute-start.9 = (bf16[2,528,256]{2,1,0:T(8,128)(2,1)S(1)}, bf16[2,528,256]{2,1,0:T(8,128)(2,1)S(1)}, u32[]{:S(2)}, u32[]{:S(2)}) collective-permute-start(bf16[2,528,256]{2,1,0:T(8,128)(2,1)S(1)} %collective-permute-done.8.refs_12_), channel_id=1, source_target_pairs={{0,4},{4,0},{8,12},{12,8},{16,20},{20,16},{24,28},{28,24},{1,5},{5... | collective-permute-start | bytes 1622024 | tf_op jit(solution)/shard_map/ppermute | solution.py:929
  44.1 9.0 %collective-permute-start.11 = (bf16[2,528,256]{2,1,0:T(8,128)(2,1)S(1)}, bf16[2,528,256]{2,1,0:T(8,128)(2,1)S(1)}, u32[]{:S(2)}, u32[]{:S(2)}) collective-permute-start(bf16[2,528,256]{2,1,0:T(8,128)(2,1)S(1)} %collective-permute-done.10.refs_14_), channel_id=1, source_target_pairs={{0,4},{4,0},{8,12},{12,8},{16,20},{20,16},{24,28},{28,24},{1,5},{5... | collective-permute-start | bytes 1622024 | tf_op jit(solution)/shard_map/ppermute | solution.py:929
  91.1 29.2 %collective-permute-start.23 = (bf16[1216,256]{1,0:T(8,128)(2,1)S(1)}, bf16[1216,256]{1,0:T(8,128)(2,1)S(1)}, u32[]{:S(2)}, u32[]{:S(2)}) collective-permute-start(bf16[1216,256]{1,0:T(8,128)(2,1)S(1)} %get-tuple-element.163), channel_id=1, source_target_pairs={{0,1},{1,0},{2,3},{3,2},{4,5},{5,4},{6,7},{7,6},{8,9},{9,8},{10,11... | collective-permute-start | bytes 1867784 | tf_op jit(solution)/shard_map/ppermute | solution.py:929
  92.3 29.1 %collective-permute-start.24 = (bf16[1216,256]{1,0:T(8,128)(2,1)S(1)}, bf16[1216,256]{1,0:T(8,128)(2,1)S(1)}, u32[]{:S(2)}, u32[]{:S(2)}) collective-permute-start(bf16[1216,256]{1,0:T(8,128)(2,1)S(1)} %get-tuple-element.164), channel_id=1, source_target_pairs={{0,2},{1,3},{2,0},{3,1},{4,6},{5,7},{6,4},{7,5},{8,10},{9,11},{10,... | collective-permute-start | bytes 1867784 | tf_op jit(solution)/shard_map/ppermute | solution.py:929
  92.8 28.6 %collective-permute-start.25 = (bf16[1216,256]{1,0:T(8,128)(2,1)}, bf16[1216,256]{1,0:T(8,128)(2,1)S(1)}, u32[]{:S(2)}, u32[]{:S(2)}) collective-permute-start(bf16[1216,256]{1,0:T(8,128)(2,1)} %get-tuple-element.165), channel_id=1, source_target_pairs={{0,3},{1,2},{2,1},{3,0},{4,7},{5,6},{6,5},{7,4},{8,11},{9,10},{10,... | collective-permute-start | bytes 1867784 | tf_op jit(solution)/shard_map/ppermute | solution.py:929
  126.9 9.5 %collective-permute-start.30 = (bf16[608,256]{1,0:T(8,128)(2,1)S(1)}, bf16[608,256]{1,0:T(8,128)(2,1)S(1)}, u32[]{:S(2)}, u32[]{:S(2)}) collective-permute-start(bf16[608,256]{1,0:T(8,128)(2,1)S(1)} %get-tuple-element.250), channel_id=1, source_target_pairs={{0,8},{4,12},{8,0},{12,4},{16,24},{20,28},{24,16},{28,20},{1,9},{5... | collective-permute-start | bytes 933896 | tf_op jit(solution)/shard_map/ppermute | solution.py:929
  128.5 15.5 %collective-permute-start.26 = (bf16[1088,256]{1,0:T(8,128)(2,1)S(1)}, bf16[1088,256]{1,0:T(8,128)(2,1)S(1)}, u32[]{:S(2)}, u32[]{:S(2)}) collective-permute-start(bf16[1088,256]{1,0:T(8,128)(2,1)S(1)} %get-tuple-element.178), channel_id=1, source_target_pairs={{0,1},{1,0},{2,3},{3,2},{4,5},{5,4},{6,7},{7,6},{8,9},{9,8},{10,11... | collective-permute-start | bytes 1671176 | tf_op jit(solution)/shard_map/ppermute | solution.py:929
  129.7 26.0 %collective-permute-start.27 = (bf16[1088,256]{1,0:T(8,128)(2,1)S(1)}, bf16[1088,256]{1,0:T(8,128)(2,1)S(1)}, u32[]{:S(2)}, u32[]{:S(2)}) collective-permute-start(bf16[1088,256]{1,0:T(8,128)(2,1)S(1)} %get-tuple-element.179), channel_id=1, source_target_pairs={{0,2},{1,3},{2,0},{3,1},{4,6},{5,7},{6,4},{7,5},{8,10},{9,11},{10,... | collective-permute-start | bytes 1671176 | tf_op jit(solution)/shard_map/ppermute | solution.py:929
  130.2 25.5 %collective-permute-start.28 = (bf16[1088,256]{1,0:T(8,128)(2,1)S(1)}, bf16[1088,256]{1,0:T(8,128)(2,1)S(1)}, u32[]{:S(2)}, u32[]{:S(2)}) collective-permute-start(bf16[1088,256]{1,0:T(8,128)(2,1)S(1)} %get-tuple-element.180), channel_id=1, source_target_pairs={{0,3},{1,2},{2,1},{3,0},{4,7},{5,6},{6,5},{7,4},{8,11},{9,10},{10,... | collective-permute-start | bytes 1671176 | tf_op jit(solution)/shard_map/ppermute | solution.py:929
  132.0 23.8 %collective-permute-start.29 = (bf16[1088,256]{1,0:T(8,128)(2,1)S(1)}, bf16[1088,256]{1,0:T(8,128)(2,1)S(1)}, u32[]{:S(2)}, u32[]{:S(2)}) collective-permute-start(bf16[1088,256]{1,0:T(8,128)(2,1)S(1)} %copy-done.17), channel_id=1, source_target_pairs={{0,4},{4,0},{8,12},{12,8},{16,20},{20,16},{24,28},{28,24},{1,5},{5... | collective-permute-start | bytes 1671176 | tf_op jit(solution)/shard_map/ppermute | solution.py:929
  136.5 19.3 %collective-permute-start.31 = (bf16[608,256]{1,0:T(8,128)(2,1)S(1)}, bf16[608,256]{1,0:T(8,128)(2,1)S(1)}, u32[]{:S(2)}, u32[]{:S(2)}) collective-permute-start(bf16[608,256]{1,0:T(8,128)(2,1)S(1)} %add_convert_fusion.9), channel_id=1, source_target_pairs={{0,16},{4,20},{8,24},{12,28},{16,0},{20,4},{24,8},{28,12},{1,17},{... | collective-permute-start | bytes 933896 | tf_op jit(solution)/shard_map/ppermute | solution.py:929
  156.3 6.8 %collective-permute-start.32 = (bf16[544,256]{1,0:T(8,128)(2,1)S(1)}, bf16[544,256]{1,0:T(8,128)(2,1)S(1)}, u32[]{:S(2)}, u32[]{:S(2)}) collective-permute-start(bf16[544,256]{1,0:T(8,128)(2,1)S(1)} %get-tuple-element.254), channel_id=1, source_target_pairs={{0,8},{4,12},{8,0},{12,4},{16,24},{20,28},{24,16},{28,20},{1,9},{5... | collective-permute-start | bytes 835592 | tf_op jit(solution)/shard_map/ppermute | solution.py:929
  163.2 12.5 %collective-permute-start.34 = (bf16[608,256]{1,0:T(8,128)(2,1)S(1)}, bf16[608,256]{1,0:T(8,128)(2,1)S(1)}, u32[]{:S(2)}, u32[]{:S(2)}) collective-permute-start(bf16[608,256]{1,0:T(8,128)(2,1)S(1)} %add_convert_fusion.8), channel_id=1, source_target_pairs={{0,8},{4,12},{8,0},{12,4},{16,24},{20,28},{24,16},{28,20},{1,9},{5... | collective-permute-start | bytes 933896 | tf_op jit(solution)/shard_map/ppermute | solution.py:929
  163.7 10.5 %collective-permute-start.33 = (bf16[544,256]{1,0:T(8,128)(2,1)S(1)}, bf16[544,256]{1,0:T(8,128)(2,1)S(1)}, u32[]{:S(2)}, u32[]{:S(2)}) collective-permute-start(bf16[544,256]{1,0:T(8,128)(2,1)S(1)} %add_convert_fusion.11), channel_id=1, source_target_pairs={{0,16},{4,20},{8,24},{12,28},{16,0},{20,4},{24,8},{28,12},{1,17},{... | collective-permute-start | bytes 835592 | tf_op jit(solution)/shard_map/ppermute | solution.py:929
  176.0 9.9 %collective-permute-start.35 = (bf16[544,256]{1,0:T(8,128)(2,1)S(1)}, bf16[544,256]{1,0:T(8,128)(2,1)S(1)}, u32[]{:S(2)}, u32[]{:S(2)}) collective-permute-start(bf16[544,256]{1,0:T(8,128)(2,1)S(1)} %add_convert_fusion.10), channel_id=1, source_target_pairs={{0,8},{4,12},{8,0},{12,4},{16,24},{20,28},{24,16},{28,20},{1,9},{5... | collective-permute-start | bytes 835592 | tf_op jit(solution)/shard_map/ppermute | solution.py:929
  (40 other events, 193.1 us)

commit v8 on v7

--- a/solution.py
+++ b/solution.py
@@ -214,7 +214,7 @@
     kinds = total_ref.shape[0]
     bias_in, bias_out = zip(*(bias_rows(w, width) for w in weights))
     second = joined([w[width : 2 * width] for w in weights], 0)
-    for rows in tiles(height, TILE):
+    for rows in tiles(height, TILE // 2):
         gates = gates_of(type_ref[rows], value_ref, len(weights) * kinds)
         if keep_gate is not None:
             for at, gate in enumerate(gates):

time: 193 us -> 192 us (level)
  no operation moved by 1% of the time
where the time goes in v8:
time: 192 us; the launch traced here: 191 us
  Pallas kernels  82.1 us (43%)
  waiting for transfers between devices  55.9 us (29%)
  starting transfers between devices  32.5 us (17%)
  other arithmetic  11.4 us (6%)
  local copies, waits for them, and re-layouts  7.81 us (4%)
    ppermute x38, waiting for transfers between devices, flip(): return lax.ppermute(array, axis, [(i, i ^ bits) for i in range(size)])  55.9 us
    ppermute x38, starting transfers between devices, flip(): return lax.ppermute(array, axis, [(i, i ^ bits) for i in range(size)])  32.5 us
    pallas_call x1, Pallas kernels, middle_call(): pl.pallas_call(functools.partial(middle_kernel, places, len(pieces), grou...  28.4 us
    pallas_call x1, Pallas kernels, backward_call(): pl.pallas_call(functools.partial(backward_kernel, places, len(pieces), ea...  25.1 us
    pallas_call x2, Pallas kernels, forward_call(): pl.pallas_call(functools.partial(forward_kernel, places, len(pieces), eac...  20.9 us
    convert_element_type x9, other arithmetic, add_low(): return level[0].astype(bf16)  5.84 us
    pallas_call x2, Pallas kernels, finish_call(): pl.pallas_call(functools.partial(finish_kernel, names, held, rows, first)...  4.47 us
  transfers between devices with their start and end apart: 38, of which 19 were waited for; matrix products, arithmetic and copies ran while one was open for 4% of the time, Pallas kernels for 27%

profile of v8, /device:TPU:0, one launch (start us, length us, event | category | flops | bytes accessed | tf_op | source)
XLA Modules:
  0.0 191.2 jit_solution(4259808825100038937)
XLA Ops:
  2.7 3.0 %collective-permute-start = (bf16[2,528,256]{2,1,0:T(8,128)(2,1)S(1)}, bf16[2,528,256]{2,1,0:T(8,128)(2,1)}, u32[]{:S(2)}, u32[]{:S(2)}) collective-permute-start(bf16[2,528,256]{2,1,0:T(8,128)(2,1)S(1)} %pad_maximum_fusion.2.refs_3_.refs_18_), channel_id=1, source_target_pairs={{0,1},{1,0},{2,3},{3,2},{4,5},{5,4},{6,7},{7,6},{8,9},{9,8},{10,11... | collective-permute-start | bytes 1622024 | tf_op jit(solution)/shard_map/ppermute | solution.py:929
  9.5 3.2 %shard_map.230 = (bf16[1024,32]{1,0:T(8,128)(2,1)}, bf16[32,1024]{1,0:T(8,128)(2,1)}, f32[20,64,128]{2,1,0:T(8,128)}, bf16[8,32,256]{2,1,0:T(8,128)(2,1)}, bf16[8,32,512]{2,1,0:T(8,128)(2,1)}) custom-call(s32[3]{0:T(128)} %pad_add_fusion.place_ref.refs_0_, s32[1,256]{1,0:T(1,128)} %bitcast.91, s32[1,256]{1,0:T(1,128)} %bitcast.92, f32[64,32]{1,0:T(8,128)} %copy.40.logit_ref, ...), custom_call_target="tpu_custom_call" | custom-call | flops 33554432 | bytes 2097152 | tf_op jit(solution)/shard_map/pallas_call | solution.py:171
  14.9 3.3 %collective-permute-done.refs_5_.refs_20_ = bf16[2,528,256]{2,1,0:T(8,128)(2,1)} collective-permute-done((bf16[2,528,256]{2,1,0:T(8,128)(2,1)S(1)}, bf16[2,528,256]{2,1,0:T(8,128)(2,1)}, u32[]{:S(2)}, u32[]{:S(2)}) %collective-permute-start) | collective-permute-done | bytes 540704 | tf_op jit(solution)/shard_map/ppermute | solution.py:929
  20.5 1.7 collective-permute-start.10
  27.0 13.8 %shard_map.231 = (f32[1,1024,256]{2,1,0:T(8,128)}, bf16[8,2,1024,256]{3,2,1,0:T(8,128)(2,1)}, bf16[8,2,1024,256]{3,2,1,0:T(8,128)(2,1)}) custom-call(f32[1024,256]{1,0:T(8,128)} %refs_0_.5, bf16[1024,32]{1,0:T(8,128)(2,1)} %get-tuple-element.117.refs_1_.refs_2_, bf16[8,32,256]{2,1,0:T(8,128)(2,1)} %get-tuple-element.118.refs_2_.refs_5_, ...), custom_call_target="tpu_custom_call" | custom-call | flops 3221225472 | bytes 17825792 | tf_op jit(solution)/shard_map/pallas_call | solution.py:432
  45.3 7.1 %shard_map.232 = (f32[1,1024,256]{2,1,0:T(8,128)}, bf16[8,2,1024,256]{3,2,1,0:T(8,128)(2,1)}, bf16[8,2,1024,256]{3,2,1,0:T(8,128)(2,1)}) custom-call(f32[1024,256]{1,0:T(8,128)} %refs_0_.5, bf16[1024,32]{1,0:T(8,128)(2,1)} %get-tuple-element.117.refs_1_.refs_2_, ...), custom_call_target="tpu_custom_call", output_to_operand_aliasing={{1}: (4, {}), {2}: (5, {})} | custom-call | flops 1073741824 | bytes 7340032 | tf_op jit(solution)/shard_map/pallas_call | solution.py:432
  55.2 28.4 %shard_map.233 = (f32[2,1024]{1,0:T(2,128)}, f32[1024,256]{1,0:T(8,128)}, bf16[3,1216,256]{2,1,0:T(8,128)(2,1)}, bf16[1216,256]{1,0:T(8,128)(2,1)}, bf16[1216,25...) custom-call(s32[3]{0:T(128)} %pad_add_fusion.place_ref.refs_0_, ...), custom_call_target="tpu_custom_call" | custom-call | flops 15032385536 | bytes 12582912 | tf_op jit(solution)/shard_map/pallas_call | solution.py:633
  87.7 2.8 %fusion = (bf16[1216,256]{1,0:T(8,128)(2,1)}, bf16[1216,256]{1,0:T(8,128)(2,1)S(1)}, bf16[1216,256]{1,0:T(8,128)(2,1)S(1)}) fusion(bf16[1216,256]{1,0:T(8,128)(2,1)S(1)} %collective-permute-done.18, bf16[3,1216,256]{2,1,0:T(8,128)(2,1)} %get-tuple-element.138, bf16[1216,256]{1,0:T(8,128)(2,1)S(1)} %collective-permute-done.17, ...), kind=kLoop, calls=%fused_computation.1 | loop fusion | flops 3735552 | bytes 5603328 | tf_op jit(solution)/shard_map/convert_element_type | solution.py:936
  92.0 1.9 collective-permute-start.25
  94.0 25.1 %shard_map.234 = (f32[1024,256]{1,0:T(8,128)}, bf16[4,1088,256]{2,1,0:T(8,128)(2,1)}, bf16[1088,256]{1,0:T(8,128)(2,1)}, bf16[1088,256]{1,0:T(8,128)(2,1)}, bf16...) custom-call(f32[1024,256]{1,0:T(8,128)} %refs_0_.5, ...), custom_call_target="tpu_custom_call" | custom-call | flops 10737418240 | bytes 29360128 | tf_op jit(solution)/shard_map/pallas_call | solution.py:838
  124.3 1.9 fusion.3
  129.4 1.9 %collective-permute-start.28 = (bf16[1088,256]{1,0:T(8,128)(2,1)S(1)}, bf16[1088,256]{1,0:T(8,128)(2,1)S(1)}, u32[]{:S(2)}, u32[]{:S(2)}) collective-permute-start(bf16[1088,256]{1,0:T(8,128)(2,1)S(1)} %get-tuple-element.180), channel_id=1, source_target_pairs={{0,3},{1,2},{2,1},{3,0},{4,7},{5,6},{6,5},{7,4},{8,11},{9,10},{10,... | collective-permute-start | bytes 1671176 | tf_op jit(solution)/shard_map/ppermute | solution.py:929
  131.4 4.3 %collective-permute-done.30 = bf16[608,256]{1,0:T(8,128)(2,1)S(1)} collective-permute-done((bf16[608,256]{1,0:T(8,128)(2,1)S(1)}, bf16[608,256]{1,0:T(8,128)(2,1)S(1)}, u32[]{:S(2)}, u32[]{:S(2)}) %collective-permute-start.30) | collective-permute-done | bytes 311328 | tf_op jit(solution)/shard_map/ppermute | solution.py:929
  135.8 2.7 %collective-permute-start.31 = (bf16[608,256]{1,0:T(8,128)(2,1)S(1)}, bf16[608,256]{1,0:T(8,128)(2,1)S(1)}, u32[]{:S(2)}, u32[]{:S(2)}) collective-permute-start(bf16[608,256]{1,0:T(8,128)(2,1)S(1)} %add_convert_fusion.9), channel_id=1, source_target_pairs={{0,16},{4,20},{8,24},{12,28},{16,0},{20,4},{24,8},{28,12},{1,17},{... | collective-permute-start | bytes 933896 | tf_op jit(solution)/shard_map/ppermute | solution.py:929
  138.4 4.9 %collective-permute-done.26 = bf16[1088,256]{1,0:T(8,128)(2,1)S(1)} collective-permute-done((bf16[1088,256]{1,0:T(8,128)(2,1)S(1)}, bf16[1088,256]{1,0:T(8,128)(2,1)S(1)}, u32[]{:S(2)}, u32[]{:S(2)}) %collective-permute-start.26) | collective-permute-done | bytes 557088 | tf_op jit(solution)/shard_map/ppermute | solution.py:929
  143.4 11.6 %collective-permute-done.27 = bf16[1088,256]{1,0:T(8,128)(2,1)S(1)} collective-permute-done((bf16[1088,256]{1,0:T(8,128)(2,1)S(1)}, bf16[1088,256]{1,0:T(8,128)(2,1)S(1)}, u32[]{:S(2)}, u32[]{:S(2)}) %collective-permute-start.27) | collective-permute-done | bytes 557088 | tf_op jit(solution)/shard_map/ppermute | solution.py:929
  156.1 6.3 %collective-permute-done.32 = bf16[544,256]{1,0:T(8,128)(2,1)S(1)} collective-permute-done((bf16[544,256]{1,0:T(8,128)(2,1)S(1)}, bf16[544,256]{1,0:T(8,128)(2,1)S(1)}, u32[]{:S(2)}, u32[]{:S(2)}) %collective-permute-start.32) | collective-permute-done | bytes 278560 | tf_op jit(solution)/shard_map/ppermute | solution.py:929
  162.9 2.6 %collective-permute-start.33 = (bf16[544,256]{1,0:T(8,128)(2,1)S(1)}, bf16[544,256]{1,0:T(8,128)(2,1)S(1)}, u32[]{:S(2)}, u32[]{:S(2)}) collective-permute-start(bf16[544,256]{1,0:T(8,128)(2,1)S(1)} %add_convert_fusion.11), channel_id=1, source_target_pairs={{0,16},{4,20},{8,24},{12,28},{16,0},{20,4},{24,8},{28,12},{1,17},{... | collective-permute-start | bytes 835592 | tf_op jit(solution)/shard_map/ppermute | solution.py:929
  165.5 7.9 %collective-permute-done.33 = bf16[544,256]{1,0:T(8,128)(2,1)S(1)} collective-permute-done((bf16[544,256]{1,0:T(8,128)(2,1)S(1)}, bf16[544,256]{1,0:T(8,128)(2,1)S(1)}, u32[]{:S(2)}, u32[]{:S(2)}) %collective-permute-start.33) | collective-permute-done | bytes 278560 | tf_op jit(solution)/shard_map/ppermute | solution.py:929
  175.3 2.7 %collective-permute-start.35 = (bf16[544,256]{1,0:T(8,128)(2,1)S(1)}, bf16[544,256]{1,0:T(8,128)(2,1)S(1)}, u32[]{:S(2)}, u32[]{:S(2)}) collective-permute-start(bf16[544,256]{1,0:T(8,128)(2,1)S(1)} %add_convert_fusion.10), channel_id=1, source_target_pairs={{0,8},{4,12},{8,0},{12,4},{16,24},{20,28},{24,16},{28,20},{1,9},{5... | collective-permute-start | bytes 835592 | tf_op jit(solution)/shard_map/ppermute | solution.py:929
  178.6 1.9 %shard_map.235 = (f32[2,4,256,256]{3,2,1,0:T(8,128)}, f32[2,4,256,256]{3,2,1,0:T(8,128)}, f32[2,4,256]{2,1,0:T(4,128)S(1)}, f32[2,4,256]{2,1,0:T(4,128)S(1)}) custom-call(s32[3]{0:T(128)S(1)} %copy-done, bf16[1216,256]{1,0:T(8,128)(2,1)S(1)} %pad_maximum_fusion.refs_1_, bf16[1216,256]{1,0:T(8,128)(2,1)S(1)} %collective-permute-done.36.refs_2_), custom_call_target="tpu_custom_call" | custom-call | bytes 3145728 | tf_op jit(solution)/shard_map/pallas_call | solution.py:912
  181.3 3.9 %collective-permute-done.35 = bf16[544,256]{1,0:T(8,128)(2,1)S(1)} collective-permute-done((bf16[544,256]{1,0:T(8,128)(2,1)S(1)}, bf16[544,256]{1,0:T(8,128)(2,1)S(1)}, u32[]{:S(2)}, u32[]{:S(2)}) %collective-permute-start.35) | collective-permute-done | bytes 278560 | tf_op jit(solution)/shard_map/ppermute | solution.py:929
  185.5 1.8 collective-permute-done.37.refs_2_
  188.5 2.5 %shard_map.236 = (f32[2,4,256,256]{3,2,1,0:T(8,128)}, f32[2,4,256,256]{3,2,1,0:T(8,128)}, f32[2,4,256]{2,1,0:T(4,128)}, f32[2,4,256]{2,1,0:T(4,128)}) custom-call(s32[3]{0:T(128)S(1)} %copy-done, bf16[1088,256]{1,0:T(8,128)(2,1)S(1)} %pad_maximum_fusion.1.refs_1_, ...), custom_call_target="tpu_custom_call", output_to_operand_aliasing={{0}: (3, {}), {1}: (4, {})} | custom-call | bytes 3145728 | tf_op jit(solution)/shard_map/pallas_call | solution.py:912
  (176 shorter events, 42.6 us)
Async XLA Ops:
  2.7 15.4 %collective-permute-start = (bf16[2,528,256]{2,1,0:T(8,128)(2,1)S(1)}, bf16[2,528,256]{2,1,0:T(8,128)(2,1)}, u32[]{:S(2)}, u32[]{:S(2)}) collective-permute-start(bf16[2,528,256]{2,1,0:T(8,128)(2,1)S(1)} %pad_maximum_fusion.2.refs_3_.refs_18_), channel_id=1, source_target_pairs={{0,1},{1,0},{2,3},{3,2},{4,5},{5,4},{6,7},{7,6},{8,9},{9,8},{10,11... | collective-permute-start | bytes 1622024 | tf_op jit(solution)/shard_map/ppermute | solution.py:929
  5.7 13.8 %collective-permute-start.1 = (bf16[2,528,256]{2,1,0:T(8,128)(2,1)S(1)}, bf16[2,528,256]{2,1,0:T(8,128)(2,1)}, u32[]{:S(2)}, u32[]{:S(2)}) collective-permute-start(bf16[2,528,256]{2,1,0:T(8,128)(2,1)S(1)} %pad_maximum_fusion.2.refs_3_.refs_18_), channel_id=1, source_target_pairs={{0,2},{1,3},{2,0},{3,1},{4,6},{5,7},{6,4},{7,5},{8,10},{9,11},{10,... | collective-permute-start | bytes 1622024 | tf_op jit(solution)/shard_map/ppermute | solution.py:929
  19.6 6.6 %collective-permute-start.3 = (bf16[2,528,256]{2,1,0:T(8,128)(2,1)}, bf16[2,528,256]{2,1,0:T(8,128)(2,1)S(1)}, u32[]{:S(2)}, u32[]{:S(2)}) collective-permute-start(bf16[2,528,256]{2,1,0:T(8,128)(2,1)} %collective-permute-done.1.refs_7_.refs_22_), channel_id=1, source_target_pairs={{0,4},{4,0},{8,12},{12,8},{16,20},{20,16},{24,28},{28,24},{1,5},{5... | collective-permute-start | bytes 1622024 | tf_op jit(solution)/shard_map/ppermute | solution.py:929
  20.1 21.3 %collective-permute-start.8 = (bf16[2,528,256]{2,1,0:T(8,128)(2,1)S(1)}, bf16[2,528,256]{2,1,0:T(8,128)(2,1)S(1)}, u32[]{:S(2)}, u32[]{:S(2)}) collective-permute-start(bf16[2,528,256]{2,1,0:T(8,128)(2,1)S(1)} %pad_maximum_fusion.4.refs_10_.refs_16_), channel_id=1, source_target_pairs={{0,1},{1,0},{2,3},{3,2},{4,5},{5,4},{6,7},{7,6},{8,9},{9,8},{10,11... | collective-permute-start | bytes 1622024 | tf_op jit(solution)/shard_map/ppermute | solution.py:929
  20.5 22.6 %collective-permute-start.10 = (bf16[2,528,256]{2,1,0:T(8,128)(2,1)S(1)}, bf16[2,528,256]{2,1,0:T(8,128)(2,1)S(1)}, u32[]{:S(2)}, u32[]{:S(2)}) collective-permute-start(bf16[2,528,256]{2,1,0:T(8,128)(2,1)S(1)} %pad_maximum_fusion.4.refs_10_.refs_16_), channel_id=1, source_target_pairs={{0,2},{1,3},{2,0},{3,1},{4,6},{5,7},{6,4},{7,5},{8,10},{9,11},{10,... | collective-permute-start | bytes 1622024 | tf_op jit(solution)/shard_map/ppermute | solution.py:929
  24.1 16.7 %collective-permute-start.4 = (bf16[1,528,256]{2,1,0:T(8,128)(2,1)S(1)}, bf16[1,528,256]{2,1,0:T(8,128)(2,1)S(1)}, u32[]{:S(2)}, u32[]{:S(2)}) collective-permute-start(bf16[1,528,256]{2,1,0:T(8,128)(2,1)S(1)} %slice.102), channel_id=1, source_target_pairs={{0,2},{1,3},{2,0},{3,1},{4,6},{5,7},{6,4},{7,5},{8,10},{9,11},{10,... | collective-permute-start | bytes 811016 | tf_op jit(solution)/shard_map/ppermute | solution.py:929
  24.5 16.3 %collective-permute-start.5 = (bf16[1,528,256]{2,1,0:T(8,128)(2,1)S(1)}, bf16[1,528,256]{2,1,0:T(8,128)(2,1)S(1)}, u32[]{:S(2)}, u32[]{:S(2)}) collective-permute-start(bf16[1,528,256]{2,1,0:T(8,128)(2,1)S(1)} %slice.103), channel_id=1, source_target_pairs={{0,1},{1,0},{2,3},{3,2},{4,5},{5,4},{6,7},{7,6},{8,9},{9,8},{10,11... | collective-permute-start | bytes 811016 | tf_op jit(solution)/shard_map/ppermute | solution.py:929
  41.5 11.0 %collective-permute-start.12 = (bf16[1,528,256]{2,1,0:T(8,128)(2,1)S(1)}, bf16[1,528,256]{2,1,0:T(8,128)(2,1)S(1)}, u32[]{:S(2)}, u32[]{:S(2)}) collective-permute-start(bf16[1,528,256]{2,1,0:T(8,128)(2,1)S(1)} %slice.134), channel_id=1, source_target_pairs={{0,2},{1,3},{2,0},{3,1},{4,6},{5,7},{6,4},{7,5},{8,10},{9,11},{10,... | collective-permute-start | bytes 811016 | tf_op jit(solution)/shard_map/ppermute | solution.py:929
  43.1 9.4 %collective-permute-start.13 = (bf16[1,528,256]{2,1,0:T(8,128)(2,1)S(1)}, bf16[1,528,256]{2,1,0:T(8,128)(2,1)S(1)}, u32[]{:S(2)}, u32[]{:S(2)}) collective-permute-start(bf16[1,528,256]{2,1,0:T(8,128)(2,1)S(1)} %slice.135), channel_id=1, source_target_pairs={{0,1},{1,0},{2,3},{3,2},{4,5},{5,4},{6,7},{7,6},{8,9},{9,8},{10,11... | collective-permute-start | bytes 811016 | tf_op jit(solution)/shard_map/ppermute | solution.py:929
  44.1 9.0 %collective-permute-start.9 = (bf16[2,528,256]{2,1,0:T(8,128)(2,1)S(1)}, bf16[2,528,256]{2,1,0:T(8,128)(2,1)S(1)}, u32[]{:S(2)}, u32[]{:S(2)}) collective-permute-start(bf16[2,528,256]{2,1,0:T(8,128)(2,1)S(1)} %collective-permute-done.8.refs_12_), channel_id=1, source_target_pairs={{0,4},{4,0},{8,12},{12,8},{16,20},{20,16},{24,28},{28,24},{1,5},{5... | collective-permute-start | bytes 1622024 | tf_op jit(solution)/shard_map/ppermute | solution.py:929
  44.1 9.0 %collective-permute-start.11 = (bf16[2,528,256]{2,1,0:T(8,128)(2,1)S(1)}, bf16[2,528,256]{2,1,0:T(8,128)(2,1)S(1)}, u32[]{:S(2)}, u32[]{:S(2)}) collective-permute-start(bf16[2,528,256]{2,1,0:T(8,128)(2,1)S(1)} %collective-permute-done.10.refs_14_), channel_id=1, source_target_pairs={{0,4},{4,0},{8,12},{12,8},{16,20},{20,16},{24,28},{28,24},{1,5},{5... | collective-permute-start | bytes 1622024 | tf_op jit(solution)/shard_map/ppermute | solution.py:929
  90.5 29.2 %collective-permute-start.23 = (bf16[1216,256]{1,0:T(8,128)(2,1)S(1)}, bf16[1216,256]{1,0:T(8,128)(2,1)S(1)}, u32[]{:S(2)}, u32[]{:S(2)}) collective-permute-start(bf16[1216,256]{1,0:T(8,128)(2,1)S(1)} %get-tuple-element.163), channel_id=1, source_target_pairs={{0,1},{1,0},{2,3},{3,2},{4,5},{5,4},{6,7},{7,6},{8,9},{9,8},{10,11... | collective-permute-start | bytes 1867784 | tf_op jit(solution)/shard_map/ppermute | solution.py:929
  91.5 29.1 %collective-permute-start.24 = (bf16[1216,256]{1,0:T(8,128)(2,1)S(1)}, bf16[1216,256]{1,0:T(8,128)(2,1)S(1)}, u32[]{:S(2)}, u32[]{:S(2)}) collective-permute-start(bf16[1216,256]{1,0:T(8,128)(2,1)S(1)} %get-tuple-element.164), channel_id=1, source_target_pairs={{0,2},{1,3},{2,0},{3,1},{4,6},{5,7},{6,4},{7,5},{8,10},{9,11},{10,... | collective-permute-start | bytes 1867784 | tf_op jit(solution)/shard_map/ppermute | solution.py:929
  92.0 28.6 %collective-permute-start.25 = (bf16[1216,256]{1,0:T(8,128)(2,1)}, bf16[1216,256]{1,0:T(8,128)(2,1)S(1)}, u32[]{:S(2)}, u32[]{:S(2)}) collective-permute-start(bf16[1216,256]{1,0:T(8,128)(2,1)} %get-tuple-element.165), channel_id=1, source_target_pairs={{0,3},{1,2},{2,1},{3,0},{4,7},{5,6},{6,5},{7,4},{8,11},{9,10},{10,... | collective-permute-start | bytes 1867784 | tf_op jit(solution)/shard_map/ppermute | solution.py:929
  126.2 9.5 %collective-permute-start.30 = (bf16[608,256]{1,0:T(8,128)(2,1)S(1)}, bf16[608,256]{1,0:T(8,128)(2,1)S(1)}, u32[]{:S(2)}, u32[]{:S(2)}) collective-permute-start(bf16[608,256]{1,0:T(8,128)(2,1)S(1)} %get-tuple-element.250), channel_id=1, source_target_pairs={{0,8},{4,12},{8,0},{12,4},{16,24},{20,28},{24,16},{28,20},{1,9},{5... | collective-permute-start | bytes 933896 | tf_op jit(solution)/shard_map/ppermute | solution.py:929
  127.9 15.5 %collective-permute-start.26 = (bf16[1088,256]{1,0:T(8,128)(2,1)S(1)}, bf16[1088,256]{1,0:T(8,128)(2,1)S(1)}, u32[]{:S(2)}, u32[]{:S(2)}) collective-permute-start(bf16[1088,256]{1,0:T(8,128)(2,1)S(1)} %get-tuple-element.178), channel_id=1, source_target_pairs={{0,1},{1,0},{2,3},{3,2},{4,5},{5,4},{6,7},{7,6},{8,9},{9,8},{10,11... | collective-permute-start | bytes 1671176 | tf_op jit(solution)/shard_map/ppermute | solution.py:929
  128.9 26.0 %collective-permute-start.27 = (bf16[1088,256]{1,0:T(8,128)(2,1)S(1)}, bf16[1088,256]{1,0:T(8,128)(2,1)S(1)}, u32[]{:S(2)}, u32[]{:S(2)}) collective-permute-start(bf16[1088,256]{1,0:T(8,128)(2,1)S(1)} %get-tuple-element.179), channel_id=1, source_target_pairs={{0,2},{1,3},{2,0},{3,1},{4,6},{5,7},{6,4},{7,5},{8,10},{9,11},{10,... | collective-permute-start | bytes 1671176 | tf_op jit(solution)/shard_map/ppermute | solution.py:929
  129.4 25.5 %collective-permute-start.28 = (bf16[1088,256]{1,0:T(8,128)(2,1)S(1)}, bf16[1088,256]{1,0:T(8,128)(2,1)S(1)}, u32[]{:S(2)}, u32[]{:S(2)}) collective-permute-start(bf16[1088,256]{1,0:T(8,128)(2,1)S(1)} %get-tuple-element.180), channel_id=1, source_target_pairs={{0,3},{1,2},{2,1},{3,0},{4,7},{5,6},{6,5},{7,4},{8,11},{9,10},{10,... | collective-permute-start | bytes 1671176 | tf_op jit(solution)/shard_map/ppermute | solution.py:929
  131.4 23.6 %collective-permute-start.29 = (bf16[1088,256]{1,0:T(8,128)(2,1)S(1)}, bf16[1088,256]{1,0:T(8,128)(2,1)S(1)}, u32[]{:S(2)}, u32[]{:S(2)}) collective-permute-start(bf16[1088,256]{1,0:T(8,128)(2,1)S(1)} %copy-done.17), channel_id=1, source_target_pairs={{0,4},{4,0},{8,12},{12,8},{16,20},{20,16},{24,28},{28,24},{1,5},{5... | collective-permute-start | bytes 1671176 | tf_op jit(solution)/shard_map/ppermute | solution.py:929
  135.8 19.2 %collective-permute-start.31 = (bf16[608,256]{1,0:T(8,128)(2,1)S(1)}, bf16[608,256]{1,0:T(8,128)(2,1)S(1)}, u32[]{:S(2)}, u32[]{:S(2)}) collective-permute-start(bf16[608,256]{1,0:T(8,128)(2,1)S(1)} %add_convert_fusion.9), channel_id=1, source_target_pairs={{0,16},{4,20},{8,24},{12,28},{16,0},{20,4},{24,8},{28,12},{1,17},{... | collective-permute-start | bytes 933896 | tf_op jit(solution)/shard_map/ppermute | solution.py:929
  155.5 6.8 %collective-permute-start.32 = (bf16[544,256]{1,0:T(8,128)(2,1)S(1)}, bf16[544,256]{1,0:T(8,128)(2,1)S(1)}, u32[]{:S(2)}, u32[]{:S(2)}) collective-permute-start(bf16[544,256]{1,0:T(8,128)(2,1)S(1)} %get-tuple-element.254), channel_id=1, source_target_pairs={{0,8},{4,12},{8,0},{12,4},{16,24},{20,28},{24,16},{28,20},{1,9},{5... | collective-permute-start | bytes 835592 | tf_op jit(solution)/shard_map/ppermute | solution.py:929
  162.4 12.6 %collective-permute-start.34 = (bf16[608,256]{1,0:T(8,128)(2,1)S(1)}, bf16[608,256]{1,0:T(8,128)(2,1)S(1)}, u32[]{:S(2)}, u32[]{:S(2)}) collective-permute-start(bf16[608,256]{1,0:T(8,128)(2,1)S(1)} %add_convert_fusion.8), channel_id=1, source_target_pairs={{0,8},{4,12},{8,0},{12,4},{16,24},{20,28},{24,16},{28,20},{1,9},{5... | collective-permute-start | bytes 933896 | tf_op jit(solution)/shard_map/ppermute | solution.py:929
  162.9 10.4 %collective-permute-start.33 = (bf16[544,256]{1,0:T(8,128)(2,1)S(1)}, bf16[544,256]{1,0:T(8,128)(2,1)S(1)}, u32[]{:S(2)}, u32[]{:S(2)}) collective-permute-start(bf16[544,256]{1,0:T(8,128)(2,1)S(1)} %add_convert_fusion.11), channel_id=1, source_target_pairs={{0,16},{4,20},{8,24},{12,28},{16,0},{20,4},{24,8},{28,12},{1,17},{... | collective-permute-start | bytes 835592 | tf_op jit(solution)/shard_map/ppermute | solution.py:929
  175.3 9.9 %collective-permute-start.35 = (bf16[544,256]{1,0:T(8,128)(2,1)S(1)}, bf16[544,256]{1,0:T(8,128)(2,1)S(1)}, u32[]{:S(2)}, u32[]{:S(2)}) collective-permute-start(bf16[544,256]{1,0:T(8,128)(2,1)S(1)} %add_convert_fusion.10), channel_id=1, source_target_pairs={{0,8},{4,12},{8,0},{12,4},{16,24},{20,28},{24,16},{28,20},{1,9},{5... | collective-permute-start | bytes 835592 | tf_op jit(solution)/shard_map/ppermute | solution.py:929
  (40 other events, 193.8 us)
